TPU v7x, 32 devices: a whole 2x2x4 slice. The times are simulated.
32 devices in a mesh: grp: 2 (over y), slc: 4 (over z), coil: 2 (over x), vol: 2 (over core).
Axes of the slice: x: 2, y: 2, z: 4, core: 2. Of those that a mesh axis runs over, the one named last changes fastest.
Arguments:
- images: bfloat16 [4, 32, 2, 220, 220], P(('grp', 'vol'), 'slc'), parts along dimension 0, may hold values from -6 to 6
- coil_maps: bfloat16 [8, 32, 2, 220, 220], P(('grp', 'coil'), 'slc'), parts along dimension 0, may hold values from -3 to 3
- kspace: bfloat16 [4, 4, 4, 2, 220, 220], P(('grp', 'vol'), 'slc', 'coil'), parts along dimension 0, may hold values from -12 to 12
- shift_index: int32 [32], P('slc'), may hold values from 0 to 7
- phase_offset: float32 [32, 220], P('slc'), may hold values from -3.140625 to 3.140625
- group_order: int32 [4], replicated, may hold values from 0 to 3, each once
Outputs:
- grad_phase: float32 [64, 220], P(('grp', 'slc')), parts along dimension 0
There are 2 independent parts, one for each index of `grp`. A program takes and returns all parts, laid end to end along the dimension named above; an argument that names none is the same for every part. Nothing has to cross between parts.
Inputs may be any that keep to these rules, and one draw needn't show every extreme that they name: group_order names each of the 4 measured rows exactly once.
All inputs are finite; a program needn't handle non-finite values.
Results may differ from a plain program's by a relative error of at most 0.0096.
Values may be sent and summed in bfloat16 or wider, within the bound.
No kernel may reach another device: no remote copies, remote signals or barrier semaphores. Data moves between devices by JAX's collectives and lax.ppermute only.
A program may use at most 64 MiB of HBM per device.

v0:
```python
import math

import jax
import jax.numpy as jnp
from jax import lax
from jax.sharding import PartitionSpec as P

MB = 8


def fourier_tables(length):
    positions = jnp.arange(length, dtype=jnp.int32)
    product = positions[:, None] * positions[None, :] % length
    radians = 2.0 * math.pi / length * product.astype(jnp.float32)
    factor = 1.0 / math.sqrt(length)
    return (
        (jnp.cos(radians) * factor).astype(jnp.bfloat16),
        (-jnp.sin(radians) * factor).astype(jnp.bfloat16),
    )


def slice_phases(shift_index, phase_offset, length):
    lines = (jnp.arange(length, dtype=jnp.int32) - length // 2).astype(jnp.float32)
    return (
        2.0 * math.pi / MB * (shift_index.astype(jnp.float32)[:, None] * lines[None, :])
        + phase_offset
    )


def body(images, coil_maps, kspace, shift_index, phase_offset, group_order):
    per_device = images.shape[1]
    matrix = images.shape[-1]
    groups = lax.axis_size("slc")
    spread = max(1, per_device // groups)
    slot_count = groups * spread
    cos_table, sin_table = fourier_tables(matrix)
    section_one = jnp.stack([jnp.stack([cos_table, -sin_table]), jnp.stack([sin_table, cos_table])])
    section_two = jnp.stack([jnp.stack([cos_table, sin_table]), jnp.stack([-sin_table, cos_table])])
    image_re = images[:, None, :, 0].astype(jnp.float32)
    image_im = images[:, None, :, 1].astype(jnp.float32)
    map_re = coil_maps[None, :, :, 0].astype(jnp.float32)
    map_im = coil_maps[None, :, :, 1].astype(jnp.float32)
    coil_image = jnp.stack(
        [map_re * image_re - map_im * image_im, map_re * image_im + map_im * image_re], axis=3
    ).astype(jnp.bfloat16)
    partly = jnp.einsum(
        "pqky,tcsqyx->tcspkx", section_one, coil_image, preferred_element_type=jnp.float32
    ).astype(jnp.bfloat16)
    spectra = jnp.einsum(
        "tcsqyx,qpkx->tcspyk", partly, section_two, preferred_element_type=jnp.float32
    )
    phase_angle = slice_phases(shift_index, phase_offset, matrix)
    cosine = jnp.cos(phase_angle)[None, None, :, :, None]
    sine = jnp.sin(phase_angle)[None, None, :, :, None]
    spec_re = spectra[:, :, :, 0]
    spec_im = spectra[:, :, :, 1]
    shifted = jnp.stack(
        [spec_re * cosine - spec_im * sine, spec_re * sine + spec_im * cosine], axis=3
    ).astype(jnp.bfloat16)
    position = lax.axis_index("slc")
    within = jnp.arange(per_device, dtype=jnp.int32)
    classes = (position * per_device + within) % groups
    class_match = (classes[:, None] == jnp.arange(groups, dtype=jnp.int32)[None, :]).astype(
        jnp.int32
    )
    target = jnp.sum(class_match * group_order[None, :], axis=1)
    slot_index = target * spread + within // groups
    onehot = (jnp.arange(slot_count, dtype=jnp.int32)[:, None] == slot_index[None, :]).astype(
        jnp.int32
    )
    source = jnp.sum(onehot * within[None, :], axis=1)
    filled = jnp.sum(onehot, axis=1)
    outgoing = jnp.take(shifted, source, axis=2)
    outgoing = jnp.where(
        filled[None, None, :, None, None, None] > 0, outgoing, jnp.zeros_like(outgoing)
    )
    incoming = lax.all_to_all(outgoing, "slc", split_axis=2, concat_axis=2, tiled=True)
    aliased = jnp.sum(incoming, axis=2, dtype=jnp.float32)
    residual = (aliased - kspace[:, 0].astype(jnp.float32)).astype(jnp.bfloat16)
    partial_value = jnp.einsum(
        "tcpyx,tcyx->py",
        incoming[:, :, :, 0],
        residual[:, :, 1],
        preferred_element_type=jnp.float32,
    )
    partial_value = partial_value - jnp.einsum(
        "tcpyx,tcyx->py",
        incoming[:, :, :, 1],
        residual[:, :, 0],
        preferred_element_type=jnp.float32,
    )
    returned = lax.all_to_all(partial_value, "slc", split_axis=0, concat_axis=0, tiled=True)
    local_grad = jnp.dot(onehot.T.astype(jnp.float32), returned, precision=lax.Precision.HIGHEST)
    summed = lax.psum(local_grad, "coil")
    summed = lax.psum(summed, "vol")
    factor = 1.0 / (
        coil_maps.shape[0] * lax.axis_size("coil") * images.shape[0] * lax.axis_size("vol")
    )
    return summed * factor


def solution(mesh):
    placed = (
        P(("grp", "vol"), "slc", None, None, None),
        P(("grp", "coil"), "slc", None, None, None),
        P(("grp", "vol"), "slc", "coil", None, None, None),
        P("slc"),
        P("slc", None),
        P(),
    )
    return jax.shard_map(
        body, mesh=mesh, in_specs=placed, out_specs=P(("grp", "slc"), None), check_vma=False
    )
```

profile of v0, /device:TPU:0, one launch (start us, length us, event | category | flops | bytes accessed | tf_op | source)
XLA Modules:
  0.0 203.2 jit_solution(2907559436263162743)
XLA Ops:
  0.0 1.0 multiply_convert_fusion
  2.0 13.7 %fusion.50 = (bf16[2,8,1,220,220]{4,2,3,1,0:T(2,128)(2,1)}, bf16[2,8,1,220,220]{4,2,3,1,0:T(2,128)(2,1)}) fusion(bf16[2,8,2,220,220]{4,2,3,1,0:T(2,128)(2,1)} %param.7), kind=kLoop, calls=%fused_computation.93 | loop fusion | bytes 6195200 | tf_op jit(solution)/shard_map/slice | solution.py:42
  15.6 8.6 %copy.97 = bf16[2,8,1,220,220]{3,4,2,1,0:T(8,128)(2,1)} copy(bf16[2,8,1,220,220]{4,2,3,1,0:T(2,128)(2,1)} %get-tuple-element.14) | data formatting | bytes 3097600
  24.2 8.7 %copy.99 = bf16[2,8,1,220,220]{3,4,2,1,0:T(8,128)(2,1)} copy(bf16[2,8,1,220,220]{4,2,3,1,0:T(2,128)(2,1)} %get-tuple-element.13) | data formatting | bytes 3097600
  32.9 2.5 %fusion.51 = (bf16[1,8,1,220,220]{4,2,3,1,0:T(2,128)(2,1)S(1)}, bf16[1,8,1,220,220]{4,2,3,1,0:T(2,128)(2,1)S(1)}) fusion(bf16[1,8,2,220,220]{4,2,3,1,0:T(2,128)(2,1)S(1)} %copy-done), kind=kLoop, calls=%fused_computation.94 | loop fusion | bytes 3097600 | tf_op jit(solution)/shard_map/slice | solution.py:39
  35.4 2.4 %fusion.19 = (f32[8,220,220]{2,0,1:T(8,128)}, f32[8,220,220]{2,0,1:T(8,128)}) fusion(bf16[1,8,1,220,220]{4,2,3,1,0:T(2,128)(2,1)S(1)} %get-tuple-element.16, bf16[1,8,1,220,220]{4,2,3,1,0:T(2,128)(2,1)S(1)} %get-tuple-element.15), kind=kLoop, calls=%fused_computation.32 | loop fusion | flops 774400 | bytes 4646400 | tf_op jit(solution)/shard_map/convert_element_type | solution.py:40
  37.8 2.1 %copy.70 = f32[8,220,220]{1,2,0:T(8,128)S(1)} copy(f32[8,220,220]{2,0,1:T(8,128)} %get-tuple-element.27) | data formatting | bytes 3097600 | tf_op jit(solution)/shard_map/convert_element_type | solution.py:40
  39.9 2.8 %copy.67 = f32[8,220,220]{1,2,0:T(8,128)} copy(f32[8,220,220]{2,0,1:T(8,128)} %get-tuple-element.28) | data formatting | bytes 3097600 | tf_op jit(solution)/shard_map/convert_element_type | solution.py:39
  43.2 5.7 %fusion.1 = (bf16[2,8,1,220,220]{3,4,2,1,0:T(8,128)(2,1)}, bf16[2,8,1,220,220]{3,4,2,1,0:T(8,128)(2,1)}) fusion(bf16[2,8,1,220,220]{3,4,2,1,0:T(8,128)(2,1)} %copy.97, bf16[2,8,1,220,220]{3,4,2,1,0:T(8,128)(2,1)} %copy.99, f32[8,220,220]{1,2,0:T(8,128)S(1)} %copy.70, f32[8,220,220]{1,2,0:T(8,128)} %copy.67), kind=kLoop, calls=%fused_computation.8 | loop fusion | flops 7744000 | bytes 9292800 | tf_op jit(solution)/shard_map/convert.5
  49.0 9.0 %fusion.11 = f32[1,2,8,2,220,220]{4,5,2,1,3,0:T(8,128)} fusion(bf16[2,8,1,220,220]{3,4,2,1,0:T(8,128)(2,1)} %get-tuple-element.10, bf16[2,8,1,220,220]{3,4,2,1,0:T(8,128)(2,1)} %get-tuple-element.9, bf16[1,2,220,220]{3,2,1,0:T(8,128)(2,1)S(1)} %get-tuple-element.20, bf16[1,2,220,220]{3,2,1,0:T(8,128)(2,1)S(1)} %get-tuple-element.23, ...), kind=kOutput, calls=%fused_computation.22 | convolution fusion | flops 2734599936 | bytes 10067200 | tf_op jit(solution)/shard_map/tcsqyx,qpkx->tcspyk/dot_general | solution.py:49
  58.0 4.3 %subtract_convert_fusion = (bf16[1,2,8,1,220,220]{4,5,2,1,3,0:T(8,128)(2,1)S(1)}, bf16[1,2,8,1,220,220]{4,5,2,1,3,0:T(8,128)(2,1)S(1)}) fusion(f32[1,2,8,2,220,220]{4,5,2,1,3,0:T(8,128)} %fusion.11, f32[8,220]{1,0:T(8,128)S(1)} %get-tuple-element.26, f32[8,220]{1,0:T(8,128)S(1)} %get-tuple-element.25), kind=kLoop, calls=%fused_computation.21 | loop fusion | flops 6195200 | bytes 9306880 | tf_op jit(solution)/shard_map/convert.3
  62.3 2.5 %maximum_bitcast_fusion.2 = bf16[2,8,2,220,220]{3,4,1,0,2:T(8,128)(2,1)} fusion(bf16[1,2,8,1,220,220]{4,5,2,1,3,0:T(8,128)(2,1)S(1)} %get-tuple-element.8, bf16[1,2,8,1,220,220]{4,5,2,1,3,0:T(8,128)(2,1)S(1)} %get-tuple-element.7), kind=kLoop, calls=%fused_computation.17 | loop fusion | flops 1548800 | bytes 6195200 | tf_op jit(solution)/shard_map/stack | solution.py:57
  64.8 4.7 %gather_fusion = bf16[8,2,2,220,220]{3,4,1,2,0:T(8,128)(2,1)} fusion(bf16[2,8,2,220,220]{3,4,1,0,2:T(8,128)(2,1)} %maximum_bitcast_fusion.2, s32[1024]{0:T(1024)S(1)} %pad_clamp_fusion), kind=kCustom, calls=%fused_computation | custom fusion | bytes 6195232 | tf_op jit(solution)/shard_map/jit(_take)/gather | solution.py:73
  69.5 4.3 %fusion.10 = bf16[1,2,8,2,220,220]{4,5,1,3,2,0:T(8,128)(2,1)} fusion(bf16[8,2,2,220,220]{3,4,1,2,0:T(8,128)(2,1)} %gather_fusion, pred[8]{0:T(512)(128)(4,1)S(1)} %get-tuple-element.31, pred[8]{0:T(512)(128)(4,1)S(1)} %get-tuple-element.32), kind=kLoop, calls=%fused_computation.19 | loop fusion | flops 3097600 | bytes 6195216 | tf_op jit(solution)/shard_map/jit(_where)/select_n | solution.py:74
  73.8 11.0 %copy.73 = bf16[1,2,8,2,220,220]{5,3,4,1,0,2:T(2,128)(2,1)} copy(bf16[1,2,8,2,220,220]{4,5,1,3,2,0:T(8,128)(2,1)} %fusion.10) | data formatting | bytes 6195200 | tf_op jit(solution)/shard_map/jit(_where)/select_n | solution.py:74
  84.8 6.5 %all-to-all-start = ((bf16[1,2,8,2,220,220]{5,3,4,1,0,2:T(2,128)(2,1)}), bf16[1,2,8,2,220,220]{5,3,4,1,0,2:T(2,128)(2,1)}, u32[]{:S(2)}, u32[]{:S(2)}) async-start(bf16[1,2,8,2,220,220]{5,3,4,1,0,2:T(2,128)(2,1)} %copy.73), calls=%async_computation | async-start | bytes 7208960 | tf_op jit(solution)/shard_map/all_to_all | solution.py:77
  91.7 80.5 %all-to-all-done = bf16[1,2,8,2,220,220]{5,3,4,1,0,2:T(2,128)(2,1)} async-done(((bf16[1,2,8,2,220,220]{5,3,4,1,0,2:T(2,128)(2,1)}), bf16[1,2,8,2,220,220]{5,3,4,1,0,2:T(2,128)(2,1)}, u32[]{:S(2)}, u32[]{:S(2)}) %all-to-all-start) | async-done | bytes 3097632 | tf_op jit(solution)/shard_map/all_to_all | solution.py:77
  172.2 3.3 %copy.74 = bf16[1,2,8,2,220,220]{5,2,4,3,1,0:T(8,128)(2,1)S(1)} copy(bf16[1,2,8,2,220,220]{5,3,4,1,0,2:T(2,128)(2,1)} %all-to-all-done) | data formatting | bytes 6195200 | tf_op jit(solution)/shard_map/all_to_all | solution.py:77
  175.5 2.0 %slice_bitcast_fusion.1 = (bf16[2,8,220,220]{3,1,2,0:T(8,128)(2,1)}, bf16[2,8,220,220]{3,1,2,0:T(8,128)(2,1)}) fusion(bf16[1,2,8,2,220,220]{5,2,4,3,1,0:T(8,128)(2,1)S(1)} %copy.74), kind=kLoop, calls=%fused_computation.24 | loop fusion | bytes 6195200 | tf_op jit(solution)/shard_map/reshape.15
  177.5 5.2 %convert_reduce_fusion = f32[2,2,220,220]{3,2,1,0:T(8,128)S(1)} fusion(bf16[1,2,8,2,220,220]{5,3,4,1,0,2:T(2,128)(2,1)} %all-to-all-done), kind=kLoop, calls=%fused_computation.2 | loop fusion | flops 2904000 | bytes 3872000 | tf_op jit(solution)/shard_map/reduce_sum | solution.py:78
  183.3 2.4 %fusion.14 = f32[220,1,8,1]{2,1,3,0:T(1,128)S(1)} fusion(bf16[2,8,220,220]{3,1,2,0:T(8,128)(2,1)} %get-tuple-element.12, bf16[2,220,220,1]{2,1,0,3:T(8,128)(2,1)S(1)} %bitcast.99), kind=kOutput, calls=%fused_computation.25 | convolution fusion | flops 1548800 | bytes 1749440 | tf_op jit(solution)/shard_map/tcpyx,tcyx->py/dot_general | solution.py:86
  186.9 8.0 %all_to_all.17 = f32[4,2,220]{2,1,0:T(2,128)S(1)} all-to-all(f32[4,2,220]{2,1,0:T(2,128)S(1)} %all_to_all.12), channel_id=1, replica_groups=mesh['grp'=2,'slc'=4,'coil'=2,'vol'=2] {'slc'}, dimensions={0} | all-to-all | bytes 14080 | tf_op jit(solution)/shard_map/all_to_all | solution.py:92
  195.2 5.0 %psum.14 = f32[8,220]{1,0:T(8,128)S(1)} all-reduce(f32[8,220]{1,0:T(8,128)S(1)} %fusion.41), channel_id=1, replica_groups=mesh['grp'=2,'slc'=4,'coil'=2,'vol'=2] {'coil'}, use_global_device_ids=true, to_apply=%region_4.5 | all-reduce | flops 1760 | bytes 14080 | tf_op jit(solution)/shard_map/psum | solution.py:94
  200.2 2.5 %psum.15 = f32[8,220]{1,0:T(8,128)S(1)} all-reduce(f32[8,220]{1,0:T(8,128)S(1)} %psum.14), channel_id=1, replica_groups=mesh['grp'=2,'slc'=4,'coil'=2,'vol'=2] {'vol'}, use_global_device_ids=true, to_apply=%region_5.6 | all-reduce | flops 1760 | bytes 14080 | tf_op jit(solution)/shard_map/psum | solution.py:95
  (38 shorter events, 4.4 us)
Async XLA Ops:
  24.2 8.7 %copy-start = (bf16[1,8,2,220,220]{4,2,3,1,0:T(2,128)(2,1)S(1)}, bf16[1,8,2,220,220]{4,2,3,1,0:T(2,128)(2,1)}, u32[]{:S(2)}) copy-start(bf16[1,8,2,220,220]{4,2,3,1,0:T(2,128)(2,1)} %param.6) | copy-start | bytes 4646404
  37.8 4.9 %copy-start.4 = (s32[8]{0:T(128)S(1)}, s32[8]{0:T(128)}, u32[]{:S(2)}) copy-start(s32[8]{0:T(128)} %param.9) | copy-start | bytes 100
  37.8 4.9 %copy-start.5 = (s32[4]{0:T(128)S(1)}, s32[4]{0:T(128)}, u32[]{:S(2)}) copy-start(s32[4]{0:T(128)} %param.11) | copy-start | bytes 52
  37.8 5.3 %copy-start.3 = (f32[8,220]{1,0:T(8,128)S(1)}, f32[8,220]{1,0:T(8,128)}, u32[]{:S(2)}) copy-start(f32[8,220]{1,0:T(8,128)} %param.10) | copy-start | bytes 21124
  84.8 6.5 %copy-start.2 = (bf16[1,1,2,2,220,220]{5,3,4,2,1,0:T(2,128)(2,1)S(1)}, bf16[1,1,2,2,220,220]{5,3,4,2,1,0:T(2,128)(2,1)}, u32[]{:S(2)}) copy-start(bf16[1,1,2,2,220,220]{5,3,4,2,1,0:T(2,128)(2,1)} %param.8) | copy-start | bytes 1161604
  84.8 87.3 %all-to-all-start = ((bf16[1,2,8,2,220,220]{5,3,4,1,0,2:T(2,128)(2,1)}), bf16[1,2,8,2,220,220]{5,3,4,1,0,2:T(2,128)(2,1)}, u32[]{:S(2)}, u32[]{:S(2)}) async-start(bf16[1,2,8,2,220,220]{5,3,4,1,0,2:T(2,128)(2,1)} %copy.73), calls=%async_computation | async-start | bytes 7208960 | tf_op jit(solution)/shard_map/all_to_all | solution.py:77
  183.1 2.9 %copy-start.1 = (bf16[2,8,220,220]{3,1,2,0:T(8,128)(2,1)S(1)}, bf16[2,8,220,220]{3,1,2,0:T(8,128)(2,1)}, u32[]{:S(2)}) copy-start(bf16[2,8,220,220]{3,1,2,0:T(8,128)(2,1)} %get-tuple-element.11) | copy-start | bytes 4646404
where the time goes:
time: 204 us; the launch traced here: 203 us
  waiting for transfers between devices  80.5 us (39%)
  local copies, waits for them, and re-layouts  60.6 us (30%)
  other arithmetic  27.6 us (14%)
  blocking collectives  15.5 us (8%)
  matrix products  12.5 us (6%)
  starting transfers between devices  6.46 us (3%)
    all_to_all x1, waiting for transfers between devices, body(): lax.all_to_all(outgoing, 'slc', split_axis=2, concat_axis=2, tiled=True)  80.5 us
    unnamed x16, local copies, waits for them, and re-layouts  18 us
    slice x1, local copies, waits for them, and re-layouts, body(): map_im = coil_maps[None, :, :, 1].astype(jnp.float32)  13.7 us
    select_n x1, local copies, waits for them, and re-layouts, body(): jnp.where(filled[None, None, :, None, None, None] > 0, outgoing, jnp.zero...  11 us
    another operation x2, other arithmetic  10 us
    dot_general x1, matrix products, body(): jnp.einsum('tcsqyx,qpkx->tcspyk', partly, section_two, preferred_element_...  9.01 us
    all_to_all x1, blocking collectives, body(): lax.all_to_all(partial_value, 'slc', split_axis=0, concat_axis=0, tiled=T...  8.03 us
    all_to_all x1, starting transfers between devices, body(): lax.all_to_all(outgoing, 'slc', split_axis=2, concat_axis=2, tiled=True)  6.46 us
  transfers between devices with their start and end apart: 1, of which 1 were waited for; matrix products, arithmetic and copies ran while one was open for 0% of the time, Pallas kernels for 0%

commit v1 on v0

v1 whole, which is shorter than its diff:
```python
import functools
import math

import jax
import jax.numpy as jnp
import ml_dtypes
import numpy as np
from jax import lax
from jax.experimental import pallas as pl
from jax.experimental.pallas import tpu as pltpu
from jax.sharding import PartitionSpec as P

MB = 8
ROW_TILE = 16
LANE_TILE = 128
ROW_PARTS = 2


def round_up(value, multiple):
    return -(-value // multiple) * multiple


def fourier_tables(length):
    positions = np.arange(length, dtype=np.int32)
    product = positions[:, None] * positions[None, :] % length
    radians = np.float32(2.0 * math.pi / length) * product.astype(np.float32)
    factor = np.float32(1.0 / math.sqrt(length))
    return (
        (np.cos(radians) * factor).astype(ml_dtypes.bfloat16),
        (-np.sin(radians) * factor).astype(ml_dtypes.bfloat16),
    )


def dft_matrices(length, rows):
    cos_table, sin_table = fourier_tables(length)
    cosine, sine = cos_table.astype(np.float64), sin_table.astype(np.float64)
    left_re = np.zeros((2 * rows, length), np.float64)
    left_im = np.zeros((2 * rows, length), np.float64)
    left_re[:length], left_re[rows : rows + length] = cosine, sine
    left_im[:length], left_im[rows : rows + length] = -sine, cosine
    gram_re = cosine.T @ cosine + sine.T @ sine
    gram_im = sine.T @ cosine - cosine.T @ sine
    gram = np.stack(
        [np.concatenate([gram_re, gram_im], 1), np.concatenate([-gram_im, gram_re], 1)]
    )
    adjoint = np.stack(
        [np.concatenate([cosine, -sine], 1), np.concatenate([sine, cosine], 1)]
    )
    left = np.stack([left_re, left_im])
    return tuple(part.astype(ml_dtypes.bfloat16) for part in (left, gram, adjoint))


def slice_phases(shift_index, phase_offset, length):
    lines = (jnp.arange(length, dtype=jnp.int32) - length // 2).astype(jnp.float32)
    return (
        2.0 * math.pi / MB * (shift_index.astype(jnp.float32)[:, None] * lines[None, :])
        + phase_offset
    )


def dot(left, right):
    return jnp.dot(left, right, preferred_element_type=jnp.float32)


def encode_kernel(slots, columns, masked, scalars, *refs):
    image_refs, refs = refs[:slots], refs[slots:]
    map_refs, refs = refs[:slots], refs[slots:]
    kspace_ref, phase_ref, left_ref, gram_ref, adjoint_ref = refs[:5]
    shifted_ref = refs[5]
    out_refs = refs[6:-1]
    total = refs[-1]
    vols, coils = image_refs[0].shape[0], map_refs[0].shape[0]
    length = image_refs[0].shape[-1]
    rows = shifted_ref.shape[-2]
    half = phase_ref.shape[1] // 2
    part = rows // len(out_refs)
    if total.shape[1] > vols * coils * 2 * length:
        total[...] = jnp.zeros_like(total)
    for vol in range(vols):
        for coil in range(coils):
            place = vol * coils + coil
            sum_re = sum_im = None
            for slot in range(slots):
                image_re = image_refs[slot][vol, 0, 0].astype(jnp.float32)
                image_im = image_refs[slot][vol, 0, 1].astype(jnp.float32)
                map_re = map_refs[slot][coil, 0, 0].astype(jnp.float32)
                map_im = map_refs[slot][coil, 0, 1].astype(jnp.float32)
                coil_re = (map_re * image_re - map_im * image_im).astype(jnp.bfloat16)
                coil_im = (map_re * image_im + map_im * image_re).astype(jnp.bfloat16)
                partly = dot(left_ref[0], coil_re) + dot(left_ref[1], coil_im)
                column = columns[slot]
                cosine = phase_ref[:, column : column + 1]
                sine = phase_ref[:, half + column : half + column + 1]
                part_re, part_im = partly[:rows], partly[rows:]
                shift_re = part_re * cosine - part_im * sine
                shift_im = part_re * sine + part_im * cosine
                shifted_ref[slot, place, 0] = shift_re.astype(jnp.bfloat16)
                shifted_ref[slot, place, 1] = shift_im.astype(jnp.bfloat16)
                sum_re = shift_re if slot == 0 else sum_re + shift_re
                sum_im = shift_im if slot == 0 else sum_im + shift_im
            mixed = dot(sum_re.astype(jnp.bfloat16), gram_ref[0]) + dot(
                sum_im.astype(jnp.bfloat16), gram_ref[1]
            )
            if masked:
                mixed = jnp.where(scalars[1] > 0, mixed, 0.0)
            total[:, place * 2 * length : (place + 1) * 2 * length] = mixed

    @pl.when(scalars[0] > 0)
    def _():
        for vol in range(vols):
            for coil in range(coils):
                place = vol * coils + coil
                measured = dot(kspace_ref[vol, 0, coil, 0], adjoint_ref[0]) + dot(
                    kspace_ref[vol, 0, coil, 1], adjoint_ref[1]
                )
                total[:length, place * 2 * length : (place + 1) * 2 * length] -= measured

    for index, out_ref in enumerate(out_refs):
        out_ref[...] = total[index * part : (index + 1) * part, :].astype(jnp.bfloat16)


def gradient_kernel(parts, terms, *refs):
    term_refs, shifted_ref, out_ref = refs[:-2], refs[-2], refs[-1]
    slots, places, _, rows, length = shifted_ref.shape
    part = rows // parts
    for index in range(parts):
        residual = None
        for ref in term_refs[index * terms : (index + 1) * terms]:
            value = ref[...].astype(jnp.float32)
            residual = value if residual is None else residual + value
        sums = [None] * slots
        for place in range(places):
            base = place * 2 * length
            resid_re = residual[:, base : base + length]
            resid_im = residual[:, base + length : base + 2 * length]
            for slot in range(slots):
                span = slice(index * part, (index + 1) * part)
                shift_re = shifted_ref[slot, place, 0, span, :].astype(jnp.float32)
                shift_im = shifted_ref[slot, place, 1, span, :].astype(jnp.float32)
                term = resid_im * shift_re - resid_re * shift_im
                sums[slot] = term if place == 0 else sums[slot] + term
        for slot in range(slots):
            out_ref[index, slot : slot + 1, :] = jnp.sum(sums[slot].T, axis=0, keepdims=True)


def chain_steps(count):
    for step in range(1, count):
        up, down = (step - 1, step), (count - step, count - step - 1)
        yield ([up, down],) if up[0] != down[0] else ([up], [down])


def chain_terms(value, axis):
    terms, payload = [value], value
    for rounds in chain_steps(lax.axis_size(axis)):
        arrived = [lax.ppermute(payload, axis, pairs) for pairs in rounds]
        received = functools.reduce(lambda a, b: a + b, arrived)
        terms.append(received)
        payload = value + received
    return terms


def body(images, coil_maps, kspace, shift_index, phase_offset, group_order):
    vols, per_device, _, _, length = images.shape
    coils = coil_maps.shape[0]
    groups = lax.axis_size("slc")
    position = lax.axis_index("slc")
    rows = round_up(length, ROW_TILE * ROW_PARTS)
    part = rows // ROW_PARTS
    places = vols * coils
    lanes = round_up(places * 2 * length, LANE_TILE)
    whole_classes = per_device % groups == 0
    slots = max(1, per_device // groups)
    left, gram, adjoint = dft_matrices(length, rows)

    phase_angle = jnp.pad(
        slice_phases(shift_index, phase_offset, length), ((0, 0), (0, rows - length))
    )
    phases = jnp.concatenate([jnp.cos(phase_angle), jnp.sin(phase_angle)], axis=0).T
    owned = (group_order == position).astype(jnp.int32)

    encoded, pieces = [], []
    for group in range(groups):
        if whole_classes:
            columns = [slot * groups + group for slot in range(slots)]
            scalars = jnp.stack([owned[group], jnp.int32(1)])
            places_of = [lambda i, scalars, w=w: (0, w, 0, 0, 0) for w in columns]
            group_phases = phases
        else:
            within = group - (position * per_device) % groups
            held = (within >= 0) & (within < per_device)
            within = jnp.where(held, within, 0).astype(jnp.int32)
            scalars = jnp.stack([owned[group], held.astype(jnp.int32), within])
            columns = [0]
            places_of = [lambda i, scalars: (0, scalars[2], 0, 0, 0)]
            group_phases = jnp.take(
                phases, jnp.stack([within, within + per_device]), axis=1
            )
        constant = lambda ndim: (lambda i, scalars: (0,) * ndim)
        whole = lambda array: pl.BlockSpec(array.shape, constant(array.ndim))
        outputs = pl.pallas_call(
            functools.partial(encode_kernel, slots, columns, not whole_classes),
            grid_spec=pltpu.PrefetchScalarGridSpec(
                num_scalar_prefetch=1,
                grid=(1,),
                in_specs=[
                    pl.BlockSpec((vols, 1, 2, length, length), place) for place in places_of
                ]
                + [pl.BlockSpec((coils, 1, 2, length, length), place) for place in places_of]
                + [whole(kspace), whole(group_phases), whole(left), whole(gram), whole(adjoint)],
                out_specs=[
                    pl.BlockSpec((slots, places, 2, rows, length), constant(5)),
                ]
                + [pl.BlockSpec((part, lanes), constant(2))] * ROW_PARTS,
                scratch_shapes=[pltpu.VMEM((rows, lanes), jnp.float32)],
            ),
            out_shape=[
                jax.ShapeDtypeStruct((slots, places, 2, rows, length), jnp.bfloat16),
            ]
            + [jax.ShapeDtypeStruct((part, lanes), jnp.bfloat16)] * ROW_PARTS,
            compiler_params=pltpu.CompilerParams(vmem_limit_bytes=40 * 1024 * 1024),
            cost_estimate=pl.CostEstimate(
                flops=places * (slots + 1) * 16 * length**3,
                bytes_accessed=6_000_000,
                transcendentals=0,
            ),
            name="encode",
        )(
            scalars,
            *([images] * slots),
            *([coil_maps] * slots),
            kspace,
            group_phases,
            left,
            gram,
            adjoint,
        )
        encoded.append(outputs[0])
        pieces.append(outputs[1:])

    gradients = []
    for group in range(groups):
        if whole_classes:
            terms = [chain_terms(piece, "slc") for piece in pieces[group]]
        else:
            terms = [[lax.psum(piece, "slc")] for piece in pieces[group]]
        flat = [term for piece in terms for term in piece]
        gradient = pl.pallas_call(
            functools.partial(gradient_kernel, ROW_PARTS, len(terms[0])),
            out_shape=jax.ShapeDtypeStruct((ROW_PARTS, slots, part), jnp.float32),
            compiler_params=pltpu.CompilerParams(vmem_limit_bytes=40 * 1024 * 1024),
            cost_estimate=pl.CostEstimate(
                flops=places * slots * 4 * length**2, bytes_accessed=3_000_000, transcendentals=0
            ),
            name="gradient",
        )(*flat, encoded[group])
        gradients.append(jnp.moveaxis(gradient, 0, 1).reshape(slots, rows)[:, :length])
    by_class = jnp.stack(gradients, axis=1)
    if whole_classes:
        local = by_class.reshape(per_device, length)
    else:
        first = (position * per_device) % groups
        local = lax.dynamic_slice_in_dim(by_class[0], first, per_device, axis=0)
    summed = lax.psum(local, ("coil", "vol"))
    factor = 1.0 / (coils * lax.axis_size("coil") * vols * lax.axis_size("vol"))
    return summed * factor


def solution(mesh):
    placed = (
        P(("grp", "vol"), "slc", None, None, None),
        P(("grp", "coil"), "slc", None, None, None),
        P(("grp", "vol"), "slc", "coil", None, None, None),
        P("slc"),
        P("slc", None),
        P(),
    )
    return jax.shard_map(
        body, mesh=mesh, in_specs=placed, out_specs=P(("grp", "slc"), None), check_vma=False
    )
```

time: 204 us -> 112 us (0.55)
  waiting for transfers between devices: 80.5 us -> 29.7 us
  local copies, waits for them, and re-layouts: 60.6 us -> 15.4 us
  starting transfers between devices: 6.46 us -> 31.1 us
  Pallas kernels: 0 us -> 17.9 us
  other arithmetic: 27.6 us -> 10.3 us
  matrix products: 12.5 us -> 0 us
  blocking collectives: 15.5 us -> 5.77 us
    all_to_all x1 -> x0, waiting for transfers between devices: 80.5 us -> none  [body(): lax.all_to_all(outgoing, 'slc', split_axis=2, concat_axis=2, tiled=True)]
    ppermute x0 -> x24, starting transfers between devices: none -> 31.1 us  [chain_terms(): arrived = [lax.ppermute(payload, axis, pairs) for pairs in rounds]]
    ppermute x0 -> x24, waiting for transfers between devices: none -> 29.7 us  [chain_terms(): arrived = [lax.ppermute(payload, axis, pairs) for pairs in rounds]]
    pallas_call x0 -> x8, Pallas kernels: none -> 17.9 us  [the longest x4 9.28 us: body(): pl.pallas_call(functools.partial(encode_kernel, slots, columns, not whole...]
    slice x5 -> x1, local copies, waits for them, and re-layouts: 16.5 us -> 0.66 us  [body(): scalars = jnp.stack([owned[group], jnp.int32(1)])]
    dot_general x4 -> x0, matrix products: 12.5 us -> none  [the longest x1 9.01 us: body(): jnp.einsum('tcsqyx,qpkx->tcspyk', partly, section_two, preferred_element_...]
    select_n x1 -> x0, local copies, waits for them, and re-layouts: 11 us -> none  [body(): jnp.where(filled[None, None, :, None, None, None] > 0, outgoing, jnp.zero...]
    another operation x4 -> x3, other arithmetic: 12.6 us -> 2.65 us  [the longest x2 2.64 us: body(): scalars = jnp.stack([owned[group], jnp.int32(1)])]
  transfers between devices with their start and end apart: 1 -> 24, of which waited for: 1 -> 10; matrix products, arithmetic and copies ran while one was open for 0% -> 6% of each run, Pallas kernels for 0% -> 12%
where the time goes in v1:
time: 112 us; the launch traced here: 111 us
  starting transfers between devices  31.1 us (28%)
  waiting for transfers between devices  29.7 us (27%)
  Pallas kernels  17.9 us (16%)
  local copies, waits for them, and re-layouts  15.4 us (14%)
  other arithmetic  10.3 us (9%)
  blocking collectives  5.77 us (5%)
    ppermute x24, starting transfers between devices, chain_terms(): arrived = [lax.ppermute(payload, axis, pairs) for pairs in rounds]  31.1 us
    ppermute x24, waiting for transfers between devices, chain_terms(): arrived = [lax.ppermute(payload, axis, pairs) for pairs in rounds]  29.7 us
    unnamed x55, local copies, waits for them, and re-layouts  14.2 us
    pallas_call x4, Pallas kernels, body(): pl.pallas_call(functools.partial(encode_kernel, slots, columns, not whole...  9.28 us
    pallas_call x4, Pallas kernels, body(): pl.pallas_call(functools.partial(gradient_kernel, ROW_PARTS, len(terms[0]...  8.67 us
    psum x1, blocking collectives, body(): summed = lax.psum(local, ('coil', 'vol'))  5.77 us
    add x16, other arithmetic, chain_terms(): payload = value + received  4.94 us
    another operation x2, other arithmetic, body(): scalars = jnp.stack([owned[group], jnp.int32(1)])  2.64 us
  transfers between devices with their start and end apart: 24, of which 10 were waited for; matrix products, arithmetic and copies ran while one was open for 6% of the time, Pallas kernels for 12%

profile of v1, /device:TPU:0, one launch (start us, length us, event | category | flops | bytes accessed | tf_op | source)
XLA Modules:
  0.0 110.7 jit_solution(2445734557252373829)
XLA Ops:
  4.2 1.8 %copy.83.refs_0_.refs_1_ = bf16[1,8,2,220,220]{4,3,2,1,0:T(8,128)(2,1)S(1)} copy(bf16[1,8,2,220,220]{4,2,3,1,0:T(2,128)(2,1)} %param.9) | data formatting | bytes 3097600 | tf_op args[0]
  6.6 1.3 %pad_add_fusion = (s32[2]{0:T(128)S(1)}, s32[2]{0:T(128)S(1)}) fusion(s32[1]{0:T(128)} %constant.18.clone.1, s32[1]{0:T(128)} %get-tuple-element.32, s32[1]{0:T(128)} %get-tuple-element.33), kind=kLoop, calls=%fused_computation.12 | loop fusion | flops 4 | bytes 28 | tf_op jit(solution)/shard_map/stack | solution.py:185
  8.0 2.2 %encode.7 = (bf16[2,2,2,224,220]{4,3,2,1,0:T(8,128)(2,1)S(1)}, bf16[112,896]{1,0:T(8,128)(2,1)S(1)}, bf16[112,896]{1,0:T(8,128)(2,1)S(1)}) custom-call(s32[2]{0:T(128)S(1)} %get-tuple-element.35.scalars, bf16[1,8,2,220,220]{4,3,2,1,0:T(8,128)(2,1)S(1)} %copy.83.refs_0_.refs_1_, bf16[1,8,2,220,220]{4,3,2,1,0:T(8,128)(2,1)S(1)} %copy.83.refs_0_.refs_1_, ...), custom_call_target="tpu_custom_call" | custom-call | flops 1022208000 | bytes 6000000 | tf_op jit(solution)/shard_map/encode/pallas_call | solution.py:200
  10.2 5.4 %collective-permute-start.18 = (bf16[112,896]{1,0:T(8,128)(2,1)S(1)}, bf16[112,896]{1,0:T(8,128)(2,1)S(1)}, u32[]{:S(2)}, u32[]{:S(2)}) collective-permute-start(bf16[112,896]{1,0:T(8,128)(2,1)S(1)} %get-tuple-element.26.refs_0_), channel_id=1, source_target_pairs={{0,4},{12,8},{1,5},{13,9},{2,6},{14,10},{3,7},{15,11},{16,20},{28,... | collective-permute-start | bytes 602120 | tf_op jit(solution)/shard_map/ppermute | solution.py:155
  15.7 1.3 %collective-permute-start.21 = (bf16[112,896]{1,0:T(8,128)(2,1)S(1)}, bf16[112,896]{1,0:T(8,128)(2,1)S(1)}, u32[]{:S(2)}, u32[]{:S(2)}) collective-permute-start(bf16[112,896]{1,0:T(8,128)(2,1)S(1)} %get-tuple-element.27.refs_4_), channel_id=1, source_target_pairs={{0,4},{12,8},{1,5},{13,9},{2,6},{14,10},{3,7},{15,11},{16,20},{28,... | collective-permute-start | bytes 602120 | tf_op jit(solution)/shard_map/ppermute | solution.py:155
  17.0 2.2 %encode.6 = (bf16[2,2,2,224,220]{4,3,2,1,0:T(8,128)(2,1)S(1)}, bf16[112,896]{1,0:T(8,128)(2,1)S(1)}, bf16[112,896]{1,0:T(8,128)(2,1)S(1)}) custom-call(s32[2]{0:T(128)S(1)} %get-tuple-element.36.scalars, bf16[1,8,2,220,220]{4,3,2,1,0:T(8,128)(2,1)S(1)} %copy.83.refs_0_.refs_1_, bf16[1,8,2,220,220]{4,3,2,1,0:T(8,128)(2,1)S(1)} %copy.83.refs_0_.refs_1_, ...), custom_call_target="tpu_custom_call" | custom-call | flops 1022208000 | bytes 6000000 | tf_op jit(solution)/shard_map/encode/pallas_call | solution.py:200
  23.1 2.7 %encode.5 = (bf16[2,2,2,224,220]{4,3,2,1,0:T(8,128)(2,1)S(1)}, bf16[112,896]{1,0:T(8,128)(2,1)S(1)}, bf16[112,896]{1,0:T(8,128)(2,1)S(1)}) custom-call(s32[2]{0:T(128)S(1)} %get-tuple-element.37.scalars, bf16[1,8,2,220,220]{4,3,2,1,0:T(8,128)(2,1)S(1)} %copy.83.refs_0_.refs_1_, bf16[1,8,2,220,220]{4,3,2,1,0:T(8,128)(2,1)S(1)} %copy.83.refs_0_.refs_1_, ...), custom_call_target="tpu_custom_call" | custom-call | flops 1022208000 | bytes 6000000 | tf_op jit(solution)/shard_map/encode/pallas_call | solution.py:200
  25.8 1.3 %collective-permute-start.6 = (bf16[112,896]{1,0:T(8,128)(2,1)S(1)}, bf16[112,896]{1,0:T(8,128)(2,1)S(1)}, u32[]{:S(2)}, u32[]{:S(2)}) collective-permute-start(bf16[112,896]{1,0:T(8,128)(2,1)S(1)} %get-tuple-element.20.refs_0_), channel_id=1, source_target_pairs={{0,4},{12,8},{1,5},{13,9},{2,6},{14,10},{3,7},{15,11},{16,20},{28,... | collective-permute-start | bytes 602120 | tf_op jit(solution)/shard_map/ppermute | solution.py:155
  27.1 2.2 %encode.4 = (bf16[2,2,2,224,220]{4,3,2,1,0:T(8,128)(2,1)S(1)}, bf16[112,896]{1,0:T(8,128)(2,1)S(1)}, bf16[112,896]{1,0:T(8,128)(2,1)S(1)}) custom-call(s32[2]{0:T(128)S(1)} %get-tuple-element.38.scalars, bf16[1,8,2,220,220]{4,3,2,1,0:T(8,128)(2,1)S(1)} %copy.83.refs_0_.refs_1_, bf16[1,8,2,220,220]{4,3,2,1,0:T(8,128)(2,1)S(1)} %copy.83.refs_0_.refs_1_, ...), custom_call_target="tpu_custom_call" | custom-call | flops 1022208000 | bytes 6000000 | tf_op jit(solution)/shard_map/encode/pallas_call | solution.py:200
  32.0 2.0 %collective-permute-start.3 = (bf16[112,896]{1,0:T(8,128)(2,1)S(1)}, bf16[112,896]{1,0:T(8,128)(2,1)S(1)}, u32[]{:S(2)}, u32[]{:S(2)}) collective-permute-start(bf16[112,896]{1,0:T(8,128)(2,1)S(1)} %get-tuple-element.18.refs_4_), channel_id=1, source_target_pairs={{0,4},{12,8},{1,5},{13,9},{2,6},{14,10},{3,7},{15,11},{16,20},{28,... | collective-permute-start | bytes 602120 | tf_op jit(solution)/shard_map/ppermute | solution.py:155
  34.9 3.3 %collective-permute-done.6.refs_1_ = bf16[112,896]{1,0:T(8,128)(2,1)S(1)} collective-permute-done((bf16[112,896]{1,0:T(8,128)(2,1)S(1)}, bf16[112,896]{1,0:T(8,128)(2,1)S(1)}, u32[]{:S(2)}, u32[]{:S(2)}) %collective-permute-start.6) | collective-permute-done | bytes 200736 | tf_op jit(solution)/shard_map/ppermute | solution.py:155
  39.0 3.6 %collective-permute-done.9.refs_5_ = bf16[112,896]{1,0:T(8,128)(2,1)S(1)} collective-permute-done((bf16[112,896]{1,0:T(8,128)(2,1)S(1)}, bf16[112,896]{1,0:T(8,128)(2,1)S(1)}, u32[]{:S(2)}, u32[]{:S(2)}) %collective-permute-start.9) | collective-permute-done | bytes 200736 | tf_op jit(solution)/shard_map/ppermute | solution.py:155
  43.3 3.6 %collective-permute-done.refs_1_ = bf16[112,896]{1,0:T(8,128)(2,1)S(1)} collective-permute-done((bf16[112,896]{1,0:T(8,128)(2,1)S(1)}, bf16[112,896]{1,0:T(8,128)(2,1)S(1)}, u32[]{:S(2)}, u32[]{:S(2)}) %collective-permute-start) | collective-permute-done | bytes 200736 | tf_op jit(solution)/shard_map/ppermute | solution.py:155
  47.5 2.5 %collective-permute-done.3.refs_5_ = bf16[112,896]{1,0:T(8,128)(2,1)S(1)} collective-permute-done((bf16[112,896]{1,0:T(8,128)(2,1)S(1)}, bf16[112,896]{1,0:T(8,128)(2,1)S(1)}, u32[]{:S(2)}, u32[]{:S(2)}) %collective-permute-start.3) | collective-permute-done | bytes 200736 | tf_op jit(solution)/shard_map/ppermute | solution.py:155
  64.0 7.7 %collective-permute-done.20.refs_3_ = bf16[112,896]{1,0:T(8,128)(2,1)S(1)} collective-permute-done((bf16[112,896]{1,0:T(8,128)(2,1)S(1)}, bf16[112,896]{1,0:T(8,128)(2,1)S(1)}, u32[]{:S(2)}, u32[]{:S(2)}) %collective-permute-start.20) | collective-permute-done | bytes 200736 | tf_op jit(solution)/shard_map/ppermute | solution.py:155
  73.0 3.0 %collective-permute-done.23.refs_7_ = bf16[112,896]{1,0:T(8,128)(2,1)S(1)} collective-permute-done((bf16[112,896]{1,0:T(8,128)(2,1)S(1)}, bf16[112,896]{1,0:T(8,128)(2,1)S(1)}, u32[]{:S(2)}, u32[]{:S(2)}) %collective-permute-start.23) | collective-permute-done | bytes 200736 | tf_op jit(solution)/shard_map/ppermute | solution.py:155
  76.0 1.5 %collective-permute-start.2 = (bf16[112,896]{1,0:T(8,128)(2,1)}, bf16[112,896]{1,0:T(8,128)(2,1)}, u32[]{:S(2)}, u32[]{:S(2)}) collective-permute-start(bf16[112,896]{1,0:T(8,128)(2,1)} %add.62), channel_id=1, source_target_pairs={{8,12},{4,0},{9,13},{5,1},{10,14},{6,2},{11,15},{7,3},{24,28},{20,... | collective-permute-start | bytes 602120 | tf_op jit(solution)/shard_map/ppermute | solution.py:155
  77.5 1.4 %gradient.7 = f32[2,2,112]{2,1,0:T(2,128)S(1)} custom-call(bf16[112,896]{1,0:T(8,128)(2,1)S(1)} %get-tuple-element.26.refs_0_, bf16[112,896]{1,0:T(8,128)(2,1)S(1)} %collective-permute-done.18.refs_1_, bf16[112,896]{1,0:T(8,128)(2,1)S(1)} %collective-permute-done.19.refs_2_, bf16[112,896]{1,0:T(8,128)(2,1)S(1)} %collective-permute-done.20.refs_3_, ...), custom_call_target="tpu_custom_call" | custom-call | flops 774400 | bytes 3000000 | tf_op jit(solution)/shard_map/gradient/pallas_call | solution.py:247
  79.0 1.4 %collective-permute-done.14.refs_3_ = bf16[112,896]{1,0:T(8,128)(2,1)} collective-permute-done((bf16[112,896]{1,0:T(8,128)(2,1)}, bf16[112,896]{1,0:T(8,128)(2,1)}, u32[]{:S(2)}, u32[]{:S(2)}) %collective-permute-start.14) | collective-permute-done | bytes 200736 | tf_op jit(solution)/shard_map/ppermute | solution.py:155
  81.7 3.0 %collective-permute-done.17.refs_7_ = bf16[112,896]{1,0:T(8,128)(2,1)} collective-permute-done((bf16[112,896]{1,0:T(8,128)(2,1)}, bf16[112,896]{1,0:T(8,128)(2,1)}, u32[]{:S(2)}, u32[]{:S(2)}) %collective-permute-start.17) | collective-permute-done | bytes 200736 | tf_op jit(solution)/shard_map/ppermute | solution.py:155
  89.6 2.4 %gradient.6 = f32[2,2,112]{2,1,0:T(2,128)S(1)} custom-call(bf16[112,896]{1,0:T(8,128)(2,1)S(1)} %get-tuple-element.23.refs_0_, bf16[112,896]{1,0:T(8,128)(2,1)S(1)} %copy-done.6, bf16[112,896]{1,0:T(8,128)(2,1)S(1)} %copy-done.22, bf16[112,896]{1,0:T(8,128)(2,1)} %collective-permute-done.14.refs_3_, bf16[112,896]{1,0:T(8,128)(2,1)S(1)} %get-tuple-element.24.refs_4_, ...), custom_call_target="tpu_custom_call" | custom-call | flops 774400 | bytes 3000000 | tf_op jit(solution)/shard_map/gradient/pallas_call | solution.py:247
  96.1 2.4 %gradient.5 = f32[2,2,112]{2,1,0:T(2,128)S(1)} custom-call(bf16[112,896]{1,0:T(8,128)(2,1)S(1)} %get-tuple-element.20.refs_0_, bf16[112,896]{1,0:T(8,128)(2,1)S(1)} %collective-permute-done.6.refs_1_, bf16[112,896]{1,0:T(8,128)(2,1)S(1)} %copy-done.16, bf16[112,896]{1,0:T(8,128)(2,1)} %collective-permute-done.8.refs_3_, ...), custom_call_target="tpu_custom_call" | custom-call | flops 774400 | bytes 3000000 | tf_op jit(solution)/shard_map/gradient/pallas_call | solution.py:247
  101.8 2.4 %gradient.4 = f32[2,2,112]{2,1,0:T(2,128)S(1)} custom-call(bf16[112,896]{1,0:T(8,128)(2,1)S(1)} %get-tuple-element.17.refs_0_, bf16[112,896]{1,0:T(8,128)(2,1)S(1)} %collective-permute-done.refs_1_, bf16[112,896]{1,0:T(8,128)(2,1)S(1)} %copy-done.14, bf16[112,896]{1,0:T(8,128)(2,1)} %collective-permute-done.2.refs_3_, ...), custom_call_target="tpu_custom_call" | custom-call | flops 774400 | bytes 3000000 | tf_op jit(solution)/shard_map/gradient/pallas_call | solution.py:247
  104.4 5.8 %psum.7 = f32[8,220]{1,0:T(8,128)S(1)} all-reduce(f32[8,220]{1,0:T(8,128)S(1)} %reshape.25), channel_id=1, replica_groups=mesh['grp'=2,'slc'=4,'coil'=2,'vol'=2] {'coil','vol'}, use_global_device_ids=true, to_apply=%region_0.1 | all-reduce | flops 1760 | bytes 14080 | tf_op jit(solution)/shard_map/psum | solution.py:263
  (130 shorter events, 43.7 us)
Async XLA Ops:
  10.2 19.1 %collective-permute-start.18 = (bf16[112,896]{1,0:T(8,128)(2,1)S(1)}, bf16[112,896]{1,0:T(8,128)(2,1)S(1)}, u32[]{:S(2)}, u32[]{:S(2)}) collective-permute-start(bf16[112,896]{1,0:T(8,128)(2,1)S(1)} %get-tuple-element.26.refs_0_), channel_id=1, source_target_pairs={{0,4},{12,8},{1,5},{13,9},{2,6},{14,10},{3,7},{15,11},{16,20},{28,... | collective-permute-start | bytes 602120 | tf_op jit(solution)/shard_map/ppermute | solution.py:155
  15.7 15.0 %collective-permute-start.21 = (bf16[112,896]{1,0:T(8,128)(2,1)S(1)}, bf16[112,896]{1,0:T(8,128)(2,1)S(1)}, u32[]{:S(2)}, u32[]{:S(2)}) collective-permute-start(bf16[112,896]{1,0:T(8,128)(2,1)S(1)} %get-tuple-element.27.refs_4_), channel_id=1, source_target_pairs={{0,4},{12,8},{1,5},{13,9},{2,6},{14,10},{3,7},{15,11},{16,20},{28,... | collective-permute-start | bytes 602120 | tf_op jit(solution)/shard_map/ppermute | solution.py:155
  19.2 12.8 %collective-permute-start.12 = (bf16[112,896]{1,0:T(8,128)(2,1)S(1)}, bf16[112,896]{1,0:T(8,128)(2,1)S(1)}, u32[]{:S(2)}, u32[]{:S(2)}) collective-permute-start(bf16[112,896]{1,0:T(8,128)(2,1)S(1)} %get-tuple-element.23.refs_0_), channel_id=1, source_target_pairs={{0,4},{12,8},{1,5},{13,9},{2,6},{14,10},{3,7},{15,11},{16,20},{28,... | collective-permute-start | bytes 602120 | tf_op jit(solution)/shard_map/ppermute | solution.py:155
  20.5 13.7 %collective-permute-start.15 = (bf16[112,896]{1,0:T(8,128)(2,1)S(1)}, bf16[112,896]{1,0:T(8,128)(2,1)S(1)}, u32[]{:S(2)}, u32[]{:S(2)}) collective-permute-start(bf16[112,896]{1,0:T(8,128)(2,1)S(1)} %get-tuple-element.24.refs_4_), channel_id=1, source_target_pairs={{0,4},{12,8},{1,5},{13,9},{2,6},{14,10},{3,7},{15,11},{16,20},{28,... | collective-permute-start | bytes 602120 | tf_op jit(solution)/shard_map/ppermute | solution.py:155
  25.8 12.4 %collective-permute-start.6 = (bf16[112,896]{1,0:T(8,128)(2,1)S(1)}, bf16[112,896]{1,0:T(8,128)(2,1)S(1)}, u32[]{:S(2)}, u32[]{:S(2)}) collective-permute-start(bf16[112,896]{1,0:T(8,128)(2,1)S(1)} %get-tuple-element.20.refs_0_), channel_id=1, source_target_pairs={{0,4},{12,8},{1,5},{13,9},{2,6},{14,10},{3,7},{15,11},{16,20},{28,... | collective-permute-start | bytes 602120 | tf_op jit(solution)/shard_map/ppermute | solution.py:155
  29.3 13.2 %collective-permute-start.9 = (bf16[112,896]{1,0:T(8,128)(2,1)S(1)}, bf16[112,896]{1,0:T(8,128)(2,1)S(1)}, u32[]{:S(2)}, u32[]{:S(2)}) collective-permute-start(bf16[112,896]{1,0:T(8,128)(2,1)S(1)} %get-tuple-element.21.refs_4_), channel_id=1, source_target_pairs={{0,4},{12,8},{1,5},{13,9},{2,6},{14,10},{3,7},{15,11},{16,20},{28,... | collective-permute-start | bytes 602120 | tf_op jit(solution)/shard_map/ppermute | solution.py:155
  30.6 16.2 %collective-permute-start = (bf16[112,896]{1,0:T(8,128)(2,1)S(1)}, bf16[112,896]{1,0:T(8,128)(2,1)S(1)}, u32[]{:S(2)}, u32[]{:S(2)}) collective-permute-start(bf16[112,896]{1,0:T(8,128)(2,1)S(1)} %get-tuple-element.17.refs_0_), channel_id=1, source_target_pairs={{0,4},{12,8},{1,5},{13,9},{2,6},{14,10},{3,7},{15,11},{16,20},{28,... | collective-permute-start | bytes 602120 | tf_op jit(solution)/shard_map/ppermute | solution.py:155
  32.0 18.0 %collective-permute-start.3 = (bf16[112,896]{1,0:T(8,128)(2,1)S(1)}, bf16[112,896]{1,0:T(8,128)(2,1)S(1)}, u32[]{:S(2)}, u32[]{:S(2)}) collective-permute-start(bf16[112,896]{1,0:T(8,128)(2,1)S(1)} %get-tuple-element.18.refs_4_), channel_id=1, source_target_pairs={{0,4},{12,8},{1,5},{13,9},{2,6},{14,10},{3,7},{15,11},{16,20},{28,... | collective-permute-start | bytes 602120 | tf_op jit(solution)/shard_map/ppermute | solution.py:155
  34.2 16.6 %collective-permute-start.19 = (bf16[112,896]{1,0:T(8,128)(2,1)S(1)}, bf16[112,896]{1,0:T(8,128)(2,1)S(1)}, u32[]{:S(2)}, u32[]{:S(2)}) collective-permute-start(bf16[112,896]{1,0:T(8,128)(2,1)S(1)} %add.73), channel_id=1, source_target_pairs={{4,8},{8,4},{5,9},{9,5},{6,10},{10,6},{7,11},{11,7},{20,24},{24,20... | collective-permute-start | bytes 602120 | tf_op jit(solution)/shard_map/ppermute | solution.py:155
  38.2 13.3 %collective-permute-start.22 = (bf16[112,896]{1,0:T(8,128)(2,1)S(1)}, bf16[112,896]{1,0:T(8,128)(2,1)S(1)}, u32[]{:S(2)}, u32[]{:S(2)}) collective-permute-start(bf16[112,896]{1,0:T(8,128)(2,1)S(1)} %add.75), channel_id=1, source_target_pairs={{4,8},{8,4},{5,9},{9,5},{6,10},{10,6},{7,11},{11,7},{20,24},{24,20... | collective-permute-start | bytes 602120 | tf_op jit(solution)/shard_map/ppermute | solution.py:155
  42.5 9.8 %collective-permute-start.13 = (bf16[112,896]{1,0:T(8,128)(2,1)S(1)}, bf16[112,896]{1,0:T(8,128)(2,1)S(1)}, u32[]{:S(2)}, u32[]{:S(2)}) collective-permute-start(bf16[112,896]{1,0:T(8,128)(2,1)S(1)} %add.69), channel_id=1, source_target_pairs={{4,8},{8,4},{5,9},{9,5},{6,10},{10,6},{7,11},{11,7},{20,24},{24,20... | collective-permute-start | bytes 602120 | tf_op jit(solution)/shard_map/ppermute | solution.py:155
  46.8 6.2 %collective-permute-start.16 = (bf16[112,896]{1,0:T(8,128)(2,1)S(1)}, bf16[112,896]{1,0:T(8,128)(2,1)S(1)}, u32[]{:S(2)}, u32[]{:S(2)}) collective-permute-start(bf16[112,896]{1,0:T(8,128)(2,1)S(1)} %add.71), channel_id=1, source_target_pairs={{4,8},{8,4},{5,9},{9,5},{6,10},{10,6},{7,11},{11,7},{20,24},{24,20... | collective-permute-start | bytes 602120 | tf_op jit(solution)/shard_map/ppermute | solution.py:155
  50.0 4.4 %collective-permute-start.7 = (bf16[112,896]{1,0:T(8,128)(2,1)S(1)}, bf16[112,896]{1,0:T(8,128)(2,1)S(1)}, u32[]{:S(2)}, u32[]{:S(2)}) collective-permute-start(bf16[112,896]{1,0:T(8,128)(2,1)S(1)} %add.65), channel_id=1, source_target_pairs={{4,8},{8,4},{5,9},{9,5},{6,10},{10,6},{7,11},{11,7},{20,24},{24,20... | collective-permute-start | bytes 602120 | tf_op jit(solution)/shard_map/ppermute | solution.py:155
  50.8 7.1 %collective-permute-start.10 = (bf16[112,896]{1,0:T(8,128)(2,1)S(1)}, bf16[112,896]{1,0:T(8,128)(2,1)S(1)}, u32[]{:S(2)}, u32[]{:S(2)}) collective-permute-start(bf16[112,896]{1,0:T(8,128)(2,1)S(1)} %add.67), channel_id=1, source_target_pairs={{4,8},{8,4},{5,9},{9,5},{6,10},{10,6},{7,11},{11,7},{20,24},{24,20... | collective-permute-start | bytes 602120 | tf_op jit(solution)/shard_map/ppermute | solution.py:155
  51.5 8.4 %collective-permute-start.1 = (bf16[112,896]{1,0:T(8,128)(2,1)S(1)}, bf16[112,896]{1,0:T(8,128)(2,1)S(1)}, u32[]{:S(2)}, u32[]{:S(2)}) collective-permute-start(bf16[112,896]{1,0:T(8,128)(2,1)S(1)} %add.61), channel_id=1, source_target_pairs={{4,8},{8,4},{5,9},{9,5},{6,10},{10,6},{7,11},{11,7},{20,24},{24,20... | collective-permute-start | bytes 602120 | tf_op jit(solution)/shard_map/ppermute | solution.py:155
  52.3 9.7 %collective-permute-start.4 = (bf16[112,896]{1,0:T(8,128)(2,1)S(1)}, bf16[112,896]{1,0:T(8,128)(2,1)S(1)}, u32[]{:S(2)}, u32[]{:S(2)}) collective-permute-start(bf16[112,896]{1,0:T(8,128)(2,1)S(1)} %add.63), channel_id=1, source_target_pairs={{4,8},{8,4},{5,9},{9,5},{6,10},{10,6},{7,11},{11,7},{20,24},{24,20... | collective-permute-start | bytes 602120 | tf_op jit(solution)/shard_map/ppermute | solution.py:155
  53.1 18.7 %collective-permute-start.20 = (bf16[112,896]{1,0:T(8,128)(2,1)S(1)}, bf16[112,896]{1,0:T(8,128)(2,1)S(1)}, u32[]{:S(2)}, u32[]{:S(2)}) collective-permute-start(bf16[112,896]{1,0:T(8,128)(2,1)S(1)} %add.74), channel_id=1, source_target_pairs={{8,12},{4,0},{9,13},{5,1},{10,14},{6,2},{11,15},{7,3},{24,28},{20,... | collective-permute-start | bytes 602120 | tf_op jit(solution)/shard_map/ppermute | solution.py:155
  54.4 21.6 %collective-permute-start.23 = (bf16[112,896]{1,0:T(8,128)(2,1)S(1)}, bf16[112,896]{1,0:T(8,128)(2,1)S(1)}, u32[]{:S(2)}, u32[]{:S(2)}) collective-permute-start(bf16[112,896]{1,0:T(8,128)(2,1)S(1)} %add.76), channel_id=1, source_target_pairs={{8,12},{4,0},{9,13},{5,1},{10,14},{6,2},{11,15},{7,3},{24,28},{20,... | collective-permute-start | bytes 602120 | tf_op jit(solution)/shard_map/ppermute | solution.py:155
  57.9 22.5 %collective-permute-start.14 = (bf16[112,896]{1,0:T(8,128)(2,1)}, bf16[112,896]{1,0:T(8,128)(2,1)}, u32[]{:S(2)}, u32[]{:S(2)}) collective-permute-start(bf16[112,896]{1,0:T(8,128)(2,1)} %add.70), channel_id=1, source_target_pairs={{8,12},{4,0},{9,13},{5,1},{10,14},{6,2},{11,15},{7,3},{24,28},{20,... | collective-permute-start | bytes 602120 | tf_op jit(solution)/shard_map/ppermute | solution.py:155
  59.9 24.8 %collective-permute-start.17 = (bf16[112,896]{1,0:T(8,128)(2,1)}, bf16[112,896]{1,0:T(8,128)(2,1)}, u32[]{:S(2)}, u32[]{:S(2)}) collective-permute-start(bf16[112,896]{1,0:T(8,128)(2,1)} %add.72), channel_id=1, source_target_pairs={{8,12},{4,0},{9,13},{5,1},{10,14},{6,2},{11,15},{7,3},{24,28},{20,... | collective-permute-start | bytes 602120 | tf_op jit(solution)/shard_map/ppermute | solution.py:155
  62.0 30.2 %collective-permute-start.8 = (bf16[112,896]{1,0:T(8,128)(2,1)}, bf16[112,896]{1,0:T(8,128)(2,1)}, u32[]{:S(2)}, u32[]{:S(2)}) collective-permute-start(bf16[112,896]{1,0:T(8,128)(2,1)} %add.66), channel_id=1, source_target_pairs={{8,12},{4,0},{9,13},{5,1},{10,14},{6,2},{11,15},{7,3},{24,28},{20,... | collective-permute-start | bytes 602120 | tf_op jit(solution)/shard_map/ppermute | solution.py:155
  71.7 21.6 %collective-permute-start.11 = (bf16[112,896]{1,0:T(8,128)(2,1)}, bf16[112,896]{1,0:T(8,128)(2,1)}, u32[]{:S(2)}, u32[]{:S(2)}) collective-permute-start(bf16[112,896]{1,0:T(8,128)(2,1)} %add.68), channel_id=1, source_target_pairs={{8,12},{4,0},{9,13},{5,1},{10,14},{6,2},{11,15},{7,3},{24,28},{20,... | collective-permute-start | bytes 602120 | tf_op jit(solution)/shard_map/ppermute | solution.py:155
  76.0 22.6 %collective-permute-start.2 = (bf16[112,896]{1,0:T(8,128)(2,1)}, bf16[112,896]{1,0:T(8,128)(2,1)}, u32[]{:S(2)}, u32[]{:S(2)}) collective-permute-start(bf16[112,896]{1,0:T(8,128)(2,1)} %add.62), channel_id=1, source_target_pairs={{8,12},{4,0},{9,13},{5,1},{10,14},{6,2},{11,15},{7,3},{24,28},{20,... | collective-permute-start | bytes 602120 | tf_op jit(solution)/shard_map/ppermute | solution.py:155
  80.4 18.6 %collective-permute-start.5 = (bf16[112,896]{1,0:T(8,128)(2,1)}, bf16[112,896]{1,0:T(8,128)(2,1)}, u32[]{:S(2)}, u32[]{:S(2)}) collective-permute-start(bf16[112,896]{1,0:T(8,128)(2,1)} %add.64), channel_id=1, source_target_pairs={{8,12},{4,0},{9,13},{5,1},{10,14},{6,2},{11,15},{7,3},{24,28},{20,... | collective-permute-start | bytes 602120 | tf_op jit(solution)/shard_map/ppermute | solution.py:155
  (26 other events, 225.1 us)

commit v2 on v1

--- a/solution.py
+++ b/solution.py
@@ -13,7 +13,7 @@
 MB = 8
 ROW_TILE = 16
 LANE_TILE = 128
-ROW_PARTS = 2
+ROW_PARTS = 1
 
 
 def round_up(value, multiple):
@@ -141,22 +141,6 @@
                 sums[slot] = term if place == 0 else sums[slot] + term
         for slot in range(slots):
             out_ref[index, slot : slot + 1, :] = jnp.sum(sums[slot].T, axis=0, keepdims=True)
-
-
-def chain_steps(count):
-    for step in range(1, count):
-        up, down = (step - 1, step), (count - step, count - step - 1)
-        yield ([up, down],) if up[0] != down[0] else ([up], [down])
-
-
-def chain_terms(value, axis):
-    terms, payload = [value], value
-    for rounds in chain_steps(lax.axis_size(axis)):
-        arrived = [lax.ppermute(payload, axis, pairs) for pairs in rounds]
-        received = functools.reduce(lambda a, b: a + b, arrived)
-        terms.append(received)
-        payload = value + received
-    return terms
 
 
 def body(images, coil_maps, kspace, shift_index, phase_offset, group_order):
@@ -237,12 +221,10 @@
         encoded.append(outputs[0])
         pieces.append(outputs[1:])
 
+    reduced = lax.psum(pieces, "slc")
     gradients = []
     for group in range(groups):
-        if whole_classes:
-            terms = [chain_terms(piece, "slc") for piece in pieces[group]]
-        else:
-            terms = [[lax.psum(piece, "slc")] for piece in pieces[group]]
+        terms = [[piece] for piece in reduced[group]]
         flat = [term for piece in terms for term in piece]
         gradient = pl.pallas_call(
             functools.partial(gradient_kernel, ROW_PARTS, len(terms[0])),

time: 112 us -> 126 us (1.12)
  waiting for transfers between devices: 29.7 us -> 74.2 us
  starting transfers between devices: 31.1 us -> 0.01 us
  between operations: 0.61 us -> 13.6 us
  local copies, waits for them, and re-layouts: 15.4 us -> 9.61 us
  other arithmetic: 10.3 us -> 5.42 us
    psum x0 -> x1, waiting for transfers between devices: none -> 74.2 us  [body(): reduced = lax.psum(pieces, 'slc')]
    ppermute x24 -> x0, starting transfers between devices: 31.1 us -> none  [chain_terms(): arrived = [lax.ppermute(payload, axis, pairs) for pairs in rounds]]
    ppermute x24 -> x0, waiting for transfers between devices: 29.7 us -> none  [chain_terms(): arrived = [lax.ppermute(payload, axis, pairs) for pairs in rounds]]
    unnamed x55 -> x23, local copies, waits for them, and re-layouts: 14.2 us -> 8.76 us
    add x16 -> x0, other arithmetic: 4.94 us -> none  [chain_terms(): payload = value + received]
    pallas_call x4, Pallas kernels: 8.67 us -> 4.36 us  [body(): pl.pallas_call(functools.partial(gradient_kernel, ROW_PARTS, len(terms[0]...]
    pallas_call x4, Pallas kernels: 9.28 us -> 12.5 us  [body(): pl.pallas_call(functools.partial(encode_kernel, slots, columns, not whole...]
  transfers between devices with their start and end apart: 24 -> 1, of which waited for: 10 -> 1; matrix products, arithmetic and copies ran while one was open for 6% -> 0% of each run, Pallas kernels for 12% -> 0%
where the time goes in v2:
time: 126 us; the launch traced here: 125 us
  waiting for transfers between devices  74.2 us (59%)
  Pallas kernels  16.9 us (13%)
  between operations  13.6 us (11%)
  local copies, waits for them, and re-layouts  9.61 us (8%)
  blocking collectives  5.79 us (5%)
  other arithmetic  5.42 us (4%)
    psum x1, waiting for transfers between devices, body(): reduced = lax.psum(pieces, 'slc')  74.2 us
    pallas_call x4, Pallas kernels, body(): pl.pallas_call(functools.partial(encode_kernel, slots, columns, not whole...  12.5 us
    unnamed x23, local copies, waits for them, and re-layouts  8.76 us
    psum x1, blocking collectives, body(): summed = lax.psum(local, ('coil', 'vol'))  5.79 us
    pallas_call x4, Pallas kernels, body(): pl.pallas_call(functools.partial(gradient_kernel, ROW_PARTS, len(terms[0]...  4.36 us
    another operation x2, other arithmetic, body(): scalars = jnp.stack([owned[group], jnp.int32(1)])  2.72 us
  transfers between devices with their start and end apart: 1, of which 1 were waited for; matrix products, arithmetic and copies ran while one was open for 0% of the time, Pallas kernels for 0%

profile of v2, /device:TPU:0, one launch (start us, length us, event | category | flops | bytes accessed | tf_op | source)
XLA Modules:
  0.0 125.4 jit_solution(11598483490955586702)
XLA Ops:
  6.5 0.7 convert_element_type.16
  7.2 0.7 compare_convert_fusion
  7.9 0.7 fusion
  8.5 0.8 multiply_add_fusion
  9.5 1.2 copy.58.refs_4_
  10.7 1.8 %copy.54.refs_0_.refs_1_ = bf16[1,8,2,220,220]{4,3,2,1,0:T(8,128)(2,1)S(1)} copy(bf16[1,8,2,220,220]{4,2,3,1,0:T(2,128)(2,1)} %param.9) | data formatting | bytes 3097600 | tf_op args[0]
  12.5 0.7 copy.56.refs_2_.refs_3_
  13.2 1.5 %pad_add_fusion = (s32[2]{0:T(128)S(1)}, s32[2]{0:T(128)S(1)}) fusion(s32[1]{0:T(128)} %constant.18.clone.1, s32[1]{0:T(128)} %get-tuple-element.28, s32[1]{0:T(128)} %get-tuple-element.29), kind=kLoop, calls=%fused_computation.12 | loop fusion | flops 4 | bytes 28 | tf_op jit(solution)/shard_map/stack | solution.py:169
  14.7 3.5 %encode.7 = (bf16[2,2,2,224,220]{4,3,2,1,0:T(8,128)(2,1)S(1)}, bf16[224,896]{1,0:T(8,128)(2,1)}) custom-call(s32[2]{0:T(128)S(1)} %get-tuple-element.31.scalars, bf16[1,8,2,220,220]{4,3,2,1,0:T(8,128)(2,1)S(1)} %copy.54.refs_0_.refs_1_, bf16[1,8,2,220,220]{4,3,2,1,0:T(8,128)(2,1)S(1)} %copy.54.refs_0_.refs_1_, ...), custom_call_target="tpu_custom_call" | custom-call | flops 1022208000 | bytes 6000000 | tf_op jit(solution)/shard_map/encode/pallas_call | solution.py:184
  18.1 3.0 %encode.6 = (bf16[2,2,2,224,220]{4,3,2,1,0:T(8,128)(2,1)S(1)}, bf16[224,896]{1,0:T(8,128)(2,1)}) custom-call(s32[2]{0:T(128)S(1)} %get-tuple-element.32.scalars, bf16[1,8,2,220,220]{4,3,2,1,0:T(8,128)(2,1)S(1)} %copy.54.refs_0_.refs_1_, bf16[1,8,2,220,220]{4,3,2,1,0:T(8,128)(2,1)S(1)} %copy.54.refs_0_.refs_1_, ...), custom_call_target="tpu_custom_call" | custom-call | flops 1022208000 | bytes 6000000 | tf_op jit(solution)/shard_map/encode/pallas_call | solution.py:184
  21.1 1.3 %pad_add_fusion.2 = (s32[2]{0:T(128)S(1)}, s32[2]{0:T(128)S(1)}) fusion(s32[1]{0:T(128)} %constant.18.clone.1, s32[1]{0:T(128)} %get-tuple-element.30, s32[1]{0:T(128)} %get-tuple-element.27), kind=kLoop, calls=%fused_computation.14 | loop fusion | flops 4 | bytes 28 | tf_op jit(solution)/shard_map/stack | solution.py:169
  22.4 2.9 %encode.5 = (bf16[2,2,2,224,220]{4,3,2,1,0:T(8,128)(2,1)S(1)}, bf16[224,896]{1,0:T(8,128)(2,1)}) custom-call(s32[2]{0:T(128)S(1)} %get-tuple-element.33.scalars, bf16[1,8,2,220,220]{4,3,2,1,0:T(8,128)(2,1)S(1)} %copy.54.refs_0_.refs_1_, bf16[1,8,2,220,220]{4,3,2,1,0:T(8,128)(2,1)S(1)} %copy.54.refs_0_.refs_1_, ...), custom_call_target="tpu_custom_call" | custom-call | flops 1022208000 | bytes 6000000 | tf_op jit(solution)/shard_map/encode/pallas_call | solution.py:184
  25.3 3.1 %encode.4 = (bf16[2,2,2,224,220]{4,3,2,1,0:T(8,128)(2,1)S(1)}, bf16[224,896]{1,0:T(8,128)(2,1)}) custom-call(s32[2]{0:T(128)S(1)} %get-tuple-element.34.scalars, bf16[1,8,2,220,220]{4,3,2,1,0:T(8,128)(2,1)S(1)} %copy.54.refs_0_.refs_1_, bf16[1,8,2,220,220]{4,3,2,1,0:T(8,128)(2,1)S(1)} %copy.54.refs_0_.refs_1_, ...), custom_call_target="tpu_custom_call" | custom-call | flops 1022208000 | bytes 6000000 | tf_op jit(solution)/shard_map/encode/pallas_call | solution.py:184
  28.4 0.9 copy-done.3
  29.4 74.2 %all-reduce.4.cloned.1.call-done = (bf16[224,896]{1,0:T(8,128)(2,1)}, bf16[224,896]{1,0:T(8,128)(2,1)}, bf16[224,896]{1,0:T(8,128)(2,1)}, bf16[224,896]{1,0:T(8,128)(2,1)}) async-done(((bf16[224,896]{1,0:T(8,128)(2,1)}, bf16[224,896]{1,0:T(8,128)(2,1)}, bf16[224,896]{1,0:T(8,128)(2,1)}, bf16[224,896]{1,0:T(8,128)(2,1)}), (bf16[224,896]{1,0:T(8,128)(2,1)}, bf16[224,896]{1,0:T(8,128)(2,1)}, ...) | async-done | bytes 1605648 | tf_op jit(solution)/shard_map/psum | solution.py:224
  103.6 1.2 copy-done.4
  104.7 1.0 copy-done.8
  105.7 1.1 gradient.4
  106.8 1.0 copy-done.7
  107.8 1.1 gradient.5
  108.9 1.0 copy-done.6
  109.9 1.1 gradient.7
  111.0 1.1 gradient.6
  112.2 5.8 %psum.39 = f32[8,220]{1,0:T(8,128)S(1)} all-reduce(f32[8,220]{1,0:T(8,128)S(1)} %reshape.9), channel_id=1, replica_groups=mesh['grp'=2,'slc'=4,'coil'=2,'vol'=2] {'coil','vol'}, use_global_device_ids=true, to_apply=%region_4.5 | all-reduce | flops 1760 | bytes 14080 | tf_op jit(solution)/shard_map/psum | solution.py:245
  (29 shorter events, 0.9 us)
Async XLA Ops:
  6.5 97.0 %all-reduce.4.cloned.1.call-start = ((), (), s32[]{:S(2)}) async-start(), calls=%async_computation | async-start | bytes 3211264 | tf_op jit(solution)/shard_map/psum | solution.py:224
  9.5 3.0 %copy-start.9 = (bf16[2,8,2,220,220]{4,2,3,1,0:T(2,128)(2,1)S(1)}, bf16[2,8,2,220,220]{4,2,3,1,0:T(2,128)(2,1)}, u32[]{:S(2)}) copy-start(bf16[2,8,2,220,220]{4,2,3,1,0:T(2,128)(2,1)} %param.10) | copy-start | bytes 9292804
  12.5 2.1 %copy-start = (bf16[2,220,440]{2,1,0:T(8,128)(2,1)S(1)}, bf16[2,220,440]{2,1,0:T(8,128)(2,1)}, u32[]{:S(2)}) copy-start(bf16[2,220,440]{2,1,0:T(8,128)(2,1)} %constant.25.clone.refs_8_) | copy-start | bytes 1161604
  12.5 2.1 %copy-start.1 = (bf16[2,220,440]{2,1,0:T(8,128)(2,1)S(1)}, bf16[2,220,440]{2,1,0:T(8,128)(2,1)}, u32[]{:S(2)}) copy-start(bf16[2,220,440]{2,1,0:T(8,128)(2,1)} %constant.24.clone.refs_7_) | copy-start | bytes 1161604
  12.5 2.1 %copy-start.2 = (bf16[2,448,220]{2,1,0:T(8,128)(2,1)S(1)}, bf16[2,448,220]{2,1,0:T(8,128)(2,1)}, u32[]{:S(2)}) copy-start(bf16[2,448,220]{2,1,0:T(8,128)(2,1)} %constant.23.clone.refs_6_) | copy-start | bytes 1182724
  28.4 0.9 copy-start.3
  103.6 1.2 copy-start.4
  104.7 1.0 copy-start.8
  105.7 5.3 %copy-start.5 = (bf16[224,896]{1,0:T(8,128)(2,1)S(1)}, bf16[224,896]{1,0:T(8,128)(2,1)}, u32[]{:S(2)}) copy-start(bf16[224,896]{1,0:T(8,128)(2,1)} %get-tuple-element.22.refs_0_) | copy-start | bytes 1204228
  106.8 1.0 copy-start.7
  108.9 1.0 copy-start.6
Sparse Core Ops, SparseCore 0:
  29.5 74.0 all-reduce.3

commit v3 on v2

v3 whole, which is shorter than its diff:
```python
import functools
import math

import jax
import jax.numpy as jnp
import ml_dtypes
import numpy as np
from jax import lax
from jax.experimental import pallas as pl
from jax.experimental.pallas import tpu as pltpu
from jax.sharding import PartitionSpec as P

MB = 8
ROW_TILE = 16
LANE_TILE = 128
ROW_PARTS = 2
LAG = 3
VMEM_BYTES = 24 * 1024 * 1024


def round_up(value, multiple):
    return -(-value // multiple) * multiple


def fourier_tables(length):
    positions = np.arange(length, dtype=np.int32)
    product = positions[:, None] * positions[None, :] % length
    radians = np.float32(2.0 * math.pi / length) * product.astype(np.float32)
    factor = np.float32(1.0 / math.sqrt(length))
    return (
        (np.cos(radians) * factor).astype(ml_dtypes.bfloat16),
        (-np.sin(radians) * factor).astype(ml_dtypes.bfloat16),
    )


def dft_matrices(length, rows):
    cos_table, sin_table = fourier_tables(length)
    cosine, sine = cos_table.astype(np.float64), sin_table.astype(np.float64)
    left_re = np.zeros((2 * rows, length), np.float64)
    left_im = np.zeros((2 * rows, length), np.float64)
    left_re[:length], left_re[rows : rows + length] = cosine, sine
    left_im[:length], left_im[rows : rows + length] = -sine, cosine
    gram_re = cosine.T @ cosine + sine.T @ sine
    gram_im = sine.T @ cosine - cosine.T @ sine
    gram = np.stack(
        [np.concatenate([gram_re, gram_im], 1), np.concatenate([-gram_im, gram_re], 1)]
    )
    adjoint = np.stack(
        [np.concatenate([cosine, -sine], 1), np.concatenate([sine, cosine], 1)]
    )
    left = np.stack([left_re, left_im])
    return tuple(part.astype(ml_dtypes.bfloat16) for part in (left, gram, adjoint))


def dot(left, right):
    return jnp.dot(left, right, preferred_element_type=jnp.float32)


def phase_columns(shift_ref, offset_ref, angle, rows_of, length):
    lines = lax.broadcasted_iota(jnp.int32, (1, length), 1) - length // 2
    angle[...] = jnp.zeros_like(angle)
    for slot, row in enumerate(rows_of):
        turns = (shift_ref[row] * lines) & (MB - 1)
        angle[slot : slot + 1, :length] = (
            2.0 * math.pi / MB * turns.astype(jnp.float32) + offset_ref[pl.ds(row, 1), :]
        )
    return jnp.cos(angle[...]).T, jnp.sin(angle[...]).T


def encode_kernel(slots, group, whole_classes, *refs):
    shift_ref, order_ref, place_ref = refs[:3]
    image_refs, refs = refs[3 : 3 + slots], refs[3 + slots :]
    map_refs, refs = refs[:slots], refs[slots:]
    kspace_ref, offset_ref, left_ref, gram_ref, adjoint_ref, shifted_ref = refs[:6]
    out_refs = refs[6:-2]
    total, angle = refs[-2:]
    vols, coils = image_refs[0].shape[0], map_refs[0].shape[0]
    length = image_refs[0].shape[-1]
    rows = shifted_ref.shape[-2]
    part = rows // len(out_refs)
    groups = order_ref.shape[0]
    if whole_classes:
        rows_of = [slot * groups + group for slot in range(slots)]
    else:
        rows_of = [place_ref[1]]
    cosines, sines = phase_columns(shift_ref, offset_ref, angle, rows_of, length)
    if total.shape[1] > vols * coils * 2 * length:
        total[...] = jnp.zeros_like(total)
    for vol in range(vols):
        for coil in range(coils):
            place = vol * coils + coil
            sum_re = sum_im = None
            for slot in range(slots):
                image_re = image_refs[slot][vol, 0, 0].astype(jnp.float32)
                image_im = image_refs[slot][vol, 0, 1].astype(jnp.float32)
                map_re = map_refs[slot][coil, 0, 0].astype(jnp.float32)
                map_im = map_refs[slot][coil, 0, 1].astype(jnp.float32)
                coil_re = (map_re * image_re - map_im * image_im).astype(jnp.bfloat16)
                coil_im = (map_re * image_im + map_im * image_re).astype(jnp.bfloat16)
                partly = dot(left_ref[0], coil_re) + dot(left_ref[1], coil_im)
                cosine = cosines[:rows, slot : slot + 1]
                sine = sines[:rows, slot : slot + 1]
                part_re, part_im = partly[:rows], partly[rows:]
                shift_re = part_re * cosine - part_im * sine
                shift_im = part_re * sine + part_im * cosine
                shifted_ref[slot, place, 0] = shift_re.astype(jnp.bfloat16)
                shifted_ref[slot, place, 1] = shift_im.astype(jnp.bfloat16)
                sum_re = shift_re if slot == 0 else sum_re + shift_re
                sum_im = shift_im if slot == 0 else sum_im + shift_im
            mixed = dot(sum_re.astype(jnp.bfloat16), gram_ref[0]) + dot(
                sum_im.astype(jnp.bfloat16), gram_ref[1]
            )
            if not whole_classes:
                mixed = jnp.where(place_ref[0] > 0, mixed, 0.0)
            total[:, place * 2 * length : (place + 1) * 2 * length] = mixed

    @pl.when(order_ref[group] == lax.axis_index("slc"))
    def _():
        for vol in range(vols):
            for coil in range(coils):
                place = vol * coils + coil
                measured = dot(kspace_ref[vol, 0, coil, 0], adjoint_ref[0]) + dot(
                    kspace_ref[vol, 0, coil, 1], adjoint_ref[1]
                )
                total[:length, place * 2 * length : (place + 1) * 2 * length] -= measured

    for index, out_ref in enumerate(out_refs):
        out_ref[...] = total[index * part : (index + 1) * part, :].astype(jnp.bfloat16)


def gradient_kernel(index, factor, on_line, *refs):
    term_refs, shifted_ref, out_ref = refs[:-2], refs[-2], refs[-1]
    slots, places, _, _, length = shifted_ref.shape
    part = out_ref.shape[1]
    terms = [ref[...].astype(jnp.float32) for ref in term_refs]
    if on_line:
        own, near, across, rest = terms
        position = lax.axis_index("slc")
        edge = (position == 0) | (position == lax.axis_size("slc") - 1)
        residual = own + jnp.where(edge, rest, near + across)
    else:
        residual = terms[0]
    sums = [None] * slots
    for place in range(places):
        base = place * 2 * length
        resid_re = residual[:, base : base + length]
        resid_im = residual[:, base + length : base + 2 * length]
        for slot in range(slots):
            span = slice(index * part, (index + 1) * part)
            shift_re = shifted_ref[slot, place, 0, span, :].astype(jnp.float32)
            shift_im = shifted_ref[slot, place, 1, span, :].astype(jnp.float32)
            term = resid_im * shift_re - resid_re * shift_im
            sums[slot] = term if place == 0 else sums[slot] + term
    for slot in range(slots):
        out_ref[slot : slot + 1, :] = factor * jnp.sum(sums[slot].T, axis=0, keepdims=True)


def line_of_four(pieces):
    position = lax.axis_index("slc")
    edge = (position == 0) | (position == 3)
    outer_pairs = [(0, 1), (1, 0), (2, 3), (3, 2)]
    inner_pairs = [(0, 0), (1, 2), (2, 1), (3, 3)]
    count = len(pieces)
    outer, inner = [], []
    for step in range(count + LAG):
        back = step - LAG
        payload = pieces[step] if step < count else None
        if back >= 0:
            others = pieces[back] + inner[back]
            payload = others if payload is None else jnp.where(edge, payload, others)
        outer.append(lax.ppermute(payload, "slc", outer_pairs))
        if step < count:
            inner.append(lax.ppermute(pieces[step] + outer[step], "slc", inner_pairs))
    return [
        (pieces[step], outer[step], inner[step], outer[step + LAG]) for step in range(count)
    ]


def body(images, coil_maps, kspace, shift_index, phase_offset, group_order):
    vols, per_device, _, _, length = images.shape
    coils = coil_maps.shape[0]
    groups = lax.axis_size("slc")
    rows = round_up(length, ROW_TILE * ROW_PARTS)
    part = rows // ROW_PARTS
    places = vols * coils
    lanes = round_up(places * 2 * length, LANE_TILE)
    whole_classes = per_device % groups == 0
    slots = max(1, per_device // groups)
    tables = dft_matrices(length, rows)
    factor = 1.0 / (coils * lax.axis_size("coil") * vols * lax.axis_size("vol"))
    first = (lax.axis_index("slc") * per_device) % groups

    def whole(array):
        return pl.BlockSpec(array.shape, lambda i, *_: (0,) * array.ndim)

    encoded, pieces = [], []
    for group in range(groups):
        if whole_classes:
            place = np.zeros((2,), np.int32)
            picks = [lambda i, *_, w=slot * groups + group: (0, w, 0, 0, 0) for slot in range(slots)]
        else:
            within = group - first
            held = (within >= 0) & (within < per_device)
            place = jnp.stack([held, jnp.where(held, within, 0)]).astype(jnp.int32)
            picks = [lambda i, shift, order, place: (0, place[1], 0, 0, 0)]
        outputs = pl.pallas_call(
            functools.partial(encode_kernel, slots, group, whole_classes),
            grid_spec=pltpu.PrefetchScalarGridSpec(
                num_scalar_prefetch=3,
                grid=(1,),
                in_specs=[pl.BlockSpec((vols, 1, 2, length, length), pick) for pick in picks]
                + [pl.BlockSpec((coils, 1, 2, length, length), pick) for pick in picks]
                + [whole(array) for array in (kspace, phase_offset, *tables)],
                out_specs=[
                    pl.BlockSpec((slots, places, 2, rows, length), lambda i, *_: (0,) * 5),
                ]
                + [pl.BlockSpec((part, lanes), lambda i, *_: (0, 0))] * ROW_PARTS,
                scratch_shapes=[
                    pltpu.VMEM((rows, lanes), jnp.float32),
                    pltpu.VMEM((round_up(slots, 8), round_up(rows, LANE_TILE)), jnp.float32),
                ],
            ),
            out_shape=[
                jax.ShapeDtypeStruct((slots, places, 2, rows, length), jnp.bfloat16),
            ]
            + [jax.ShapeDtypeStruct((part, lanes), jnp.bfloat16)] * ROW_PARTS,
            compiler_params=pltpu.CompilerParams(vmem_limit_bytes=VMEM_BYTES),
            cost_estimate=pl.CostEstimate(
                flops=places * (slots + 1) * 16 * length**3,
                bytes_accessed=6_000_000,
                transcendentals=0,
            ),
            name="encode",
        )(
            shift_index,
            group_order,
            place,
            *([images] * slots),
            *([coil_maps] * slots),
            kspace,
            phase_offset,
            *tables,
        )
        encoded.append(outputs[0])
        pieces.extend(outputs[1:])

    on_line = whole_classes and groups == 4
    if on_line:
        terms = line_of_four(pieces)
    else:
        terms = [(piece,) for piece in lax.psum(pieces, "slc")]
    gradients = []
    for step, term in enumerate(terms):
        group, index = divmod(step, ROW_PARTS)
        gradient = pl.pallas_call(
            functools.partial(gradient_kernel, index, factor, on_line),
            out_shape=jax.ShapeDtypeStruct((slots, part), jnp.float32),
            compiler_params=pltpu.CompilerParams(vmem_limit_bytes=VMEM_BYTES),
            cost_estimate=pl.CostEstimate(
                flops=places * slots * 4 * length**2, bytes_accessed=1_500_000, transcendentals=0
            ),
            name="gradient",
        )(*term, encoded[group])
        gradients.append(gradient)
    by_class = jnp.stack(
        [
            jnp.concatenate(gradients[group * ROW_PARTS : (group + 1) * ROW_PARTS], axis=1)
            for group in range(groups)
        ],
        axis=1,
    )[:, :, :length]
    if whole_classes:
        local = by_class.reshape(per_device, length)
    else:
        local = lax.dynamic_slice_in_dim(by_class[0], first, per_device, axis=0)
    return lax.psum(local, ("coil", "vol"))


def solution(mesh):
    placed = (
        P(("grp", "vol"), "slc", None, None, None),
        P(("grp", "coil"), "slc", None, None, None),
        P(("grp", "vol"), "slc", "coil", None, None, None),
        P("slc"),
        P("slc", None),
        P(),
    )
    return jax.shard_map(
        body, mesh=mesh, in_specs=placed, out_specs=P(("grp", "slc"), None), check_vma=False
    )
```

time: 126 us -> 92.9 us (0.74)
  waiting for transfers between devices: 74.2 us -> 9.87 us
  starting transfers between devices: 0.01 us -> 38.8 us
  between operations: 13.6 us -> 0.38 us
  Pallas kernels: 16.9 us -> 19.7 us
    psum x1 -> x0, waiting for transfers between devices: 74.2 us -> none  [body(): reduced = lax.psum(pieces, 'slc')]
    ppermute x0 -> x19, starting transfers between devices: none -> 38.8 us  [the longest x11 30.4 us: line_of_four(): outer.append(lax.ppermute(payload, 'slc', outer_pairs))]
    ppermute x0 -> x19, waiting for transfers between devices: none -> 9.87 us  [the longest x11 9.84 us: line_of_four(): outer.append(lax.ppermute(payload, 'slc', outer_pairs))]
    select_n x0 -> x5, other arithmetic: none -> 3.01 us  [line_of_four(): payload = others if payload is None else jnp.where(edge, payload, others)]
    pallas_call x8 -> x12, Pallas kernels: 16.9 us -> 19.7 us  [the longest x4 10.8 us: body(): pl.pallas_call(functools.partial(encode_kernel, slots, group, whole_class...]
    add x1 -> x11, other arithmetic: 0.77 us -> 3.31 us  [the longest x8 3.16 us: line_of_four(): inner.append(lax.ppermute(pieces[step] + outer[step], 'slc', inner_pairs))]
    another operation x3 -> x5, other arithmetic: 2.72 us -> 0.31 us  [body(): jnp.stack([jnp.concatenate(gradients[group * ROW_PARTS:(group + 1) * ROW_...]
    unnamed x23 -> x41, local copies, waits for them, and re-layouts: 8.76 us -> 10.4 us
  transfers between devices with their start and end apart: 1 -> 19, of which waited for: 1 -> 6; matrix products, arithmetic and copies ran while one was open for 0% -> 7% of each run, Pallas kernels for 0% -> 17%
where the time goes in v3:
time: 92.9 us; the launch traced here: 92.2 us
  starting transfers between devices  38.8 us (42%)
  Pallas kernels  19.7 us (21%)
  local copies, waits for them, and re-layouts  10.5 us (11%)
  waiting for transfers between devices  9.87 us (11%)
  other arithmetic  6.63 us (7%)
  blocking collectives  6.35 us (7%)
    ppermute x11, starting transfers between devices, line_of_four(): outer.append(lax.ppermute(payload, 'slc', outer_pairs))  30.4 us
    pallas_call x4, Pallas kernels, body(): pl.pallas_call(functools.partial(encode_kernel, slots, group, whole_class...  10.8 us
    unnamed x41, local copies, waits for them, and re-layouts  10.4 us
    ppermute x11, waiting for transfers between devices, line_of_four(): outer.append(lax.ppermute(payload, 'slc', outer_pairs))  9.84 us
    pallas_call x8, Pallas kernels, body(): pl.pallas_call(functools.partial(gradient_kernel, index, factor, on_line)...  8.95 us
    ppermute x8, starting transfers between devices, line_of_four(): inner.append(lax.ppermute(pieces[step] + outer[step], 'slc', inner_pairs))  8.42 us
    psum x1, blocking collectives, body(): return lax.psum(local, ('coil', 'vol'))  6.35 us
    add x8, other arithmetic, line_of_four(): inner.append(lax.ppermute(pieces[step] + outer[step], 'slc', inner_pairs))  3.16 us
  transfers between devices with their start and end apart: 19, of which 6 were waited for; matrix products, arithmetic and copies ran while one was open for 7% of the time, Pallas kernels for 17%

profile of v3, /device:TPU:0, one launch (start us, length us, event | category | flops | bytes accessed | tf_op | source)
XLA Modules:
  0.0 92.2 jit_solution(9817193108609575759)
XLA Ops:
  0.0 2.8 %copy.36.refs_5_.refs_6_ = bf16[2,8,2,220,220]{4,3,2,1,0:T(8,128)(2,1)S(1)} copy(bf16[2,8,2,220,220]{4,2,3,1,0:T(2,128)(2,1)} %param.14) | data formatting | bytes 6195200 | tf_op args[1]
  5.6 2.9 %encode.4 = (bf16[2,2,2,224,220]{4,3,2,1,0:T(8,128)(2,1)S(1)}, bf16[112,896]{1,0:T(8,128)(2,1)S(1)}, bf16[112,896]{1,0:T(8,128)(2,1)}) custom-call(s32[8]{0:T(128)S(1)} %copy-done.15, s32[4]{0:T(128)S(1)} %copy-done.16, s32[2]{0:T(128)S(1)} %call_exported.0.refs_2_, bf16[1,8,2,220,220]{4,3,2,1,0:T(8,128)(2,1)S(1)} %copy.34.refs_3_.refs_4_, ...), custom_call_target="tpu_custom_call" | custom-call | flops 1022208000 | bytes 6000000 | tf_op jit(solution)/shard_map/encode/pallas_call | solution.py:206
  9.4 3.0 %collective-permute-start = (bf16[112,896]{1,0:T(8,128)(2,1)S(1)}, bf16[112,896]{1,0:T(8,128)(2,1)S(1)}, u32[]{:S(2)}, u32[]{:S(2)}) collective-permute-start(bf16[112,896]{1,0:T(8,128)(2,1)S(1)} %get-tuple-element.17.refs_0_), channel_id=1, source_target_pairs={{0,4},{4,0},{8,12},{12,8},{1,5},{5,1},{9,13},{13,9},{2,6},{6,2},{1... | collective-permute-start | bytes 602120 | tf_op jit(solution)/shard_map/ppermute | solution.py:171
  12.5 3.4 %encode.5 = (bf16[2,2,2,224,220]{4,3,2,1,0:T(8,128)(2,1)S(1)}, bf16[112,896]{1,0:T(8,128)(2,1)}, bf16[112,896]{1,0:T(8,128)(2,1)S(1)}) custom-call(s32[8]{0:T(128)S(1)} %copy-done.15, s32[4]{0:T(128)S(1)} %copy-done.16, s32[2]{0:T(128)S(1)} %call_exported.0.refs_2_, bf16[1,8,2,220,220]{4,3,2,1,0:T(8,128)(2,1)S(1)} %copy.34.refs_3_.refs_4_, ...), custom_call_target="tpu_custom_call" | custom-call | flops 1022208000 | bytes 6000000 | tf_op jit(solution)/shard_map/encode/pallas_call | solution.py:206
  16.8 1.5 %collective-permute-start.6 = (bf16[112,896]{1,0:T(8,128)(2,1)}, bf16[112,896]{1,0:T(8,128)(2,1)}, u32[]{:S(2)}, u32[]{:S(2)}) collective-permute-start(bf16[112,896]{1,0:T(8,128)(2,1)} %get-tuple-element.22.refs_0_), channel_id=1, source_target_pairs={{0,4},{4,0},{8,12},{12,8},{1,5},{5,1},{9,13},{13,9},{2,6},{6,2},{1... | collective-permute-start | bytes 602120 | tf_op jit(solution)/shard_map/ppermute | solution.py:171
  19.1 3.4 %collective-permute-start.1 = (bf16[112,896]{1,0:T(8,128)(2,1)}, bf16[112,896]{1,0:T(8,128)(2,1)}, u32[]{:S(2)}, u32[]{:S(2)}) collective-permute-start(bf16[112,896]{1,0:T(8,128)(2,1)} %add.50), channel_id=1, source_target_pairs={{0,0},{4,8},{8,4},{12,12},{1,1},{5,9},{9,5},{13,13},{2,2},{6,10},{... | collective-permute-start | bytes 602120 | tf_op jit(solution)/shard_map/ppermute | solution.py:173
  22.5 2.0 %copy-done.1 = bf16[2,8,2,220,220]{4,3,2,1,0:T(8,128)(2,1)S(1)} copy-done((bf16[2,8,2,220,220]{4,3,2,1,0:T(8,128)(2,1)S(1)}, bf16[2,8,2,220,220]{4,3,2,1,0:T(8,128)(2,1)}, u32[]{:S(2)}) %copy-start.1) | copy-done | bytes 3097624
  25.5 2.2 %encode.6 = (bf16[2,2,2,224,220]{4,3,2,1,0:T(8,128)(2,1)S(1)}, bf16[112,896]{1,0:T(8,128)(2,1)S(1)}, bf16[112,896]{1,0:T(8,128)(2,1)S(1)}) custom-call(s32[8]{0:T(128)S(1)} %copy-done.15, s32[4]{0:T(128)S(1)} %copy-done.16, s32[2]{0:T(128)S(1)} %call_exported.0.refs_2_, bf16[1,8,2,220,220]{4,3,2,1,0:T(8,128)(2,1)S(1)} %copy.34.refs_3_.refs_4_, ...), custom_call_target="tpu_custom_call" | custom-call | flops 1022208000 | bytes 6000000 | tf_op jit(solution)/shard_map/encode/pallas_call | solution.py:206
  32.3 7.2 %collective-permute-start.2 = (bf16[112,896]{1,0:T(8,128)(2,1)S(1)}, bf16[112,896]{1,0:T(8,128)(2,1)S(1)}, u32[]{:S(2)}, u32[]{:S(2)}) collective-permute-start(bf16[112,896]{1,0:T(8,128)(2,1)S(1)} %add_select_fusion.4), channel_id=1, source_target_pairs={{0,4},{4,0},{8,12},{12,8},{1,5},{5,1},{9,13},{13,9},{2,6},{6,2},{1... | collective-permute-start | bytes 602120 | tf_op jit(solution)/shard_map/ppermute | solution.py:171
  42.6 1.9 %collective-permute-start.8 = (bf16[112,896]{1,0:T(8,128)(2,1)S(1)}, bf16[112,896]{1,0:T(8,128)(2,1)S(1)}, u32[]{:S(2)}, u32[]{:S(2)}) collective-permute-start(bf16[112,896]{1,0:T(8,128)(2,1)S(1)} %add_select_fusion.2), channel_id=1, source_target_pairs={{0,4},{4,0},{8,12},{12,8},{1,5},{5,1},{9,13},{13,9},{2,6},{6,2},{1... | collective-permute-start | bytes 602120 | tf_op jit(solution)/shard_map/ppermute | solution.py:171
  46.1 2.2 %encode.7 = (bf16[2,2,2,224,220]{4,3,2,1,0:T(8,128)(2,1)S(1)}, bf16[112,896]{1,0:T(8,128)(2,1)S(1)}, bf16[112,896]{1,0:T(8,128)(2,1)S(1)}) custom-call(s32[8]{0:T(128)S(1)} %copy-done.15, s32[4]{0:T(128)S(1)} %copy-done.16, s32[2]{0:T(128)S(1)} %call_exported.0.refs_2_, bf16[1,8,2,220,220]{4,3,2,1,0:T(8,128)(2,1)S(1)} %copy.34.refs_3_.refs_4_, ...), custom_call_target="tpu_custom_call" | custom-call | flops 1022208000 | bytes 6000000 | tf_op jit(solution)/shard_map/encode/pallas_call | solution.py:206
  48.4 1.3 %collective-permute-done.5.refs_3_.refs_1_ = bf16[112,896]{1,0:T(8,128)(2,1)S(1)} collective-permute-done((bf16[112,896]{1,0:T(8,128)(2,1)S(1)}, bf16[112,896]{1,0:T(8,128)(2,1)S(1)}, u32[]{:S(2)}, u32[]{:S(2)}) %collective-permute-start.5) | collective-permute-done | bytes 200736 | tf_op jit(solution)/shard_map/ppermute | solution.py:171
  50.6 1.3 %collective-permute-done.8.refs_3_.refs_1_ = bf16[112,896]{1,0:T(8,128)(2,1)S(1)} collective-permute-done((bf16[112,896]{1,0:T(8,128)(2,1)S(1)}, bf16[112,896]{1,0:T(8,128)(2,1)S(1)}, u32[]{:S(2)}, u32[]{:S(2)}) %collective-permute-start.8) | collective-permute-done | bytes 200736 | tf_op jit(solution)/shard_map/ppermute | solution.py:171
  52.6 5.9 %collective-permute-start.10 = (bf16[112,896]{1,0:T(8,128)(2,1)S(1)}, bf16[112,896]{1,0:T(8,128)(2,1)S(1)}, u32[]{:S(2)}, u32[]{:S(2)}) collective-permute-start(bf16[112,896]{1,0:T(8,128)(2,1)S(1)} %add_select_fusion.1), channel_id=1, source_target_pairs={{0,4},{4,0},{8,12},{12,8},{1,5},{5,1},{9,13},{13,9},{2,6},{6,2},{1... | collective-permute-start | bytes 602120 | tf_op jit(solution)/shard_map/ppermute | solution.py:171
  58.5 2.9 %collective-permute-start.12 = (bf16[112,896]{1,0:T(8,128)(2,1)S(1)}, bf16[112,896]{1,0:T(8,128)(2,1)S(1)}, u32[]{:S(2)}, u32[]{:S(2)}) collective-permute-start(bf16[112,896]{1,0:T(8,128)(2,1)S(1)} %add_select_fusion), channel_id=1, source_target_pairs={{0,4},{4,0},{8,12},{12,8},{1,5},{5,1},{9,13},{13,9},{2,6},{6,2},{1... | collective-permute-start | bytes 602120 | tf_op jit(solution)/shard_map/ppermute | solution.py:171
  61.5 2.7 %collective-permute-start.14 = (bf16[112,896]{1,0:T(8,128)(2,1)S(1)}, bf16[112,896]{1,0:T(8,128)(2,1)S(1)}, u32[]{:S(2)}, u32[]{:S(2)}) collective-permute-start(bf16[112,896]{1,0:T(8,128)(2,1)S(1)} %add.61), channel_id=1, source_target_pairs={{0,4},{4,0},{8,12},{12,8},{1,5},{5,1},{9,13},{13,9},{2,6},{6,2},{1... | collective-permute-start | bytes 602120 | tf_op jit(solution)/shard_map/ppermute | solution.py:171
  64.9 1.6 %collective-permute-done.12.refs_3_.refs_1_ = bf16[112,896]{1,0:T(8,128)(2,1)S(1)} collective-permute-done((bf16[112,896]{1,0:T(8,128)(2,1)S(1)}, bf16[112,896]{1,0:T(8,128)(2,1)S(1)}, u32[]{:S(2)}, u32[]{:S(2)}) %collective-permute-start.12) | collective-permute-done | bytes 200736 | tf_op jit(solution)/shard_map/ppermute | solution.py:171
  67.4 1.7 %gradient.8 = f32[2,112]{1,0:T(2,128)S(1)} custom-call(bf16[112,896]{1,0:T(8,128)(2,1)S(1)} %copy-done.11, bf16[112,896]{1,0:T(8,128)(2,1)S(1)} %copy-done.13, bf16[112,896]{1,0:T(8,128)(2,1)} %collective-permute-done.1.refs_2_, bf16[112,896]{1,0:T(8,128)(2,1)S(1)} %collective-permute-done.2.refs_3_.refs_1_, bf16[2,2,2,224,220]{4,3,2,1,0:T(8,128)(2,1)S(1)} %copy-done.9), custom_call_target="tpu_custom_call" | custom-call | flops 774400 | bytes 1500000 | tf_op jit(solution)/shard_map/gradient/pallas_call | solution.py:255
  69.1 1.8 %gradient.9 = f32[2,112]{1,0:T(2,128)S(1)} custom-call(bf16[112,896]{1,0:T(8,128)(2,1)} %get-tuple-element.20.refs_0_, bf16[112,896]{1,0:T(8,128)(2,1)} %collective-permute-done.3.refs_1_, bf16[112,896]{1,0:T(8,128)(2,1)S(1)} %collective-permute-done.4.refs_2_, bf16[112,896]{1,0:T(8,128)(2,1)S(1)} %collective-permute-done.5.refs_3_.refs_1_, ...), custom_call_target="tpu_custom_call" | custom-call | flops 774400 | bytes 1500000 | tf_op jit(solution)/shard_map/gradient/pallas_call | solution.py:255
  70.9 1.8 %gradient.10 = f32[2,112]{1,0:T(2,128)S(1)} custom-call(bf16[112,896]{1,0:T(8,128)(2,1)} %get-tuple-element.22.refs_0_, bf16[112,896]{1,0:T(8,128)(2,1)} %collective-permute-done.6.refs_1_, bf16[112,896]{1,0:T(8,128)(2,1)S(1)} %collective-permute-done.7.refs_2_, bf16[112,896]{1,0:T(8,128)(2,1)S(1)} %collective-permute-done.8.refs_3_.refs_1_, ...), custom_call_target="tpu_custom_call" | custom-call | flops 774400 | bytes 1500000 | tf_op jit(solution)/shard_map/gradient/pallas_call | solution.py:255
  75.0 4.1 %collective-permute-start.16 = (bf16[112,896]{1,0:T(8,128)(2,1)S(1)}, bf16[112,896]{1,0:T(8,128)(2,1)S(1)}, u32[]{:S(2)}, u32[]{:S(2)}) collective-permute-start(bf16[112,896]{1,0:T(8,128)(2,1)S(1)} %add.63), channel_id=1, source_target_pairs={{0,4},{4,0},{8,12},{12,8},{1,5},{5,1},{9,13},{13,9},{2,6},{6,2},{1... | collective-permute-start | bytes 602120 | tf_op jit(solution)/shard_map/ppermute | solution.py:171
  79.4 3.4 %collective-permute-done.16.refs_3_ = bf16[112,896]{1,0:T(8,128)(2,1)S(1)} collective-permute-done((bf16[112,896]{1,0:T(8,128)(2,1)S(1)}, bf16[112,896]{1,0:T(8,128)(2,1)S(1)}, u32[]{:S(2)}, u32[]{:S(2)}) %collective-permute-start.16) | collective-permute-done | bytes 200736 | tf_op jit(solution)/shard_map/ppermute | solution.py:171
  83.6 1.4 %collective-permute-done.18.refs_3_ = bf16[112,896]{1,0:T(8,128)(2,1)S(1)} collective-permute-done((bf16[112,896]{1,0:T(8,128)(2,1)S(1)}, bf16[112,896]{1,0:T(8,128)(2,1)S(1)}, u32[]{:S(2)}, u32[]{:S(2)}) %collective-permute-start.18) | collective-permute-done | bytes 200736 | tf_op jit(solution)/shard_map/ppermute | solution.py:171
  85.8 6.3 %psum.7 = f32[8,220]{1,0:T(8,128)} all-reduce(f32[8,220]{1,0:T(8,128)S(1)} %reshape.3), channel_id=1, replica_groups=mesh['grp'=2,'slc'=4,'coil'=2,'vol'=2] {'coil','vol'}, use_global_device_ids=true, to_apply=%region_0.1 | all-reduce | flops 1760 | bytes 14080 | tf_op jit(solution)/shard_map/psum | solution.py:276
  (92 shorter events, 23.1 us)
Async XLA Ops:
  2.8 9.7 %copy-start = (bf16[2,8,2,220,220]{4,3,2,1,0:T(8,128)(2,1)}, bf16[2,8,2,220,220]{4,3,2,1,0:T(8,128)(2,1)S(1)}, u32[]{:S(2)}) copy-start(bf16[2,8,2,220,220]{4,3,2,1,0:T(8,128)(2,1)S(1)} %copy.36.refs_5_.refs_6_) | copy-start | bytes 9292804
  9.4 8.9 %copy-start.10 = (bf16[112,896]{1,0:T(8,128)(2,1)}, bf16[112,896]{1,0:T(8,128)(2,1)S(1)}, u32[]{:S(2)}) copy-start(bf16[112,896]{1,0:T(8,128)(2,1)S(1)} %get-tuple-element.17.refs_0_) | copy-start | bytes 602116
  9.4 8.9 %collective-permute-start = (bf16[112,896]{1,0:T(8,128)(2,1)S(1)}, bf16[112,896]{1,0:T(8,128)(2,1)S(1)}, u32[]{:S(2)}, u32[]{:S(2)}) collective-permute-start(bf16[112,896]{1,0:T(8,128)(2,1)S(1)} %get-tuple-element.17.refs_0_), channel_id=1, source_target_pairs={{0,4},{4,0},{8,12},{12,8},{1,5},{5,1},{9,13},{13,9},{2,6},{6,2},{1... | collective-permute-start | bytes 602120 | tf_op jit(solution)/shard_map/ppermute | solution.py:171
  12.5 15.3 %collective-permute-start.3 = (bf16[112,896]{1,0:T(8,128)(2,1)}, bf16[112,896]{1,0:T(8,128)(2,1)}, u32[]{:S(2)}, u32[]{:S(2)}) collective-permute-start(bf16[112,896]{1,0:T(8,128)(2,1)} %get-tuple-element.20.refs_0_), channel_id=1, source_target_pairs={{0,4},{4,0},{8,12},{12,8},{1,5},{5,1},{9,13},{13,9},{2,6},{6,2},{1... | collective-permute-start | bytes 602120 | tf_op jit(solution)/shard_map/ppermute | solution.py:171
  16.8 12.7 %collective-permute-start.6 = (bf16[112,896]{1,0:T(8,128)(2,1)}, bf16[112,896]{1,0:T(8,128)(2,1)}, u32[]{:S(2)}, u32[]{:S(2)}) collective-permute-start(bf16[112,896]{1,0:T(8,128)(2,1)} %get-tuple-element.22.refs_0_), channel_id=1, source_target_pairs={{0,4},{4,0},{8,12},{12,8},{1,5},{5,1},{9,13},{13,9},{2,6},{6,2},{1... | collective-permute-start | bytes 602120 | tf_op jit(solution)/shard_map/ppermute | solution.py:171
  19.1 12.2 %collective-permute-start.1 = (bf16[112,896]{1,0:T(8,128)(2,1)}, bf16[112,896]{1,0:T(8,128)(2,1)}, u32[]{:S(2)}, u32[]{:S(2)}) collective-permute-start(bf16[112,896]{1,0:T(8,128)(2,1)} %add.50), channel_id=1, source_target_pairs={{0,0},{4,8},{8,4},{12,12},{1,1},{5,9},{9,5},{13,13},{2,2},{6,10},{... | collective-permute-start | bytes 602120 | tf_op jit(solution)/shard_map/ppermute | solution.py:173
  28.9 10.7 %collective-permute-start.4 = (bf16[112,896]{1,0:T(8,128)(2,1)S(1)}, bf16[112,896]{1,0:T(8,128)(2,1)S(1)}, u32[]{:S(2)}, u32[]{:S(2)}) collective-permute-start(bf16[112,896]{1,0:T(8,128)(2,1)S(1)} %add.52), channel_id=1, source_target_pairs={{0,0},{4,8},{8,4},{12,12},{1,1},{5,9},{9,5},{13,13},{2,2},{6,10},{... | collective-permute-start | bytes 602120 | tf_op jit(solution)/shard_map/ppermute | solution.py:173
  30.6 11.0 %collective-permute-start.7 = (bf16[112,896]{1,0:T(8,128)(2,1)S(1)}, bf16[112,896]{1,0:T(8,128)(2,1)S(1)}, u32[]{:S(2)}, u32[]{:S(2)}) collective-permute-start(bf16[112,896]{1,0:T(8,128)(2,1)S(1)} %add.54), channel_id=1, source_target_pairs={{0,0},{4,8},{8,4},{12,12},{1,1},{5,9},{9,5},{13,13},{2,2},{6,10},{... | collective-permute-start | bytes 602120 | tf_op jit(solution)/shard_map/ppermute | solution.py:173
  32.3 13.1 %collective-permute-start.2 = (bf16[112,896]{1,0:T(8,128)(2,1)S(1)}, bf16[112,896]{1,0:T(8,128)(2,1)S(1)}, u32[]{:S(2)}, u32[]{:S(2)}) collective-permute-start(bf16[112,896]{1,0:T(8,128)(2,1)S(1)} %add_select_fusion.4), channel_id=1, source_target_pairs={{0,4},{4,0},{8,12},{12,8},{1,5},{5,1},{9,13},{13,9},{2,6},{6,2},{1... | collective-permute-start | bytes 602120 | tf_op jit(solution)/shard_map/ppermute | solution.py:171
  40.5 9.2 %collective-permute-start.5 = (bf16[112,896]{1,0:T(8,128)(2,1)S(1)}, bf16[112,896]{1,0:T(8,128)(2,1)S(1)}, u32[]{:S(2)}, u32[]{:S(2)}) collective-permute-start(bf16[112,896]{1,0:T(8,128)(2,1)S(1)} %add_select_fusion.3), channel_id=1, source_target_pairs={{0,4},{4,0},{8,12},{12,8},{1,5},{5,1},{9,13},{13,9},{2,6},{6,2},{1... | collective-permute-start | bytes 602120 | tf_op jit(solution)/shard_map/ppermute | solution.py:171
  42.6 9.3 %collective-permute-start.8 = (bf16[112,896]{1,0:T(8,128)(2,1)S(1)}, bf16[112,896]{1,0:T(8,128)(2,1)S(1)}, u32[]{:S(2)}, u32[]{:S(2)}) collective-permute-start(bf16[112,896]{1,0:T(8,128)(2,1)S(1)} %add_select_fusion.2), channel_id=1, source_target_pairs={{0,4},{4,0},{8,12},{12,8},{1,5},{5,1},{9,13},{13,9},{2,6},{6,2},{1... | collective-permute-start | bytes 602120 | tf_op jit(solution)/shard_map/ppermute | solution.py:171
  45.4 7.1 %collective-permute-start.9 = (bf16[112,896]{1,0:T(8,128)(2,1)S(1)}, bf16[112,896]{1,0:T(8,128)(2,1)S(1)}, u32[]{:S(2)}, u32[]{:S(2)}) collective-permute-start(bf16[112,896]{1,0:T(8,128)(2,1)S(1)} %add.56), channel_id=1, source_target_pairs={{0,0},{4,8},{8,4},{12,12},{1,1},{5,9},{9,5},{13,13},{2,2},{6,10},{... | collective-permute-start | bytes 602120 | tf_op jit(solution)/shard_map/ppermute | solution.py:173
  48.4 19.0 %copy-start.9 = (bf16[2,2,2,224,220]{4,3,2,1,0:T(8,128)(2,1)S(1)}, bf16[2,2,2,224,220]{4,3,2,1,0:T(8,128)(2,1)}, u32[]{:S(2)}) copy-start(bf16[2,2,2,224,220]{4,3,2,1,0:T(8,128)(2,1)} %copy-done.8) | copy-start | bytes 2365444
  48.4 19.0 %copy-start.13 = (bf16[112,896]{1,0:T(8,128)(2,1)S(1)}, bf16[112,896]{1,0:T(8,128)(2,1)}, u32[]{:S(2)}) copy-start(bf16[112,896]{1,0:T(8,128)(2,1)} %copy-done.12) | copy-start | bytes 602116
  49.7 21.1 %copy-start.7 = (bf16[2,2,2,224,220]{4,3,2,1,0:T(8,128)(2,1)S(1)}, bf16[2,2,2,224,220]{4,3,2,1,0:T(8,128)(2,1)}, u32[]{:S(2)}) copy-start(bf16[2,2,2,224,220]{4,3,2,1,0:T(8,128)(2,1)} %copy-done.6) | copy-start | bytes 2365444
  49.7 8.7 %collective-permute-start.11 = (bf16[112,896]{1,0:T(8,128)(2,1)S(1)}, bf16[112,896]{1,0:T(8,128)(2,1)S(1)}, u32[]{:S(2)}, u32[]{:S(2)}) collective-permute-start(bf16[112,896]{1,0:T(8,128)(2,1)S(1)} %add.58), channel_id=1, source_target_pairs={{0,0},{4,8},{8,4},{12,12},{1,1},{5,9},{9,5},{13,13},{2,2},{6,10},{... | collective-permute-start | bytes 602120 | tf_op jit(solution)/shard_map/ppermute | solution.py:173
  51.9 9.5 %collective-permute-start.13 = (bf16[112,896]{1,0:T(8,128)(2,1)S(1)}, bf16[112,896]{1,0:T(8,128)(2,1)S(1)}, u32[]{:S(2)}, u32[]{:S(2)}) collective-permute-start(bf16[112,896]{1,0:T(8,128)(2,1)S(1)} %add.60), channel_id=1, source_target_pairs={{0,0},{4,8},{8,4},{12,12},{1,1},{5,9},{9,5},{13,13},{2,2},{6,10},{... | collective-permute-start | bytes 602120 | tf_op jit(solution)/shard_map/ppermute | solution.py:173
  52.6 11.5 %collective-permute-start.10 = (bf16[112,896]{1,0:T(8,128)(2,1)S(1)}, bf16[112,896]{1,0:T(8,128)(2,1)S(1)}, u32[]{:S(2)}, u32[]{:S(2)}) collective-permute-start(bf16[112,896]{1,0:T(8,128)(2,1)S(1)} %add_select_fusion.1), channel_id=1, source_target_pairs={{0,4},{4,0},{8,12},{12,8},{1,5},{5,1},{9,13},{13,9},{2,6},{6,2},{1... | collective-permute-start | bytes 602120 | tf_op jit(solution)/shard_map/ppermute | solution.py:171
  58.5 7.9 %collective-permute-start.12 = (bf16[112,896]{1,0:T(8,128)(2,1)S(1)}, bf16[112,896]{1,0:T(8,128)(2,1)S(1)}, u32[]{:S(2)}, u32[]{:S(2)}) collective-permute-start(bf16[112,896]{1,0:T(8,128)(2,1)S(1)} %add_select_fusion), channel_id=1, source_target_pairs={{0,4},{4,0},{8,12},{12,8},{1,5},{5,1},{9,13},{13,9},{2,6},{6,2},{1... | collective-permute-start | bytes 602120 | tf_op jit(solution)/shard_map/ppermute | solution.py:171
  61.5 12.8 %collective-permute-start.14 = (bf16[112,896]{1,0:T(8,128)(2,1)S(1)}, bf16[112,896]{1,0:T(8,128)(2,1)S(1)}, u32[]{:S(2)}, u32[]{:S(2)}) collective-permute-start(bf16[112,896]{1,0:T(8,128)(2,1)S(1)} %add.61), channel_id=1, source_target_pairs={{0,4},{4,0},{8,12},{12,8},{1,5},{5,1},{9,13},{13,9},{2,6},{6,2},{1... | collective-permute-start | bytes 602120 | tf_op jit(solution)/shard_map/ppermute | solution.py:171
  64.2 10.8 %collective-permute-start.15 = (bf16[112,896]{1,0:T(8,128)(2,1)S(1)}, bf16[112,896]{1,0:T(8,128)(2,1)S(1)}, u32[]{:S(2)}, u32[]{:S(2)}) collective-permute-start(bf16[112,896]{1,0:T(8,128)(2,1)S(1)} %add.62), channel_id=1, source_target_pairs={{0,0},{4,8},{8,4},{12,12},{1,1},{5,9},{9,5},{13,13},{2,2},{6,10},{... | collective-permute-start | bytes 602120 | tf_op jit(solution)/shard_map/ppermute | solution.py:173
  66.5 12.6 %collective-permute-start.17 = (bf16[112,896]{1,0:T(8,128)(2,1)S(1)}, bf16[112,896]{1,0:T(8,128)(2,1)S(1)}, u32[]{:S(2)}, u32[]{:S(2)}) collective-permute-start(bf16[112,896]{1,0:T(8,128)(2,1)S(1)} %add.64), channel_id=1, source_target_pairs={{0,0},{4,8},{8,4},{12,12},{1,1},{5,9},{9,5},{13,13},{2,2},{6,10},{... | collective-permute-start | bytes 602120 | tf_op jit(solution)/shard_map/ppermute | solution.py:173
  75.0 7.8 %collective-permute-start.16 = (bf16[112,896]{1,0:T(8,128)(2,1)S(1)}, bf16[112,896]{1,0:T(8,128)(2,1)S(1)}, u32[]{:S(2)}, u32[]{:S(2)}) collective-permute-start(bf16[112,896]{1,0:T(8,128)(2,1)S(1)} %add.63), channel_id=1, source_target_pairs={{0,4},{4,0},{8,12},{12,8},{1,5},{5,1},{9,13},{13,9},{2,6},{6,2},{1... | collective-permute-start | bytes 602120 | tf_op jit(solution)/shard_map/ppermute | solution.py:171
  79.2 5.8 %collective-permute-start.18 = (bf16[112,896]{1,0:T(8,128)(2,1)S(1)}, bf16[112,896]{1,0:T(8,128)(2,1)S(1)}, u32[]{:S(2)}, u32[]{:S(2)}) collective-permute-start(bf16[112,896]{1,0:T(8,128)(2,1)S(1)} %add.65), channel_id=1, source_target_pairs={{0,4},{4,0},{8,12},{12,8},{1,5},{5,1},{9,13},{13,9},{2,6},{6,2},{1... | collective-permute-start | bytes 602120 | tf_op jit(solution)/shard_map/ppermute | solution.py:171
  (14 other events, 30.6 us)

commit v4 on v3

--- a/solution.py
+++ b/solution.py
@@ -68,14 +68,11 @@
 
 
 def encode_kernel(slots, group, whole_classes, *refs):
-    shift_ref, order_ref, place_ref = refs[:3]
-    image_refs, refs = refs[3 : 3 + slots], refs[3 + slots :]
-    map_refs, refs = refs[:slots], refs[slots:]
-    kspace_ref, offset_ref, left_ref, gram_ref, adjoint_ref, shifted_ref = refs[:6]
-    out_refs = refs[6:-2]
+    shift_ref, order_ref, place_ref, image_ref, map_ref, kspace_ref, offset_ref = refs[:7]
+    left_ref, gram_ref, adjoint_ref, shifted_ref = refs[7:11]
+    out_refs = refs[11:-2]
     total, angle = refs[-2:]
-    vols, coils = image_refs[0].shape[0], map_refs[0].shape[0]
-    length = image_refs[0].shape[-1]
+    vols, coils, length = image_ref.shape[0], map_ref.shape[0], image_ref.shape[-1]
     rows = shifted_ref.shape[-2]
     part = rows // len(out_refs)
     groups = order_ref.shape[0]
@@ -91,10 +88,10 @@
             place = vol * coils + coil
             sum_re = sum_im = None
             for slot in range(slots):
-                image_re = image_refs[slot][vol, 0, 0].astype(jnp.float32)
-                image_im = image_refs[slot][vol, 0, 1].astype(jnp.float32)
-                map_re = map_refs[slot][coil, 0, 0].astype(jnp.float32)
-                map_im = map_refs[slot][coil, 0, 1].astype(jnp.float32)
+                image_re = image_ref[vol, slot, 0].astype(jnp.float32)
+                image_im = image_ref[vol, slot, 1].astype(jnp.float32)
+                map_re = map_ref[coil, slot, 0].astype(jnp.float32)
+                map_im = map_ref[coil, slot, 1].astype(jnp.float32)
                 coil_re = (map_re * image_re - map_im * image_im).astype(jnp.bfloat16)
                 coil_im = (map_re * image_im + map_im * image_re).astype(jnp.bfloat16)
                 partly = dot(left_ref[0], coil_re) + dot(left_ref[1], coil_im)
@@ -155,25 +152,84 @@
         out_ref[slot : slot + 1, :] = factor * jnp.sum(sums[slot].T, axis=0, keepdims=True)
 
 
-def line_of_four(pieces):
+def after(value, *earlier):
+    return lax.optimization_barrier((value, *earlier))[0]
+
+
+def select_slices(array, group, slots, groups, within):
+    lead, per_device = array.shape[:2]
+    if within is None:
+        return array.reshape(lead, slots, groups, *array.shape[2:])[:, :, group]
+    return lax.dynamic_slice_in_dim(array, within, 1, axis=1)
+
+
+def sum_over_replicas(value):
+    axes = ("coil", "vol")
+    if any(lax.axis_size(axis) != 2 for axis in axes):
+        return lax.psum(value, axes)
+    swapped = [
+        lax.ppermute(value, axes, [(index, index ^ mask) for index in range(4)])
+        for mask in (1, 2, 3)
+    ]
+    return (value + swapped[0]) + (swapped[1] + swapped[2])
+
+
+def line_of_four(encode, gradient, count):
     position = lax.axis_index("slc")
     edge = (position == 0) | (position == 3)
     outer_pairs = [(0, 1), (1, 0), (2, 3), (3, 2)]
     inner_pairs = [(0, 0), (1, 2), (2, 1), (3, 3)]
-    count = len(pieces)
-    outer, inner = [], []
-    for step in range(count + LAG):
+    parts = ROW_PARTS
+    pieces, shifted, outer, inner, gradients = [], [], [], [], []
+
+    def encode_next(*earlier):
+        group = len(shifted)
+        if group * parts < count:
+            encoded = encode(group, *earlier)
+            shifted.append(encoded[0])
+            pieces.extend(encoded[1:])
+
+    def outer_next(*earlier):
+        step = len(outer)
         back = step - LAG
         payload = pieces[step] if step < count else None
         if back >= 0:
             others = pieces[back] + inner[back]
             payload = others if payload is None else jnp.where(edge, payload, others)
+        if earlier:
+            payload = after(payload, *earlier)
         outer.append(lax.ppermute(payload, "slc", outer_pairs))
-        if step < count:
-            inner.append(lax.ppermute(pieces[step] + outer[step], "slc", inner_pairs))
-    return [
-        (pieces[step], outer[step], inner[step], outer[step + LAG]) for step in range(count)
-    ]
+        return payload
+
+    def gradient_next(*earlier):
+        step = len(gradients)
+        terms = (pieces[step], outer[step], inner[step], outer[step + LAG])
+        own = after(terms[0], *earlier) if earlier else terms[0]
+        gradients.append(gradient(step, (own, *terms[1:]), shifted[step // parts]))
+
+    encode_next()
+    for _ in range(parts):
+        outer_next()
+    while len(pieces) < LAG:
+        encode_next()
+    while len(outer) < LAG:
+        outer_next()
+    latest = ()
+    for step in range(count):
+        half = pieces[step] + after(outer[step], *latest)
+        inner.append(lax.ppermute(half, "slc", inner_pairs))
+        if len(pieces) < min(count, step + LAG + 1):
+            encode_next(half)
+        latest = ()
+        if step >= 1:
+            latest = (outer_next(half),)
+        if step >= LAG + 1:
+            gradient_next(*latest)
+            latest = (*latest, gradients[-1])
+    last = outer_next(*latest)
+    while len(gradients) < count:
+        gradient_next(last)
+    return gradients
 
 
 def body(images, coil_maps, kspace, shift_index, phase_offset, group_order):
@@ -189,41 +245,32 @@
     tables = dft_matrices(length, rows)
     factor = 1.0 / (coils * lax.axis_size("coil") * vols * lax.axis_size("vol"))
     first = (lax.axis_index("slc") * per_device) % groups
-
-    def whole(array):
-        return pl.BlockSpec(array.shape, lambda i, *_: (0,) * array.ndim)
-
-    encoded, pieces = [], []
-    for group in range(groups):
+    on_line = whole_classes and groups == 4
+    in_vmem = pl.BlockSpec(memory_space=pltpu.VMEM)
+    in_smem = pl.BlockSpec(memory_space=pltpu.SMEM)
+
+    def encode(group, *earlier):
         if whole_classes:
-            place = np.zeros((2,), np.int32)
-            picks = [lambda i, *_, w=slot * groups + group: (0, w, 0, 0, 0) for slot in range(slots)]
+            within, place = None, np.zeros((2,), np.int32)
         else:
             within = group - first
             held = (within >= 0) & (within < per_device)
-            place = jnp.stack([held, jnp.where(held, within, 0)]).astype(jnp.int32)
-            picks = [lambda i, shift, order, place: (0, place[1], 0, 0, 0)]
-        outputs = pl.pallas_call(
+            within = jnp.where(held, within, 0)
+            place = jnp.stack([held, within]).astype(jnp.int32)
+        image, coil_map = images, coil_maps
+        if earlier:
+            image, coil_map, _ = lax.optimization_barrier((image, coil_map, earlier[0]))
+        return pl.pallas_call(
             functools.partial(encode_kernel, slots, group, whole_classes),
-            grid_spec=pltpu.PrefetchScalarGridSpec(
-                num_scalar_prefetch=3,
-                grid=(1,),
-                in_specs=[pl.BlockSpec((vols, 1, 2, length, length), pick) for pick in picks]
-                + [pl.BlockSpec((coils, 1, 2, length, length), pick) for pick in picks]
-                + [whole(array) for array in (kspace, phase_offset, *tables)],
-                out_specs=[
-                    pl.BlockSpec((slots, places, 2, rows, length), lambda i, *_: (0,) * 5),
-                ]
-                + [pl.BlockSpec((part, lanes), lambda i, *_: (0, 0))] * ROW_PARTS,
-                scratch_shapes=[
-                    pltpu.VMEM((rows, lanes), jnp.float32),
-                    pltpu.VMEM((round_up(slots, 8), round_up(rows, LANE_TILE)), jnp.float32),
-                ],
-            ),
+            in_specs=[in_smem] * 3 + [in_vmem] * 7,
             out_shape=[
                 jax.ShapeDtypeStruct((slots, places, 2, rows, length), jnp.bfloat16),
             ]
             + [jax.ShapeDtypeStruct((part, lanes), jnp.bfloat16)] * ROW_PARTS,
+            scratch_shapes=[
+                pltpu.VMEM((rows, lanes), jnp.float32),
+                pltpu.VMEM((round_up(slots, 8), round_up(rows, LANE_TILE)), jnp.float32),
+            ],
             compiler_params=pltpu.CompilerParams(vmem_limit_bytes=VMEM_BYTES),
             cost_estimate=pl.CostEstimate(
                 flops=places * (slots + 1) * 16 * length**3,
@@ -235,33 +282,34 @@
             shift_index,
             group_order,
             place,
-            *([images] * slots),
-            *([coil_maps] * slots),
+            select_slices(image, group, slots, groups, within),
+            select_slices(coil_map, group, slots, groups, within),
             kspace,
             phase_offset,
             *tables,
         )
-        encoded.append(outputs[0])
-        pieces.extend(outputs[1:])
-
-    on_line = whole_classes and groups == 4
-    if on_line:
-        terms = line_of_four(pieces)
-    else:
-        terms = [(piece,) for piece in lax.psum(pieces, "slc")]
-    gradients = []
-    for step, term in enumerate(terms):
-        group, index = divmod(step, ROW_PARTS)
-        gradient = pl.pallas_call(
-            functools.partial(gradient_kernel, index, factor, on_line),
+
+    def gradient(step, terms, encoded):
+        return pl.pallas_call(
+            functools.partial(gradient_kernel, step % ROW_PARTS, factor, on_line),
             out_shape=jax.ShapeDtypeStruct((slots, part), jnp.float32),
             compiler_params=pltpu.CompilerParams(vmem_limit_bytes=VMEM_BYTES),
             cost_estimate=pl.CostEstimate(
                 flops=places * slots * 4 * length**2, bytes_accessed=1_500_000, transcendentals=0
             ),
             name="gradient",
-        )(*term, encoded[group])
-        gradients.append(gradient)
+        )(*terms, encoded)
+
+    if on_line:
+        gradients = line_of_four(encode, gradient, groups * ROW_PARTS)
+    else:
+        encoded = [encode(group) for group in range(groups)]
+        reduced = lax.psum([list(outputs[1:]) for outputs in encoded], "slc")
+        gradients = [
+            gradient(index, (piece,), encoded[group][0])
+            for group in range(groups)
+            for index, piece in enumerate(reduced[group])
+        ]
     by_class = jnp.stack(
         [
             jnp.concatenate(gradients[group * ROW_PARTS : (group + 1) * ROW_PARTS], axis=1)
@@ -273,7 +321,7 @@
         local = by_class.reshape(per_device, length)
     else:
         local = lax.dynamic_slice_in_dim(by_class[0], first, per_device, axis=0)
-    return lax.psum(local, ("coil", "vol"))
+    return sum_over_replicas(local)
 
 
 def solution(mesh):

time: 92.9 us -> 83.6 us (0.90)
  blocking collectives: 6.35 us -> 0 us
  waiting for transfers between devices: 9.87 us -> 15.4 us
  other arithmetic: 6.63 us -> 2.36 us
  Pallas kernels: 19.7 us -> 15.5 us
    unnamed x41 -> x33, local copies, waits for them, and re-layouts: 10.4 us -> 1.45 us
    slice x0 -> x6, local copies, waits for them, and re-layouts: none -> 7.85 us  [select_slices(): return array.reshape(lead, slots, groups, *array.shape[2:])[:, :, group]]
    psum x1 -> x0, blocking collectives: 6.35 us -> none  [body(): return lax.psum(local, ('coil', 'vol'))]
    ppermute x19 -> x22, waiting for transfers between devices: 9.87 us -> 15.4 us  [the longest x11 12.6 us: outer_next(): outer.append(lax.ppermute(payload, 'slc', outer_pairs))]
    pallas_call x12, Pallas kernels: 19.7 us -> 15.5 us  [the longest x4 9.56 us: encode(): pl.pallas_call(functools.partial(encode_kernel, slots, group, whole_class...]
    select_n x5, other arithmetic: 3.01 us -> 0.21 us  [outer_next(): payload = others if payload is None else jnp.where(edge, payload, others)]
    add x11 -> x12, other arithmetic: 3.31 us -> 1.84 us  [the longest x8 1.08 us: line_of_four(): half = pieces[step] + after(outer[step], *latest)]
    ppermute x19 -> x22, starting transfers between devices: 38.8 us -> 39.5 us  [the longest x11 30.9 us: outer_next(): outer.append(lax.ppermute(payload, 'slc', outer_pairs))]
  transfers between devices with their start and end apart: 19 -> 22, of which waited for: 6 -> 7; matrix products, arithmetic and copies ran while one was open for 7% -> 8% of each run, Pallas kernels for 17% -> 15%
where the time goes in v4:
time: 83.6 us; the launch traced here: 82.9 us
  starting transfers between devices  39.5 us (47%)
  Pallas kernels  15.5 us (19%)
  waiting for transfers between devices  15.4 us (18%)
  local copies, waits for them, and re-layouts  9.71 us (12%)
  other arithmetic  2.36 us (3%)
    ppermute x11, starting transfers between devices, outer_next(): outer.append(lax.ppermute(payload, 'slc', outer_pairs))  30.9 us
    ppermute x11, waiting for transfers between devices, outer_next(): outer.append(lax.ppermute(payload, 'slc', outer_pairs))  12.6 us
    pallas_call x4, Pallas kernels, encode(): pl.pallas_call(functools.partial(encode_kernel, slots, group, whole_class...  9.56 us
    slice x6, local copies, waits for them, and re-layouts, select_slices(): return array.reshape(lead, slots, groups, *array.shape[2:])[:, :, group]  7.85 us
    ppermute x8, starting transfers between devices, line_of_four(): inner.append(lax.ppermute(half, 'slc', inner_pairs))  6.6 us
    pallas_call x8, Pallas kernels, gradient(): pl.pallas_call(functools.partial(gradient_kernel, step % ROW_PARTS, facto...  5.94 us
    ppermute x3, waiting for transfers between devices, sum_over_replicas(): lax.ppermute(value, axes, [(index, index ^ mask) for index in range(4)])  2.78 us
    ppermute x3, starting transfers between devices, sum_over_replicas(): lax.ppermute(value, axes, [(index, index ^ mask) for index in range(4)])  1.93 us
  transfers between devices with their start and end apart: 22, of which 7 were waited for; matrix products, arithmetic and copies ran while one was open for 8% of the time, Pallas kernels for 15%

profile of v4, /device:TPU:0, one launch (start us, length us, event | category | flops | bytes accessed | tf_op | source)
XLA Modules:
  0.0 82.9 jit_solution(11171678227109869558)
XLA Ops:
  0.0 2.8 %fusion = (bf16[2,2,1,2,220,220]{5,3,4,2,1,0:T(2,128)(2,1)S(1)}, bf16[2,2,1,2,220,220]{5,3,4,2,1,0:T(2,128)(2,1)S(1)}) fusion(bf16[2,2,4,2,220,220]{5,3,4,2,1,0:T(2,128)(2,1)} %bitcast.38), kind=kLoop, calls=%fused_computation.21 | loop fusion | bytes 3097600 | tf_op jit(solution)/shard_map/slice | solution.py:162
  5.0 2.3 %encode.4 = (bf16[2,2,2,224,220]{4,3,2,1,0:T(8,128)(2,1)S(1)}, bf16[112,896]{1,0:T(8,128)(2,1)S(1)}, bf16[112,896]{1,0:T(8,128)(2,1)S(1)}) custom-call(s32[8]{0:T(128)S(1)} %copy-done.3, s32[4]{0:T(128)S(1)} %copy-done.4, s32[2]{0:T(128)S(1)} %call_exported.0.refs_2_, bf16[1,2,2,220,220]{4,3,2,1,0:T(8,128)(2,1)S(1)} %get-tuple-element.86.refs_3_, ...), custom_call_target="tpu_custom_call" | custom-call | flops 1022208000 | bytes 6000000 | tf_op jit(solution)/shard_map/encode/pallas_call | solution.py:263
  7.3 3.6 %collective-permute-start = (bf16[112,896]{1,0:T(8,128)(2,1)S(1)}, bf16[112,896]{1,0:T(8,128)(2,1)S(1)}, u32[]{:S(2)}, u32[]{:S(2)}) collective-permute-start(bf16[112,896]{1,0:T(8,128)(2,1)S(1)} %get-tuple-element.61.refs_0_), channel_id=1, source_target_pairs={{0,4},{4,0},{8,12},{12,8},{1,5},{5,1},{9,13},{13,9},{2,6},{6,2},{1... | collective-permute-start | bytes 602120 | tf_op jit(solution)/shard_map/ppermute | solution.py:201
  11.0 5.7 %collective-permute-done.refs_1_ = bf16[112,896]{1,0:T(8,128)(2,1)S(1)} collective-permute-done((bf16[112,896]{1,0:T(8,128)(2,1)S(1)}, bf16[112,896]{1,0:T(8,128)(2,1)S(1)}, u32[]{:S(2)}, u32[]{:S(2)}) %collective-permute-start) | collective-permute-done | bytes 200736 | tf_op jit(solution)/shard_map/ppermute | solution.py:201
  17.4 1.6 %collective-permute-start.1 = (bf16[112,896]{1,0:T(8,128)(2,1)}, bf16[112,896]{1,0:T(8,128)(2,1)S(1)}, u32[]{:S(2)}, u32[]{:S(2)}) collective-permute-start(bf16[112,896]{1,0:T(8,128)(2,1)} %add.57), channel_id=1, source_target_pairs={{0,0},{4,8},{8,4},{12,12},{1,1},{5,9},{9,5},{13,13},{2,2},{6,10},{... | collective-permute-start | bytes 602120 | tf_op jit(solution)/shard_map/ppermute | solution.py:220
  19.0 2.8 %encode.5 = (bf16[2,2,2,224,220]{4,3,2,1,0:T(8,128)(2,1)S(1)}, bf16[112,896]{1,0:T(8,128)(2,1)S(1)}, bf16[112,896]{1,0:T(8,128)(2,1)S(1)}) custom-call(s32[8]{0:T(128)S(1)} %copy-done.3, s32[4]{0:T(128)S(1)} %copy-done.4, s32[2]{0:T(128)S(1)} %call_exported.0.refs_2_, bf16[1,2,2,220,220]{4,3,2,1,0:T(8,128)(2,1)S(1)} %get-tuple-element.85.refs_3_, ...), custom_call_target="tpu_custom_call" | custom-call | flops 1022208000 | bytes 6000000 | tf_op jit(solution)/shard_map/encode/pallas_call | solution.py:263
  21.8 3.0 %collective-permute-start.5 = (bf16[112,896]{1,0:T(8,128)(2,1)S(1)}, bf16[112,896]{1,0:T(8,128)(2,1)S(1)}, u32[]{:S(2)}, u32[]{:S(2)}) collective-permute-start(bf16[112,896]{1,0:T(8,128)(2,1)S(1)} %get-tuple-element.69.refs_0_), channel_id=1, source_target_pairs={{0,4},{4,0},{8,12},{12,8},{1,5},{5,1},{9,13},{13,9},{2,6},{6,2},{1... | collective-permute-start | bytes 602120 | tf_op jit(solution)/shard_map/ppermute | solution.py:201
  25.7 2.0 %slice.41 = bf16[2,2,1,2,220,220]{5,3,4,2,1,0:T(2,128)(2,1)S(1)} slice(bf16[2,2,4,2,220,220]{5,3,4,2,1,0:T(2,128)(2,1)} %bitcast.39), slice={[0:2], [0:2], [2:3], [0:2], [0:220], [0:220]} | slice | bytes 1548800 | tf_op jit(solution)/shard_map/slice | solution.py:162
  28.3 2.3 %encode.6 = (bf16[2,2,2,224,220]{4,3,2,1,0:T(8,128)(2,1)S(1)}, bf16[112,896]{1,0:T(8,128)(2,1)S(1)}, bf16[112,896]{1,0:T(8,128)(2,1)S(1)}) custom-call(s32[8]{0:T(128)S(1)} %copy-done.3, s32[4]{0:T(128)S(1)} %copy-done.4, s32[2]{0:T(128)S(1)} %call_exported.0.refs_2_, bf16[1,2,2,220,220]{4,3,2,1,0:T(8,128)(2,1)S(1)} %bitcast.37, ...), custom_call_target="tpu_custom_call" | custom-call | flops 1022208000 | bytes 6000000 | tf_op jit(solution)/shard_map/encode/pallas_call | solution.py:263
  30.6 2.5 %collective-permute-start.3 = (bf16[112,896]{1,0:T(8,128)(2,1)S(1)}, bf16[112,896]{1,0:T(8,128)(2,1)S(1)}, u32[]{:S(2)}, u32[]{:S(2)}) collective-permute-start(bf16[112,896]{1,0:T(8,128)(2,1)S(1)} %add_select_fusion.4), channel_id=1, source_target_pairs={{0,4},{4,0},{8,12},{12,8},{1,5},{5,1},{9,13},{13,9},{2,6},{6,2},{1... | collective-permute-start | bytes 602120 | tf_op jit(solution)/shard_map/ppermute | solution.py:201
  33.9 2.4 %collective-permute-start.7 = (bf16[112,896]{1,0:T(8,128)(2,1)S(1)}, bf16[112,896]{1,0:T(8,128)(2,1)S(1)}, u32[]{:S(2)}, u32[]{:S(2)}) collective-permute-start(bf16[112,896]{1,0:T(8,128)(2,1)S(1)} %add_select_fusion.3), channel_id=1, source_target_pairs={{0,4},{4,0},{8,12},{12,8},{1,5},{5,1},{9,13},{13,9},{2,6},{6,2},{1... | collective-permute-start | bytes 602120 | tf_op jit(solution)/shard_map/ppermute | solution.py:201
  36.2 1.9 %collective-permute-done.3.refs_3_.refs_1_ = bf16[112,896]{1,0:T(8,128)(2,1)S(1)} collective-permute-done((bf16[112,896]{1,0:T(8,128)(2,1)S(1)}, bf16[112,896]{1,0:T(8,128)(2,1)S(1)}, u32[]{:S(2)}, u32[]{:S(2)}) %collective-permute-start.3) | collective-permute-done | bytes 200736 | tf_op jit(solution)/shard_map/ppermute | solution.py:201
  39.0 1.8 %slice.43 = bf16[2,2,1,2,220,220]{5,3,4,2,1,0:T(2,128)(2,1)S(1)} slice(bf16[2,2,4,2,220,220]{5,3,4,2,1,0:T(2,128)(2,1)} %bitcast.40), slice={[0:2], [0:2], [3:4], [0:2], [0:220], [0:220]} | slice | bytes 1548800 | tf_op jit(solution)/shard_map/slice | solution.py:162
  41.3 4.2 %collective-permute-start.10 = (bf16[112,896]{1,0:T(8,128)(2,1)S(1)}, bf16[112,896]{1,0:T(8,128)(2,1)S(1)}, u32[]{:S(2)}, u32[]{:S(2)}) collective-permute-start(bf16[112,896]{1,0:T(8,128)(2,1)S(1)} %add_select_fusion.1), channel_id=1, source_target_pairs={{0,4},{4,0},{8,12},{12,8},{1,5},{5,1},{9,13},{13,9},{2,6},{6,2},{1... | collective-permute-start | bytes 602120 | tf_op jit(solution)/shard_map/ppermute | solution.py:201
  46.4 2.3 %encode.7 = (bf16[2,2,2,224,220]{4,3,2,1,0:T(8,128)(2,1)S(1)}, bf16[112,896]{1,0:T(8,128)(2,1)S(1)}, bf16[112,896]{1,0:T(8,128)(2,1)S(1)}) custom-call(s32[8]{0:T(128)S(1)} %copy-done.3, s32[4]{0:T(128)S(1)} %copy-done.4, s32[2]{0:T(128)S(1)} %call_exported.0.refs_2_, bf16[1,2,2,220,220]{4,3,2,1,0:T(8,128)(2,1)S(1)} %bitcast.36, ...), custom_call_target="tpu_custom_call" | custom-call | flops 1022208000 | bytes 6000000 | tf_op jit(solution)/shard_map/encode/pallas_call | solution.py:263
  48.8 2.2 %collective-permute-start.12 = (bf16[112,896]{1,0:T(8,128)(2,1)S(1)}, bf16[112,896]{1,0:T(8,128)(2,1)S(1)}, u32[]{:S(2)}, u32[]{:S(2)}) collective-permute-start(bf16[112,896]{1,0:T(8,128)(2,1)S(1)} %add_select_fusion.2), channel_id=1, source_target_pairs={{0,4},{4,0},{8,12},{12,8},{1,5},{5,1},{9,13},{13,9},{2,6},{6,2},{1... | collective-permute-start | bytes 602120 | tf_op jit(solution)/shard_map/ppermute | solution.py:201
  52.5 3.8 %collective-permute-start.14 = (bf16[112,896]{1,0:T(8,128)(2,1)S(1)}, bf16[112,896]{1,0:T(8,128)(2,1)S(1)}, u32[]{:S(2)}, u32[]{:S(2)}) collective-permute-start(bf16[112,896]{1,0:T(8,128)(2,1)S(1)} %add_select_fusion), channel_id=1, source_target_pairs={{0,4},{4,0},{8,12},{12,8},{1,5},{5,1},{9,13},{13,9},{2,6},{6,2},{1... | collective-permute-start | bytes 602120 | tf_op jit(solution)/shard_map/ppermute | solution.py:201
  58.6 1.5 %collective-permute-done.14.refs_3_.refs_1_ = bf16[112,896]{1,0:T(8,128)(2,1)S(1)} collective-permute-done((bf16[112,896]{1,0:T(8,128)(2,1)S(1)}, bf16[112,896]{1,0:T(8,128)(2,1)S(1)}, u32[]{:S(2)}, u32[]{:S(2)}) %collective-permute-start.14) | collective-permute-done | bytes 200736 | tf_op jit(solution)/shard_map/ppermute | solution.py:201
  60.8 4.2 %collective-permute-start.16 = (bf16[112,896]{1,0:T(8,128)(2,1)S(1)}, bf16[112,896]{1,0:T(8,128)(2,1)S(1)}, u32[]{:S(2)}, u32[]{:S(2)}) collective-permute-start(bf16[112,896]{1,0:T(8,128)(2,1)S(1)} %add.68), channel_id=1, source_target_pairs={{0,4},{4,0},{8,12},{12,8},{1,5},{5,1},{9,13},{13,9},{2,6},{6,2},{1... | collective-permute-start | bytes 602120 | tf_op jit(solution)/shard_map/ppermute | solution.py:201
  66.0 4.9 %collective-permute-start.17 = (bf16[112,896]{1,0:T(8,128)(2,1)S(1)}, bf16[112,896]{1,0:T(8,128)(2,1)S(1)}, u32[]{:S(2)}, u32[]{:S(2)}) collective-permute-start(bf16[112,896]{1,0:T(8,128)(2,1)S(1)} %add.70), channel_id=1, source_target_pairs={{0,4},{4,0},{8,12},{12,8},{1,5},{5,1},{9,13},{13,9},{2,6},{6,2},{1... | collective-permute-start | bytes 602120 | tf_op jit(solution)/shard_map/ppermute | solution.py:201
  72.6 2.0 %collective-permute-done.17.refs_3_ = bf16[112,896]{1,0:T(8,128)(2,1)S(1)} collective-permute-done((bf16[112,896]{1,0:T(8,128)(2,1)S(1)}, bf16[112,896]{1,0:T(8,128)(2,1)S(1)}, u32[]{:S(2)}, u32[]{:S(2)}) %collective-permute-start.17) | collective-permute-done | bytes 200736 | tf_op jit(solution)/shard_map/ppermute | solution.py:201
  75.4 1.4 %collective-permute-done.18.refs_3_ = bf16[112,896]{1,0:T(8,128)(2,1)S(1)} collective-permute-done((bf16[112,896]{1,0:T(8,128)(2,1)S(1)}, bf16[112,896]{1,0:T(8,128)(2,1)S(1)}, u32[]{:S(2)}, u32[]{:S(2)}) %collective-permute-start.18) | collective-permute-done | bytes 200736 | tf_op jit(solution)/shard_map/ppermute | solution.py:201
  77.7 1.6 %collective-permute-start.20 = (f32[8,220]{1,0:T(8,128)S(1)}, f32[8,220]{1,0:T(8,128)S(1)}, u32[]{:S(2)}, u32[]{:S(2)}) collective-permute-start(f32[8,220]{1,0:T(8,128)S(1)} %reshape.29), channel_id=1, source_target_pairs={{0,2},{1,3},{2,0},{3,1},{4,6},{5,7},{6,4},{7,5},{8,10},{9,11},{10,... | collective-permute-start | bytes 21128 | tf_op jit(solution)/shard_map/ppermute | solution.py:171
  79.6 1.9 %collective-permute-done.20 = f32[8,220]{1,0:T(8,128)S(1)} collective-permute-done((f32[8,220]{1,0:T(8,128)S(1)}, f32[8,220]{1,0:T(8,128)S(1)}, u32[]{:S(2)}, u32[]{:S(2)}) %collective-permute-start.20) | collective-permute-done | bytes 7072 | tf_op jit(solution)/shard_map/ppermute | solution.py:171
  (98 shorter events, 17.9 us)
Async XLA Ops:
  0.0 3.5 %copy-start.13 = (bf16[1,1,2,2,220,220]{5,3,4,2,1,0:T(2,128)(2,1)S(1)}, bf16[1,1,2,2,220,220]{5,3,4,2,1,0:T(2,128)(2,1)}, u32[]{:S(2)}) copy-start(bf16[1,1,2,2,220,220]{5,3,4,2,1,0:T(2,128)(2,1)} %param.15) | copy-start | bytes 1161604
  3.6 15.4 %copy-start = (bf16[1,1,2,2,220,220]{5,4,3,2,1,0:T(8,128)(2,1)}, bf16[1,1,2,2,220,220]{5,4,3,2,1,0:T(8,128)(2,1)S(1)}, u32[]{:S(2)}) copy-start(bf16[1,1,2,2,220,220]{5,4,3,2,1,0:T(8,128)(2,1)S(1)} %copy.22.refs_5_) | copy-start | bytes 1161604
  7.3 9.4 %collective-permute-start = (bf16[112,896]{1,0:T(8,128)(2,1)S(1)}, bf16[112,896]{1,0:T(8,128)(2,1)S(1)}, u32[]{:S(2)}, u32[]{:S(2)}) collective-permute-start(bf16[112,896]{1,0:T(8,128)(2,1)S(1)} %get-tuple-element.61.refs_0_), channel_id=1, source_target_pairs={{0,4},{4,0},{8,12},{12,8},{1,5},{5,1},{9,13},{13,9},{2,6},{6,2},{1... | collective-permute-start | bytes 602120 | tf_op jit(solution)/shard_map/ppermute | solution.py:201
  10.9 14.0 %collective-permute-start.2 = (bf16[112,896]{1,0:T(8,128)(2,1)S(1)}, bf16[112,896]{1,0:T(8,128)(2,1)S(1)}, u32[]{:S(2)}, u32[]{:S(2)}) collective-permute-start(bf16[112,896]{1,0:T(8,128)(2,1)S(1)} %get-tuple-element.66.refs_0_), channel_id=1, source_target_pairs={{0,4},{4,0},{8,12},{12,8},{1,5},{5,1},{9,13},{13,9},{2,6},{6,2},{1... | collective-permute-start | bytes 602120 | tf_op jit(solution)/shard_map/ppermute | solution.py:201
  17.4 13.1 %collective-permute-start.1 = (bf16[112,896]{1,0:T(8,128)(2,1)}, bf16[112,896]{1,0:T(8,128)(2,1)S(1)}, u32[]{:S(2)}, u32[]{:S(2)}) collective-permute-start(bf16[112,896]{1,0:T(8,128)(2,1)} %add.57), channel_id=1, source_target_pairs={{0,0},{4,8},{8,4},{12,12},{1,1},{5,9},{9,5},{13,13},{2,2},{6,10},{... | collective-permute-start | bytes 602120 | tf_op jit(solution)/shard_map/ppermute | solution.py:220
  21.8 11.3 %collective-permute-start.5 = (bf16[112,896]{1,0:T(8,128)(2,1)S(1)}, bf16[112,896]{1,0:T(8,128)(2,1)S(1)}, u32[]{:S(2)}, u32[]{:S(2)}) collective-permute-start(bf16[112,896]{1,0:T(8,128)(2,1)S(1)} %get-tuple-element.69.refs_0_), channel_id=1, source_target_pairs={{0,4},{4,0},{8,12},{12,8},{1,5},{5,1},{9,13},{13,9},{2,6},{6,2},{1... | collective-permute-start | bytes 602120 | tf_op jit(solution)/shard_map/ppermute | solution.py:201
  24.9 8.9 %collective-permute-start.4 = (bf16[112,896]{1,0:T(8,128)(2,1)S(1)}, bf16[112,896]{1,0:T(8,128)(2,1)S(1)}, u32[]{:S(2)}, u32[]{:S(2)}) collective-permute-start(bf16[112,896]{1,0:T(8,128)(2,1)S(1)} %add.59), channel_id=1, source_target_pairs={{0,0},{4,8},{8,4},{12,12},{1,1},{5,9},{9,5},{13,13},{2,2},{6,10},{... | collective-permute-start | bytes 602120 | tf_op jit(solution)/shard_map/ppermute | solution.py:220
  30.6 7.6 %collective-permute-start.3 = (bf16[112,896]{1,0:T(8,128)(2,1)S(1)}, bf16[112,896]{1,0:T(8,128)(2,1)S(1)}, u32[]{:S(2)}, u32[]{:S(2)}) collective-permute-start(bf16[112,896]{1,0:T(8,128)(2,1)S(1)} %add_select_fusion.4), channel_id=1, source_target_pairs={{0,4},{4,0},{8,12},{12,8},{1,5},{5,1},{9,13},{13,9},{2,6},{6,2},{1... | collective-permute-start | bytes 602120 | tf_op jit(solution)/shard_map/ppermute | solution.py:201
  33.1 5.8 %collective-permute-start.8 = (bf16[112,896]{1,0:T(8,128)(2,1)S(1)}, bf16[112,896]{1,0:T(8,128)(2,1)S(1)}, u32[]{:S(2)}, u32[]{:S(2)}) collective-permute-start(bf16[112,896]{1,0:T(8,128)(2,1)S(1)} %add.61), channel_id=1, source_target_pairs={{0,0},{4,8},{8,4},{12,12},{1,1},{5,9},{9,5},{13,13},{2,2},{6,10},{... | collective-permute-start | bytes 602120 | tf_op jit(solution)/shard_map/ppermute | solution.py:220
  33.9 11.6 %collective-permute-start.7 = (bf16[112,896]{1,0:T(8,128)(2,1)S(1)}, bf16[112,896]{1,0:T(8,128)(2,1)S(1)}, u32[]{:S(2)}, u32[]{:S(2)}) collective-permute-start(bf16[112,896]{1,0:T(8,128)(2,1)S(1)} %add_select_fusion.3), channel_id=1, source_target_pairs={{0,4},{4,0},{8,12},{12,8},{1,5},{5,1},{9,13},{13,9},{2,6},{6,2},{1... | collective-permute-start | bytes 602120 | tf_op jit(solution)/shard_map/ppermute | solution.py:201
  38.2 10.5 %collective-permute-start.6 = (bf16[112,896]{1,0:T(8,128)(2,1)S(1)}, bf16[112,896]{1,0:T(8,128)(2,1)S(1)}, u32[]{:S(2)}, u32[]{:S(2)}) collective-permute-start(bf16[112,896]{1,0:T(8,128)(2,1)S(1)} %add.62), channel_id=1, source_target_pairs={{0,0},{4,8},{8,4},{12,12},{1,1},{5,9},{9,5},{13,13},{2,2},{6,10},{... | collective-permute-start | bytes 602120 | tf_op jit(solution)/shard_map/ppermute | solution.py:220
  41.3 10.4 %collective-permute-start.10 = (bf16[112,896]{1,0:T(8,128)(2,1)S(1)}, bf16[112,896]{1,0:T(8,128)(2,1)S(1)}, u32[]{:S(2)}, u32[]{:S(2)}) collective-permute-start(bf16[112,896]{1,0:T(8,128)(2,1)S(1)} %add_select_fusion.1), channel_id=1, source_target_pairs={{0,4},{4,0},{8,12},{12,8},{1,5},{5,1},{9,13},{13,9},{2,6},{6,2},{1... | collective-permute-start | bytes 602120 | tf_op jit(solution)/shard_map/ppermute | solution.py:201
  45.6 6.9 %collective-permute-start.9 = (bf16[112,896]{1,0:T(8,128)(2,1)S(1)}, bf16[112,896]{1,0:T(8,128)(2,1)S(1)}, u32[]{:S(2)}, u32[]{:S(2)}) collective-permute-start(bf16[112,896]{1,0:T(8,128)(2,1)S(1)} %add.65), channel_id=1, source_target_pairs={{0,0},{4,8},{8,4},{12,12},{1,1},{5,9},{9,5},{13,13},{2,2},{6,10},{... | collective-permute-start | bytes 602120 | tf_op jit(solution)/shard_map/ppermute | solution.py:220
  48.8 8.2 %collective-permute-start.12 = (bf16[112,896]{1,0:T(8,128)(2,1)S(1)}, bf16[112,896]{1,0:T(8,128)(2,1)S(1)}, u32[]{:S(2)}, u32[]{:S(2)}) collective-permute-start(bf16[112,896]{1,0:T(8,128)(2,1)S(1)} %add_select_fusion.2), channel_id=1, source_target_pairs={{0,4},{4,0},{8,12},{12,8},{1,5},{5,1},{9,13},{13,9},{2,6},{6,2},{1... | collective-permute-start | bytes 602120 | tf_op jit(solution)/shard_map/ppermute | solution.py:201
  51.7 6.0 %collective-permute-start.11 = (bf16[112,896]{1,0:T(8,128)(2,1)S(1)}, bf16[112,896]{1,0:T(8,128)(2,1)S(1)}, u32[]{:S(2)}, u32[]{:S(2)}) collective-permute-start(bf16[112,896]{1,0:T(8,128)(2,1)S(1)} %add.67), channel_id=1, source_target_pairs={{0,0},{4,8},{8,4},{12,12},{1,1},{5,9},{9,5},{13,13},{2,2},{6,10},{... | collective-permute-start | bytes 602120 | tf_op jit(solution)/shard_map/ppermute | solution.py:220
  52.5 7.6 %collective-permute-start.14 = (bf16[112,896]{1,0:T(8,128)(2,1)S(1)}, bf16[112,896]{1,0:T(8,128)(2,1)S(1)}, u32[]{:S(2)}, u32[]{:S(2)}) collective-permute-start(bf16[112,896]{1,0:T(8,128)(2,1)S(1)} %add_select_fusion), channel_id=1, source_target_pairs={{0,4},{4,0},{8,12},{12,8},{1,5},{5,1},{9,13},{13,9},{2,6},{6,2},{1... | collective-permute-start | bytes 602120 | tf_op jit(solution)/shard_map/ppermute | solution.py:201
  57.1 8.1 %collective-permute-start.13 = (bf16[112,896]{1,0:T(8,128)(2,1)S(1)}, bf16[112,896]{1,0:T(8,128)(2,1)S(1)}, u32[]{:S(2)}, u32[]{:S(2)}) collective-permute-start(bf16[112,896]{1,0:T(8,128)(2,1)S(1)} %add.69), channel_id=1, source_target_pairs={{0,0},{4,8},{8,4},{12,12},{1,1},{5,9},{9,5},{13,13},{2,2},{6,10},{... | collective-permute-start | bytes 602120 | tf_op jit(solution)/shard_map/ppermute | solution.py:220
  60.1 5.1 %collective-permute-start.15 = (bf16[112,896]{1,0:T(8,128)(2,1)S(1)}, bf16[112,896]{1,0:T(8,128)(2,1)S(1)}, u32[]{:S(2)}, u32[]{:S(2)}) collective-permute-start(bf16[112,896]{1,0:T(8,128)(2,1)S(1)} %add.71), channel_id=1, source_target_pairs={{0,0},{4,8},{8,4},{12,12},{1,1},{5,9},{9,5},{13,13},{2,2},{6,10},{... | collective-permute-start | bytes 602120 | tf_op jit(solution)/shard_map/ppermute | solution.py:220
  60.8 10.9 %collective-permute-start.16 = (bf16[112,896]{1,0:T(8,128)(2,1)S(1)}, bf16[112,896]{1,0:T(8,128)(2,1)S(1)}, u32[]{:S(2)}, u32[]{:S(2)}) collective-permute-start(bf16[112,896]{1,0:T(8,128)(2,1)S(1)} %add.68), channel_id=1, source_target_pairs={{0,4},{4,0},{8,12},{12,8},{1,5},{5,1},{9,13},{13,9},{2,6},{6,2},{1... | collective-permute-start | bytes 602120 | tf_op jit(solution)/shard_map/ppermute | solution.py:201
  66.0 8.6 %collective-permute-start.17 = (bf16[112,896]{1,0:T(8,128)(2,1)S(1)}, bf16[112,896]{1,0:T(8,128)(2,1)S(1)}, u32[]{:S(2)}, u32[]{:S(2)}) collective-permute-start(bf16[112,896]{1,0:T(8,128)(2,1)S(1)} %add.70), channel_id=1, source_target_pairs={{0,4},{4,0},{8,12},{12,8},{1,5},{5,1},{9,13},{13,9},{2,6},{6,2},{1... | collective-permute-start | bytes 602120 | tf_op jit(solution)/shard_map/ppermute | solution.py:201
  70.9 5.8 %collective-permute-start.18 = (bf16[112,896]{1,0:T(8,128)(2,1)S(1)}, bf16[112,896]{1,0:T(8,128)(2,1)S(1)}, u32[]{:S(2)}, u32[]{:S(2)}) collective-permute-start(bf16[112,896]{1,0:T(8,128)(2,1)S(1)} %add.72), channel_id=1, source_target_pairs={{0,4},{4,0},{8,12},{12,8},{1,5},{5,1},{9,13},{13,9},{2,6},{6,2},{1... | collective-permute-start | bytes 602120 | tf_op jit(solution)/shard_map/ppermute | solution.py:201
  77.6 1.9 %collective-permute-start.19 = (f32[8,220]{1,0:T(8,128)S(1)}, f32[8,220]{1,0:T(8,128)S(1)}, u32[]{:S(2)}, u32[]{:S(2)}) collective-permute-start(f32[8,220]{1,0:T(8,128)S(1)} %reshape.29), channel_id=1, source_target_pairs={{0,1},{1,0},{2,3},{3,2},{4,5},{5,4},{6,7},{7,6},{8,9},{9,8},{10,11... | collective-permute-start | bytes 21128 | tf_op jit(solution)/shard_map/ppermute | solution.py:171
  77.7 3.7 %collective-permute-start.20 = (f32[8,220]{1,0:T(8,128)S(1)}, f32[8,220]{1,0:T(8,128)S(1)}, u32[]{:S(2)}, u32[]{:S(2)}) collective-permute-start(f32[8,220]{1,0:T(8,128)S(1)} %reshape.29), channel_id=1, source_target_pairs={{0,2},{1,3},{2,0},{3,1},{4,6},{5,7},{6,4},{7,5},{8,10},{9,11},{10,... | collective-permute-start | bytes 21128 | tf_op jit(solution)/shard_map/ppermute | solution.py:171
  79.3 3.1 %collective-permute-start.21 = (f32[8,220]{1,0:T(8,128)S(1)}, f32[8,220]{1,0:T(8,128)S(1)}, u32[]{:S(2)}, u32[]{:S(2)}) collective-permute-start(f32[8,220]{1,0:T(8,128)S(1)} %reshape.29), channel_id=1, source_target_pairs={{0,3},{1,2},{2,1},{3,0},{4,7},{5,6},{6,5},{7,4},{8,11},{9,10},{10,... | collective-permute-start | bytes 21128 | tf_op jit(solution)/shard_map/ppermute | solution.py:171
  (12 other events, 25.5 us)

commit v5 on v4

--- a/solution.py
+++ b/solution.py
@@ -69,11 +69,12 @@
 
 def encode_kernel(slots, group, whole_classes, *refs):
     shift_ref, order_ref, place_ref, image_ref, map_ref, kspace_ref, offset_ref = refs[:7]
-    left_ref, gram_ref, adjoint_ref, shifted_ref = refs[7:11]
-    out_refs = refs[11:-2]
-    total, angle = refs[-2:]
+    left_ref, gram_ref, adjoint_ref, kept_ref = refs[7:11]
+    out_refs = refs[11:-4]
+    total, angle, shifted_ref, copied = refs[-4:]
     vols, coils, length = image_ref.shape[0], map_ref.shape[0], image_ref.shape[-1]
     rows = shifted_ref.shape[-2]
+    copies = []
     part = rows // len(out_refs)
     groups = order_ref.shape[0]
     if whole_classes:
@@ -87,11 +88,11 @@
         for coil in range(coils):
             place = vol * coils + coil
             sum_re = sum_im = None
-            for slot in range(slots):
-                image_re = image_ref[vol, slot, 0].astype(jnp.float32)
-                image_im = image_ref[vol, slot, 1].astype(jnp.float32)
-                map_re = map_ref[coil, slot, 0].astype(jnp.float32)
-                map_im = map_ref[coil, slot, 1].astype(jnp.float32)
+            for slot, pick in enumerate(rows_of):
+                image_re = image_ref[vol, pick, 0].astype(jnp.float32)
+                image_im = image_ref[vol, pick, 1].astype(jnp.float32)
+                map_re = map_ref[coil, pick, 0].astype(jnp.float32)
+                map_im = map_ref[coil, pick, 1].astype(jnp.float32)
                 coil_re = (map_re * image_re - map_im * image_im).astype(jnp.bfloat16)
                 coil_im = (map_re * image_im + map_im * image_re).astype(jnp.bfloat16)
                 partly = dot(left_ref[0], coil_re) + dot(left_ref[1], coil_im)
@@ -102,6 +103,11 @@
                 shift_im = part_re * sine + part_im * cosine
                 shifted_ref[slot, place, 0] = shift_re.astype(jnp.bfloat16)
                 shifted_ref[slot, place, 1] = shift_im.astype(jnp.bfloat16)
+                copy = pltpu.make_async_copy(
+                    shifted_ref.at[slot, place], kept_ref.at[slot, place], copied.at[slot, place]
+                )
+                copy.start()
+                copies.append(copy)
                 sum_re = shift_re if slot == 0 else sum_re + shift_re
                 sum_im = shift_im if slot == 0 else sum_im + shift_im
             mixed = dot(sum_re.astype(jnp.bfloat16), gram_ref[0]) + dot(
@@ -123,6 +129,8 @@
 
     for index, out_ref in enumerate(out_refs):
         out_ref[...] = total[index * part : (index + 1) * part, :].astype(jnp.bfloat16)
+    for copy in copies:
+        copy.wait()
 
 
 def gradient_kernel(index, factor, on_line, *refs):
@@ -156,13 +164,6 @@
     return lax.optimization_barrier((value, *earlier))[0]
 
 
-def select_slices(array, group, slots, groups, within):
-    lead, per_device = array.shape[:2]
-    if within is None:
-        return array.reshape(lead, slots, groups, *array.shape[2:])[:, :, group]
-    return lax.dynamic_slice_in_dim(array, within, 1, axis=1)
-
-
 def sum_over_replicas(value):
     axes = ("coil", "vol")
     if any(lax.axis_size(axis) != 2 for axis in axes):
@@ -214,7 +215,7 @@
         encode_next()
     while len(outer) < LAG:
         outer_next()
-    latest = ()
+    latest = (pieces[-1],)
     for step in range(count):
         half = pieces[step] + after(outer[step], *latest)
         inner.append(lax.ppermute(half, "slc", inner_pairs))
@@ -251,18 +252,17 @@
 
     def encode(group, *earlier):
         if whole_classes:
-            within, place = None, np.zeros((2,), np.int32)
+            place = np.zeros((2,), np.int32)
         else:
             within = group - first
             held = (within >= 0) & (within < per_device)
             within = jnp.where(held, within, 0)
             place = jnp.stack([held, within]).astype(jnp.int32)
-        image, coil_map = images, coil_maps
-        if earlier:
-            image, coil_map, _ = lax.optimization_barrier((image, coil_map, earlier[0]))
+        offset = after(phase_offset, *earlier) if earlier else phase_offset
         return pl.pallas_call(
             functools.partial(encode_kernel, slots, group, whole_classes),
             in_specs=[in_smem] * 3 + [in_vmem] * 7,
+            out_specs=[pl.BlockSpec(memory_space=pl.ANY)] + [in_vmem] * ROW_PARTS,
             out_shape=[
                 jax.ShapeDtypeStruct((slots, places, 2, rows, length), jnp.bfloat16),
             ]
@@ -270,6 +270,8 @@
             scratch_shapes=[
                 pltpu.VMEM((rows, lanes), jnp.float32),
                 pltpu.VMEM((round_up(slots, 8), round_up(rows, LANE_TILE)), jnp.float32),
+                pltpu.VMEM((slots, places, 2, rows, length), jnp.bfloat16),
+                pltpu.SemaphoreType.DMA((slots, places)),
             ],
             compiler_params=pltpu.CompilerParams(vmem_limit_bytes=VMEM_BYTES),
             cost_estimate=pl.CostEstimate(
@@ -282,10 +284,10 @@
             shift_index,
             group_order,
             place,
-            select_slices(image, group, slots, groups, within),
-            select_slices(coil_map, group, slots, groups, within),
+            images,
+            coil_maps,
             kspace,
-            phase_offset,
+            offset,
             *tables,
         )
 

time: 83.6 us -> 90.8 us (1.086)
  waiting for transfers between devices: 15.4 us -> 3.21 us
  Pallas kernels: 15.5 us -> 27.5 us
  other arithmetic: 2.36 us -> 7.24 us
  starting transfers between devices: 39.5 us -> 42.5 us
    ppermute x11, waiting for transfers between devices: 12.6 us -> 1.32 us  [outer_next(): outer.append(lax.ppermute(payload, 'slc', outer_pairs))]
    pallas_call x4, Pallas kernels: 9.56 us -> 18.5 us  [encode(): pl.pallas_call(functools.partial(encode_kernel, slots, group, whole_class...]
    slice x6 -> x0, local copies, waits for them, and re-layouts: 7.85 us -> none  [select_slices(): return array.reshape(lead, slots, groups, *array.shape[2:])[:, :, group]]
    unnamed x33 -> x39, local copies, waits for them, and re-layouts: 1.45 us -> 9.2 us
    pallas_call x8, Pallas kernels: 5.94 us -> 8.94 us  [gradient(): pl.pallas_call(functools.partial(gradient_kernel, step % ROW_PARTS, facto...]
    select_n x5, other arithmetic: 0.21 us -> 3.02 us  [outer_next(): payload = others if payload is None else jnp.where(edge, payload, others)]
    add x8, other arithmetic: 1.08 us -> 3.16 us  [line_of_four(): half = pieces[step] + after(outer[step], *latest)]
    ppermute x8, starting transfers between devices: 6.6 us -> 8.23 us  [line_of_four(): inner.append(lax.ppermute(half, 'slc', inner_pairs))]
  transfers between devices with their start and end apart: 22 -> 22, of which waited for: 7 -> 3; matrix products, arithmetic and copies ran while one was open for 8% -> 7% of each run, Pallas kernels for 15% -> 24%
where the time goes in v5:
time: 90.8 us; the launch traced here: 90.1 us
  starting transfers between devices  42.5 us (47%)
  Pallas kernels  27.5 us (30%)
  local copies, waits for them, and re-layouts  9.21 us (10%)
  other arithmetic  7.24 us (8%)
  waiting for transfers between devices  3.21 us (4%)
    ppermute x11, starting transfers between devices, outer_next(): outer.append(lax.ppermute(payload, 'slc', outer_pairs))  32.3 us
    pallas_call x4, Pallas kernels, encode(): pl.pallas_call(functools.partial(encode_kernel, slots, group, whole_class...  18.5 us
    unnamed x39, local copies, waits for them, and re-layouts  9.2 us
    pallas_call x8, Pallas kernels, gradient(): pl.pallas_call(functools.partial(gradient_kernel, step % ROW_PARTS, facto...  8.94 us
    ppermute x8, starting transfers between devices, line_of_four(): inner.append(lax.ppermute(half, 'slc', inner_pairs))  8.23 us
    add x8, other arithmetic, line_of_four(): half = pieces[step] + after(outer[step], *latest)  3.16 us
    select_n x5, other arithmetic, outer_next(): payload = others if payload is None else jnp.where(edge, payload, others)  3.02 us
    ppermute x3, starting transfers between devices, sum_over_replicas(): lax.ppermute(value, axes, [(index, index ^ mask) for index in range(4)])  1.92 us
  transfers between devices with their start and end apart: 22, of which 3 were waited for; matrix products, arithmetic and copies ran while one was open for 7% of the time, Pallas kernels for 24%

profile of v5, /device:TPU:0, one launch (start us, length us, event | category | flops | bytes accessed | tf_op | source)
XLA Modules:
  0.0 90.1 jit_solution(7893041762650318248)
XLA Ops:
  0.0 1.2 %copy.28.refs_5_ = bf16[1,1,2,2,220,220]{5,4,3,2,1,0:T(8,128)(2,1)S(1)} copy(bf16[1,1,2,2,220,220]{5,3,4,2,1,0:T(2,128)(2,1)} %param.15) | data formatting | bytes 774400 | tf_op args[2]
  1.2 1.8 %copy.26.refs_3_ = bf16[1,8,2,220,220]{4,3,2,1,0:T(8,128)(2,1)S(1)} copy(bf16[1,8,2,220,220]{4,2,3,1,0:T(2,128)(2,1)} %param.13) | data formatting | bytes 3097600 | tf_op args[0]
  4.3 4.8 %encode.4 = (bf16[2,2,2,224,220]{4,3,2,1,0:T(8,128)(2,1)S(1)}, bf16[112,896]{1,0:T(8,128)(2,1)S(1)}, bf16[112,896]{1,0:T(8,128)(2,1)}) custom-call(s32[8]{0:T(128)S(1)} %copy-done.15, s32[4]{0:T(128)S(1)} %copy-done.16, s32[2]{0:T(128)S(1)} %call_exported.0.refs_2_, bf16[1,8,2,220,220]{4,3,2,1,0:T(8,128)(2,1)S(1)} %copy.26.refs_3_, ...), custom_call_target="tpu_custom_call" | custom-call | flops 1022208000 | bytes 6000000 | tf_op jit(solution)/shard_map/encode/pallas_call | solution.py:262
  10.1 3.0 %collective-permute-start = (bf16[112,896]{1,0:T(8,128)(2,1)S(1)}, bf16[112,896]{1,0:T(8,128)(2,1)S(1)}, u32[]{:S(2)}, u32[]{:S(2)}) collective-permute-start(bf16[112,896]{1,0:T(8,128)(2,1)S(1)} %get-tuple-element.59.refs_0_), channel_id=1, source_target_pairs={{0,4},{4,0},{8,12},{12,8},{1,5},{5,1},{9,13},{13,9},{2,6},{6,2},{1... | collective-permute-start | bytes 602120 | tf_op jit(solution)/shard_map/ppermute | solution.py:202
  13.2 5.3 %encode.5 = (bf16[2,2,2,224,220]{4,3,2,1,0:T(8,128)(2,1)S(1)}, bf16[112,896]{1,0:T(8,128)(2,1)}, bf16[112,896]{1,0:T(8,128)(2,1)S(1)}) custom-call(s32[8]{0:T(128)S(1)} %copy-done.15, s32[4]{0:T(128)S(1)} %copy-done.16, s32[2]{0:T(128)S(1)} %call_exported.0.refs_2_, bf16[1,8,2,220,220]{4,3,2,1,0:T(8,128)(2,1)S(1)} %copy.26.refs_3_, ...), custom_call_target="tpu_custom_call" | custom-call | flops 1022208000 | bytes 6000000 | tf_op jit(solution)/shard_map/encode/pallas_call | solution.py:262
  20.2 3.4 %collective-permute-start.1 = (bf16[112,896]{1,0:T(8,128)(2,1)}, bf16[112,896]{1,0:T(8,128)(2,1)}, u32[]{:S(2)}, u32[]{:S(2)}) collective-permute-start(bf16[112,896]{1,0:T(8,128)(2,1)} %add.57), channel_id=1, source_target_pairs={{0,0},{4,8},{8,4},{12,12},{1,1},{5,9},{9,5},{13,13},{2,2},{6,10},{... | collective-permute-start | bytes 602120 | tf_op jit(solution)/shard_map/ppermute | solution.py:221
  23.5 2.3 %collective-permute-start.5 = (bf16[112,896]{1,0:T(8,128)(2,1)}, bf16[112,896]{1,0:T(8,128)(2,1)}, u32[]{:S(2)}, u32[]{:S(2)}) collective-permute-start(bf16[112,896]{1,0:T(8,128)(2,1)} %get-tuple-element.67.refs_0_), channel_id=1, source_target_pairs={{0,4},{4,0},{8,12},{12,8},{1,5},{5,1},{9,13},{13,9},{2,6},{6,2},{1... | collective-permute-start | bytes 602120 | tf_op jit(solution)/shard_map/ppermute | solution.py:202
  25.8 1.1 %add.59 = bf16[112,896]{1,0:T(8,128)(2,1)S(1)} add(bf16[112,896]{1,0:T(8,128)(2,1)} %get-tuple-element.64.refs_0_, bf16[112,896]{1,0:T(8,128)(2,1)} %collective-permute-done.2.refs_1_) | non-fusion elementwise | flops 100352 | bytes 602112 | tf_op jit(solution)/shard_map/add | solution.py:220
  27.6 2.0 %copy-done.1 = bf16[2,8,2,220,220]{4,3,2,1,0:T(8,128)(2,1)S(1)} copy-done((bf16[2,8,2,220,220]{4,3,2,1,0:T(8,128)(2,1)S(1)}, bf16[2,8,2,220,220]{4,3,2,1,0:T(8,128)(2,1)}, u32[]{:S(2)}) %copy-start.1) | copy-done | bytes 3097624
  30.6 4.1 %encode.6 = (bf16[2,2,2,224,220]{4,3,2,1,0:T(8,128)(2,1)S(1)}, bf16[112,896]{1,0:T(8,128)(2,1)S(1)}, bf16[112,896]{1,0:T(8,128)(2,1)S(1)}) custom-call(s32[8]{0:T(128)S(1)} %copy-done.15, s32[4]{0:T(128)S(1)} %copy-done.16, s32[2]{0:T(128)S(1)} %call_exported.0.refs_2_, bf16[1,8,2,220,220]{4,3,2,1,0:T(8,128)(2,1)S(1)} %copy.26.refs_3_, ...), custom_call_target="tpu_custom_call" | custom-call | flops 1022208000 | bytes 6000000 | tf_op jit(solution)/shard_map/encode/pallas_call | solution.py:262
  35.8 4.3 %collective-permute-start.3 = (bf16[112,896]{1,0:T(8,128)(2,1)S(1)}, bf16[112,896]{1,0:T(8,128)(2,1)S(1)}, u32[]{:S(2)}, u32[]{:S(2)}) collective-permute-start(bf16[112,896]{1,0:T(8,128)(2,1)S(1)} %add_select_fusion.4), channel_id=1, source_target_pairs={{0,4},{4,0},{8,12},{12,8},{1,5},{5,1},{9,13},{13,9},{2,6},{6,2},{1... | collective-permute-start | bytes 602120 | tf_op jit(solution)/shard_map/ppermute | solution.py:202
  42.8 1.3 %collective-permute-start.7 = (bf16[112,896]{1,0:T(8,128)(2,1)S(1)}, bf16[112,896]{1,0:T(8,128)(2,1)S(1)}, u32[]{:S(2)}, u32[]{:S(2)}) collective-permute-start(bf16[112,896]{1,0:T(8,128)(2,1)S(1)} %add_select_fusion.3), channel_id=1, source_target_pairs={{0,4},{4,0},{8,12},{12,8},{1,5},{5,1},{9,13},{13,9},{2,6},{6,2},{1... | collective-permute-start | bytes 602120 | tf_op jit(solution)/shard_map/ppermute | solution.py:202
  45.9 4.9 %collective-permute-start.10 = (bf16[112,896]{1,0:T(8,128)(2,1)S(1)}, bf16[112,896]{1,0:T(8,128)(2,1)S(1)}, u32[]{:S(2)}, u32[]{:S(2)}) collective-permute-start(bf16[112,896]{1,0:T(8,128)(2,1)S(1)} %add_select_fusion.1), channel_id=1, source_target_pairs={{0,4},{4,0},{8,12},{12,8},{1,5},{5,1},{9,13},{13,9},{2,6},{6,2},{1... | collective-permute-start | bytes 602120 | tf_op jit(solution)/shard_map/ppermute | solution.py:202
  51.6 4.3 %encode.7 = (bf16[2,2,2,224,220]{4,3,2,1,0:T(8,128)(2,1)S(1)}, bf16[112,896]{1,0:T(8,128)(2,1)S(1)}, bf16[112,896]{1,0:T(8,128)(2,1)S(1)}) custom-call(s32[8]{0:T(128)S(1)} %copy-done.15, s32[4]{0:T(128)S(1)} %copy-done.16, s32[2]{0:T(128)S(1)} %call_exported.0.refs_2_, bf16[1,8,2,220,220]{4,3,2,1,0:T(8,128)(2,1)S(1)} %copy.26.refs_3_, ...), custom_call_target="tpu_custom_call" | custom-call | flops 1022208000 | bytes 6000000 | tf_op jit(solution)/shard_map/encode/pallas_call | solution.py:262
  56.0 3.7 %collective-permute-start.12 = (bf16[112,896]{1,0:T(8,128)(2,1)S(1)}, bf16[112,896]{1,0:T(8,128)(2,1)S(1)}, u32[]{:S(2)}, u32[]{:S(2)}) collective-permute-start(bf16[112,896]{1,0:T(8,128)(2,1)S(1)} %add_select_fusion.2), channel_id=1, source_target_pairs={{0,4},{4,0},{8,12},{12,8},{1,5},{5,1},{9,13},{13,9},{2,6},{6,2},{1... | collective-permute-start | bytes 602120 | tf_op jit(solution)/shard_map/ppermute | solution.py:202
  59.7 1.7 %gradient.8 = f32[2,112]{1,0:T(2,128)S(1)} custom-call(bf16[112,896]{1,0:T(8,128)(2,1)S(1)} %copy-done.11, bf16[112,896]{1,0:T(8,128)(2,1)S(1)} %copy-done.13, bf16[112,896]{1,0:T(8,128)(2,1)} %collective-permute-done.1.refs_2_, bf16[112,896]{1,0:T(8,128)(2,1)S(1)} %collective-permute-done.3.refs_3_.refs_1_, bf16[2,2,2,224,220]{4,3,2,1,0:T(8,128)(2,1)S(1)} %copy-done.9), custom_call_target="tpu_custom_call" | custom-call | flops 774400 | bytes 1500000 | tf_op jit(solution)/shard_map/gradient/pallas_call | solution.py:295
  62.2 1.4 %collective-permute-start.14 = (bf16[112,896]{1,0:T(8,128)(2,1)S(1)}, bf16[112,896]{1,0:T(8,128)(2,1)S(1)}, u32[]{:S(2)}, u32[]{:S(2)}) collective-permute-start(bf16[112,896]{1,0:T(8,128)(2,1)S(1)} %add_select_fusion), channel_id=1, source_target_pairs={{0,4},{4,0},{8,12},{12,8},{1,5},{5,1},{9,13},{13,9},{2,6},{6,2},{1... | collective-permute-start | bytes 602120 | tf_op jit(solution)/shard_map/ppermute | solution.py:202
  63.6 1.8 %gradient.9 = f32[2,112]{1,0:T(2,128)S(1)} custom-call(bf16[112,896]{1,0:T(8,128)(2,1)} %get-tuple-element.64.refs_0_, bf16[112,896]{1,0:T(8,128)(2,1)} %collective-permute-done.2.refs_1_, bf16[112,896]{1,0:T(8,128)(2,1)S(1)} %collective-permute-done.4.refs_2_, bf16[112,896]{1,0:T(8,128)(2,1)S(1)} %collective-permute-done.7.refs_3_.refs_1_, ...), custom_call_target="tpu_custom_call" | custom-call | flops 774400 | bytes 1500000 | tf_op jit(solution)/shard_map/gradient/pallas_call | solution.py:295
  66.2 1.8 %gradient.10 = f32[2,112]{1,0:T(2,128)S(1)} custom-call(bf16[112,896]{1,0:T(8,128)(2,1)} %get-tuple-element.67.refs_0_, bf16[112,896]{1,0:T(8,128)(2,1)} %collective-permute-done.5.refs_1_, bf16[112,896]{1,0:T(8,128)(2,1)S(1)} %collective-permute-done.8.refs_2_, bf16[112,896]{1,0:T(8,128)(2,1)S(1)} %collective-permute-done.10.refs_3_.refs_1_, ...), custom_call_target="tpu_custom_call" | custom-call | flops 774400 | bytes 1500000 | tf_op jit(solution)/shard_map/gradient/pallas_call | solution.py:295
  68.8 6.2 %collective-permute-start.16 = (bf16[112,896]{1,0:T(8,128)(2,1)S(1)}, bf16[112,896]{1,0:T(8,128)(2,1)S(1)}, u32[]{:S(2)}, u32[]{:S(2)}) collective-permute-start(bf16[112,896]{1,0:T(8,128)(2,1)S(1)} %add.68), channel_id=1, source_target_pairs={{0,4},{4,0},{8,12},{12,8},{1,5},{5,1},{9,13},{13,9},{2,6},{6,2},{1... | collective-permute-start | bytes 602120 | tf_op jit(solution)/shard_map/ppermute | solution.py:202
  76.3 4.8 %collective-permute-start.18 = (bf16[112,896]{1,0:T(8,128)(2,1)S(1)}, bf16[112,896]{1,0:T(8,128)(2,1)S(1)}, u32[]{:S(2)}, u32[]{:S(2)}) collective-permute-start(bf16[112,896]{1,0:T(8,128)(2,1)S(1)} %add.72), channel_id=1, source_target_pairs={{0,4},{4,0},{8,12},{12,8},{1,5},{5,1},{9,13},{13,9},{2,6},{6,2},{1... | collective-permute-start | bytes 602120 | tf_op jit(solution)/shard_map/ppermute | solution.py:202
  83.5 1.3 %collective-permute-done.18.refs_3_ = bf16[112,896]{1,0:T(8,128)(2,1)S(1)} collective-permute-done((bf16[112,896]{1,0:T(8,128)(2,1)S(1)}, bf16[112,896]{1,0:T(8,128)(2,1)S(1)}, u32[]{:S(2)}, u32[]{:S(2)}) %collective-permute-start.18) | collective-permute-done | bytes 200736 | tf_op jit(solution)/shard_map/ppermute | solution.py:202
  85.8 1.6 %collective-permute-start.20 = (f32[8,220]{1,0:T(8,128)S(1)}, f32[8,220]{1,0:T(8,128)S(1)}, u32[]{:S(2)}, u32[]{:S(2)}) collective-permute-start(f32[8,220]{1,0:T(8,128)S(1)} %reshape.3), channel_id=1, source_target_pairs={{0,2},{1,3},{2,0},{3,1},{4,6},{5,7},{6,4},{7,5},{8,10},{9,11},{10,... | collective-permute-start | bytes 21128 | tf_op jit(solution)/shard_map/ppermute | solution.py:172
  87.6 1.3 %collective-permute-done.21 = f32[8,220]{1,0:T(8,128)S(1)} collective-permute-done((f32[8,220]{1,0:T(8,128)S(1)}, f32[8,220]{1,0:T(8,128)S(1)}, u32[]{:S(2)}, u32[]{:S(2)}) %collective-permute-start.21) | collective-permute-done | bytes 7072 | tf_op jit(solution)/shard_map/ppermute | solution.py:172
  (96 shorter events, 20.4 us)
Async XLA Ops:
  3.8 9.4 %copy-start = (bf16[2,8,2,220,220]{4,3,2,1,0:T(8,128)(2,1)}, bf16[2,8,2,220,220]{4,3,2,1,0:T(8,128)(2,1)S(1)}, u32[]{:S(2)}) copy-start(bf16[2,8,2,220,220]{4,3,2,1,0:T(8,128)(2,1)S(1)} %copy.27.refs_4_) | copy-start | bytes 9292804
  10.1 9.3 %collective-permute-start = (bf16[112,896]{1,0:T(8,128)(2,1)S(1)}, bf16[112,896]{1,0:T(8,128)(2,1)S(1)}, u32[]{:S(2)}, u32[]{:S(2)}) collective-permute-start(bf16[112,896]{1,0:T(8,128)(2,1)S(1)} %get-tuple-element.59.refs_0_), channel_id=1, source_target_pairs={{0,4},{4,0},{8,12},{12,8},{1,5},{5,1},{9,13},{13,9},{2,6},{6,2},{1... | collective-permute-start | bytes 602120 | tf_op jit(solution)/shard_map/ppermute | solution.py:202
  13.1 12.7 %collective-permute-start.2 = (bf16[112,896]{1,0:T(8,128)(2,1)}, bf16[112,896]{1,0:T(8,128)(2,1)}, u32[]{:S(2)}, u32[]{:S(2)}) collective-permute-start(bf16[112,896]{1,0:T(8,128)(2,1)} %get-tuple-element.64.refs_0_), channel_id=1, source_target_pairs={{0,4},{4,0},{8,12},{12,8},{1,5},{5,1},{9,13},{13,9},{2,6},{6,2},{1... | collective-permute-start | bytes 602120 | tf_op jit(solution)/shard_map/ppermute | solution.py:202
  20.2 14.6 %collective-permute-start.1 = (bf16[112,896]{1,0:T(8,128)(2,1)}, bf16[112,896]{1,0:T(8,128)(2,1)}, u32[]{:S(2)}, u32[]{:S(2)}) collective-permute-start(bf16[112,896]{1,0:T(8,128)(2,1)} %add.57), channel_id=1, source_target_pairs={{0,0},{4,8},{8,4},{12,12},{1,1},{5,9},{9,5},{13,13},{2,2},{6,10},{... | collective-permute-start | bytes 602120 | tf_op jit(solution)/shard_map/ppermute | solution.py:221
  23.5 16.5 %collective-permute-start.5 = (bf16[112,896]{1,0:T(8,128)(2,1)}, bf16[112,896]{1,0:T(8,128)(2,1)}, u32[]{:S(2)}, u32[]{:S(2)}) collective-permute-start(bf16[112,896]{1,0:T(8,128)(2,1)} %get-tuple-element.67.refs_0_), channel_id=1, source_target_pairs={{0,4},{4,0},{8,12},{12,8},{1,5},{5,1},{9,13},{13,9},{2,6},{6,2},{1... | collective-permute-start | bytes 602120 | tf_op jit(solution)/shard_map/ppermute | solution.py:202
  26.9 14.9 %collective-permute-start.4 = (bf16[112,896]{1,0:T(8,128)(2,1)S(1)}, bf16[112,896]{1,0:T(8,128)(2,1)S(1)}, u32[]{:S(2)}, u32[]{:S(2)}) collective-permute-start(bf16[112,896]{1,0:T(8,128)(2,1)S(1)} %add.59), channel_id=1, source_target_pairs={{0,0},{4,8},{8,4},{12,12},{1,1},{5,9},{9,5},{13,13},{2,2},{6,10},{... | collective-permute-start | bytes 602120 | tf_op jit(solution)/shard_map/ppermute | solution.py:221
  35.8 8.4 %collective-permute-start.3 = (bf16[112,896]{1,0:T(8,128)(2,1)S(1)}, bf16[112,896]{1,0:T(8,128)(2,1)S(1)}, u32[]{:S(2)}, u32[]{:S(2)}) collective-permute-start(bf16[112,896]{1,0:T(8,128)(2,1)S(1)} %add_select_fusion.4), channel_id=1, source_target_pairs={{0,4},{4,0},{8,12},{12,8},{1,5},{5,1},{9,13},{13,9},{2,6},{6,2},{1... | collective-permute-start | bytes 602120 | tf_op jit(solution)/shard_map/ppermute | solution.py:202
  41.1 3.8 %collective-permute-start.8 = (bf16[112,896]{1,0:T(8,128)(2,1)S(1)}, bf16[112,896]{1,0:T(8,128)(2,1)S(1)}, u32[]{:S(2)}, u32[]{:S(2)}) collective-permute-start(bf16[112,896]{1,0:T(8,128)(2,1)S(1)} %add.61), channel_id=1, source_target_pairs={{0,0},{4,8},{8,4},{12,12},{1,1},{5,9},{9,5},{13,13},{2,2},{6,10},{... | collective-permute-start | bytes 602120 | tf_op jit(solution)/shard_map/ppermute | solution.py:221
  42.8 7.9 %collective-permute-start.7 = (bf16[112,896]{1,0:T(8,128)(2,1)S(1)}, bf16[112,896]{1,0:T(8,128)(2,1)S(1)}, u32[]{:S(2)}, u32[]{:S(2)}) collective-permute-start(bf16[112,896]{1,0:T(8,128)(2,1)S(1)} %add_select_fusion.3), channel_id=1, source_target_pairs={{0,4},{4,0},{8,12},{12,8},{1,5},{5,1},{9,13},{13,9},{2,6},{6,2},{1... | collective-permute-start | bytes 602120 | tf_op jit(solution)/shard_map/ppermute | solution.py:202
  44.2 11.8 %collective-permute-start.6 = (bf16[112,896]{1,0:T(8,128)(2,1)S(1)}, bf16[112,896]{1,0:T(8,128)(2,1)S(1)}, u32[]{:S(2)}, u32[]{:S(2)}) collective-permute-start(bf16[112,896]{1,0:T(8,128)(2,1)S(1)} %add.62), channel_id=1, source_target_pairs={{0,0},{4,8},{8,4},{12,12},{1,1},{5,9},{9,5},{13,13},{2,2},{6,10},{... | collective-permute-start | bytes 602120 | tf_op jit(solution)/shard_map/ppermute | solution.py:221
  45.9 15.5 %collective-permute-start.10 = (bf16[112,896]{1,0:T(8,128)(2,1)S(1)}, bf16[112,896]{1,0:T(8,128)(2,1)S(1)}, u32[]{:S(2)}, u32[]{:S(2)}) collective-permute-start(bf16[112,896]{1,0:T(8,128)(2,1)S(1)} %add_select_fusion.1), channel_id=1, source_target_pairs={{0,4},{4,0},{8,12},{12,8},{1,5},{5,1},{9,13},{13,9},{2,6},{6,2},{1... | collective-permute-start | bytes 602120 | tf_op jit(solution)/shard_map/ppermute | solution.py:202
  50.8 11.3 %collective-permute-start.9 = (bf16[112,896]{1,0:T(8,128)(2,1)S(1)}, bf16[112,896]{1,0:T(8,128)(2,1)S(1)}, u32[]{:S(2)}, u32[]{:S(2)}) collective-permute-start(bf16[112,896]{1,0:T(8,128)(2,1)S(1)} %add.65), channel_id=1, source_target_pairs={{0,0},{4,8},{8,4},{12,12},{1,1},{5,9},{9,5},{13,13},{2,2},{6,10},{... | collective-permute-start | bytes 602120 | tf_op jit(solution)/shard_map/ppermute | solution.py:221
  56.0 10.3 %copy-start.7 = (bf16[2,2,2,224,220]{4,3,2,1,0:T(8,128)(2,1)S(1)}, bf16[2,2,2,224,220]{4,3,2,1,0:T(8,128)(2,1)}, u32[]{:S(2)}) copy-start(bf16[2,2,2,224,220]{4,3,2,1,0:T(8,128)(2,1)} %copy-done.6) | copy-start | bytes 2365444
  56.0 9.4 %collective-permute-start.12 = (bf16[112,896]{1,0:T(8,128)(2,1)S(1)}, bf16[112,896]{1,0:T(8,128)(2,1)S(1)}, u32[]{:S(2)}, u32[]{:S(2)}) collective-permute-start(bf16[112,896]{1,0:T(8,128)(2,1)S(1)} %add_select_fusion.2), channel_id=1, source_target_pairs={{0,4},{4,0},{8,12},{12,8},{1,5},{5,1},{9,13},{13,9},{2,6},{6,2},{1... | collective-permute-start | bytes 602120 | tf_op jit(solution)/shard_map/ppermute | solution.py:202
  61.5 4.7 %collective-permute-start.11 = (bf16[112,896]{1,0:T(8,128)(2,1)S(1)}, bf16[112,896]{1,0:T(8,128)(2,1)S(1)}, u32[]{:S(2)}, u32[]{:S(2)}) collective-permute-start(bf16[112,896]{1,0:T(8,128)(2,1)S(1)} %add.67), channel_id=1, source_target_pairs={{0,0},{4,8},{8,4},{12,12},{1,1},{5,9},{9,5},{13,13},{2,2},{6,10},{... | collective-permute-start | bytes 602120 | tf_op jit(solution)/shard_map/ppermute | solution.py:221
  62.2 5.8 %collective-permute-start.14 = (bf16[112,896]{1,0:T(8,128)(2,1)S(1)}, bf16[112,896]{1,0:T(8,128)(2,1)S(1)}, u32[]{:S(2)}, u32[]{:S(2)}) collective-permute-start(bf16[112,896]{1,0:T(8,128)(2,1)S(1)} %add_select_fusion), channel_id=1, source_target_pairs={{0,4},{4,0},{8,12},{12,8},{1,5},{5,1},{9,13},{13,9},{2,6},{6,2},{1... | collective-permute-start | bytes 602120 | tf_op jit(solution)/shard_map/ppermute | solution.py:202
  65.5 9.6 %collective-permute-start.13 = (bf16[112,896]{1,0:T(8,128)(2,1)S(1)}, bf16[112,896]{1,0:T(8,128)(2,1)S(1)}, u32[]{:S(2)}, u32[]{:S(2)}) collective-permute-start(bf16[112,896]{1,0:T(8,128)(2,1)S(1)} %add.69), channel_id=1, source_target_pairs={{0,0},{4,8},{8,4},{12,12},{1,1},{5,9},{9,5},{13,13},{2,2},{6,10},{... | collective-permute-start | bytes 602120 | tf_op jit(solution)/shard_map/ppermute | solution.py:221
  68.1 7.4 %collective-permute-start.15 = (bf16[112,896]{1,0:T(8,128)(2,1)S(1)}, bf16[112,896]{1,0:T(8,128)(2,1)S(1)}, u32[]{:S(2)}, u32[]{:S(2)}) collective-permute-start(bf16[112,896]{1,0:T(8,128)(2,1)S(1)} %add.71), channel_id=1, source_target_pairs={{0,0},{4,8},{8,4},{12,12},{1,1},{5,9},{9,5},{13,13},{2,2},{6,10},{... | collective-permute-start | bytes 602120 | tf_op jit(solution)/shard_map/ppermute | solution.py:221
  68.8 13.1 %collective-permute-start.16 = (bf16[112,896]{1,0:T(8,128)(2,1)S(1)}, bf16[112,896]{1,0:T(8,128)(2,1)S(1)}, u32[]{:S(2)}, u32[]{:S(2)}) collective-permute-start(bf16[112,896]{1,0:T(8,128)(2,1)S(1)} %add.68), channel_id=1, source_target_pairs={{0,4},{4,0},{8,12},{12,8},{1,5},{5,1},{9,13},{13,9},{2,6},{6,2},{1... | collective-permute-start | bytes 602120 | tf_op jit(solution)/shard_map/ppermute | solution.py:202
  75.1 7.7 %collective-permute-start.17 = (bf16[112,896]{1,0:T(8,128)(2,1)S(1)}, bf16[112,896]{1,0:T(8,128)(2,1)S(1)}, u32[]{:S(2)}, u32[]{:S(2)}) collective-permute-start(bf16[112,896]{1,0:T(8,128)(2,1)S(1)} %add.70), channel_id=1, source_target_pairs={{0,4},{4,0},{8,12},{12,8},{1,5},{5,1},{9,13},{13,9},{2,6},{6,2},{1... | collective-permute-start | bytes 602120 | tf_op jit(solution)/shard_map/ppermute | solution.py:202
  76.3 8.5 %collective-permute-start.18 = (bf16[112,896]{1,0:T(8,128)(2,1)S(1)}, bf16[112,896]{1,0:T(8,128)(2,1)S(1)}, u32[]{:S(2)}, u32[]{:S(2)}) collective-permute-start(bf16[112,896]{1,0:T(8,128)(2,1)S(1)} %add.72), channel_id=1, source_target_pairs={{0,4},{4,0},{8,12},{12,8},{1,5},{5,1},{9,13},{13,9},{2,6},{6,2},{1... | collective-permute-start | bytes 602120 | tf_op jit(solution)/shard_map/ppermute | solution.py:202
  85.7 3.2 %collective-permute-start.21 = (f32[8,220]{1,0:T(8,128)S(1)}, f32[8,220]{1,0:T(8,128)S(1)}, u32[]{:S(2)}, u32[]{:S(2)}) collective-permute-start(f32[8,220]{1,0:T(8,128)S(1)} %reshape.3), channel_id=1, source_target_pairs={{0,3},{1,2},{2,1},{3,0},{4,7},{5,6},{6,5},{7,4},{8,11},{9,10},{10,... | collective-permute-start | bytes 21128 | tf_op jit(solution)/shard_map/ppermute | solution.py:172
  85.8 3.7 %collective-permute-start.20 = (f32[8,220]{1,0:T(8,128)S(1)}, f32[8,220]{1,0:T(8,128)S(1)}, u32[]{:S(2)}, u32[]{:S(2)}) collective-permute-start(f32[8,220]{1,0:T(8,128)S(1)} %reshape.3), channel_id=1, source_target_pairs={{0,2},{1,3},{2,0},{3,1},{4,6},{5,7},{6,4},{7,5},{8,10},{9,11},{10,... | collective-permute-start | bytes 21128 | tf_op jit(solution)/shard_map/ppermute | solution.py:172
  87.3 2.2 %collective-permute-start.19 = (f32[8,220]{1,0:T(8,128)S(1)}, f32[8,220]{1,0:T(8,128)S(1)}, u32[]{:S(2)}, u32[]{:S(2)}) collective-permute-start(f32[8,220]{1,0:T(8,128)S(1)} %reshape.3), channel_id=1, source_target_pairs={{0,1},{1,0},{2,3},{3,2},{4,5},{5,4},{6,7},{7,6},{8,9},{9,8},{10,11... | collective-permute-start | bytes 21128 | tf_op jit(solution)/shard_map/ppermute | solution.py:172
  (16 other events, 47.2 us)

commit v6 on v4

--- a/solution.py
+++ b/solution.py
@@ -13,8 +13,8 @@
 MB = 8
 ROW_TILE = 16
 LANE_TILE = 128
-ROW_PARTS = 2
-LAG = 3
+ROW_PARTS = 1
+LAG = 2
 VMEM_BYTES = 24 * 1024 * 1024
 
 
@@ -207,18 +207,16 @@
         own = after(terms[0], *earlier) if earlier else terms[0]
         gradients.append(gradient(step, (own, *terms[1:]), shifted[step // parts]))
 
+    while len(outer) < LAG:
+        encode_next()
+        while len(outer) < min(LAG, len(pieces)):
+            outer_next()
     encode_next()
-    for _ in range(parts):
-        outer_next()
-    while len(pieces) < LAG:
-        encode_next()
-    while len(outer) < LAG:
-        outer_next()
-    latest = ()
+    latest = (pieces[-1],)
     for step in range(count):
         half = pieces[step] + after(outer[step], *latest)
         inner.append(lax.ppermute(half, "slc", inner_pairs))
-        if len(pieces) < min(count, step + LAG + 1):
+        if len(pieces) < min(count, step + LAG + 2):
             encode_next(half)
         latest = ()
         if step >= 1:

time: 83.6 us -> 79.9 us (0.956); the launches traced: 82.9 us -> 80.2 us
  starting transfers between devices: 39.5 us -> 28.4 us
  waiting for transfers between devices: 15.4 us -> 24.9 us
  Pallas kernels: 15.5 us -> 14.1 us
    ppermute x11 -> x6, waiting for transfers between devices: 12.6 us -> 22.5 us  [outer_next(): outer.append(lax.ppermute(payload, 'slc', outer_pairs))]
    ppermute x11 -> x6, starting transfers between devices: 30.9 us -> 22.2 us  [outer_next(): outer.append(lax.ppermute(payload, 'slc', outer_pairs))]
    ppermute x8 -> x4, starting transfers between devices: 6.6 us -> 3.95 us  [line_of_four(): inner.append(lax.ppermute(half, 'slc', inner_pairs))]
    pallas_call x8 -> x4, Pallas kernels: 5.94 us -> 4.51 us  [gradient(): pl.pallas_call(functools.partial(gradient_kernel, step % ROW_PARTS, facto...]
    unnamed x33 -> x39, local copies, waits for them, and re-layouts: 1.45 us -> 2.38 us
    slice x6 -> x4, local copies, waits for them, and re-layouts: 7.85 us -> 7.4 us  [select_slices(): return array.reshape(lead, slots, groups, *array.shape[2:])[:, :, group]]
  transfers between devices with their start and end apart: 22 -> 13, of which waited for: 7 -> 8; matrix products, arithmetic and copies ran while one was open for 8% -> 6% of each run, Pallas kernels for 15% -> 13%
where the time goes in v6:
time: 79.9 us; the launch traced here: 80.2 us
  starting transfers between devices  28.4 us (36%)
  waiting for transfers between devices  24.9 us (31%)
  Pallas kernels  14.1 us (18%)
  local copies, waits for them, and re-layouts  10.2 us (13%)
  other arithmetic  2.14 us (3%)
    ppermute x6, waiting for transfers between devices, outer_next(): outer.append(lax.ppermute(payload, 'slc', outer_pairs))  22.5 us
    ppermute x6, starting transfers between devices, outer_next(): outer.append(lax.ppermute(payload, 'slc', outer_pairs))  22.2 us
    pallas_call x4, Pallas kernels, encode(): pl.pallas_call(functools.partial(encode_kernel, slots, group, whole_class...  9.62 us
    slice x4, local copies, waits for them, and re-layouts, select_slices(): return array.reshape(lead, slots, groups, *array.shape[2:])[:, :, group]  7.4 us
    pallas_call x4, Pallas kernels, gradient(): pl.pallas_call(functools.partial(gradient_kernel, step % ROW_PARTS, facto...  4.51 us
    ppermute x4, starting transfers between devices, line_of_four(): inner.append(lax.ppermute(half, 'slc', inner_pairs))  3.95 us
    ppermute x3, waiting for transfers between devices, sum_over_replicas(): lax.ppermute(value, axes, [(index, index ^ mask) for index in range(4)])  2.43 us
    unnamed x39, local copies, waits for them, and re-layouts  2.38 us
  transfers between devices with their start and end apart: 13, of which 8 were waited for; matrix products, arithmetic and copies ran while one was open for 6% of the time, Pallas kernels for 13%

profile of v6, /device:TPU:0, one launch (start us, length us, event | category | flops | bytes accessed | tf_op | source)
XLA Modules:
  0.0 80.2 jit_solution(15310920758905219375)
XLA Ops:
  0.0 2.4 %fusion.1 = (bf16[1,2,1,2,220,220]{5,3,4,2,1,0:T(2,128)(2,1)S(1)}, bf16[1,2,1,2,220,220]{5,3,4,2,1,0:T(2,128)(2,1)S(1)}, bf16[1,2,1,2,220,220]{5,3,4,2,1,0:T(2,128)(2,1)S(1)}) fusion(bf16[1,2,4,2,220,220]{5,3,4,2,1,0:T(2,128)(2,1)} %bitcast.38), kind=kLoop, calls=%fused_computation.15 | loop fusion | bytes 2323200 | tf_op jit(solution)/shard_map/slice | solution.py:162
  2.5 1.9 %fusion = (bf16[2,2,1,2,220,220]{5,3,4,2,1,0:T(2,128)(2,1)S(1)}, bf16[2,2,1,2,220,220]{5,3,4,2,1,0:T(2,128)(2,1)S(1)}, bf16[2,2,1,2,220,220]{5,3,4,2,1,0:T(2,128)(2,1)S(1)}) fusion(bf16[2,2,4,2,220,220]{5,3,4,2,1,0:T(2,128)(2,1)S(1)} %bitcast.37), kind=kLoop, calls=%fused_computation.14 | loop fusion | bytes 4646400 | tf_op jit(solution)/shard_map/slice | solution.py:162
  4.7 2.2 %encode.4 = (bf16[2,2,2,224,220]{4,3,2,1,0:T(8,128)(2,1)S(1)}, bf16[224,896]{1,0:T(8,128)(2,1)S(1)}) custom-call(s32[8]{0:T(128)S(1)} %copy-done.7, s32[4]{0:T(128)S(1)} %copy-done.8, s32[2]{0:T(128)S(1)} %call_exported.0.refs_2_, bf16[1,2,2,220,220]{4,3,2,1,0:T(8,128)(2,1)S(1)} %bitcast.30, bf16[2,2,2,220,220]{4,3,2,1,0:T(8,128)(2,1)S(1)} %bitcast.29, ...), custom_call_target="tpu_custom_call" | custom-call | flops 1022208000 | bytes 6000000 | tf_op jit(solution)/shard_map/encode/pallas_call | solution.py:261
  7.0 3.1 %collective-permute-start = (bf16[224,896]{1,0:T(8,128)(2,1)S(1)}, bf16[224,896]{1,0:T(8,128)(2,1)S(1)}, u32[]{:S(2)}, u32[]{:S(2)}) collective-permute-start(bf16[224,896]{1,0:T(8,128)(2,1)S(1)} %get-tuple-element.38.refs_0_), channel_id=1, source_target_pairs={{0,4},{4,0},{8,12},{12,8},{1,5},{5,1},{9,13},{13,9},{2,6},{6,2},{1... | collective-permute-start | bytes 1204232 | tf_op jit(solution)/shard_map/ppermute | solution.py:201
  10.5 2.7 %encode.6 = (bf16[2,2,2,224,220]{4,3,2,1,0:T(8,128)(2,1)S(1)}, bf16[224,896]{1,0:T(8,128)(2,1)S(1)}) custom-call(s32[8]{0:T(128)S(1)} %copy-done.7, s32[4]{0:T(128)S(1)} %copy-done.8, s32[2]{0:T(128)S(1)} %call_exported.0.refs_2_, bf16[1,2,2,220,220]{4,3,2,1,0:T(8,128)(2,1)S(1)} %get-tuple-element.53.refs_3_, ...), custom_call_target="tpu_custom_call" | custom-call | flops 1022208000 | bytes 6000000 | tf_op jit(solution)/shard_map/encode/pallas_call | solution.py:261
  14.2 2.2 %encode.5 = (bf16[2,2,2,224,220]{4,3,2,1,0:T(8,128)(2,1)S(1)}, bf16[224,896]{1,0:T(8,128)(2,1)S(1)}) custom-call(s32[8]{0:T(128)S(1)} %copy-done.7, s32[4]{0:T(128)S(1)} %copy-done.8, s32[2]{0:T(128)S(1)} %call_exported.0.refs_2_, bf16[1,2,2,220,220]{4,3,2,1,0:T(8,128)(2,1)S(1)} %get-tuple-element.54.refs_3_, ...), custom_call_target="tpu_custom_call" | custom-call | flops 1022208000 | bytes 6000000 | tf_op jit(solution)/shard_map/encode/pallas_call | solution.py:261
  17.3 2.8 %collective-permute-done.refs_1_ = bf16[224,896]{1,0:T(8,128)(2,1)S(1)} collective-permute-done((bf16[224,896]{1,0:T(8,128)(2,1)S(1)}, bf16[224,896]{1,0:T(8,128)(2,1)S(1)}, u32[]{:S(2)}, u32[]{:S(2)}) %collective-permute-start) | collective-permute-done | bytes 401440 | tf_op jit(solution)/shard_map/ppermute | solution.py:201
  21.1 1.6 %collective-permute-start.1 = (bf16[224,896]{1,0:T(8,128)(2,1)}, bf16[224,896]{1,0:T(8,128)(2,1)S(1)}, u32[]{:S(2)}, u32[]{:S(2)}) collective-permute-start(bf16[224,896]{1,0:T(8,128)(2,1)} %add.33), channel_id=1, source_target_pairs={{0,0},{4,8},{8,4},{12,12},{1,1},{5,9},{9,5},{13,13},{2,2},{6,10},{... | collective-permute-start | bytes 1204232 | tf_op jit(solution)/shard_map/ppermute | solution.py:218
  22.7 5.3 %collective-permute-done.2.refs_1_ = bf16[224,896]{1,0:T(8,128)(2,1)S(1)} collective-permute-done((bf16[224,896]{1,0:T(8,128)(2,1)S(1)}, bf16[224,896]{1,0:T(8,128)(2,1)S(1)}, u32[]{:S(2)}, u32[]{:S(2)}) %collective-permute-start.2) | collective-permute-done | bytes 401440 | tf_op jit(solution)/shard_map/ppermute | solution.py:201
  29.0 6.5 %collective-permute-start.3 = (bf16[224,896]{1,0:T(8,128)(2,1)S(1)}, bf16[224,896]{1,0:T(8,128)(2,1)S(1)}, u32[]{:S(2)}, u32[]{:S(2)}) collective-permute-start(bf16[224,896]{1,0:T(8,128)(2,1)S(1)} %add_select_fusion.1), channel_id=1, source_target_pairs={{0,4},{4,0},{8,12},{12,8},{1,5},{5,1},{9,13},{13,9},{2,6},{6,2},{1... | collective-permute-start | bytes 1204232 | tf_op jit(solution)/shard_map/ppermute | solution.py:201
  35.6 1.3 %slice.42 = bf16[1,2,1,2,220,220]{5,3,4,2,1,0:T(2,128)(2,1)S(1)} slice(bf16[1,2,4,2,220,220]{5,3,4,2,1,0:T(2,128)(2,1)} %bitcast.39), slice={[0:1], [0:2], [3:4], [0:2], [0:220], [0:220]} | slice | bytes 774400 | tf_op jit(solution)/shard_map/slice | solution.py:162
  37.0 1.8 %slice.43 = bf16[2,2,1,2,220,220]{5,3,4,2,1,0:T(2,128)(2,1)S(1)} slice(bf16[2,2,4,2,220,220]{5,3,4,2,1,0:T(2,128)(2,1)} %bitcast.36), slice={[0:2], [0:2], [3:4], [0:2], [0:220], [0:220]} | slice | bytes 1548800 | tf_op jit(solution)/shard_map/slice | solution.py:162
  38.9 2.4 %encode.7 = (bf16[2,2,2,224,220]{4,3,2,1,0:T(8,128)(2,1)S(1)}, bf16[224,896]{1,0:T(8,128)(2,1)S(1)}) custom-call(s32[8]{0:T(128)S(1)} %copy-done.7, s32[4]{0:T(128)S(1)} %copy-done.8, s32[2]{0:T(128)S(1)} %call_exported.0.refs_2_, bf16[1,2,2,220,220]{4,3,2,1,0:T(8,128)(2,1)S(1)} %bitcast.31, bf16[2,2,2,220,220]{4,3,2,1,0:T(8,128)(2,1)S(1)} %bitcast.28, ...), custom_call_target="tpu_custom_call" | custom-call | flops 1022208000 | bytes 6000000 | tf_op jit(solution)/shard_map/encode/pallas_call | solution.py:261
  42.5 1.8 %collective-permute-start.6 = (bf16[224,896]{1,0:T(8,128)(2,1)S(1)}, bf16[224,896]{1,0:T(8,128)(2,1)S(1)}, u32[]{:S(2)}, u32[]{:S(2)}) collective-permute-start(bf16[224,896]{1,0:T(8,128)(2,1)S(1)} %add_select_fusion), channel_id=1, source_target_pairs={{0,4},{4,0},{8,12},{12,8},{1,5},{5,1},{9,13},{13,9},{2,6},{6,2},{1... | collective-permute-start | bytes 1204232 | tf_op jit(solution)/shard_map/ppermute | solution.py:201
  45.0 7.3 %collective-permute-done.6.refs_3_.refs_1_ = bf16[224,896]{1,0:T(8,128)(2,1)S(1)} collective-permute-done((bf16[224,896]{1,0:T(8,128)(2,1)S(1)}, bf16[224,896]{1,0:T(8,128)(2,1)S(1)}, u32[]{:S(2)}, u32[]{:S(2)}) %collective-permute-start.6) | collective-permute-done | bytes 401440 | tf_op jit(solution)/shard_map/ppermute | solution.py:201
  53.4 4.6 %collective-permute-start.8 = (bf16[224,896]{1,0:T(8,128)(2,1)S(1)}, bf16[224,896]{1,0:T(8,128)(2,1)S(1)}, u32[]{:S(2)}, u32[]{:S(2)}) collective-permute-start(bf16[224,896]{1,0:T(8,128)(2,1)S(1)} %add.37), channel_id=1, source_target_pairs={{0,4},{4,0},{8,12},{12,8},{1,5},{5,1},{9,13},{13,9},{2,6},{6,2},{1... | collective-permute-start | bytes 1204232 | tf_op jit(solution)/shard_map/ppermute | solution.py:201
  58.0 1.1 %gradient.4 = f32[2,224]{1,0:T(2,128)S(1)} custom-call(bf16[224,896]{1,0:T(8,128)(2,1)S(1)} %get-tuple-element.38.refs_0_, bf16[224,896]{1,0:T(8,128)(2,1)S(1)} %collective-permute-done.refs_1_, bf16[224,896]{1,0:T(8,128)(2,1)S(1)} %collective-permute-done.1.refs_2_, bf16[224,896]{1,0:T(8,128)(2,1)S(1)} %collective-permute-done.3.refs_3_.refs_1_, ...), custom_call_target="tpu_custom_call" | custom-call | flops 774400 | bytes 1500000 | tf_op jit(solution)/shard_map/gradient/pallas_call | solution.py:291
  59.3 6.2 %collective-permute-start.9 = (bf16[224,896]{1,0:T(8,128)(2,1)S(1)}, bf16[224,896]{1,0:T(8,128)(2,1)S(1)}, u32[]{:S(2)}, u32[]{:S(2)}) collective-permute-start(bf16[224,896]{1,0:T(8,128)(2,1)S(1)} %add.40), channel_id=1, source_target_pairs={{0,4},{4,0},{8,12},{12,8},{1,5},{5,1},{9,13},{13,9},{2,6},{6,2},{1... | collective-permute-start | bytes 1204232 | tf_op jit(solution)/shard_map/ppermute | solution.py:201
  65.5 1.1 %gradient.5 = f32[2,224]{1,0:T(2,128)S(1)} custom-call(bf16[224,896]{1,0:T(8,128)(2,1)S(1)} %get-tuple-element.41.refs_0_, bf16[224,896]{1,0:T(8,128)(2,1)S(1)} %collective-permute-done.2.refs_1_, bf16[224,896]{1,0:T(8,128)(2,1)S(1)} %collective-permute-done.5.refs_2_, bf16[224,896]{1,0:T(8,128)(2,1)S(1)} %collective-permute-done.6.refs_3_.refs_1_, ...), custom_call_target="tpu_custom_call" | custom-call | flops 774400 | bytes 1500000 | tf_op jit(solution)/shard_map/gradient/pallas_call | solution.py:291
  67.1 1.1 %gradient.6 = f32[2,224]{1,0:T(2,128)S(1)} custom-call(bf16[224,896]{1,0:T(8,128)(2,1)S(1)} %get-tuple-element.43.refs_0_, bf16[224,896]{1,0:T(8,128)(2,1)S(1)} %collective-permute-done.3.refs_3_.refs_1_, bf16[224,896]{1,0:T(8,128)(2,1)S(1)} %collective-permute-done.4.refs_2_, bf16[224,896]{1,0:T(8,128)(2,1)S(1)} %collective-permute-done.8.refs_3_, ...), custom_call_target="tpu_custom_call" | custom-call | flops 774400 | bytes 1500000 | tf_op jit(solution)/shard_map/gradient/pallas_call | solution.py:291
  68.2 5.6 %collective-permute-done.9.refs_3_ = bf16[224,896]{1,0:T(8,128)(2,1)S(1)} collective-permute-done((bf16[224,896]{1,0:T(8,128)(2,1)S(1)}, bf16[224,896]{1,0:T(8,128)(2,1)S(1)}, u32[]{:S(2)}, u32[]{:S(2)}) %collective-permute-start.9) | collective-permute-done | bytes 401440 | tf_op jit(solution)/shard_map/ppermute | solution.py:201
  73.8 1.1 %gradient.7 = f32[2,224]{1,0:T(2,128)S(1)} custom-call(bf16[224,896]{1,0:T(8,128)(2,1)S(1)} %get-tuple-element.45.refs_0_, bf16[224,896]{1,0:T(8,128)(2,1)S(1)} %collective-permute-done.6.refs_3_.refs_1_, bf16[224,896]{1,0:T(8,128)(2,1)S(1)} %collective-permute-done.7.refs_2_, bf16[224,896]{1,0:T(8,128)(2,1)S(1)} %collective-permute-done.9.refs_3_, ...), custom_call_target="tpu_custom_call" | custom-call | flops 774400 | bytes 1500000 | tf_op jit(solution)/shard_map/gradient/pallas_call | solution.py:291
  75.0 1.6 %collective-permute-start.11 = (f32[8,220]{1,0:T(8,128)S(1)}, f32[8,220]{1,0:T(8,128)S(1)}, u32[]{:S(2)}, u32[]{:S(2)}) collective-permute-start(f32[8,220]{1,0:T(8,128)S(1)} %reshape.23), channel_id=1, source_target_pairs={{0,2},{1,3},{2,0},{3,1},{4,6},{5,7},{6,4},{7,5},{8,10},{9,11},{10,... | collective-permute-start | bytes 21128 | tf_op jit(solution)/shard_map/ppermute | solution.py:171
  77.2 1.5 %collective-permute-done.11 = f32[8,220]{1,0:T(8,128)S(1)} collective-permute-done((f32[8,220]{1,0:T(8,128)S(1)}, f32[8,220]{1,0:T(8,128)S(1)}, u32[]{:S(2)}, u32[]{:S(2)}) %collective-permute-start.11) | collective-permute-done | bytes 7072 | tf_op jit(solution)/shard_map/ppermute | solution.py:171
  (68 shorter events, 10.3 us)
Async XLA Ops:
  0.0 2.4 %copy-start.15 = (bf16[2,8,2,220,220]{4,2,3,1,0:T(2,128)(2,1)S(1)}, bf16[2,8,2,220,220]{4,2,3,1,0:T(2,128)(2,1)}, u32[]{:S(2)}) copy-start(bf16[2,8,2,220,220]{4,2,3,1,0:T(2,128)(2,1)} %param.14) | copy-start | bytes 9292804
  2.5 2.2 %copy-start.6 = (f32[8,220]{1,0:T(8,128)S(1)}, f32[8,220]{1,0:T(8,128)}, u32[]{:S(2)}) copy-start(f32[8,220]{1,0:T(8,128)} %refs_6_.7) | copy-start | bytes 21124
  2.5 2.2 %copy-start.7 = (s32[8]{0:T(128)S(1)}, s32[8]{0:T(128)}, u32[]{:S(2)}) copy-start(s32[8]{0:T(128)} %refs_0_.7) | copy-start | bytes 100
  2.5 2.2 %copy-start.8 = (s32[4]{0:T(128)S(1)}, s32[4]{0:T(128)}, u32[]{:S(2)}) copy-start(s32[4]{0:T(128)} %refs_1_.7) | copy-start | bytes 52
  4.7 9.5 %copy-start.4 = (bf16[1,1,2,2,220,220]{5,4,3,2,1,0:T(8,128)(2,1)}, bf16[1,1,2,2,220,220]{5,4,3,2,1,0:T(8,128)(2,1)S(1)}, u32[]{:S(2)}) copy-start(bf16[1,1,2,2,220,220]{5,4,3,2,1,0:T(8,128)(2,1)S(1)} %copy.22.refs_5_) | copy-start | bytes 1161604
  7.0 13.2 %collective-permute-start = (bf16[224,896]{1,0:T(8,128)(2,1)S(1)}, bf16[224,896]{1,0:T(8,128)(2,1)S(1)}, u32[]{:S(2)}, u32[]{:S(2)}) collective-permute-start(bf16[224,896]{1,0:T(8,128)(2,1)S(1)} %get-tuple-element.38.refs_0_), channel_id=1, source_target_pairs={{0,4},{4,0},{8,12},{12,8},{1,5},{5,1},{9,13},{13,9},{2,6},{6,2},{1... | collective-permute-start | bytes 1204232 | tf_op jit(solution)/shard_map/ppermute | solution.py:201
  14.2 13.8 %collective-permute-start.2 = (bf16[224,896]{1,0:T(8,128)(2,1)S(1)}, bf16[224,896]{1,0:T(8,128)(2,1)S(1)}, u32[]{:S(2)}, u32[]{:S(2)}) collective-permute-start(bf16[224,896]{1,0:T(8,128)(2,1)S(1)} %get-tuple-element.41.refs_0_), channel_id=1, source_target_pairs={{0,4},{4,0},{8,12},{12,8},{1,5},{5,1},{9,13},{13,9},{2,6},{6,2},{1... | collective-permute-start | bytes 1204232 | tf_op jit(solution)/shard_map/ppermute | solution.py:201
  21.1 7.9 %collective-permute-start.1 = (bf16[224,896]{1,0:T(8,128)(2,1)}, bf16[224,896]{1,0:T(8,128)(2,1)S(1)}, u32[]{:S(2)}, u32[]{:S(2)}) collective-permute-start(bf16[224,896]{1,0:T(8,128)(2,1)} %add.33), channel_id=1, source_target_pairs={{0,0},{4,8},{8,4},{12,12},{1,1},{5,9},{9,5},{13,13},{2,2},{6,10},{... | collective-permute-start | bytes 1204232 | tf_op jit(solution)/shard_map/ppermute | solution.py:218
  28.1 10.8 %copy-start.5 = (bf16[1,1,2,2,220,220]{5,4,3,2,1,0:T(8,128)(2,1)S(1)}, bf16[1,1,2,2,220,220]{5,4,3,2,1,0:T(8,128)(2,1)}, u32[]{:S(2)}) copy-start(bf16[1,1,2,2,220,220]{5,4,3,2,1,0:T(8,128)(2,1)} %copy-done.4) | copy-start | bytes 1161604
  28.1 10.8 %copy-start.10 = (bf16[2,448,220]{2,1,0:T(8,128)(2,1)S(1)}, bf16[2,448,220]{2,1,0:T(8,128)(2,1)}, u32[]{:S(2)}) copy-start(bf16[2,448,220]{2,1,0:T(8,128)(2,1)} %constant.18.clone.refs_7_) | copy-start | bytes 1182724
  28.1 10.8 %copy-start.12 = (bf16[2,220,440]{2,1,0:T(8,128)(2,1)S(1)}, bf16[2,220,440]{2,1,0:T(8,128)(2,1)}, u32[]{:S(2)}) copy-start(bf16[2,220,440]{2,1,0:T(8,128)(2,1)} %constant.19.clone.refs_8_) | copy-start | bytes 1161604
  28.1 10.8 %copy-start.14 = (bf16[2,220,440]{2,1,0:T(8,128)(2,1)S(1)}, bf16[2,220,440]{2,1,0:T(8,128)(2,1)}, u32[]{:S(2)}) copy-start(bf16[2,220,440]{2,1,0:T(8,128)(2,1)} %constant.20.clone.refs_9_) | copy-start | bytes 1161604
  28.1 13.3 %collective-permute-start.5 = (bf16[224,896]{1,0:T(8,128)(2,1)S(1)}, bf16[224,896]{1,0:T(8,128)(2,1)S(1)}, u32[]{:S(2)}, u32[]{:S(2)}) collective-permute-start(bf16[224,896]{1,0:T(8,128)(2,1)S(1)} %add.35), channel_id=1, source_target_pairs={{0,0},{4,8},{8,4},{12,12},{1,1},{5,9},{9,5},{13,13},{2,2},{6,10},{... | collective-permute-start | bytes 1204232 | tf_op jit(solution)/shard_map/ppermute | solution.py:218
  29.0 13.4 %collective-permute-start.3 = (bf16[224,896]{1,0:T(8,128)(2,1)S(1)}, bf16[224,896]{1,0:T(8,128)(2,1)S(1)}, u32[]{:S(2)}, u32[]{:S(2)}) collective-permute-start(bf16[224,896]{1,0:T(8,128)(2,1)S(1)} %add_select_fusion.1), channel_id=1, source_target_pairs={{0,4},{4,0},{8,12},{12,8},{1,5},{5,1},{9,13},{13,9},{2,6},{6,2},{1... | collective-permute-start | bytes 1204232 | tf_op jit(solution)/shard_map/ppermute | solution.py:201
  41.5 24.0 %copy-start.1 = (bf16[2,2,2,224,220]{4,3,2,1,0:T(8,128)(2,1)S(1)}, bf16[2,2,2,224,220]{4,3,2,1,0:T(8,128)(2,1)}, u32[]{:S(2)}) copy-start(bf16[2,2,2,224,220]{4,3,2,1,0:T(8,128)(2,1)} %copy-done) | copy-start | bytes 2365444
  42.5 9.8 %collective-permute-start.6 = (bf16[224,896]{1,0:T(8,128)(2,1)S(1)}, bf16[224,896]{1,0:T(8,128)(2,1)S(1)}, u32[]{:S(2)}, u32[]{:S(2)}) collective-permute-start(bf16[224,896]{1,0:T(8,128)(2,1)S(1)} %add_select_fusion), channel_id=1, source_target_pairs={{0,4},{4,0},{8,12},{12,8},{1,5},{5,1},{9,13},{13,9},{2,6},{6,2},{1... | collective-permute-start | bytes 1204232 | tf_op jit(solution)/shard_map/ppermute | solution.py:201
  44.3 9.0 %collective-permute-start.4 = (bf16[224,896]{1,0:T(8,128)(2,1)S(1)}, bf16[224,896]{1,0:T(8,128)(2,1)S(1)}, u32[]{:S(2)}, u32[]{:S(2)}) collective-permute-start(bf16[224,896]{1,0:T(8,128)(2,1)S(1)} %add.36), channel_id=1, source_target_pairs={{0,0},{4,8},{8,4},{12,12},{1,1},{5,9},{9,5},{13,13},{2,2},{6,10},{... | collective-permute-start | bytes 1204232 | tf_op jit(solution)/shard_map/ppermute | solution.py:218
  52.5 14.6 %copy-start.3 = (bf16[2,2,2,224,220]{4,3,2,1,0:T(8,128)(2,1)S(1)}, bf16[2,2,2,224,220]{4,3,2,1,0:T(8,128)(2,1)}, u32[]{:S(2)}) copy-start(bf16[2,2,2,224,220]{4,3,2,1,0:T(8,128)(2,1)} %copy-done.2) | copy-start | bytes 2365444
  52.5 6.7 %collective-permute-start.7 = (bf16[224,896]{1,0:T(8,128)(2,1)S(1)}, bf16[224,896]{1,0:T(8,128)(2,1)S(1)}, u32[]{:S(2)}, u32[]{:S(2)}) collective-permute-start(bf16[224,896]{1,0:T(8,128)(2,1)S(1)} %add.39), channel_id=1, source_target_pairs={{0,0},{4,8},{8,4},{12,12},{1,1},{5,9},{9,5},{13,13},{2,2},{6,10},{... | collective-permute-start | bytes 1204232 | tf_op jit(solution)/shard_map/ppermute | solution.py:218
  53.4 13.7 %collective-permute-start.8 = (bf16[224,896]{1,0:T(8,128)(2,1)S(1)}, bf16[224,896]{1,0:T(8,128)(2,1)S(1)}, u32[]{:S(2)}, u32[]{:S(2)}) collective-permute-start(bf16[224,896]{1,0:T(8,128)(2,1)S(1)} %add.37), channel_id=1, source_target_pairs={{0,4},{4,0},{8,12},{12,8},{1,5},{5,1},{9,13},{13,9},{2,6},{6,2},{1... | collective-permute-start | bytes 1204232 | tf_op jit(solution)/shard_map/ppermute | solution.py:201
  59.3 14.6 %collective-permute-start.9 = (bf16[224,896]{1,0:T(8,128)(2,1)S(1)}, bf16[224,896]{1,0:T(8,128)(2,1)S(1)}, u32[]{:S(2)}, u32[]{:S(2)}) collective-permute-start(bf16[224,896]{1,0:T(8,128)(2,1)S(1)} %add.40), channel_id=1, source_target_pairs={{0,4},{4,0},{8,12},{12,8},{1,5},{5,1},{9,13},{13,9},{2,6},{6,2},{1... | collective-permute-start | bytes 1204232 | tf_op jit(solution)/shard_map/ppermute | solution.py:201
  75.0 3.7 %collective-permute-start.11 = (f32[8,220]{1,0:T(8,128)S(1)}, f32[8,220]{1,0:T(8,128)S(1)}, u32[]{:S(2)}, u32[]{:S(2)}) collective-permute-start(f32[8,220]{1,0:T(8,128)S(1)} %reshape.23), channel_id=1, source_target_pairs={{0,2},{1,3},{2,0},{3,1},{4,6},{5,7},{6,4},{7,5},{8,10},{9,11},{10,... | collective-permute-start | bytes 21128 | tf_op jit(solution)/shard_map/ppermute | solution.py:171
  76.6 3.1 %collective-permute-start.12 = (f32[8,220]{1,0:T(8,128)S(1)}, f32[8,220]{1,0:T(8,128)S(1)}, u32[]{:S(2)}, u32[]{:S(2)}) collective-permute-start(f32[8,220]{1,0:T(8,128)S(1)} %reshape.23), channel_id=1, source_target_pairs={{0,3},{1,2},{2,1},{3,0},{4,7},{5,6},{6,5},{7,4},{8,11},{9,10},{10,... | collective-permute-start | bytes 21128 | tf_op jit(solution)/shard_map/ppermute | solution.py:171
  76.6 3.1 %collective-permute-start.10 = (f32[8,220]{1,0:T(8,128)S(1)}, f32[8,220]{1,0:T(8,128)S(1)}, u32[]{:S(2)}, u32[]{:S(2)}) collective-permute-start(f32[8,220]{1,0:T(8,128)S(1)} %reshape.23), channel_id=1, source_target_pairs={{0,1},{1,0},{2,3},{3,2},{4,5},{5,4},{6,7},{7,6},{8,9},{9,8},{10,11... | collective-permute-start | bytes 21128 | tf_op jit(solution)/shard_map/ppermute | solution.py:171
  (6 other events, 10.7 us)

commit v7 on v5

--- a/solution.py
+++ b/solution.py
@@ -15,6 +15,7 @@
 LANE_TILE = 128
 ROW_PARTS = 2
 LAG = 3
+HALVES = 2
 VMEM_BYTES = 24 * 1024 * 1024
 
 
@@ -43,10 +44,10 @@
     gram_re = cosine.T @ cosine + sine.T @ sine
     gram_im = sine.T @ cosine - cosine.T @ sine
     gram = np.stack(
-        [np.concatenate([gram_re, gram_im], 1), np.concatenate([-gram_im, gram_re], 1)]
+        [np.concatenate([gram_im, -gram_re], 1), np.concatenate([gram_re, gram_im], 1)]
     )
     adjoint = np.stack(
-        [np.concatenate([cosine, -sine], 1), np.concatenate([sine, cosine], 1)]
+        [np.concatenate([-sine, -cosine], 1), np.concatenate([cosine, -sine], 1)]
     )
     left = np.stack([left_re, left_im])
     return tuple(part.astype(ml_dtypes.bfloat16) for part in (left, gram, adjoint))
@@ -67,55 +68,61 @@
     return jnp.cos(angle[...]).T, jnp.sin(angle[...]).T
 
 
-def encode_kernel(slots, group, whole_classes, *refs):
+def encode_kernel(slots, group, picks, *refs):
     shift_ref, order_ref, place_ref, image_ref, map_ref, kspace_ref, offset_ref = refs[:7]
     left_ref, gram_ref, adjoint_ref, kept_ref = refs[7:11]
     out_refs = refs[11:-4]
-    total, angle, shifted_ref, copied = refs[-4:]
+    total, angle, shifted, copied = refs[-4:]
     vols, coils, length = image_ref.shape[0], map_ref.shape[0], image_ref.shape[-1]
-    rows = shifted_ref.shape[-2]
-    copies = []
+    _, rows, lanes = shifted.shape
     part = rows // len(out_refs)
     groups = order_ref.shape[0]
+    whole_classes = picks is not None
     if whole_classes:
         rows_of = [slot * groups + group for slot in range(slots)]
     else:
-        rows_of = [place_ref[1]]
+        rows_of = picks = [place_ref[1]]
     cosines, sines = phase_columns(shift_ref, offset_ref, angle, rows_of, length)
-    if total.shape[1] > vols * coils * 2 * length:
-        total[...] = jnp.zeros_like(total)
-    for vol in range(vols):
-        for coil in range(coils):
-            place = vol * coils + coil
-            sum_re = sum_im = None
-            for slot, pick in enumerate(rows_of):
-                image_re = image_ref[vol, pick, 0].astype(jnp.float32)
-                image_im = image_ref[vol, pick, 1].astype(jnp.float32)
+    if lanes > vols * coils * 2 * length:
+        last = slice(lanes - LANE_TILE, lanes)
+        total[:, last] = jnp.zeros((rows, LANE_TILE), jnp.float32)
+        for slot in range(slots):
+            shifted[slot, :, last] = jnp.zeros((rows, LANE_TILE), jnp.bfloat16)
+    sums, copies = [None] * (vols * coils), []
+    for slot, pick in enumerate(picks):
+        cosine = cosines[:rows, slot : slot + 1]
+        sine = sines[:rows, slot : slot + 1]
+        for vol in range(vols):
+            image_re = image_ref[vol, pick, 0].astype(jnp.float32)
+            image_im = image_ref[vol, pick, 1].astype(jnp.float32)
+            for coil in range(coils):
+                place = vol * coils + coil
+                base = place * 2 * length
                 map_re = map_ref[coil, pick, 0].astype(jnp.float32)
                 map_im = map_ref[coil, pick, 1].astype(jnp.float32)
                 coil_re = (map_re * image_re - map_im * image_im).astype(jnp.bfloat16)
                 coil_im = (map_re * image_im + map_im * image_re).astype(jnp.bfloat16)
                 partly = dot(left_ref[0], coil_re) + dot(left_ref[1], coil_im)
-                cosine = cosines[:rows, slot : slot + 1]
-                sine = sines[:rows, slot : slot + 1]
                 part_re, part_im = partly[:rows], partly[rows:]
                 shift_re = part_re * cosine - part_im * sine
                 shift_im = part_re * sine + part_im * cosine
-                shifted_ref[slot, place, 0] = shift_re.astype(jnp.bfloat16)
-                shifted_ref[slot, place, 1] = shift_im.astype(jnp.bfloat16)
-                copy = pltpu.make_async_copy(
-                    shifted_ref.at[slot, place], kept_ref.at[slot, place], copied.at[slot, place]
+                shifted[slot, :, base : base + length] = shift_re.astype(jnp.bfloat16)
+                shifted[slot, :, base + length : base + 2 * length] = shift_im.astype(
+                    jnp.bfloat16
                 )
-                copy.start()
-                copies.append(copy)
-                sum_re = shift_re if slot == 0 else sum_re + shift_re
-                sum_im = shift_im if slot == 0 else sum_im + shift_im
-            mixed = dot(sum_re.astype(jnp.bfloat16), gram_ref[0]) + dot(
-                sum_im.astype(jnp.bfloat16), gram_ref[1]
-            )
-            if not whole_classes:
-                mixed = jnp.where(place_ref[0] > 0, mixed, 0.0)
-            total[:, place * 2 * length : (place + 1) * 2 * length] = mixed
+                if slot > 0:
+                    shift_re, shift_im = sums[place][0] + shift_re, sums[place][1] + shift_im
+                sums[place] = (shift_re, shift_im)
+        copy = pltpu.make_async_copy(shifted.at[slot], kept_ref.at[slot], copied.at[slot])
+        copy.start()
+        copies.append(copy)
+    for place, (sum_re, sum_im) in enumerate(sums):
+        mixed = dot(sum_re.astype(jnp.bfloat16), gram_ref[0]) + dot(
+            sum_im.astype(jnp.bfloat16), gram_ref[1]
+        )
+        if not whole_classes:
+            mixed = jnp.where(place_ref[0] > 0, mixed, 0.0)
+        total[:, place * 2 * length : (place + 1) * 2 * length] = mixed
 
     @pl.when(order_ref[group] == lax.axis_index("slc"))
     def _():
@@ -135,7 +142,7 @@
 
 def gradient_kernel(index, factor, on_line, *refs):
     term_refs, shifted_ref, out_ref = refs[:-2], refs[-2], refs[-1]
-    slots, places, _, _, length = shifted_ref.shape
+    slots, _, lanes = shifted_ref.shape
     part = out_ref.shape[1]
     terms = [ref[...].astype(jnp.float32) for ref in term_refs]
     if on_line:
@@ -145,19 +152,12 @@
         residual = own + jnp.where(edge, rest, near + across)
     else:
         residual = terms[0]
-    sums = [None] * slots
-    for place in range(places):
-        base = place * 2 * length
-        resid_re = residual[:, base : base + length]
-        resid_im = residual[:, base + length : base + 2 * length]
-        for slot in range(slots):
-            span = slice(index * part, (index + 1) * part)
-            shift_re = shifted_ref[slot, place, 0, span, :].astype(jnp.float32)
-            shift_im = shifted_ref[slot, place, 1, span, :].astype(jnp.float32)
-            term = resid_im * shift_re - resid_re * shift_im
-            sums[slot] = term if place == 0 else sums[slot] + term
     for slot in range(slots):
-        out_ref[slot : slot + 1, :] = factor * jnp.sum(sums[slot].T, axis=0, keepdims=True)
+        shifted = shifted_ref[slot, index * part : (index + 1) * part, :].astype(jnp.float32)
+        product = residual * shifted
+        tiles = [product[:, at : at + LANE_TILE] for at in range(0, lanes, LANE_TILE)]
+        folded = functools.reduce(lambda a, b: a + b, tiles)
+        out_ref[slot : slot + 1, :] = factor * jnp.sum(folded.T, axis=0, keepdims=True)
 
 
 def after(value, *earlier):
@@ -208,22 +208,19 @@
         own = after(terms[0], *earlier) if earlier else terms[0]
         gradients.append(gradient(step, (own, *terms[1:]), shifted[step // parts]))
 
-    encode_next()
-    for _ in range(parts):
-        outer_next()
-    while len(pieces) < LAG:
+    while len(outer) < LAG:
         encode_next()
-    while len(outer) < LAG:
-        outer_next()
+        while len(outer) < min(LAG, len(pieces)):
+            outer_next()
     latest = (pieces[-1],)
     for step in range(count):
         half = pieces[step] + after(outer[step], *latest)
         inner.append(lax.ppermute(half, "slc", inner_pairs))
-        if len(pieces) < min(count, step + LAG + 1):
-            encode_next(half)
         latest = ()
         if step >= 1:
             latest = (outer_next(half),)
+        if len(pieces) < min(count, step + LAG + 2):
+            encode_next(*(latest or (half,)))
         if step >= LAG + 1:
             gradient_next(*latest)
             latest = (*latest, gradients[-1])
@@ -250,28 +247,45 @@
     in_vmem = pl.BlockSpec(memory_space=pltpu.VMEM)
     in_smem = pl.BlockSpec(memory_space=pltpu.SMEM)
 
+    per_half = groups // HALVES
+
+    @functools.cache
+    def halves(half):
+        lead = lambda array: array.reshape(
+            array.shape[0], slots, groups, *array.shape[2:]
+        )[:, :, half * per_half : (half + 1) * per_half].reshape(
+            array.shape[0], slots * per_half, *array.shape[2:]
+        )
+        pair = (images, coil_maps)
+        if half > 0:
+            pair = lax.optimization_barrier((*pair, *held_back))[:2]
+        return tuple(lead(array) for array in pair)
+
+    held_back = []
+
     def encode(group, *earlier):
         if whole_classes:
             place = np.zeros((2,), np.int32)
+            image, coil_map = halves(group // per_half)
+            picks = [slot * per_half + group % per_half for slot in range(slots)]
         else:
             within = group - first
             held = (within >= 0) & (within < per_device)
             within = jnp.where(held, within, 0)
             place = jnp.stack([held, within]).astype(jnp.int32)
+            image, coil_map, picks = images, coil_maps, None
         offset = after(phase_offset, *earlier) if earlier else phase_offset
-        return pl.pallas_call(
-            functools.partial(encode_kernel, slots, group, whole_classes),
+        outputs = pl.pallas_call(
+            functools.partial(encode_kernel, slots, group, picks),
             in_specs=[in_smem] * 3 + [in_vmem] * 7,
-            out_specs=[pl.BlockSpec(memory_space=pl.ANY)] + [in_vmem] * ROW_PARTS,
-            out_shape=[
-                jax.ShapeDtypeStruct((slots, places, 2, rows, length), jnp.bfloat16),
-            ]
+            out_specs=[pl.BlockSpec(memory_space=pltpu.HBM)] + [in_vmem] * ROW_PARTS,
+            out_shape=[jax.ShapeDtypeStruct((slots, rows, lanes), jnp.bfloat16)]
             + [jax.ShapeDtypeStruct((part, lanes), jnp.bfloat16)] * ROW_PARTS,
             scratch_shapes=[
                 pltpu.VMEM((rows, lanes), jnp.float32),
                 pltpu.VMEM((round_up(slots, 8), round_up(rows, LANE_TILE)), jnp.float32),
-                pltpu.VMEM((slots, places, 2, rows, length), jnp.bfloat16),
-                pltpu.SemaphoreType.DMA((slots, places)),
+                pltpu.VMEM((slots, rows, lanes), jnp.bfloat16),
+                pltpu.SemaphoreType.DMA((slots,)),
             ],
             compiler_params=pltpu.CompilerParams(vmem_limit_bytes=VMEM_BYTES),
             cost_estimate=pl.CostEstimate(
@@ -284,12 +298,14 @@
             shift_index,
             group_order,
             place,
-            images,
-            coil_maps,
+            image,
+            coil_map,
             kspace,
             offset,
             *tables,
         )
+        held_back.append(outputs[1])
+        return outputs
 
     def gradient(step, terms, encoded):
         return pl.pallas_call(

time: 90.8 us -> 91.1 us (level)
  Pallas kernels: 27.5 us -> 18.9 us
  local copies, waits for them, and re-layouts: 9.21 us -> 14.2 us
  waiting for transfers between devices: 3.21 us -> 7.62 us
    slice x0 -> x4, local copies, waits for them, and re-layouts: none -> 5.04 us  [halves(): array.reshape(array.shape[0], slots, groups, *array.shape[2:])]
    pallas_call x4, Pallas kernels: 18.5 us -> 13.8 us  [encode(): pl.pallas_call(functools.partial(encode_kernel, slots, group, picks), in_...]
    ppermute x11, waiting for transfers between devices: 1.32 us -> 5.73 us  [outer_next(): outer.append(lax.ppermute(payload, 'slc', outer_pairs))]
    pallas_call x8, Pallas kernels: 8.94 us -> 5.1 us  [gradient(): pl.pallas_call(functools.partial(gradient_kernel, step % ROW_PARTS, facto...]
    unnamed x39 -> x45, local copies, waits for them, and re-layouts: 9.2 us -> 9.18 us
  transfers between devices with their start and end apart: 22 -> 22, of which waited for: 3 -> 7; matrix products, arithmetic and copies ran while one was open for 7% -> 10% of each run, Pallas kernels for 24% -> 16%
where the time goes in v7:
time: 91.1 us; the launch traced here: 90.4 us
  starting transfers between devices  42 us (46%)
  Pallas kernels  18.9 us (21%)
  local copies, waits for them, and re-layouts  14.2 us (16%)
  waiting for transfers between devices  7.62 us (8%)
  other arithmetic  7.23 us (8%)
    ppermute x11, starting transfers between devices, outer_next(): outer.append(lax.ppermute(payload, 'slc', outer_pairs))  31.7 us
    pallas_call x4, Pallas kernels, encode(): pl.pallas_call(functools.partial(encode_kernel, slots, group, picks), in_...  13.8 us
    unnamed x45, local copies, waits for them, and re-layouts  9.18 us
    ppermute x8, starting transfers between devices, line_of_four(): inner.append(lax.ppermute(half, 'slc', inner_pairs))  8.36 us
    ppermute x11, waiting for transfers between devices, outer_next(): outer.append(lax.ppermute(payload, 'slc', outer_pairs))  5.73 us
    pallas_call x8, Pallas kernels, gradient(): pl.pallas_call(functools.partial(gradient_kernel, step % ROW_PARTS, facto...  5.1 us
    slice x4, local copies, waits for them, and re-layouts, halves(): array.reshape(array.shape[0], slots, groups, *array.shape[2:])  5.04 us
    add x8, other arithmetic, line_of_four(): half = pieces[step] + after(outer[step], *latest)  3.14 us
  transfers between devices with their start and end apart: 22, of which 7 were waited for; matrix products, arithmetic and copies ran while one was open for 10% of the time, Pallas kernels for 16%

profile of v7, /device:TPU:0, one launch (start us, length us, event | category | flops | bytes accessed | tf_op | source)
XLA Modules:
  0.0 90.4 jit_solution(16539214011220842810)
XLA Ops:
  1.1 1.9 %slice.20 = bf16[1,2,2,2,220,220]{5,3,4,2,1,0:T(2,128)(2,1)S(1)} slice(bf16[1,2,4,2,220,220]{5,3,4,2,1,0:T(2,128)(2,1)} %bitcast.26), slice={[0:1], [0:2], [0:2], [0:2], [0:220], [0:220]} | slice | bytes 1548800 | tf_op jit(solution)/shard_map/slice | solution.py:254
  3.4 1.2 %slice.21 = bf16[2,2,2,2,220,220]{5,3,4,2,1,0:T(2,128)(2,1)S(1)} slice(bf16[2,2,4,2,220,220]{5,3,4,2,1,0:T(2,128)(2,1)S(1)} %bitcast.24), slice={[0:2], [0:2], [0:2], [0:2], [0:220], [0:220]} | slice | bytes 3097600 | tf_op jit(solution)/shard_map/slice | solution.py:254
  5.9 4.1 %encode.4 = (bf16[2,224,896]{2,1,0:T(8,128)(2,1)S(1)}, bf16[112,896]{1,0:T(8,128)(2,1)S(1)}, bf16[112,896]{1,0:T(8,128)(2,1)}) custom-call(s32[8]{0:T(128)S(1)} %copy-done.15, s32[4]{0:T(128)S(1)} %copy-done.16, s32[2]{0:T(128)S(1)} %call_exported.0.refs_2_, bf16[1,4,2,220,220]{4,3,2,1,0:T(8,128)(2,1)S(1)} %bitcast.22, ...), custom_call_target="tpu_custom_call" | custom-call | flops 1022208000 | bytes 6000000 | tf_op jit(solution)/shard_map/encode/pallas_call | solution.py:278
  10.9 2.5 %collective-permute-start = (bf16[112,896]{1,0:T(8,128)(2,1)S(1)}, bf16[112,896]{1,0:T(8,128)(2,1)S(1)}, u32[]{:S(2)}, u32[]{:S(2)}) collective-permute-start(bf16[112,896]{1,0:T(8,128)(2,1)S(1)} %get-tuple-element.63.refs_0_), channel_id=1, source_target_pairs={{0,4},{4,0},{8,12},{12,8},{1,5},{5,1},{9,13},{13,9},{2,6},{6,2},{1... | collective-permute-start | bytes 602120 | tf_op jit(solution)/shard_map/ppermute | solution.py:202
  13.5 3.6 %encode.5 = (bf16[2,224,896]{2,1,0:T(8,128)(2,1)S(1)}, bf16[112,896]{1,0:T(8,128)(2,1)}, bf16[112,896]{1,0:T(8,128)(2,1)S(1)}) custom-call(s32[8]{0:T(128)S(1)} %copy-done.15, s32[4]{0:T(128)S(1)} %copy-done.16, s32[2]{0:T(128)S(1)} %call_exported.0.refs_2_, bf16[1,4,2,220,220]{4,3,2,1,0:T(8,128)(2,1)S(1)} %bitcast.23, ...), custom_call_target="tpu_custom_call" | custom-call | flops 1022208000 | bytes 6000000 | tf_op jit(solution)/shard_map/encode/pallas_call | solution.py:278
  18.0 1.3 %collective-permute-done.refs_1_ = bf16[112,896]{1,0:T(8,128)(2,1)S(1)} collective-permute-done((bf16[112,896]{1,0:T(8,128)(2,1)S(1)}, bf16[112,896]{1,0:T(8,128)(2,1)S(1)}, u32[]{:S(2)}, u32[]{:S(2)}) %collective-permute-start) | collective-permute-done | bytes 200736 | tf_op jit(solution)/shard_map/ppermute | solution.py:202
  20.0 3.4 %collective-permute-start.4 = (bf16[112,896]{1,0:T(8,128)(2,1)}, bf16[112,896]{1,0:T(8,128)(2,1)}, u32[]{:S(2)}, u32[]{:S(2)}) collective-permute-start(bf16[112,896]{1,0:T(8,128)(2,1)} %add.57), channel_id=1, source_target_pairs={{0,0},{4,8},{8,4},{12,12},{1,1},{5,9},{9,5},{13,13},{2,2},{6,10},{... | collective-permute-start | bytes 602120 | tf_op jit(solution)/shard_map/ppermute | solution.py:218
  23.4 2.2 %collective-permute-start.3 = (bf16[112,896]{1,0:T(8,128)(2,1)}, bf16[112,896]{1,0:T(8,128)(2,1)}, u32[]{:S(2)}, u32[]{:S(2)}) collective-permute-start(bf16[112,896]{1,0:T(8,128)(2,1)} %get-tuple-element.71.refs_0_), channel_id=1, source_target_pairs={{0,4},{4,0},{8,12},{12,8},{1,5},{5,1},{9,13},{13,9},{2,6},{6,2},{1... | collective-permute-start | bytes 602120 | tf_op jit(solution)/shard_map/ppermute | solution.py:202
  26.4 1.3 %copy-done.18 = bf16[2,8,2,220,220]{4,2,3,1,0:T(2,128)(2,1)S(1)} copy-done((bf16[2,8,2,220,220]{4,2,3,1,0:T(2,128)(2,1)S(1)}, bf16[2,8,2,220,220]{4,2,3,1,0:T(2,128)(2,1)}, u32[]{:S(2)}) %copy-start.18) | copy-done | bytes 3097624
  34.0 3.1 %encode.6 = (bf16[2,224,896]{2,1,0:T(8,128)(2,1)S(1)}, bf16[112,896]{1,0:T(8,128)(2,1)S(1)}, bf16[112,896]{1,0:T(8,128)(2,1)S(1)}) custom-call(s32[8]{0:T(128)S(1)} %copy-done.15, s32[4]{0:T(128)S(1)} %copy-done.16, s32[2]{0:T(128)S(1)} %call_exported.0.refs_2_, bf16[1,4,2,220,220]{4,3,2,1,0:T(8,128)(2,1)S(1)} %bitcast.20, ...), custom_call_target="tpu_custom_call" | custom-call | flops 1022208000 | bytes 6000000 | tf_op jit(solution)/shard_map/encode/pallas_call | solution.py:278
  38.1 4.8 %collective-permute-start.5 = (bf16[112,896]{1,0:T(8,128)(2,1)S(1)}, bf16[112,896]{1,0:T(8,128)(2,1)S(1)}, u32[]{:S(2)}, u32[]{:S(2)}) collective-permute-start(bf16[112,896]{1,0:T(8,128)(2,1)S(1)} %add_select_fusion.3), channel_id=1, source_target_pairs={{0,4},{4,0},{8,12},{12,8},{1,5},{5,1},{9,13},{13,9},{2,6},{6,2},{1... | collective-permute-start | bytes 602120 | tf_op jit(solution)/shard_map/ppermute | solution.py:202
  45.7 1.3 %collective-permute-start.7 = (bf16[112,896]{1,0:T(8,128)(2,1)S(1)}, bf16[112,896]{1,0:T(8,128)(2,1)S(1)}, u32[]{:S(2)}, u32[]{:S(2)}) collective-permute-start(bf16[112,896]{1,0:T(8,128)(2,1)S(1)} %add_select_fusion.4), channel_id=1, source_target_pairs={{0,4},{4,0},{8,12},{12,8},{1,5},{5,1},{9,13},{13,9},{2,6},{6,2},{1... | collective-permute-start | bytes 602120 | tf_op jit(solution)/shard_map/ppermute | solution.py:202
  47.0 2.9 %encode.7 = (bf16[2,224,896]{2,1,0:T(8,128)(2,1)S(1)}, bf16[112,896]{1,0:T(8,128)(2,1)S(1)}, bf16[112,896]{1,0:T(8,128)(2,1)S(1)}) custom-call(s32[8]{0:T(128)S(1)} %copy-done.15, s32[4]{0:T(128)S(1)} %copy-done.16, s32[2]{0:T(128)S(1)} %call_exported.0.refs_2_, bf16[1,4,2,220,220]{4,3,2,1,0:T(8,128)(2,1)S(1)} %bitcast.21, ...), custom_call_target="tpu_custom_call" | custom-call | flops 1022208000 | bytes 6000000 | tf_op jit(solution)/shard_map/encode/pallas_call | solution.py:278
  51.9 3.8 %collective-permute-start.10 = (bf16[112,896]{1,0:T(8,128)(2,1)S(1)}, bf16[112,896]{1,0:T(8,128)(2,1)S(1)}, u32[]{:S(2)}, u32[]{:S(2)}) collective-permute-start(bf16[112,896]{1,0:T(8,128)(2,1)S(1)} %add_select_fusion.1), channel_id=1, source_target_pairs={{0,4},{4,0},{8,12},{12,8},{1,5},{5,1},{9,13},{13,9},{2,6},{6,2},{1... | collective-permute-start | bytes 602120 | tf_op jit(solution)/shard_map/ppermute | solution.py:202
  56.5 3.3 %collective-permute-start.12 = (bf16[112,896]{1,0:T(8,128)(2,1)S(1)}, bf16[112,896]{1,0:T(8,128)(2,1)S(1)}, u32[]{:S(2)}, u32[]{:S(2)}) collective-permute-start(bf16[112,896]{1,0:T(8,128)(2,1)S(1)} %add_select_fusion.2), channel_id=1, source_target_pairs={{0,4},{4,0},{8,12},{12,8},{1,5},{5,1},{9,13},{13,9},{2,6},{6,2},{1... | collective-permute-start | bytes 602120 | tf_op jit(solution)/shard_map/ppermute | solution.py:202
  62.0 4.1 %collective-permute-start.14 = (bf16[112,896]{1,0:T(8,128)(2,1)S(1)}, bf16[112,896]{1,0:T(8,128)(2,1)S(1)}, u32[]{:S(2)}, u32[]{:S(2)}) collective-permute-start(bf16[112,896]{1,0:T(8,128)(2,1)S(1)} %add_select_fusion), channel_id=1, source_target_pairs={{0,4},{4,0},{8,12},{12,8},{1,5},{5,1},{9,13},{13,9},{2,6},{6,2},{1... | collective-permute-start | bytes 602120 | tf_op jit(solution)/shard_map/ppermute | solution.py:202
  66.0 1.3 %gradient.9 = f32[2,112]{1,0:T(2,128)S(1)} custom-call(bf16[112,896]{1,0:T(8,128)(2,1)} %get-tuple-element.68.refs_0_, bf16[112,896]{1,0:T(8,128)(2,1)} %collective-permute-done.1.refs_1_, bf16[112,896]{1,0:T(8,128)(2,1)S(1)} %collective-permute-done.2.refs_2_, bf16[112,896]{1,0:T(8,128)(2,1)S(1)} %collective-permute-done.7.refs_3_.refs_1_, ...), custom_call_target="tpu_custom_call" | custom-call | flops 774400 | bytes 1500000 | tf_op jit(solution)/shard_map/gradient/pallas_call | solution.py:311
  68.2 1.3 %gradient.10 = f32[2,112]{1,0:T(2,128)S(1)} custom-call(bf16[112,896]{1,0:T(8,128)(2,1)} %get-tuple-element.71.refs_0_, bf16[112,896]{1,0:T(8,128)(2,1)} %collective-permute-done.3.refs_1_, bf16[112,896]{1,0:T(8,128)(2,1)S(1)} %collective-permute-done.8.refs_2_, bf16[112,896]{1,0:T(8,128)(2,1)S(1)} %collective-permute-done.10.refs_3_.refs_1_, ...), custom_call_target="tpu_custom_call" | custom-call | flops 774400 | bytes 1500000 | tf_op jit(solution)/shard_map/gradient/pallas_call | solution.py:311
  70.5 5.8 %collective-permute-start.16 = (bf16[112,896]{1,0:T(8,128)(2,1)S(1)}, bf16[112,896]{1,0:T(8,128)(2,1)S(1)}, u32[]{:S(2)}, u32[]{:S(2)}) collective-permute-start(bf16[112,896]{1,0:T(8,128)(2,1)S(1)} %add.68), channel_id=1, source_target_pairs={{0,4},{4,0},{8,12},{12,8},{1,5},{5,1},{9,13},{13,9},{2,6},{6,2},{1... | collective-permute-start | bytes 602120 | tf_op jit(solution)/shard_map/ppermute | solution.py:202
  77.0 3.6 %collective-permute-start.18 = (bf16[112,896]{1,0:T(8,128)(2,1)S(1)}, bf16[112,896]{1,0:T(8,128)(2,1)S(1)}, u32[]{:S(2)}, u32[]{:S(2)}) collective-permute-start(bf16[112,896]{1,0:T(8,128)(2,1)S(1)} %add.72), channel_id=1, source_target_pairs={{0,4},{4,0},{8,12},{12,8},{1,5},{5,1},{9,13},{13,9},{2,6},{6,2},{1... | collective-permute-start | bytes 602120 | tf_op jit(solution)/shard_map/ppermute | solution.py:202
  81.8 1.7 %collective-permute-done.17.refs_3_ = bf16[112,896]{1,0:T(8,128)(2,1)S(1)} collective-permute-done((bf16[112,896]{1,0:T(8,128)(2,1)S(1)}, bf16[112,896]{1,0:T(8,128)(2,1)S(1)}, u32[]{:S(2)}, u32[]{:S(2)}) %collective-permute-start.17) | collective-permute-done | bytes 200736 | tf_op jit(solution)/shard_map/ppermute | solution.py:202
  83.8 1.9 %collective-permute-done.18.refs_3_ = bf16[112,896]{1,0:T(8,128)(2,1)S(1)} collective-permute-done((bf16[112,896]{1,0:T(8,128)(2,1)S(1)}, bf16[112,896]{1,0:T(8,128)(2,1)S(1)}, u32[]{:S(2)}, u32[]{:S(2)}) %collective-permute-start.18) | collective-permute-done | bytes 200736 | tf_op jit(solution)/shard_map/ppermute | solution.py:202
  86.1 1.6 %collective-permute-start.20 = (f32[8,220]{1,0:T(8,128)S(1)}, f32[8,220]{1,0:T(8,128)S(1)}, u32[]{:S(2)}, u32[]{:S(2)}) collective-permute-start(f32[8,220]{1,0:T(8,128)S(1)} %reshape.35), channel_id=1, source_target_pairs={{0,2},{1,3},{2,0},{3,1},{4,6},{5,7},{6,4},{7,5},{8,10},{9,11},{10,... | collective-permute-start | bytes 21128 | tf_op jit(solution)/shard_map/ppermute | solution.py:172
  88.0 1.3 %collective-permute-done.21 = f32[8,220]{1,0:T(8,128)S(1)} collective-permute-done((f32[8,220]{1,0:T(8,128)S(1)}, f32[8,220]{1,0:T(8,128)S(1)}, u32[]{:S(2)}, u32[]{:S(2)}) %collective-permute-start.21) | collective-permute-done | bytes 7072 | tf_op jit(solution)/shard_map/ppermute | solution.py:172
  (106 shorter events, 26.6 us)
Async XLA Ops:
  10.9 8.3 %collective-permute-start = (bf16[112,896]{1,0:T(8,128)(2,1)S(1)}, bf16[112,896]{1,0:T(8,128)(2,1)S(1)}, u32[]{:S(2)}, u32[]{:S(2)}) collective-permute-start(bf16[112,896]{1,0:T(8,128)(2,1)S(1)} %get-tuple-element.63.refs_0_), channel_id=1, source_target_pairs={{0,4},{4,0},{8,12},{12,8},{1,5},{5,1},{9,13},{13,9},{2,6},{6,2},{1... | collective-permute-start | bytes 602120 | tf_op jit(solution)/shard_map/ppermute | solution.py:202
  13.5 12.2 %copy-start.19 = (bf16[1,8,2,220,220]{4,2,3,1,0:T(2,128)(2,1)S(1)}, bf16[1,8,2,220,220]{4,2,3,1,0:T(2,128)(2,1)}, u32[]{:S(2)}) copy-start(bf16[1,8,2,220,220]{4,2,3,1,0:T(2,128)(2,1)} %param.13) | copy-start | bytes 4646404
  13.5 15.7 %collective-permute-start.1 = (bf16[112,896]{1,0:T(8,128)(2,1)}, bf16[112,896]{1,0:T(8,128)(2,1)}, u32[]{:S(2)}, u32[]{:S(2)}) collective-permute-start(bf16[112,896]{1,0:T(8,128)(2,1)} %get-tuple-element.68.refs_0_), channel_id=1, source_target_pairs={{0,4},{4,0},{8,12},{12,8},{1,5},{5,1},{9,13},{13,9},{2,6},{6,2},{1... | collective-permute-start | bytes 602120 | tf_op jit(solution)/shard_map/ppermute | solution.py:202
  20.0 17.1 %collective-permute-start.4 = (bf16[112,896]{1,0:T(8,128)(2,1)}, bf16[112,896]{1,0:T(8,128)(2,1)}, u32[]{:S(2)}, u32[]{:S(2)}) collective-permute-start(bf16[112,896]{1,0:T(8,128)(2,1)} %add.57), channel_id=1, source_target_pairs={{0,0},{4,8},{8,4},{12,12},{1,1},{5,9},{9,5},{13,13},{2,2},{6,10},{... | collective-permute-start | bytes 602120 | tf_op jit(solution)/shard_map/ppermute | solution.py:218
  23.4 19.5 %collective-permute-start.3 = (bf16[112,896]{1,0:T(8,128)(2,1)}, bf16[112,896]{1,0:T(8,128)(2,1)}, u32[]{:S(2)}, u32[]{:S(2)}) collective-permute-start(bf16[112,896]{1,0:T(8,128)(2,1)} %get-tuple-element.71.refs_0_), channel_id=1, source_target_pairs={{0,4},{4,0},{8,12},{12,8},{1,5},{5,1},{9,13},{13,9},{2,6},{6,2},{1... | collective-permute-start | bytes 602120 | tf_op jit(solution)/shard_map/ppermute | solution.py:202
  30.3 14.4 %collective-permute-start.2 = (bf16[112,896]{1,0:T(8,128)(2,1)S(1)}, bf16[112,896]{1,0:T(8,128)(2,1)S(1)}, u32[]{:S(2)}, u32[]{:S(2)}) collective-permute-start(bf16[112,896]{1,0:T(8,128)(2,1)S(1)} %add.58), channel_id=1, source_target_pairs={{0,0},{4,8},{8,4},{12,12},{1,1},{5,9},{9,5},{13,13},{2,2},{6,10},{... | collective-permute-start | bytes 602120 | tf_op jit(solution)/shard_map/ppermute | solution.py:218
  38.1 11.9 %collective-permute-start.5 = (bf16[112,896]{1,0:T(8,128)(2,1)S(1)}, bf16[112,896]{1,0:T(8,128)(2,1)S(1)}, u32[]{:S(2)}, u32[]{:S(2)}) collective-permute-start(bf16[112,896]{1,0:T(8,128)(2,1)S(1)} %add_select_fusion.3), channel_id=1, source_target_pairs={{0,4},{4,0},{8,12},{12,8},{1,5},{5,1},{9,13},{13,9},{2,6},{6,2},{1... | collective-permute-start | bytes 602120 | tf_op jit(solution)/shard_map/ppermute | solution.py:202
  44.0 6.9 %collective-permute-start.8 = (bf16[112,896]{1,0:T(8,128)(2,1)S(1)}, bf16[112,896]{1,0:T(8,128)(2,1)S(1)}, u32[]{:S(2)}, u32[]{:S(2)}) collective-permute-start(bf16[112,896]{1,0:T(8,128)(2,1)S(1)} %add.61), channel_id=1, source_target_pairs={{0,0},{4,8},{8,4},{12,12},{1,1},{5,9},{9,5},{13,13},{2,2},{6,10},{... | collective-permute-start | bytes 602120 | tf_op jit(solution)/shard_map/ppermute | solution.py:218
  45.7 10.0 %collective-permute-start.7 = (bf16[112,896]{1,0:T(8,128)(2,1)S(1)}, bf16[112,896]{1,0:T(8,128)(2,1)S(1)}, u32[]{:S(2)}, u32[]{:S(2)}) collective-permute-start(bf16[112,896]{1,0:T(8,128)(2,1)S(1)} %add_select_fusion.4), channel_id=1, source_target_pairs={{0,4},{4,0},{8,12},{12,8},{1,5},{5,1},{9,13},{13,9},{2,6},{6,2},{1... | collective-permute-start | bytes 602120 | tf_op jit(solution)/shard_map/ppermute | solution.py:202
  50.0 9.8 %copy-start.9 = (bf16[2,224,896]{2,1,0:T(8,128)(2,1)S(1)}, bf16[2,224,896]{2,1,0:T(8,128)(2,1)}, u32[]{:S(2)}) copy-start(bf16[2,224,896]{2,1,0:T(8,128)(2,1)} %copy-done.8) | copy-start | bytes 2408452
  50.1 6.4 %collective-permute-start.6 = (bf16[112,896]{1,0:T(8,128)(2,1)S(1)}, bf16[112,896]{1,0:T(8,128)(2,1)S(1)}, u32[]{:S(2)}, u32[]{:S(2)}) collective-permute-start(bf16[112,896]{1,0:T(8,128)(2,1)S(1)} %add.62), channel_id=1, source_target_pairs={{0,0},{4,8},{8,4},{12,12},{1,1},{5,9},{9,5},{13,13},{2,2},{6,10},{... | collective-permute-start | bytes 602120 | tf_op jit(solution)/shard_map/ppermute | solution.py:218
  51.9 9.2 %collective-permute-start.10 = (bf16[112,896]{1,0:T(8,128)(2,1)S(1)}, bf16[112,896]{1,0:T(8,128)(2,1)S(1)}, u32[]{:S(2)}, u32[]{:S(2)}) collective-permute-start(bf16[112,896]{1,0:T(8,128)(2,1)S(1)} %add_select_fusion.1), channel_id=1, source_target_pairs={{0,4},{4,0},{8,12},{12,8},{1,5},{5,1},{9,13},{13,9},{2,6},{6,2},{1... | collective-permute-start | bytes 602120 | tf_op jit(solution)/shard_map/ppermute | solution.py:202
  55.8 6.2 %collective-permute-start.9 = (bf16[112,896]{1,0:T(8,128)(2,1)S(1)}, bf16[112,896]{1,0:T(8,128)(2,1)S(1)}, u32[]{:S(2)}, u32[]{:S(2)}) collective-permute-start(bf16[112,896]{1,0:T(8,128)(2,1)S(1)} %add.65), channel_id=1, source_target_pairs={{0,0},{4,8},{8,4},{12,12},{1,1},{5,9},{9,5},{13,13},{2,2},{6,10},{... | collective-permute-start | bytes 602120 | tf_op jit(solution)/shard_map/ppermute | solution.py:218
  56.5 10.8 %collective-permute-start.12 = (bf16[112,896]{1,0:T(8,128)(2,1)S(1)}, bf16[112,896]{1,0:T(8,128)(2,1)S(1)}, u32[]{:S(2)}, u32[]{:S(2)}) collective-permute-start(bf16[112,896]{1,0:T(8,128)(2,1)S(1)} %add_select_fusion.2), channel_id=1, source_target_pairs={{0,4},{4,0},{8,12},{12,8},{1,5},{5,1},{9,13},{13,9},{2,6},{6,2},{1... | collective-permute-start | bytes 602120 | tf_op jit(solution)/shard_map/ppermute | solution.py:202
  61.1 7.0 %collective-permute-start.11 = (bf16[112,896]{1,0:T(8,128)(2,1)S(1)}, bf16[112,896]{1,0:T(8,128)(2,1)S(1)}, u32[]{:S(2)}, u32[]{:S(2)}) collective-permute-start(bf16[112,896]{1,0:T(8,128)(2,1)S(1)} %add.67), channel_id=1, source_target_pairs={{0,0},{4,8},{8,4},{12,12},{1,1},{5,9},{9,5},{13,13},{2,2},{6,10},{... | collective-permute-start | bytes 602120 | tf_op jit(solution)/shard_map/ppermute | solution.py:218
  62.0 7.7 %collective-permute-start.14 = (bf16[112,896]{1,0:T(8,128)(2,1)S(1)}, bf16[112,896]{1,0:T(8,128)(2,1)S(1)}, u32[]{:S(2)}, u32[]{:S(2)}) collective-permute-start(bf16[112,896]{1,0:T(8,128)(2,1)S(1)} %add_select_fusion), channel_id=1, source_target_pairs={{0,4},{4,0},{8,12},{12,8},{1,5},{5,1},{9,13},{13,9},{2,6},{6,2},{1... | collective-permute-start | bytes 602120 | tf_op jit(solution)/shard_map/ppermute | solution.py:202
  67.4 9.0 %collective-permute-start.13 = (bf16[112,896]{1,0:T(8,128)(2,1)S(1)}, bf16[112,896]{1,0:T(8,128)(2,1)S(1)}, u32[]{:S(2)}, u32[]{:S(2)}) collective-permute-start(bf16[112,896]{1,0:T(8,128)(2,1)S(1)} %add.69), channel_id=1, source_target_pairs={{0,0},{4,8},{8,4},{12,12},{1,1},{5,9},{9,5},{13,13},{2,2},{6,10},{... | collective-permute-start | bytes 602120 | tf_op jit(solution)/shard_map/ppermute | solution.py:218
  69.8 6.8 %collective-permute-start.15 = (bf16[112,896]{1,0:T(8,128)(2,1)S(1)}, bf16[112,896]{1,0:T(8,128)(2,1)S(1)}, u32[]{:S(2)}, u32[]{:S(2)}) collective-permute-start(bf16[112,896]{1,0:T(8,128)(2,1)S(1)} %add.71), channel_id=1, source_target_pairs={{0,0},{4,8},{8,4},{12,12},{1,1},{5,9},{9,5},{13,13},{2,2},{6,10},{... | collective-permute-start | bytes 602120 | tf_op jit(solution)/shard_map/ppermute | solution.py:218
  70.5 10.9 %collective-permute-start.16 = (bf16[112,896]{1,0:T(8,128)(2,1)S(1)}, bf16[112,896]{1,0:T(8,128)(2,1)S(1)}, u32[]{:S(2)}, u32[]{:S(2)}) collective-permute-start(bf16[112,896]{1,0:T(8,128)(2,1)S(1)} %add.68), channel_id=1, source_target_pairs={{0,4},{4,0},{8,12},{12,8},{1,5},{5,1},{9,13},{13,9},{2,6},{6,2},{1... | collective-permute-start | bytes 602120 | tf_op jit(solution)/shard_map/ppermute | solution.py:202
  76.4 7.1 %collective-permute-start.17 = (bf16[112,896]{1,0:T(8,128)(2,1)S(1)}, bf16[112,896]{1,0:T(8,128)(2,1)S(1)}, u32[]{:S(2)}, u32[]{:S(2)}) collective-permute-start(bf16[112,896]{1,0:T(8,128)(2,1)S(1)} %add.70), channel_id=1, source_target_pairs={{0,4},{4,0},{8,12},{12,8},{1,5},{5,1},{9,13},{13,9},{2,6},{6,2},{1... | collective-permute-start | bytes 602120 | tf_op jit(solution)/shard_map/ppermute | solution.py:202
  77.0 8.7 %collective-permute-start.18 = (bf16[112,896]{1,0:T(8,128)(2,1)S(1)}, bf16[112,896]{1,0:T(8,128)(2,1)S(1)}, u32[]{:S(2)}, u32[]{:S(2)}) collective-permute-start(bf16[112,896]{1,0:T(8,128)(2,1)S(1)} %add.72), channel_id=1, source_target_pairs={{0,4},{4,0},{8,12},{12,8},{1,5},{5,1},{9,13},{13,9},{2,6},{6,2},{1... | collective-permute-start | bytes 602120 | tf_op jit(solution)/shard_map/ppermute | solution.py:202
  86.0 3.2 %collective-permute-start.21 = (f32[8,220]{1,0:T(8,128)S(1)}, f32[8,220]{1,0:T(8,128)S(1)}, u32[]{:S(2)}, u32[]{:S(2)}) collective-permute-start(f32[8,220]{1,0:T(8,128)S(1)} %reshape.35), channel_id=1, source_target_pairs={{0,3},{1,2},{2,1},{3,0},{4,7},{5,6},{6,5},{7,4},{8,11},{9,10},{10,... | collective-permute-start | bytes 21128 | tf_op jit(solution)/shard_map/ppermute | solution.py:172
  86.1 3.7 %collective-permute-start.20 = (f32[8,220]{1,0:T(8,128)S(1)}, f32[8,220]{1,0:T(8,128)S(1)}, u32[]{:S(2)}, u32[]{:S(2)}) collective-permute-start(f32[8,220]{1,0:T(8,128)S(1)} %reshape.35), channel_id=1, source_target_pairs={{0,2},{1,3},{2,0},{3,1},{4,6},{5,7},{6,4},{7,5},{8,10},{9,11},{10,... | collective-permute-start | bytes 21128 | tf_op jit(solution)/shard_map/ppermute | solution.py:172
  87.7 2.2 %collective-permute-start.19 = (f32[8,220]{1,0:T(8,128)S(1)}, f32[8,220]{1,0:T(8,128)S(1)}, u32[]{:S(2)}, u32[]{:S(2)}) collective-permute-start(f32[8,220]{1,0:T(8,128)S(1)} %reshape.35), channel_id=1, source_target_pairs={{0,1},{1,0},{2,3},{3,2},{4,5},{5,4},{6,7},{7,6},{8,9},{9,8},{10,11... | collective-permute-start | bytes 21128 | tf_op jit(solution)/shard_map/ppermute | solution.py:172
  (18 other events, 45.5 us)

commit v8 on v7

--- a/solution.py
+++ b/solution.py
@@ -15,7 +15,6 @@
 LANE_TILE = 128
 ROW_PARTS = 2
 LAG = 3
-HALVES = 2
 VMEM_BYTES = 24 * 1024 * 1024
 
 
@@ -50,6 +49,7 @@
         [np.concatenate([-sine, -cosine], 1), np.concatenate([cosine, -sine], 1)]
     )
     left = np.stack([left_re, left_im])
+    gram = np.pad(gram, ((0, 0), (0, round_up(length, LANE_TILE) - length), (0, 0)))
     return tuple(part.astype(ml_dtypes.bfloat16) for part in (left, gram, adjoint))
 
 
@@ -68,54 +68,93 @@
     return jnp.cos(angle[...]).T, jnp.sin(angle[...]).T
 
 
-def encode_kernel(slots, group, picks, *refs):
+def encode_kernel(slots, group, whole_classes, *refs):
     shift_ref, order_ref, place_ref, image_ref, map_ref, kspace_ref, offset_ref = refs[:7]
-    left_ref, gram_ref, adjoint_ref, kept_ref = refs[7:11]
-    out_refs = refs[11:-4]
-    total, angle, shifted, copied = refs[-4:]
+    left_ref, gram_ref, adjoint_ref, shifted = refs[7:11]
+    out_refs = refs[11:-9]
+    total, angle, wide, raw_image, raw_map, raw_kspace, adjoint, arrived, owner_arrived = refs[-9:]
     vols, coils, length = image_ref.shape[0], map_ref.shape[0], image_ref.shape[-1]
     _, rows, lanes = shifted.shape
     part = rows // len(out_refs)
     groups = order_ref.shape[0]
-    whole_classes = picks is not None
     if whole_classes:
         rows_of = [slot * groups + group for slot in range(slots)]
     else:
-        rows_of = picks = [place_ref[1]]
-    cosines, sines = phase_columns(shift_ref, offset_ref, angle, rows_of, length)
+        rows_of = [place_ref[1]]
+    owner = order_ref[group] == lax.axis_index("slc")
+
+    image_copies, map_copies = {}, {}
+    for slot, row in enumerate(rows_of):
+        for vol in range(vols):
+            image_copies[slot, vol] = pltpu.make_async_copy(
+                image_ref.at[vol, row], raw_image.at[vol, slot], arrived.at[slot, vol]
+            )
+            image_copies[slot, vol].start()
+        for coil in range(coils):
+            map_copies[slot, coil] = pltpu.make_async_copy(
+                map_ref.at[coil, row], raw_map.at[coil, slot], arrived.at[slot, vols + coil]
+            )
+            map_copies[slot, coil].start()
+    owner_copies = [
+        pltpu.make_async_copy(kspace_ref, raw_kspace, owner_arrived.at[0]),
+        pltpu.make_async_copy(adjoint_ref, adjoint, owner_arrived.at[1]),
+    ]
+
+    @pl.when(owner)
+    def _():
+        for copy in owner_copies:
+            copy.start()
+
+    tiles = wide.shape[1]
+
+    def planes(raw, buffer):
+        mixed = raw.reshape(2 * length, length)[...].astype(jnp.float32)
+        for tile in range(tiles):
+            at, end = tile * LANE_TILE, min(length, (tile + 1) * LANE_TILE)
+            wide[buffer, tile, :, : end - at] = mixed[:, at:end]
+        return [
+            jnp.concatenate(
+                [wide[buffer, tile, pl.ds(kind, length, stride=2), :] for tile in range(tiles)],
+                axis=1,
+            )
+            for kind in range(2)
+        ]
+
+    if tiles * LANE_TILE > length:
+        for buffer in range(wide.shape[0]):
+            wide[buffer, tiles - 1] = jnp.zeros((2 * length, LANE_TILE), jnp.float32)
     if lanes > vols * coils * 2 * length:
         last = slice(lanes - LANE_TILE, lanes)
         total[:, last] = jnp.zeros((rows, LANE_TILE), jnp.float32)
         for slot in range(slots):
             shifted[slot, :, last] = jnp.zeros((rows, LANE_TILE), jnp.bfloat16)
-    sums, copies = [None] * (vols * coils), []
-    for slot, pick in enumerate(picks):
+    cosines, sines = phase_columns(shift_ref, offset_ref, angle, rows_of, length)
+    sums = [None] * (vols * coils)
+    for slot in range(slots):
         cosine = cosines[:rows, slot : slot + 1]
         sine = sines[:rows, slot : slot + 1]
         for vol in range(vols):
-            image_re = image_ref[vol, pick, 0].astype(jnp.float32)
-            image_im = image_ref[vol, pick, 1].astype(jnp.float32)
+            image_copies[slot, vol].wait()
+            image_re, image_im = planes(raw_image.at[vol, slot], 0)
             for coil in range(coils):
                 place = vol * coils + coil
                 base = place * 2 * length
-                map_re = map_ref[coil, pick, 0].astype(jnp.float32)
-                map_im = map_ref[coil, pick, 1].astype(jnp.float32)
+                if vol == 0:
+                    map_copies[slot, coil].wait()
+                map_re, map_im = planes(raw_map.at[coil, slot], 1 + coil % 2)
                 coil_re = (map_re * image_re - map_im * image_im).astype(jnp.bfloat16)
                 coil_im = (map_re * image_im + map_im * image_re).astype(jnp.bfloat16)
                 partly = dot(left_ref[0], coil_re) + dot(left_ref[1], coil_im)
                 part_re, part_im = partly[:rows], partly[rows:]
                 shift_re = part_re * cosine - part_im * sine
                 shift_im = part_re * sine + part_im * cosine
-                shifted[slot, :, base : base + length] = shift_re.astype(jnp.bfloat16)
-                shifted[slot, :, base + length : base + 2 * length] = shift_im.astype(
+                shifted[slot, :, base : base + length] = shift_re[:, :length].astype(jnp.bfloat16)
+                shifted[slot, :, base + length : base + 2 * length] = shift_im[:, :length].astype(
                     jnp.bfloat16
                 )
                 if slot > 0:
                     shift_re, shift_im = sums[place][0] + shift_re, sums[place][1] + shift_im
                 sums[place] = (shift_re, shift_im)
-        copy = pltpu.make_async_copy(shifted.at[slot], kept_ref.at[slot], copied.at[slot])
-        copy.start()
-        copies.append(copy)
     for place, (sum_re, sum_im) in enumerate(sums):
         mixed = dot(sum_re.astype(jnp.bfloat16), gram_ref[0]) + dot(
             sum_im.astype(jnp.bfloat16), gram_ref[1]
@@ -124,20 +163,21 @@
             mixed = jnp.where(place_ref[0] > 0, mixed, 0.0)
         total[:, place * 2 * length : (place + 1) * 2 * length] = mixed
 
-    @pl.when(order_ref[group] == lax.axis_index("slc"))
+    @pl.when(owner)
     def _():
+        for copy in owner_copies:
+            copy.wait()
         for vol in range(vols):
             for coil in range(coils):
                 place = vol * coils + coil
-                measured = dot(kspace_ref[vol, 0, coil, 0], adjoint_ref[0]) + dot(
-                    kspace_ref[vol, 0, coil, 1], adjoint_ref[1]
+                real, imaginary = planes(raw_kspace.at[vol, 0, coil], 0)
+                measured = dot(real[:, :length].astype(jnp.bfloat16), adjoint[0]) + dot(
+                    imaginary[:, :length].astype(jnp.bfloat16), adjoint[1]
                 )
                 total[:length, place * 2 * length : (place + 1) * 2 * length] -= measured
 
     for index, out_ref in enumerate(out_refs):
         out_ref[...] = total[index * part : (index + 1) * part, :].astype(jnp.bfloat16)
-    for copy in copies:
-        copy.wait()
 
 
 def gradient_kernel(index, factor, on_line, *refs):
@@ -221,6 +261,7 @@
             latest = (outer_next(half),)
         if len(pieces) < min(count, step + LAG + 2):
             encode_next(*(latest or (half,)))
+            latest = (*latest, pieces[-1])
         if step >= LAG + 1:
             gradient_next(*latest)
             latest = (*latest, gradients[-1])
@@ -246,46 +287,42 @@
     on_line = whole_classes and groups == 4
     in_vmem = pl.BlockSpec(memory_space=pltpu.VMEM)
     in_smem = pl.BlockSpec(memory_space=pltpu.SMEM)
-
-    per_half = groups // HALVES
-
-    @functools.cache
-    def halves(half):
-        lead = lambda array: array.reshape(
-            array.shape[0], slots, groups, *array.shape[2:]
-        )[:, :, half * per_half : (half + 1) * per_half].reshape(
-            array.shape[0], slots * per_half, *array.shape[2:]
-        )
-        pair = (images, coil_maps)
-        if half > 0:
-            pair = lax.optimization_barrier((*pair, *held_back))[:2]
-        return tuple(lead(array) for array in pair)
-
-    held_back = []
+    in_place = pl.BlockSpec(memory_space=pl.ANY)
+
+    def as_it_lies(array):
+        view = jnp.swapaxes(array, -3, -2)
+        return pltpu.with_memory_space_constraint(view, pltpu.HBM)
+
+    padded = round_up(length, LANE_TILE)
+    left, gram, adjoint = tables
+    sources = [as_it_lies(array) for array in (images, coil_maps, kspace)]
+    adjoint = pltpu.with_memory_space_constraint(jnp.asarray(adjoint), pltpu.HBM)
 
     def encode(group, *earlier):
         if whole_classes:
             place = np.zeros((2,), np.int32)
-            image, coil_map = halves(group // per_half)
-            picks = [slot * per_half + group % per_half for slot in range(slots)]
         else:
             within = group - first
             held = (within >= 0) & (within < per_device)
             within = jnp.where(held, within, 0)
             place = jnp.stack([held, within]).astype(jnp.int32)
-            image, coil_map, picks = images, coil_maps, None
         offset = after(phase_offset, *earlier) if earlier else phase_offset
-        outputs = pl.pallas_call(
-            functools.partial(encode_kernel, slots, group, picks),
-            in_specs=[in_smem] * 3 + [in_vmem] * 7,
-            out_specs=[pl.BlockSpec(memory_space=pltpu.HBM)] + [in_vmem] * ROW_PARTS,
+        return pl.pallas_call(
+            functools.partial(encode_kernel, slots, group, whole_classes),
+            in_specs=[in_smem] * 3 + [in_place] * 3 + [in_vmem] * 3 + [in_place],
+            out_specs=[in_vmem] * (1 + ROW_PARTS),
             out_shape=[jax.ShapeDtypeStruct((slots, rows, lanes), jnp.bfloat16)]
             + [jax.ShapeDtypeStruct((part, lanes), jnp.bfloat16)] * ROW_PARTS,
             scratch_shapes=[
                 pltpu.VMEM((rows, lanes), jnp.float32),
                 pltpu.VMEM((round_up(slots, 8), round_up(rows, LANE_TILE)), jnp.float32),
-                pltpu.VMEM((slots, rows, lanes), jnp.bfloat16),
-                pltpu.SemaphoreType.DMA((slots,)),
+                pltpu.VMEM((3, padded // LANE_TILE, 2 * length, LANE_TILE), jnp.float32),
+                pltpu.VMEM((vols, slots, length, 2, length), jnp.bfloat16),
+                pltpu.VMEM((coils, slots, length, 2, length), jnp.bfloat16),
+                pltpu.VMEM((vols, 1, coils, length, 2, length), jnp.bfloat16),
+                pltpu.VMEM((2, length, 2 * length), jnp.bfloat16),
+                pltpu.SemaphoreType.DMA((slots, vols + coils)),
+                pltpu.SemaphoreType.DMA((2,)),
             ],
             compiler_params=pltpu.CompilerParams(vmem_limit_bytes=VMEM_BYTES),
             cost_estimate=pl.CostEstimate(
@@ -294,18 +331,7 @@
                 transcendentals=0,
             ),
             name="encode",
-        )(
-            shift_index,
-            group_order,
-            place,
-            image,
-            coil_map,
-            kspace,
-            offset,
-            *tables,
-        )
-        held_back.append(outputs[1])
-        return outputs
+        )(shift_index, group_order, place, *sources, offset, left, gram, adjoint)
 
     def gradient(step, terms, encoded):
         return pl.pallas_call(

time: 91.1 us -> 86.1 us (0.945)
  local copies, waits for them, and re-layouts: 14.2 us -> 4.11 us
  Pallas kernels: 18.9 us -> 25.1 us
  other arithmetic: 7.23 us -> 5.2 us
  waiting for transfers between devices: 7.62 us -> 8.87 us
    pallas_call x4, Pallas kernels: 13.8 us -> 20.2 us  [encode(): pl.pallas_call(functools.partial(encode_kernel, slots, group, whole_class...]
    unnamed x45 -> x24, local copies, waits for them, and re-layouts: 9.18 us -> 4.09 us
    slice x4 -> x0, local copies, waits for them, and re-layouts: 5.04 us -> none  [halves(): array.reshape(array.shape[0], slots, groups, *array.shape[2:])]
    select_n x5, other arithmetic: 3.03 us -> 1.16 us  [outer_next(): payload = others if payload is None else jnp.where(edge, payload, others)]
  transfers between devices with their start and end apart: 22 -> 22, of which waited for: 7 -> 7; matrix products, arithmetic and copies ran while one was open for 10% -> 5% of each run, Pallas kernels for 16% -> 23%
where the time goes in v8:
time: 86.1 us; the launch traced here: 85.4 us
  starting transfers between devices  41.8 us (49%)
  Pallas kernels  25.1 us (29%)
  waiting for transfers between devices  8.87 us (10%)
  other arithmetic  5.2 us (6%)
  local copies, waits for them, and re-layouts  4.11 us (5%)
    ppermute x11, starting transfers between devices, outer_next(): outer.append(lax.ppermute(payload, 'slc', outer_pairs))  31.6 us
    pallas_call x4, Pallas kernels, encode(): pl.pallas_call(functools.partial(encode_kernel, slots, group, whole_class...  20.2 us
    ppermute x8, starting transfers between devices, line_of_four(): inner.append(lax.ppermute(half, 'slc', inner_pairs))  8.3 us
    ppermute x11, waiting for transfers between devices, outer_next(): outer.append(lax.ppermute(payload, 'slc', outer_pairs))  6.08 us
    pallas_call x8, Pallas kernels, gradient(): pl.pallas_call(functools.partial(gradient_kernel, step % ROW_PARTS, facto...  4.9 us
    unnamed x24, local copies, waits for them, and re-layouts  4.09 us
    add x8, other arithmetic, line_of_four(): half = pieces[step] + after(outer[step], *latest)  2.98 us
    ppermute x3, waiting for transfers between devices, sum_over_replicas(): lax.ppermute(value, axes, [(index, index ^ mask) for index in range(4)])  2.76 us
  transfers between devices with their start and end apart: 22, of which 7 were waited for; matrix products, arithmetic and copies ran while one was open for 5% of the time, Pallas kernels for 23%

profile of v8, /device:TPU:0, one launch (start us, length us, event | category | flops | bytes accessed | tf_op | source)
XLA Modules:
  0.0 85.4 jit_solution(18040748329001430572)
XLA Ops:
  0.0 1.0 %copy-done = bf16[2,256,440]{2,1,0:T(8,128)(2,1)S(1)} copy-done((bf16[2,256,440]{2,1,0:T(8,128)(2,1)S(1)}, bf16[2,256,440]{2,1,0:T(8,128)(2,1)}, u32[]{:S(2)}) %copy-start) | copy-done | bytes 450584
  1.0 1.0 %copy-done.2 = bf16[2,448,220]{2,1,0:T(8,128)(2,1)S(1)} copy-done((bf16[2,448,220]{2,1,0:T(8,128)(2,1)S(1)}, bf16[2,448,220]{2,1,0:T(8,128)(2,1)}, u32[]{:S(2)}) %copy-start.2) | copy-done | bytes 394264
  4.1 4.9 %encode.4 = (bf16[2,224,896]{2,1,0:T(8,128)(2,1)S(1)}, bf16[112,896]{1,0:T(8,128)(2,1)S(1)}, bf16[112,896]{1,0:T(8,128)(2,1)S(1)}) custom-call(s32[8]{0:T(128)S(1)} %copy-done.8, s32[4]{0:T(128)S(1)} %copy-done.10, s32[2]{0:T(128)S(1)} %call_exported.0.refs_2_, bf16[1,8,220,2,220]{4,3,2,1,0:T(2,128)(2,1)} %bitcast.15, bf16[2,8,220,2,220]{4,3,2,1,0:T(2,128)(2,1)} %bitcast.11, ...), custom_call_target="tpu_custom_call" | custom-call | flops 1022208000 | bytes 6000000 | tf_op jit(solution)/shard_map/encode/pallas_call | solution.py:310
  9.0 3.1 %collective-permute-start = (bf16[112,896]{1,0:T(8,128)(2,1)S(1)}, bf16[112,896]{1,0:T(8,128)(2,1)S(1)}, u32[]{:S(2)}, u32[]{:S(2)}) collective-permute-start(bf16[112,896]{1,0:T(8,128)(2,1)S(1)} %get-tuple-element.62.refs_0_), channel_id=1, source_target_pairs={{0,4},{4,0},{8,12},{12,8},{1,5},{5,1},{9,13},{13,9},{2,6},{6,2},{1... | collective-permute-start | bytes 602120 | tf_op jit(solution)/shard_map/ppermute | solution.py:242
  12.2 4.9 %encode.5 = (bf16[2,224,896]{2,1,0:T(8,128)(2,1)S(1)}, bf16[112,896]{1,0:T(8,128)(2,1)S(1)}, bf16[112,896]{1,0:T(8,128)(2,1)S(1)}) custom-call(s32[8]{0:T(128)S(1)} %copy-done.8, s32[4]{0:T(128)S(1)} %copy-done.10, s32[2]{0:T(128)S(1)} %call_exported.0.refs_2_, bf16[1,8,220,2,220]{4,3,2,1,0:T(2,128)(2,1)} %bitcast.16, bf16[2,8,220,2,220]{4,3,2,1,0:T(2,128)(2,1)} %bitcast.12, ...), custom_call_target="tpu_custom_call" | custom-call | flops 1022208000 | bytes 6000000 | tf_op jit(solution)/shard_map/encode/pallas_call | solution.py:310
  18.6 3.4 %collective-permute-start.4 = (bf16[112,896]{1,0:T(8,128)(2,1)}, bf16[112,896]{1,0:T(8,128)(2,1)}, u32[]{:S(2)}, u32[]{:S(2)}) collective-permute-start(bf16[112,896]{1,0:T(8,128)(2,1)} %add.57), channel_id=1, source_target_pairs={{0,0},{4,8},{8,4},{12,12},{1,1},{5,9},{9,5},{13,13},{2,2},{6,10},{... | collective-permute-start | bytes 602120 | tf_op jit(solution)/shard_map/ppermute | solution.py:258
  22.0 2.9 %collective-permute-start.3 = (bf16[112,896]{1,0:T(8,128)(2,1)S(1)}, bf16[112,896]{1,0:T(8,128)(2,1)}, u32[]{:S(2)}, u32[]{:S(2)}) collective-permute-start(bf16[112,896]{1,0:T(8,128)(2,1)S(1)} %get-tuple-element.69.refs_0_), channel_id=1, source_target_pairs={{0,4},{4,0},{8,12},{12,8},{1,5},{5,1},{9,13},{13,9},{2,6},{6,2},{1... | collective-permute-start | bytes 602120 | tf_op jit(solution)/shard_map/ppermute | solution.py:242
  25.0 4.9 %encode.6 = (bf16[2,224,896]{2,1,0:T(8,128)(2,1)S(1)}, bf16[112,896]{1,0:T(8,128)(2,1)S(1)}, bf16[112,896]{1,0:T(8,128)(2,1)S(1)}) custom-call(s32[8]{0:T(128)S(1)} %copy-done.9, s32[4]{0:T(128)S(1)} %copy-done.11, s32[2]{0:T(128)S(1)} %call_exported.0.refs_2_, bf16[1,8,220,2,220]{4,3,2,1,0:T(2,128)(2,1)} %bitcast.17, bf16[2,8,220,2,220]{4,3,2,1,0:T(2,128)(2,1)} %bitcast.13, ...), custom_call_target="tpu_custom_call" | custom-call | flops 1022208000 | bytes 6000000 | tf_op jit(solution)/shard_map/encode/pallas_call | solution.py:310
  32.5 3.6 %collective-permute-start.5 = (bf16[112,896]{1,0:T(8,128)(2,1)S(1)}, bf16[112,896]{1,0:T(8,128)(2,1)S(1)}, u32[]{:S(2)}, u32[]{:S(2)}) collective-permute-start(bf16[112,896]{1,0:T(8,128)(2,1)S(1)} %add_select_fusion.3), channel_id=1, source_target_pairs={{0,4},{4,0},{8,12},{12,8},{1,5},{5,1},{9,13},{13,9},{2,6},{6,2},{1... | collective-permute-start | bytes 602120 | tf_op jit(solution)/shard_map/ppermute | solution.py:242
  36.1 1.0 %add.61 = bf16[112,896]{1,0:T(8,128)(2,1)S(1)} add(bf16[112,896]{1,0:T(8,128)(2,1)S(1)} %get-tuple-element.69.refs_0_, bf16[112,896]{1,0:T(8,128)(2,1)} %collective-permute-done.3.refs_1_) | non-fusion elementwise | flops 100352 | bytes 602112 | tf_op jit(solution)/shard_map/add | solution.py:257
  38.0 1.3 %collective-permute-start.7 = (bf16[112,896]{1,0:T(8,128)(2,1)S(1)}, bf16[112,896]{1,0:T(8,128)(2,1)S(1)}, u32[]{:S(2)}, u32[]{:S(2)}) collective-permute-start(bf16[112,896]{1,0:T(8,128)(2,1)S(1)} %add_select_fusion.4), channel_id=1, source_target_pairs={{0,4},{4,0},{8,12},{12,8},{1,5},{5,1},{9,13},{13,9},{2,6},{6,2},{1... | collective-permute-start | bytes 602120 | tf_op jit(solution)/shard_map/ppermute | solution.py:242
  39.4 5.6 %encode.7 = (bf16[2,224,896]{2,1,0:T(8,128)(2,1)S(1)}, bf16[112,896]{1,0:T(8,128)(2,1)S(1)}, bf16[112,896]{1,0:T(8,128)(2,1)S(1)}) custom-call(s32[8]{0:T(128)S(1)} %copy-done.9, s32[4]{0:T(128)S(1)} %copy-done.11, s32[2]{0:T(128)S(1)} %call_exported.0.refs_2_, bf16[1,8,220,2,220]{4,3,2,1,0:T(2,128)(2,1)} %bitcast.18, bf16[2,8,220,2,220]{4,3,2,1,0:T(2,128)(2,1)} %bitcast.14, ...), custom_call_target="tpu_custom_call" | custom-call | flops 1022208000 | bytes 6000000 | tf_op jit(solution)/shard_map/encode/pallas_call | solution.py:310
  45.7 3.0 %collective-permute-start.10 = (bf16[112,896]{1,0:T(8,128)(2,1)S(1)}, bf16[112,896]{1,0:T(8,128)(2,1)S(1)}, u32[]{:S(2)}, u32[]{:S(2)}) collective-permute-start(bf16[112,896]{1,0:T(8,128)(2,1)S(1)} %add_select_fusion.1), channel_id=1, source_target_pairs={{0,4},{4,0},{8,12},{12,8},{1,5},{5,1},{9,13},{13,9},{2,6},{6,2},{1... | collective-permute-start | bytes 602120 | tf_op jit(solution)/shard_map/ppermute | solution.py:242
  49.6 5.1 %collective-permute-start.12 = (bf16[112,896]{1,0:T(8,128)(2,1)S(1)}, bf16[112,896]{1,0:T(8,128)(2,1)S(1)}, u32[]{:S(2)}, u32[]{:S(2)}) collective-permute-start(bf16[112,896]{1,0:T(8,128)(2,1)S(1)} %add_select_fusion.2), channel_id=1, source_target_pairs={{0,4},{4,0},{8,12},{12,8},{1,5},{5,1},{9,13},{13,9},{2,6},{6,2},{1... | collective-permute-start | bytes 602120 | tf_op jit(solution)/shard_map/ppermute | solution.py:242
  54.7 1.2 %gradient.8 = f32[2,112]{1,0:T(2,128)S(1)} custom-call(bf16[112,896]{1,0:T(8,128)(2,1)S(1)} %get-tuple-element.62.refs_0_, bf16[112,896]{1,0:T(8,128)(2,1)S(1)} %copy-done.5, bf16[112,896]{1,0:T(8,128)(2,1)} %collective-permute-done.4.refs_2_, bf16[112,896]{1,0:T(8,128)(2,1)S(1)} %collective-permute-done.5.refs_3_.refs_1_, ...), custom_call_target="tpu_custom_call" | custom-call | flops 774400 | bytes 1500000 | tf_op jit(solution)/shard_map/gradient/pallas_call | solution.py:337
  56.7 2.1 %collective-permute-start.14 = (bf16[112,896]{1,0:T(8,128)(2,1)S(1)}, bf16[112,896]{1,0:T(8,128)(2,1)S(1)}, u32[]{:S(2)}, u32[]{:S(2)}) collective-permute-start(bf16[112,896]{1,0:T(8,128)(2,1)S(1)} %add_select_fusion), channel_id=1, source_target_pairs={{0,4},{4,0},{8,12},{12,8},{1,5},{5,1},{9,13},{13,9},{2,6},{6,2},{1... | collective-permute-start | bytes 602120 | tf_op jit(solution)/shard_map/ppermute | solution.py:242
  58.7 1.2 %gradient.9 = f32[2,112]{1,0:T(2,128)S(1)} custom-call(bf16[112,896]{1,0:T(8,128)(2,1)S(1)} %get-tuple-element.66.refs_0_, bf16[112,896]{1,0:T(8,128)(2,1)} %collective-permute-done.1.refs_1_, bf16[112,896]{1,0:T(8,128)(2,1)S(1)} %collective-permute-done.2.refs_2_, bf16[112,896]{1,0:T(8,128)(2,1)S(1)} %collective-permute-done.7.refs_3_.refs_1_, ...), custom_call_target="tpu_custom_call" | custom-call | flops 774400 | bytes 1500000 | tf_op jit(solution)/shard_map/gradient/pallas_call | solution.py:337
  60.8 1.2 %gradient.10 = f32[2,112]{1,0:T(2,128)S(1)} custom-call(bf16[112,896]{1,0:T(8,128)(2,1)S(1)} %get-tuple-element.69.refs_0_, bf16[112,896]{1,0:T(8,128)(2,1)} %collective-permute-done.3.refs_1_, bf16[112,896]{1,0:T(8,128)(2,1)S(1)} %collective-permute-done.8.refs_2_, bf16[112,896]{1,0:T(8,128)(2,1)S(1)} %collective-permute-done.10.refs_3_.refs_1_, ...), custom_call_target="tpu_custom_call" | custom-call | flops 774400 | bytes 1500000 | tf_op jit(solution)/shard_map/gradient/pallas_call | solution.py:337
  63.2 6.5 %collective-permute-start.16 = (bf16[112,896]{1,0:T(8,128)(2,1)S(1)}, bf16[112,896]{1,0:T(8,128)(2,1)S(1)}, u32[]{:S(2)}, u32[]{:S(2)}) collective-permute-start(bf16[112,896]{1,0:T(8,128)(2,1)S(1)} %add.68), channel_id=1, source_target_pairs={{0,4},{4,0},{8,12},{12,8},{1,5},{5,1},{9,13},{13,9},{2,6},{6,2},{1... | collective-permute-start | bytes 602120 | tf_op jit(solution)/shard_map/ppermute | solution.py:242
  70.2 3.7 %collective-permute-start.17 = (bf16[112,896]{1,0:T(8,128)(2,1)S(1)}, bf16[112,896]{1,0:T(8,128)(2,1)S(1)}, u32[]{:S(2)}, u32[]{:S(2)}) collective-permute-start(bf16[112,896]{1,0:T(8,128)(2,1)S(1)} %add.70), channel_id=1, source_target_pairs={{0,4},{4,0},{8,12},{12,8},{1,5},{5,1},{9,13},{13,9},{2,6},{6,2},{1... | collective-permute-start | bytes 602120 | tf_op jit(solution)/shard_map/ppermute | solution.py:242
  75.4 2.2 %collective-permute-done.17.refs_3_ = bf16[112,896]{1,0:T(8,128)(2,1)S(1)} collective-permute-done((bf16[112,896]{1,0:T(8,128)(2,1)S(1)}, bf16[112,896]{1,0:T(8,128)(2,1)S(1)}, u32[]{:S(2)}, u32[]{:S(2)}) %collective-permute-start.17) | collective-permute-done | bytes 200736 | tf_op jit(solution)/shard_map/ppermute | solution.py:242
  77.9 1.9 %collective-permute-done.18.refs_3_ = bf16[112,896]{1,0:T(8,128)(2,1)S(1)} collective-permute-done((bf16[112,896]{1,0:T(8,128)(2,1)S(1)}, bf16[112,896]{1,0:T(8,128)(2,1)S(1)}, u32[]{:S(2)}, u32[]{:S(2)}) %collective-permute-start.18) | collective-permute-done | bytes 200736 | tf_op jit(solution)/shard_map/ppermute | solution.py:242
  80.2 1.5 %collective-permute-start.20 = (f32[8,220]{1,0:T(8,128)S(1)}, f32[8,220]{1,0:T(8,128)S(1)}, u32[]{:S(2)}, u32[]{:S(2)}) collective-permute-start(f32[8,220]{1,0:T(8,128)S(1)} %reshape.3), channel_id=1, source_target_pairs={{0,2},{1,3},{2,0},{3,1},{4,6},{5,7},{6,4},{7,5},{8,10},{9,11},{10,... | collective-permute-start | bytes 21128 | tf_op jit(solution)/shard_map/ppermute | solution.py:212
  82.1 1.9 %collective-permute-done.20 = f32[8,220]{1,0:T(8,128)S(1)} collective-permute-done((f32[8,220]{1,0:T(8,128)S(1)}, f32[8,220]{1,0:T(8,128)S(1)}, u32[]{:S(2)}, u32[]{:S(2)}) %collective-permute-start.20) | collective-permute-done | bytes 7072 | tf_op jit(solution)/shard_map/ppermute | solution.py:212
  (81 shorter events, 16.0 us)
Async XLA Ops:
  9.0 8.9 %collective-permute-start = (bf16[112,896]{1,0:T(8,128)(2,1)S(1)}, bf16[112,896]{1,0:T(8,128)(2,1)S(1)}, u32[]{:S(2)}, u32[]{:S(2)}) collective-permute-start(bf16[112,896]{1,0:T(8,128)(2,1)S(1)} %get-tuple-element.62.refs_0_), channel_id=1, source_target_pairs={{0,4},{4,0},{8,12},{12,8},{1,5},{5,1},{9,13},{13,9},{2,6},{6,2},{1... | collective-permute-start | bytes 602120 | tf_op jit(solution)/shard_map/ppermute | solution.py:242
  12.1 12.9 %copy-start.11 = (s32[4]{0:T(128)S(1)}, s32[4]{0:T(128)}, u32[]{:S(2)}) copy-start(s32[4]{0:T(128)} %refs_1_.7) | copy-start | bytes 52
  12.1 17.8 %collective-permute-start.1 = (bf16[112,896]{1,0:T(8,128)(2,1)S(1)}, bf16[112,896]{1,0:T(8,128)(2,1)}, u32[]{:S(2)}, u32[]{:S(2)}) collective-permute-start(bf16[112,896]{1,0:T(8,128)(2,1)S(1)} %get-tuple-element.66.refs_0_), channel_id=1, source_target_pairs={{0,4},{4,0},{8,12},{12,8},{1,5},{5,1},{9,13},{13,9},{2,6},{6,2},{1... | collective-permute-start | bytes 602120 | tf_op jit(solution)/shard_map/ppermute | solution.py:242
  18.6 12.9 %collective-permute-start.4 = (bf16[112,896]{1,0:T(8,128)(2,1)}, bf16[112,896]{1,0:T(8,128)(2,1)}, u32[]{:S(2)}, u32[]{:S(2)}) collective-permute-start(bf16[112,896]{1,0:T(8,128)(2,1)} %add.57), channel_id=1, source_target_pairs={{0,0},{4,8},{8,4},{12,12},{1,1},{5,9},{9,5},{13,13},{2,2},{6,10},{... | collective-permute-start | bytes 602120 | tf_op jit(solution)/shard_map/ppermute | solution.py:258
  22.0 14.1 %collective-permute-start.3 = (bf16[112,896]{1,0:T(8,128)(2,1)S(1)}, bf16[112,896]{1,0:T(8,128)(2,1)}, u32[]{:S(2)}, u32[]{:S(2)}) collective-permute-start(bf16[112,896]{1,0:T(8,128)(2,1)S(1)} %get-tuple-element.69.refs_0_), channel_id=1, source_target_pairs={{0,4},{4,0},{8,12},{12,8},{1,5},{5,1},{9,13},{13,9},{2,6},{6,2},{1... | collective-permute-start | bytes 602120 | tf_op jit(solution)/shard_map/ppermute | solution.py:242
  30.8 7.1 %collective-permute-start.2 = (bf16[112,896]{1,0:T(8,128)(2,1)S(1)}, bf16[112,896]{1,0:T(8,128)(2,1)S(1)}, u32[]{:S(2)}, u32[]{:S(2)}) collective-permute-start(bf16[112,896]{1,0:T(8,128)(2,1)S(1)} %add.58), channel_id=1, source_target_pairs={{0,0},{4,8},{8,4},{12,12},{1,1},{5,9},{9,5},{13,13},{2,2},{6,10},{... | collective-permute-start | bytes 602120 | tf_op jit(solution)/shard_map/ppermute | solution.py:258
  32.5 12.4 %collective-permute-start.5 = (bf16[112,896]{1,0:T(8,128)(2,1)S(1)}, bf16[112,896]{1,0:T(8,128)(2,1)S(1)}, u32[]{:S(2)}, u32[]{:S(2)}) collective-permute-start(bf16[112,896]{1,0:T(8,128)(2,1)S(1)} %add_select_fusion.3), channel_id=1, source_target_pairs={{0,4},{4,0},{8,12},{12,8},{1,5},{5,1},{9,13},{13,9},{2,6},{6,2},{1... | collective-permute-start | bytes 602120 | tf_op jit(solution)/shard_map/ppermute | solution.py:242
  37.1 8.6 %collective-permute-start.8 = (bf16[112,896]{1,0:T(8,128)(2,1)S(1)}, bf16[112,896]{1,0:T(8,128)(2,1)S(1)}, u32[]{:S(2)}, u32[]{:S(2)}) collective-permute-start(bf16[112,896]{1,0:T(8,128)(2,1)S(1)} %add.61), channel_id=1, source_target_pairs={{0,0},{4,8},{8,4},{12,12},{1,1},{5,9},{9,5},{13,13},{2,2},{6,10},{... | collective-permute-start | bytes 602120 | tf_op jit(solution)/shard_map/ppermute | solution.py:258
  38.0 16.6 %copy-start.5 = (bf16[112,896]{1,0:T(8,128)(2,1)S(1)}, bf16[112,896]{1,0:T(8,128)(2,1)}, u32[]{:S(2)}) copy-start(bf16[112,896]{1,0:T(8,128)(2,1)} %copy-done.4) | copy-start | bytes 602116
  38.0 10.7 %collective-permute-start.7 = (bf16[112,896]{1,0:T(8,128)(2,1)S(1)}, bf16[112,896]{1,0:T(8,128)(2,1)S(1)}, u32[]{:S(2)}, u32[]{:S(2)}) collective-permute-start(bf16[112,896]{1,0:T(8,128)(2,1)S(1)} %add_select_fusion.4), channel_id=1, source_target_pairs={{0,4},{4,0},{8,12},{12,8},{1,5},{5,1},{9,13},{13,9},{2,6},{6,2},{1... | collective-permute-start | bytes 602120 | tf_op jit(solution)/shard_map/ppermute | solution.py:242
  45.0 4.5 %collective-permute-start.6 = (bf16[112,896]{1,0:T(8,128)(2,1)S(1)}, bf16[112,896]{1,0:T(8,128)(2,1)S(1)}, u32[]{:S(2)}, u32[]{:S(2)}) collective-permute-start(bf16[112,896]{1,0:T(8,128)(2,1)S(1)} %add.62), channel_id=1, source_target_pairs={{0,0},{4,8},{8,4},{12,12},{1,1},{5,9},{9,5},{13,13},{2,2},{6,10},{... | collective-permute-start | bytes 602120 | tf_op jit(solution)/shard_map/ppermute | solution.py:258
  45.7 10.1 %collective-permute-start.10 = (bf16[112,896]{1,0:T(8,128)(2,1)S(1)}, bf16[112,896]{1,0:T(8,128)(2,1)S(1)}, u32[]{:S(2)}, u32[]{:S(2)}) collective-permute-start(bf16[112,896]{1,0:T(8,128)(2,1)S(1)} %add_select_fusion.1), channel_id=1, source_target_pairs={{0,4},{4,0},{8,12},{12,8},{1,5},{5,1},{9,13},{13,9},{2,6},{6,2},{1... | collective-permute-start | bytes 602120 | tf_op jit(solution)/shard_map/ppermute | solution.py:242
  48.8 7.8 %collective-permute-start.9 = (bf16[112,896]{1,0:T(8,128)(2,1)S(1)}, bf16[112,896]{1,0:T(8,128)(2,1)S(1)}, u32[]{:S(2)}, u32[]{:S(2)}) collective-permute-start(bf16[112,896]{1,0:T(8,128)(2,1)S(1)} %add.65), channel_id=1, source_target_pairs={{0,0},{4,8},{8,4},{12,12},{1,1},{5,9},{9,5},{13,13},{2,2},{6,10},{... | collective-permute-start | bytes 602120 | tf_op jit(solution)/shard_map/ppermute | solution.py:258
  49.6 10.4 %collective-permute-start.12 = (bf16[112,896]{1,0:T(8,128)(2,1)S(1)}, bf16[112,896]{1,0:T(8,128)(2,1)S(1)}, u32[]{:S(2)}, u32[]{:S(2)}) collective-permute-start(bf16[112,896]{1,0:T(8,128)(2,1)S(1)} %add_select_fusion.2), channel_id=1, source_target_pairs={{0,4},{4,0},{8,12},{12,8},{1,5},{5,1},{9,13},{13,9},{2,6},{6,2},{1... | collective-permute-start | bytes 602120 | tf_op jit(solution)/shard_map/ppermute | solution.py:242
  55.9 4.8 %collective-permute-start.11 = (bf16[112,896]{1,0:T(8,128)(2,1)S(1)}, bf16[112,896]{1,0:T(8,128)(2,1)S(1)}, u32[]{:S(2)}, u32[]{:S(2)}) collective-permute-start(bf16[112,896]{1,0:T(8,128)(2,1)S(1)} %add.67), channel_id=1, source_target_pairs={{0,0},{4,8},{8,4},{12,12},{1,1},{5,9},{9,5},{13,13},{2,2},{6,10},{... | collective-permute-start | bytes 602120 | tf_op jit(solution)/shard_map/ppermute | solution.py:258
  56.7 5.8 %collective-permute-start.14 = (bf16[112,896]{1,0:T(8,128)(2,1)S(1)}, bf16[112,896]{1,0:T(8,128)(2,1)S(1)}, u32[]{:S(2)}, u32[]{:S(2)}) collective-permute-start(bf16[112,896]{1,0:T(8,128)(2,1)S(1)} %add_select_fusion), channel_id=1, source_target_pairs={{0,4},{4,0},{8,12},{12,8},{1,5},{5,1},{9,13},{13,9},{2,6},{6,2},{1... | collective-permute-start | bytes 602120 | tf_op jit(solution)/shard_map/ppermute | solution.py:242
  60.0 9.8 %collective-permute-start.13 = (bf16[112,896]{1,0:T(8,128)(2,1)S(1)}, bf16[112,896]{1,0:T(8,128)(2,1)S(1)}, u32[]{:S(2)}, u32[]{:S(2)}) collective-permute-start(bf16[112,896]{1,0:T(8,128)(2,1)S(1)} %add.69), channel_id=1, source_target_pairs={{0,0},{4,8},{8,4},{12,12},{1,1},{5,9},{9,5},{13,13},{2,2},{6,10},{... | collective-permute-start | bytes 602120 | tf_op jit(solution)/shard_map/ppermute | solution.py:258
  62.5 7.3 %collective-permute-start.15 = (bf16[112,896]{1,0:T(8,128)(2,1)S(1)}, bf16[112,896]{1,0:T(8,128)(2,1)S(1)}, u32[]{:S(2)}, u32[]{:S(2)}) collective-permute-start(bf16[112,896]{1,0:T(8,128)(2,1)S(1)} %add.71), channel_id=1, source_target_pairs={{0,0},{4,8},{8,4},{12,12},{1,1},{5,9},{9,5},{13,13},{2,2},{6,10},{... | collective-permute-start | bytes 602120 | tf_op jit(solution)/shard_map/ppermute | solution.py:258
  63.2 11.8 %collective-permute-start.16 = (bf16[112,896]{1,0:T(8,128)(2,1)S(1)}, bf16[112,896]{1,0:T(8,128)(2,1)S(1)}, u32[]{:S(2)}, u32[]{:S(2)}) collective-permute-start(bf16[112,896]{1,0:T(8,128)(2,1)S(1)} %add.68), channel_id=1, source_target_pairs={{0,4},{4,0},{8,12},{12,8},{1,5},{5,1},{9,13},{13,9},{2,6},{6,2},{1... | collective-permute-start | bytes 602120 | tf_op jit(solution)/shard_map/ppermute | solution.py:242
  70.2 7.4 %collective-permute-start.17 = (bf16[112,896]{1,0:T(8,128)(2,1)S(1)}, bf16[112,896]{1,0:T(8,128)(2,1)S(1)}, u32[]{:S(2)}, u32[]{:S(2)}) collective-permute-start(bf16[112,896]{1,0:T(8,128)(2,1)S(1)} %add.70), channel_id=1, source_target_pairs={{0,4},{4,0},{8,12},{12,8},{1,5},{5,1},{9,13},{13,9},{2,6},{6,2},{1... | collective-permute-start | bytes 602120 | tf_op jit(solution)/shard_map/ppermute | solution.py:242
  73.9 5.8 %collective-permute-start.18 = (bf16[112,896]{1,0:T(8,128)(2,1)S(1)}, bf16[112,896]{1,0:T(8,128)(2,1)S(1)}, u32[]{:S(2)}, u32[]{:S(2)}) collective-permute-start(bf16[112,896]{1,0:T(8,128)(2,1)S(1)} %add.72), channel_id=1, source_target_pairs={{0,4},{4,0},{8,12},{12,8},{1,5},{5,1},{9,13},{13,9},{2,6},{6,2},{1... | collective-permute-start | bytes 602120 | tf_op jit(solution)/shard_map/ppermute | solution.py:242
  80.1 1.9 %collective-permute-start.19 = (f32[8,220]{1,0:T(8,128)S(1)}, f32[8,220]{1,0:T(8,128)S(1)}, u32[]{:S(2)}, u32[]{:S(2)}) collective-permute-start(f32[8,220]{1,0:T(8,128)S(1)} %reshape.3), channel_id=1, source_target_pairs={{0,1},{1,0},{2,3},{3,2},{4,5},{5,4},{6,7},{7,6},{8,9},{9,8},{10,11... | collective-permute-start | bytes 21128 | tf_op jit(solution)/shard_map/ppermute | solution.py:212
  80.2 3.7 %collective-permute-start.20 = (f32[8,220]{1,0:T(8,128)S(1)}, f32[8,220]{1,0:T(8,128)S(1)}, u32[]{:S(2)}, u32[]{:S(2)}) collective-permute-start(f32[8,220]{1,0:T(8,128)S(1)} %reshape.3), channel_id=1, source_target_pairs={{0,2},{1,3},{2,0},{3,1},{4,6},{5,7},{6,4},{7,5},{8,10},{9,11},{10,... | collective-permute-start | bytes 21128 | tf_op jit(solution)/shard_map/ppermute | solution.py:212
  81.7 3.1 %collective-permute-start.21 = (f32[8,220]{1,0:T(8,128)S(1)}, f32[8,220]{1,0:T(8,128)S(1)}, u32[]{:S(2)}, u32[]{:S(2)}) collective-permute-start(f32[8,220]{1,0:T(8,128)S(1)} %reshape.3), channel_id=1, source_target_pairs={{0,3},{1,2},{2,1},{3,0},{4,7},{5,6},{6,5},{7,4},{8,11},{9,10},{10,... | collective-permute-start | bytes 21128 | tf_op jit(solution)/shard_map/ppermute | solution.py:212
  (10 other events, 59.8 us)

commit v9 on v7

--- a/solution.py
+++ b/solution.py
@@ -15,7 +15,6 @@
 LANE_TILE = 128
 ROW_PARTS = 2
 LAG = 3
-HALVES = 2
 VMEM_BYTES = 24 * 1024 * 1024
 
 
@@ -37,8 +36,8 @@
 def dft_matrices(length, rows):
     cos_table, sin_table = fourier_tables(length)
     cosine, sine = cos_table.astype(np.float64), sin_table.astype(np.float64)
-    left_re = np.zeros((2 * rows, length), np.float64)
-    left_im = np.zeros((2 * rows, length), np.float64)
+    left_re = np.zeros((2 * rows + 8, length), np.float64)
+    left_im = np.zeros((2 * rows + 8, length), np.float64)
     left_re[:length], left_re[rows : rows + length] = cosine, sine
     left_im[:length], left_im[rows : rows + length] = -sine, cosine
     gram_re = cosine.T @ cosine + sine.T @ sine
@@ -57,52 +56,110 @@
     return jnp.dot(left, right, preferred_element_type=jnp.float32)
 
 
-def phase_columns(shift_ref, offset_ref, angle, rows_of, length):
+def start_all(copies):
+    for copy in copies:
+        copy.start()
+
+
+def slice_copies(image_ref, map_ref, image_out, map_out, arrived, rows_of):
+    vols, coils = image_ref.shape[0], map_ref.shape[0]
+    return [
+        pltpu.make_async_copy(
+            image_ref.at[vol, row], image_out.at[vol, slot], arrived.at[slot, vol]
+        )
+        for slot, row in enumerate(rows_of)
+        for vol in range(vols)
+    ] + [
+        pltpu.make_async_copy(
+            map_ref.at[coil, row], map_out.at[coil, slot], arrived.at[slot, vols + coil]
+        )
+        for slot, row in enumerate(rows_of)
+        for coil in range(coils)
+    ]
+
+
+def fetch_kernel(rows_of, *refs):
+    if rows_of is None:
+        rows_of, refs = [refs[0][1]], refs[1:]
+    shift_ref, offset_ref, image_ref, map_ref, left_ref = refs[:5]
+    image_out, map_out, left_out, phase_out = refs[5:9]
+    shift, offset, angle, arrived, small = refs[9:]
+    copies = slice_copies(image_ref, map_ref, image_out, map_out, arrived, rows_of)
+    copies.append(pltpu.make_async_copy(left_ref, left_out, small.at[0]))
+    early = [
+        pltpu.make_async_copy(shift_ref, shift, small.at[1]),
+        pltpu.make_async_copy(offset_ref, offset, small.at[2]),
+    ]
+    start_all(early)
+    start_all(copies)
+    for copy in early:
+        copy.wait()
+    per_device, length = offset.shape
     lines = lax.broadcasted_iota(jnp.int32, (1, length), 1) - length // 2
     angle[...] = jnp.zeros_like(angle)
-    for slot, row in enumerate(rows_of):
-        turns = (shift_ref[row] * lines) & (MB - 1)
-        angle[slot : slot + 1, :length] = (
-            2.0 * math.pi / MB * turns.astype(jnp.float32) + offset_ref[pl.ds(row, 1), :]
+    for row in range(per_device):
+        turns = (shift[row] * lines) & (MB - 1)
+        angle[row : row + 1, :length] = (
+            2.0 * math.pi / MB * turns.astype(jnp.float32) + offset[row : row + 1, :]
         )
-    return jnp.cos(angle[...]).T, jnp.sin(angle[...]).T
-
-
-def encode_kernel(slots, group, picks, *refs):
-    shift_ref, order_ref, place_ref, image_ref, map_ref, kspace_ref, offset_ref = refs[:7]
-    left_ref, gram_ref, adjoint_ref, kept_ref = refs[7:11]
-    out_refs = refs[11:-4]
-    total, angle, shifted, copied = refs[-4:]
-    vols, coils, length = image_ref.shape[0], map_ref.shape[0], image_ref.shape[-1]
+    phase_out[0] = jnp.cos(angle[...]).T
+    phase_out[1] = jnp.sin(angle[...]).T
+    for copy in copies:
+        copy.wait()
+
+
+def encode_kernel(slots, group, rows_of, next_rows, *refs):
+    whole_classes = rows_of is not None
+    if not whole_classes:
+        place_ref, refs = refs[0], refs[1:]
+        next_rows = next_rows and [place_ref[2]]
+    phase_ref, image, coil_map, left_ref = refs[:4]
+    order_ref, gram_ref, adjoint_ref, kspace_ref, image_ref, map_ref = refs[4:10]
+    shifted, refs = refs[10], refs[11:]
+    out_refs, refs = refs[:ROW_PARTS], refs[ROW_PARTS:]
+    if next_rows:
+        next_image, next_map, refs = refs[0], refs[1], refs[2:]
+    total, wide, raw_kspace, gram, adjoint, order, arrived, small = refs
+    vols, coils, length = image.shape[0], coil_map.shape[0], image.shape[-1]
     _, rows, lanes = shifted.shape
     part = rows // len(out_refs)
-    groups = order_ref.shape[0]
-    whole_classes = picks is not None
-    if whole_classes:
-        rows_of = [slot * groups + group for slot in range(slots)]
-    else:
-        rows_of = picks = [place_ref[1]]
-    cosines, sines = phase_columns(shift_ref, offset_ref, angle, rows_of, length)
+    order_copy = pltpu.make_async_copy(order_ref, order, small.at[0])
+    gram_copy = pltpu.make_async_copy(gram_ref, gram, small.at[1])
+    owner_copies = [
+        pltpu.make_async_copy(kspace_ref, raw_kspace, small.at[2]),
+        pltpu.make_async_copy(adjoint_ref, adjoint, small.at[3]),
+    ]
+    next_copies = []
+    if next_rows:
+        next_copies = slice_copies(image_ref, map_ref, next_image, next_map, arrived, next_rows)
+    start_all([order_copy, gram_copy, *next_copies])
+
     if lanes > vols * coils * 2 * length:
         last = slice(lanes - LANE_TILE, lanes)
         total[:, last] = jnp.zeros((rows, LANE_TILE), jnp.float32)
         for slot in range(slots):
             shifted[slot, :, last] = jnp.zeros((rows, LANE_TILE), jnp.bfloat16)
-    sums, copies = [None] * (vols * coils), []
-    for slot, pick in enumerate(picks):
-        cosine = cosines[:rows, slot : slot + 1]
-        sine = sines[:rows, slot : slot + 1]
+    sums = [None] * (vols * coils)
+    for slot in range(slots):
+        if whole_classes:
+            column = rows_of[slot]
+            cosine = phase_ref[0, :rows, column : column + 1]
+            sine = phase_ref[1, :rows, column : column + 1]
+        else:
+            cosine, sine = phase_ref[0, :rows], phase_ref[1, :rows]
         for vol in range(vols):
-            image_re = image_ref[vol, pick, 0].astype(jnp.float32)
-            image_im = image_ref[vol, pick, 1].astype(jnp.float32)
+            image_re = image[vol, slot, 0].astype(jnp.float32)
+            image_im = image[vol, slot, 1].astype(jnp.float32)
             for coil in range(coils):
                 place = vol * coils + coil
                 base = place * 2 * length
-                map_re = map_ref[coil, pick, 0].astype(jnp.float32)
-                map_im = map_ref[coil, pick, 1].astype(jnp.float32)
+                map_re = coil_map[coil, slot, 0].astype(jnp.float32)
+                map_im = coil_map[coil, slot, 1].astype(jnp.float32)
                 coil_re = (map_re * image_re - map_im * image_im).astype(jnp.bfloat16)
                 coil_im = (map_re * image_im + map_im * image_re).astype(jnp.bfloat16)
-                partly = dot(left_ref[0], coil_re) + dot(left_ref[1], coil_im)
+                partly = dot(left_ref[0, : 2 * rows], coil_re) + dot(
+                    left_ref[1, : 2 * rows], coil_im
+                )
                 part_re, part_im = partly[:rows], partly[rows:]
                 shift_re = part_re * cosine - part_im * sine
                 shift_im = part_re * sine + part_im * cosine
@@ -113,30 +170,47 @@
                 if slot > 0:
                     shift_re, shift_im = sums[place][0] + shift_re, sums[place][1] + shift_im
                 sums[place] = (shift_re, shift_im)
-        copy = pltpu.make_async_copy(shifted.at[slot], kept_ref.at[slot], copied.at[slot])
-        copy.start()
-        copies.append(copy)
+        if slot == 0:
+            order_copy.wait()
+            owner = order[group] == lax.axis_index("slc")
+
+            @pl.when(owner)
+            def _():
+                start_all(owner_copies)
+
+    gram_copy.wait()
     for place, (sum_re, sum_im) in enumerate(sums):
-        mixed = dot(sum_re.astype(jnp.bfloat16), gram_ref[0]) + dot(
-            sum_im.astype(jnp.bfloat16), gram_ref[1]
+        mixed = dot(sum_re.astype(jnp.bfloat16), gram[0]) + dot(
+            sum_im.astype(jnp.bfloat16), gram[1]
         )
         if not whole_classes:
             mixed = jnp.where(place_ref[0] > 0, mixed, 0.0)
         total[:, place * 2 * length : (place + 1) * 2 * length] = mixed
 
-    @pl.when(order_ref[group] == lax.axis_index("slc"))
+    @pl.when(owner)
     def _():
+        for copy in owner_copies:
+            copy.wait()
         for vol in range(vols):
             for coil in range(coils):
                 place = vol * coils + coil
-                measured = dot(kspace_ref[vol, 0, coil, 0], adjoint_ref[0]) + dot(
-                    kspace_ref[vol, 0, coil, 1], adjoint_ref[1]
-                )
+                lying = raw_kspace.at[vol, 0, coil].reshape(2 * length, length)[...]
+                measured = None
+                for kind in range(2):
+                    for tile in range(wide.shape[0]):
+                        at, end = tile * LANE_TILE, min(length, (tile + 1) * LANE_TILE)
+                        if kind == 0:
+                            wide[tile, :, : end - at] = lying[:, at:end].astype(jnp.float32)
+                        rows_read = wide[tile, pl.ds(kind, length, stride=2), :]
+                        term = dot(
+                            rows_read[:, : end - at].astype(jnp.bfloat16), adjoint[kind, at:end, :]
+                        )
+                        measured = term if measured is None else measured + term
                 total[:length, place * 2 * length : (place + 1) * 2 * length] -= measured
 
     for index, out_ref in enumerate(out_refs):
         out_ref[...] = total[index * part : (index + 1) * part, :].astype(jnp.bfloat16)
-    for copy in copies:
+    for copy in next_copies:
         copy.wait()
 
 
@@ -221,6 +295,7 @@
             latest = (outer_next(half),)
         if len(pieces) < min(count, step + LAG + 2):
             encode_next(*(latest or (half,)))
+            latest = (*latest, pieces[-1])
         if step >= LAG + 1:
             gradient_next(*latest)
             latest = (*latest, gradients[-1])
@@ -246,46 +321,83 @@
     on_line = whole_classes and groups == 4
     in_vmem = pl.BlockSpec(memory_space=pltpu.VMEM)
     in_smem = pl.BlockSpec(memory_space=pltpu.SMEM)
-
-    per_half = groups // HALVES
-
-    @functools.cache
-    def halves(half):
-        lead = lambda array: array.reshape(
-            array.shape[0], slots, groups, *array.shape[2:]
-        )[:, :, half * per_half : (half + 1) * per_half].reshape(
-            array.shape[0], slots * per_half, *array.shape[2:]
-        )
-        pair = (images, coil_maps)
-        if half > 0:
-            pair = lax.optimization_barrier((*pair, *held_back))[:2]
-        return tuple(lead(array) for array in pair)
-
-    held_back = []
+    in_place = pl.BlockSpec(memory_space=pl.ANY)
+
+    def in_hbm(array):
+        return pltpu.with_memory_space_constraint(jnp.asarray(array), pltpu.HBM)
+
+    def rows_of_class(group):
+        return [slot * groups + group for slot in range(slots)] if whole_classes else None
+
+    def place_of(group):
+        if whole_classes:
+            return ()
+        held = [(group + step - first, per_device) for step in range(2)]
+        inside = [(within >= 0) & (within < size) for within, size in held]
+        rows_held = [jnp.where(yes, held[i][0], 0) for i, yes in enumerate(inside)]
+        return (jnp.stack([inside[0], rows_held[0], rows_held[1]]).astype(jnp.int32),)
+
+    left, gram, adjoint = (in_hbm(table) for table in tables)
+    lying = [in_hbm(jnp.swapaxes(array, -3, -2)) for array in (images, coil_maps, kspace)]
+    order = in_hbm(group_order)
+    tiles = round_up(length, LANE_TILE) // LANE_TILE
+    raw_shapes = [
+        jax.ShapeDtypeStruct((count, slots, length, 2, length), jnp.bfloat16)
+        for count in (vols, coils)
+    ]
+    scalar_specs = [] if whole_classes else [in_smem]
+    padded_rows = round_up(rows, LANE_TILE)
+    slice_semaphores = pltpu.SemaphoreType.DMA((slots, vols + coils))
+    *raw, left, phases = pl.pallas_call(
+        functools.partial(fetch_kernel, rows_of_class(0)),
+        in_specs=scalar_specs + [in_place] * 5,
+        out_specs=[in_vmem] * 4,
+        out_shape=raw_shapes
+        + [
+            jax.ShapeDtypeStruct(left.shape, left.dtype),
+            jax.ShapeDtypeStruct((2, padded_rows, per_device), jnp.float32),
+        ],
+        scratch_shapes=[
+            pltpu.SMEM((per_device,), jnp.int32),
+            pltpu.VMEM((per_device, length), jnp.float32),
+            pltpu.VMEM((per_device, padded_rows), jnp.float32),
+            slice_semaphores,
+            pltpu.SemaphoreType.DMA((3,)),
+        ],
+        compiler_params=pltpu.CompilerParams(vmem_limit_bytes=VMEM_BYTES),
+        name="fetch",
+    )(*place_of(0), in_hbm(shift_index), in_hbm(phase_offset), *lying[:2], left)
 
     def encode(group, *earlier):
-        if whole_classes:
-            place = np.zeros((2,), np.int32)
-            image, coil_map = halves(group // per_half)
-            picks = [slot * per_half + group % per_half for slot in range(slots)]
-        else:
-            within = group - first
-            held = (within >= 0) & (within < per_device)
-            within = jnp.where(held, within, 0)
-            place = jnp.stack([held, within]).astype(jnp.int32)
-            image, coil_map, picks = images, coil_maps, None
-        offset = after(phase_offset, *earlier) if earlier else phase_offset
+        image, coil_map = (jnp.swapaxes(array, -3, -2) for array in raw)
+        has_next = group + 1 < groups
+        place, group_phases = place_of(group), phases
+        if not whole_classes:
+            group_phases = lax.dynamic_slice_in_dim(phases, place[0][1], 1, axis=2)
+        if earlier:
+            image = after(image, *earlier)
         outputs = pl.pallas_call(
-            functools.partial(encode_kernel, slots, group, picks),
-            in_specs=[in_smem] * 3 + [in_vmem] * 7,
-            out_specs=[pl.BlockSpec(memory_space=pltpu.HBM)] + [in_vmem] * ROW_PARTS,
+            functools.partial(
+                encode_kernel,
+                slots,
+                group,
+                rows_of_class(group),
+                (rows_of_class(group + 1) or [0]) if has_next else None,
+            ),
+            in_specs=scalar_specs + [in_vmem] * 4 + [in_place] * 6,
+            out_specs=[in_vmem] * (1 + ROW_PARTS + 2 * has_next),
             out_shape=[jax.ShapeDtypeStruct((slots, rows, lanes), jnp.bfloat16)]
-            + [jax.ShapeDtypeStruct((part, lanes), jnp.bfloat16)] * ROW_PARTS,
+            + [jax.ShapeDtypeStruct((part, lanes), jnp.bfloat16)] * ROW_PARTS
+            + raw_shapes * has_next,
             scratch_shapes=[
                 pltpu.VMEM((rows, lanes), jnp.float32),
-                pltpu.VMEM((round_up(slots, 8), round_up(rows, LANE_TILE)), jnp.float32),
-                pltpu.VMEM((slots, rows, lanes), jnp.bfloat16),
-                pltpu.SemaphoreType.DMA((slots,)),
+                pltpu.VMEM((tiles, 2 * length, LANE_TILE), jnp.float32),
+                pltpu.VMEM(lying[2].shape, jnp.bfloat16),
+                pltpu.VMEM(gram.shape, jnp.bfloat16),
+                pltpu.VMEM(adjoint.shape, jnp.bfloat16),
+                pltpu.SMEM((groups,), jnp.int32),
+                slice_semaphores,
+                pltpu.SemaphoreType.DMA((4,)),
             ],
             compiler_params=pltpu.CompilerParams(vmem_limit_bytes=VMEM_BYTES),
             cost_estimate=pl.CostEstimate(
@@ -295,17 +407,19 @@
             ),
             name="encode",
         )(
-            shift_index,
-            group_order,
-            place,
+            *place,
+            group_phases,
             image,
             coil_map,
-            kspace,
-            offset,
-            *tables,
+            left,
+            order,
+            gram,
+            adjoint,
+            lying[2],
+            *lying[:2],
         )
-        held_back.append(outputs[1])
-        return outputs
+        raw[:] = outputs[1 + ROW_PARTS :]
+        return outputs[: 1 + ROW_PARTS]
 
     def gradient(step, terms, encoded):
         return pl.pallas_call(

time: 91.1 us -> 84.2 us (0.924)
  local copies, waits for them, and re-layouts: 14.2 us -> 4.67 us
  waiting for transfers between devices: 7.62 us -> 9.62 us
    unnamed x45 -> x12, local copies, waits for them, and re-layouts: 9.18 us -> 1.96 us
    slice x4 -> x0, local copies, waits for them, and re-layouts: 5.04 us -> none  [halves(): array.reshape(array.shape[0], slots, groups, *array.shape[2:])]
    pallas_call x0 -> x8, local copies, waits for them, and re-layouts: none -> 2.7 us  [the longest x6 2.51 us: encode(): pl.pallas_call(functools.partial(encode_kernel, slots, group, rows_of_cla...]
    ppermute x11, starting transfers between devices: 31.7 us -> 32.7 us  [outer_next(): outer.append(lax.ppermute(payload, 'slc', outer_pairs))]
    ppermute x11, waiting for transfers between devices: 5.73 us -> 6.75 us  [outer_next(): outer.append(lax.ppermute(payload, 'slc', outer_pairs))]
    ppermute x3, waiting for transfers between devices: 1.87 us -> 2.85 us  [sum_over_replicas(): lax.ppermute(value, axes, [(index, index ^ mask) for index in range(4)])]
    pallas_call x4 -> x5, Pallas kernels: 13.8 us -> 13.3 us  [the longest x4 11.7 us: encode(): pl.pallas_call(functools.partial(encode_kernel, slots, group, rows_of_cla...]
  transfers between devices with their start and end apart: 22 -> 22, of which waited for: 7 -> 7; matrix products, arithmetic and copies ran while one was open for 10% -> 11% of each run, Pallas kernels for 16% -> 16%
where the time goes in v9:
time: 84.2 us; the launch traced here: 83.3 us
  starting transfers between devices  42.9 us (51%)
  Pallas kernels  18.4 us (22%)
  waiting for transfers between devices  9.62 us (11%)
  other arithmetic  7.27 us (9%)
  local copies, waits for them, and re-layouts  4.67 us (6%)
    ppermute x11, starting transfers between devices, outer_next(): outer.append(lax.ppermute(payload, 'slc', outer_pairs))  32.7 us
    pallas_call x4, Pallas kernels, encode(): pl.pallas_call(functools.partial(encode_kernel, slots, group, rows_of_cla...  11.7 us
    ppermute x8, starting transfers between devices, line_of_four(): inner.append(lax.ppermute(half, 'slc', inner_pairs))  8.28 us
    ppermute x11, waiting for transfers between devices, outer_next(): outer.append(lax.ppermute(payload, 'slc', outer_pairs))  6.75 us
    pallas_call x8, Pallas kernels, gradient(): pl.pallas_call(functools.partial(gradient_kernel, step % ROW_PARTS, facto...  5.1 us
    add x8, other arithmetic, line_of_four(): half = pieces[step] + after(outer[step], *latest)  3.2 us
    select_n x5, other arithmetic, outer_next(): payload = others if payload is None else jnp.where(edge, payload, others)  3.01 us
    ppermute x3, waiting for transfers between devices, sum_over_replicas(): lax.ppermute(value, axes, [(index, index ^ mask) for index in range(4)])  2.85 us
  transfers between devices with their start and end apart: 22, of which 7 were waited for; matrix products, arithmetic and copies ran while one was open for 11% of the time, Pallas kernels for 16%

profile of v9, /device:TPU:0, one launch (start us, length us, event | category | flops | bytes accessed | tf_op | source)
XLA Modules:
  0.0 83.3 jit_solution(4963836447421834199)
XLA Ops:
  0.0 1.7 %fetch.1 = (bf16[1,2,220,2,220]{4,3,2,1,0:T(2,128)(2,1)S(1)}, bf16[2,2,220,2,220]{4,3,2,1,0:T(2,128)(2,1)S(1)}, bf16[2,456,220]{2,1,0:T(8,128)(2,1)S(1)}, f32[2,256,8]{2,1,0:T(8,128)S(1)}) custom-call(s32[8]{0:T(128)} %refs_0_.1, f32[8,220]{1,0:T(8,128)} %refs_1_.1, bf16[1,8,220,2,220]{4,3,2,1,0:T(2,128)(2,1)} %bitcast.48, ...), custom_call_target="tpu_custom_call" | custom-call | tf_op jit(solution)/shard_map/fetch/pallas_call | solution.py:351
  1.9 2.9 %encode.4 = (bf16[2,224,896]{2,1,0:T(8,128)(2,1)S(1)}, bf16[112,896]{1,0:T(8,128)(2,1)S(1)}, bf16[112,896]{1,0:T(8,128)(2,1)}, bf16[1,2,220,2,220]{4,3,2,1,0:T(2,128)(2,1)S(1)}, bf16[2,2,220,2,220]{4,3,2,1,0:T(2,128)(2,1)S(1)}) custom-call(f32[2,256,8]{2,1,0:T(8,128)S(1)} %get-tuple-element.53.refs_0_, bf16[1,2,2,220,220]{4,3,2,1,0:T(8,128)(2,1)S(1)} %bitcast.41, ...), custom_call_target="tpu_custom_call" | custom-call | flops 1022208000 | bytes 6000000 | tf_op jit(solution)/shard_map/encode/pallas_call | solution.py:379
  4.8 3.1 %collective-permute-start = (bf16[112,896]{1,0:T(8,128)(2,1)S(1)}, bf16[112,896]{1,0:T(8,128)(2,1)S(1)}, u32[]{:S(2)}, u32[]{:S(2)}) collective-permute-start(bf16[112,896]{1,0:T(8,128)(2,1)S(1)} %get-tuple-element.82.refs_0_), channel_id=1, source_target_pairs={{0,4},{4,0},{8,12},{12,8},{1,5},{5,1},{9,13},{13,9},{2,6},{6,2},{1... | collective-permute-start | bytes 602120 | tf_op jit(solution)/shard_map/ppermute | solution.py:276
  8.2 4.4 %encode.5 = (bf16[2,224,896]{2,1,0:T(8,128)(2,1)S(1)}, bf16[112,896]{1,0:T(8,128)(2,1)}, bf16[112,896]{1,0:T(8,128)(2,1)S(1)}, bf16[1,2,220,2,220]{4,3,2,1,0:T(2,128)(2,1)S(1)}, bf16[2,2,220,2,220]{4,3,2,1,0:T(2,128)(2,1)S(1)}) custom-call(f32[2,256,8]{2,1,0:T(8,128)S(1)} %get-tuple-element.53.refs_0_, bf16[1,2,2,220,220]{4,3,2,1,0:T(8,128)(2,1)S(1)} %bitcast.42, ...), custom_call_target="tpu_custom_call" | custom-call | flops 1022208000 | bytes 6000000 | tf_op jit(solution)/shard_map/encode/pallas_call | solution.py:379
  14.5 3.4 %collective-permute-start.4 = (bf16[112,896]{1,0:T(8,128)(2,1)}, bf16[112,896]{1,0:T(8,128)(2,1)}, u32[]{:S(2)}, u32[]{:S(2)}) collective-permute-start(bf16[112,896]{1,0:T(8,128)(2,1)} %add.57), channel_id=1, source_target_pairs={{0,0},{4,8},{8,4},{12,12},{1,1},{5,9},{9,5},{13,13},{2,2},{6,10},{... | collective-permute-start | bytes 602120 | tf_op jit(solution)/shard_map/ppermute | solution.py:292
  17.9 3.7 %collective-permute-start.3 = (bf16[112,896]{1,0:T(8,128)(2,1)}, bf16[112,896]{1,0:T(8,128)(2,1)}, u32[]{:S(2)}, u32[]{:S(2)}) collective-permute-start(bf16[112,896]{1,0:T(8,128)(2,1)} %get-tuple-element.89.refs_0_), channel_id=1, source_target_pairs={{0,4},{4,0},{8,12},{12,8},{1,5},{5,1},{9,13},{13,9},{2,6},{6,2},{1... | collective-permute-start | bytes 602120 | tf_op jit(solution)/shard_map/ppermute | solution.py:276
  22.4 1.3 %copy.36 = bf16[2,2,220,2,220]{4,2,3,1,0:T(8,128)(2,1)S(1)} copy(bf16[2,2,220,2,220]{4,3,2,1,0:T(2,128)(2,1)} %copy-done.3) | data formatting | bytes 1548800 | tf_op jit(solution)/shard_map/encode/pallas_call | solution.py:379
  24.8 2.2 %encode.6 = (bf16[2,224,896]{2,1,0:T(8,128)(2,1)S(1)}, bf16[112,896]{1,0:T(8,128)(2,1)S(1)}, bf16[112,896]{1,0:T(8,128)(2,1)S(1)}, bf16[1,2,220,2,220]{4,3,2,1,0...) custom-call(f32[2,256,8]{2,1,0:T(8,128)S(1)} %get-tuple-element.53.refs_0_, bf16[1,2,2,220,220]{4,3,2,1,0:T(8,128)(2,1)S(1)} %bitcast.40, ...), custom_call_target="tpu_custom_call" | custom-call | flops 1022208000 | bytes 6000000 | tf_op jit(solution)/shard_map/encode/pallas_call | solution.py:379
  26.9 1.1 %add.58 = bf16[112,896]{1,0:T(8,128)(2,1)S(1)} add(bf16[112,896]{1,0:T(8,128)(2,1)} %get-tuple-element.86.refs_0_, bf16[112,896]{1,0:T(8,128)(2,1)} %collective-permute-done.1.refs_1_) | non-fusion elementwise | flops 100352 | bytes 602112 | tf_op jit(solution)/shard_map/add | solution.py:291
  29.9 2.8 %collective-permute-start.5 = (bf16[112,896]{1,0:T(8,128)(2,1)S(1)}, bf16[112,896]{1,0:T(8,128)(2,1)S(1)}, u32[]{:S(2)}, u32[]{:S(2)}) collective-permute-start(bf16[112,896]{1,0:T(8,128)(2,1)S(1)} %add_select_fusion.3), channel_id=1, source_target_pairs={{0,4},{4,0},{8,12},{12,8},{1,5},{5,1},{9,13},{13,9},{2,6},{6,2},{1... | collective-permute-start | bytes 602120 | tf_op jit(solution)/shard_map/ppermute | solution.py:276
  35.5 3.9 %collective-permute-start.7 = (bf16[112,896]{1,0:T(8,128)(2,1)S(1)}, bf16[112,896]{1,0:T(8,128)(2,1)S(1)}, u32[]{:S(2)}, u32[]{:S(2)}) collective-permute-start(bf16[112,896]{1,0:T(8,128)(2,1)S(1)} %add_select_fusion.4), channel_id=1, source_target_pairs={{0,4},{4,0},{8,12},{12,8},{1,5},{5,1},{9,13},{13,9},{2,6},{6,2},{1... | collective-permute-start | bytes 602120 | tf_op jit(solution)/shard_map/ppermute | solution.py:276
  39.4 2.2 %encode.7 = (bf16[2,224,896]{2,1,0:T(8,128)(2,1)S(1)}, bf16[112,896]{1,0:T(8,128)(2,1)S(1)}, bf16[112,896]{1,0:T(8,128)(2,1)S(1)}) custom-call(f32[2,256,8]{2,1,0:T(8,128)S(1)} %get-tuple-element.53.refs_0_, bf16[1,2,2,220,220]{4,3,2,1,0:T(8,128)(2,1)S(1)} %bitcast.39, bf16[2,2,2,220,220]{4,3,2,1,0:T(8,128)(2,1)S(1)} %bitcast.35, ...), custom_call_target="tpu_custom_call" | custom-call | flops 1022208000 | bytes 6000000 | tf_op jit(solution)/shard_map/encode/pallas_call | solution.py:379
  43.3 1.9 %collective-permute-start.10 = (bf16[112,896]{1,0:T(8,128)(2,1)S(1)}, bf16[112,896]{1,0:T(8,128)(2,1)S(1)}, u32[]{:S(2)}, u32[]{:S(2)}) collective-permute-start(bf16[112,896]{1,0:T(8,128)(2,1)S(1)} %add_select_fusion.1), channel_id=1, source_target_pairs={{0,4},{4,0},{8,12},{12,8},{1,5},{5,1},{9,13},{13,9},{2,6},{6,2},{1... | collective-permute-start | bytes 602120 | tf_op jit(solution)/shard_map/ppermute | solution.py:276
  46.0 4.3 %collective-permute-start.12 = (bf16[112,896]{1,0:T(8,128)(2,1)S(1)}, bf16[112,896]{1,0:T(8,128)(2,1)S(1)}, u32[]{:S(2)}, u32[]{:S(2)}) collective-permute-start(bf16[112,896]{1,0:T(8,128)(2,1)S(1)} %add_select_fusion.2), channel_id=1, source_target_pairs={{0,4},{4,0},{8,12},{12,8},{1,5},{5,1},{9,13},{13,9},{2,6},{6,2},{1... | collective-permute-start | bytes 602120 | tf_op jit(solution)/shard_map/ppermute | solution.py:276
  50.2 1.2 %gradient.8 = f32[2,112]{1,0:T(2,128)S(1)} custom-call(bf16[112,896]{1,0:T(8,128)(2,1)S(1)} %copy-done.2, bf16[112,896]{1,0:T(8,128)(2,1)S(1)} %copy-done.5, bf16[112,896]{1,0:T(8,128)(2,1)} %collective-permute-done.4.refs_2_, bf16[112,896]{1,0:T(8,128)(2,1)S(1)} %collective-permute-done.5.refs_3_.refs_1_, bf16[2,224,896]{2,1,0:T(8,128)(2,1)S(1)} %get-tuple-element.83.refs_4_), custom_call_target="tpu_custom_call" | custom-call | flops 774400 | bytes 1500000 | tf_op jit(solution)/shard_map/gradient/pallas_call | solution.py:425
  52.4 3.9 %collective-permute-start.14 = (bf16[112,896]{1,0:T(8,128)(2,1)S(1)}, bf16[112,896]{1,0:T(8,128)(2,1)S(1)}, u32[]{:S(2)}, u32[]{:S(2)}) collective-permute-start(bf16[112,896]{1,0:T(8,128)(2,1)S(1)} %add_select_fusion), channel_id=1, source_target_pairs={{0,4},{4,0},{8,12},{12,8},{1,5},{5,1},{9,13},{13,9},{2,6},{6,2},{1... | collective-permute-start | bytes 602120 | tf_op jit(solution)/shard_map/ppermute | solution.py:276
  56.4 1.3 %gradient.9 = f32[2,112]{1,0:T(2,128)S(1)} custom-call(bf16[112,896]{1,0:T(8,128)(2,1)} %get-tuple-element.86.refs_0_, bf16[112,896]{1,0:T(8,128)(2,1)} %collective-permute-done.1.refs_1_, bf16[112,896]{1,0:T(8,128)(2,1)S(1)} %collective-permute-done.2.refs_2_, bf16[112,896]{1,0:T(8,128)(2,1)S(1)} %collective-permute-done.7.refs_3_.refs_1_, ...), custom_call_target="tpu_custom_call" | custom-call | flops 774400 | bytes 1500000 | tf_op jit(solution)/shard_map/gradient/pallas_call | solution.py:425
  58.5 1.3 %gradient.10 = f32[2,112]{1,0:T(2,128)S(1)} custom-call(bf16[112,896]{1,0:T(8,128)(2,1)} %get-tuple-element.89.refs_0_, bf16[112,896]{1,0:T(8,128)(2,1)} %collective-permute-done.3.refs_1_, bf16[112,896]{1,0:T(8,128)(2,1)S(1)} %collective-permute-done.8.refs_2_, bf16[112,896]{1,0:T(8,128)(2,1)S(1)} %collective-permute-done.10.refs_3_.refs_1_, ...), custom_call_target="tpu_custom_call" | custom-call | flops 774400 | bytes 1500000 | tf_op jit(solution)/shard_map/gradient/pallas_call | solution.py:425
  60.8 4.7 %collective-permute-start.16 = (bf16[112,896]{1,0:T(8,128)(2,1)S(1)}, bf16[112,896]{1,0:T(8,128)(2,1)S(1)}, u32[]{:S(2)}, u32[]{:S(2)}) collective-permute-start(bf16[112,896]{1,0:T(8,128)(2,1)S(1)} %add.68), channel_id=1, source_target_pairs={{0,4},{4,0},{8,12},{12,8},{1,5},{5,1},{9,13},{13,9},{2,6},{6,2},{1... | collective-permute-start | bytes 602120 | tf_op jit(solution)/shard_map/ppermute | solution.py:276
  66.0 4.3 %collective-permute-start.17 = (bf16[112,896]{1,0:T(8,128)(2,1)S(1)}, bf16[112,896]{1,0:T(8,128)(2,1)S(1)}, u32[]{:S(2)}, u32[]{:S(2)}) collective-permute-start(bf16[112,896]{1,0:T(8,128)(2,1)S(1)} %add.70), channel_id=1, source_target_pairs={{0,4},{4,0},{8,12},{12,8},{1,5},{5,1},{9,13},{13,9},{2,6},{6,2},{1... | collective-permute-start | bytes 602120 | tf_op jit(solution)/shard_map/ppermute | solution.py:276
  71.8 3.6 %collective-permute-done.17.refs_3_ = bf16[112,896]{1,0:T(8,128)(2,1)S(1)} collective-permute-done((bf16[112,896]{1,0:T(8,128)(2,1)S(1)}, bf16[112,896]{1,0:T(8,128)(2,1)S(1)}, u32[]{:S(2)}, u32[]{:S(2)}) %collective-permute-start.17) | collective-permute-done | bytes 200736 | tf_op jit(solution)/shard_map/ppermute | solution.py:276
  75.7 1.9 %collective-permute-done.18.refs_3_ = bf16[112,896]{1,0:T(8,128)(2,1)S(1)} collective-permute-done((bf16[112,896]{1,0:T(8,128)(2,1)S(1)}, bf16[112,896]{1,0:T(8,128)(2,1)S(1)}, u32[]{:S(2)}, u32[]{:S(2)}) %collective-permute-start.18) | collective-permute-done | bytes 200736 | tf_op jit(solution)/shard_map/ppermute | solution.py:276
  78.0 1.6 %collective-permute-start.20 = (f32[8,220]{1,0:T(8,128)S(1)}, f32[8,220]{1,0:T(8,128)S(1)}, u32[]{:S(2)}, u32[]{:S(2)}) collective-permute-start(f32[8,220]{1,0:T(8,128)S(1)} %reshape.3), channel_id=1, source_target_pairs={{0,2},{1,3},{2,0},{3,1},{4,6},{5,7},{6,4},{7,5},{8,10},{9,11},{10,... | collective-permute-start | bytes 21128 | tf_op jit(solution)/shard_map/ppermute | solution.py:246
  79.9 1.9 %collective-permute-done.20 = f32[8,220]{1,0:T(8,128)S(1)} collective-permute-done((f32[8,220]{1,0:T(8,128)S(1)}, f32[8,220]{1,0:T(8,128)S(1)}, u32[]{:S(2)}, u32[]{:S(2)}) %collective-permute-start.20) | collective-permute-done | bytes 7072 | tf_op jit(solution)/shard_map/ppermute | solution.py:246
  (77 shorter events, 18.6 us)
Async XLA Ops:
  4.8 8.9 %copy-start.1 = (bf16[112,896]{1,0:T(8,128)(2,1)}, bf16[112,896]{1,0:T(8,128)(2,1)S(1)}, u32[]{:S(2)}) copy-start(bf16[112,896]{1,0:T(8,128)(2,1)S(1)} %get-tuple-element.82.refs_0_) | copy-start | bytes 602116
  4.8 8.9 %collective-permute-start = (bf16[112,896]{1,0:T(8,128)(2,1)S(1)}, bf16[112,896]{1,0:T(8,128)(2,1)S(1)}, u32[]{:S(2)}, u32[]{:S(2)}) collective-permute-start(bf16[112,896]{1,0:T(8,128)(2,1)S(1)} %get-tuple-element.82.refs_0_), channel_id=1, source_target_pairs={{0,4},{4,0},{8,12},{12,8},{1,5},{5,1},{9,13},{13,9},{2,6},{6,2},{1... | collective-permute-start | bytes 602120 | tf_op jit(solution)/shard_map/ppermute | solution.py:276
  7.9 19.0 %collective-permute-start.1 = (bf16[112,896]{1,0:T(8,128)(2,1)}, bf16[112,896]{1,0:T(8,128)(2,1)}, u32[]{:S(2)}, u32[]{:S(2)}) collective-permute-start(bf16[112,896]{1,0:T(8,128)(2,1)} %get-tuple-element.86.refs_0_), channel_id=1, source_target_pairs={{0,4},{4,0},{8,12},{12,8},{1,5},{5,1},{9,13},{13,9},{2,6},{6,2},{1... | collective-permute-start | bytes 602120 | tf_op jit(solution)/shard_map/ppermute | solution.py:276
  14.5 14.4 %collective-permute-start.4 = (bf16[112,896]{1,0:T(8,128)(2,1)}, bf16[112,896]{1,0:T(8,128)(2,1)}, u32[]{:S(2)}, u32[]{:S(2)}) collective-permute-start(bf16[112,896]{1,0:T(8,128)(2,1)} %add.57), channel_id=1, source_target_pairs={{0,0},{4,8},{8,4},{12,12},{1,1},{5,9},{9,5},{13,13},{2,2},{6,10},{... | collective-permute-start | bytes 602120 | tf_op jit(solution)/shard_map/ppermute | solution.py:292
  17.9 14.8 %collective-permute-start.3 = (bf16[112,896]{1,0:T(8,128)(2,1)}, bf16[112,896]{1,0:T(8,128)(2,1)}, u32[]{:S(2)}, u32[]{:S(2)}) collective-permute-start(bf16[112,896]{1,0:T(8,128)(2,1)} %get-tuple-element.89.refs_0_), channel_id=1, source_target_pairs={{0,4},{4,0},{8,12},{12,8},{1,5},{5,1},{9,13},{13,9},{2,6},{6,2},{1... | collective-permute-start | bytes 602120 | tf_op jit(solution)/shard_map/ppermute | solution.py:276
  28.0 6.4 %collective-permute-start.2 = (bf16[112,896]{1,0:T(8,128)(2,1)S(1)}, bf16[112,896]{1,0:T(8,128)(2,1)S(1)}, u32[]{:S(2)}, u32[]{:S(2)}) collective-permute-start(bf16[112,896]{1,0:T(8,128)(2,1)S(1)} %add.58), channel_id=1, source_target_pairs={{0,0},{4,8},{8,4},{12,12},{1,1},{5,9},{9,5},{13,13},{2,2},{6,10},{... | collective-permute-start | bytes 602120 | tf_op jit(solution)/shard_map/ppermute | solution.py:292
  29.9 11.7 %collective-permute-start.5 = (bf16[112,896]{1,0:T(8,128)(2,1)S(1)}, bf16[112,896]{1,0:T(8,128)(2,1)S(1)}, u32[]{:S(2)}, u32[]{:S(2)}) collective-permute-start(bf16[112,896]{1,0:T(8,128)(2,1)S(1)} %add_select_fusion.3), channel_id=1, source_target_pairs={{0,4},{4,0},{8,12},{12,8},{1,5},{5,1},{9,13},{13,9},{2,6},{6,2},{1... | collective-permute-start | bytes 602120 | tf_op jit(solution)/shard_map/ppermute | solution.py:276
  33.8 8.5 %collective-permute-start.8 = (bf16[112,896]{1,0:T(8,128)(2,1)S(1)}, bf16[112,896]{1,0:T(8,128)(2,1)S(1)}, u32[]{:S(2)}, u32[]{:S(2)}) collective-permute-start(bf16[112,896]{1,0:T(8,128)(2,1)S(1)} %add.61), channel_id=1, source_target_pairs={{0,0},{4,8},{8,4},{12,12},{1,1},{5,9},{9,5},{13,13},{2,2},{6,10},{... | collective-permute-start | bytes 602120 | tf_op jit(solution)/shard_map/ppermute | solution.py:292
  35.5 9.7 %collective-permute-start.7 = (bf16[112,896]{1,0:T(8,128)(2,1)S(1)}, bf16[112,896]{1,0:T(8,128)(2,1)S(1)}, u32[]{:S(2)}, u32[]{:S(2)}) collective-permute-start(bf16[112,896]{1,0:T(8,128)(2,1)S(1)} %add_select_fusion.4), channel_id=1, source_target_pairs={{0,4},{4,0},{8,12},{12,8},{1,5},{5,1},{9,13},{13,9},{2,6},{6,2},{1... | collective-permute-start | bytes 602120 | tf_op jit(solution)/shard_map/ppermute | solution.py:276
  39.4 10.9 %copy-start.5 = (bf16[112,896]{1,0:T(8,128)(2,1)S(1)}, bf16[112,896]{1,0:T(8,128)(2,1)}, u32[]{:S(2)}) copy-start(bf16[112,896]{1,0:T(8,128)(2,1)} %copy-done.4) | copy-start | bytes 602116
  41.6 4.3 %collective-permute-start.6 = (bf16[112,896]{1,0:T(8,128)(2,1)S(1)}, bf16[112,896]{1,0:T(8,128)(2,1)S(1)}, u32[]{:S(2)}, u32[]{:S(2)}) collective-permute-start(bf16[112,896]{1,0:T(8,128)(2,1)S(1)} %add.62), channel_id=1, source_target_pairs={{0,0},{4,8},{8,4},{12,12},{1,1},{5,9},{9,5},{13,13},{2,2},{6,10},{... | collective-permute-start | bytes 602120 | tf_op jit(solution)/shard_map/ppermute | solution.py:292
  43.3 8.2 %collective-permute-start.10 = (bf16[112,896]{1,0:T(8,128)(2,1)S(1)}, bf16[112,896]{1,0:T(8,128)(2,1)S(1)}, u32[]{:S(2)}, u32[]{:S(2)}) collective-permute-start(bf16[112,896]{1,0:T(8,128)(2,1)S(1)} %add_select_fusion.1), channel_id=1, source_target_pairs={{0,4},{4,0},{8,12},{12,8},{1,5},{5,1},{9,13},{13,9},{2,6},{6,2},{1... | collective-permute-start | bytes 602120 | tf_op jit(solution)/shard_map/ppermute | solution.py:276
  45.2 7.1 %collective-permute-start.9 = (bf16[112,896]{1,0:T(8,128)(2,1)S(1)}, bf16[112,896]{1,0:T(8,128)(2,1)S(1)}, u32[]{:S(2)}, u32[]{:S(2)}) collective-permute-start(bf16[112,896]{1,0:T(8,128)(2,1)S(1)} %add.65), channel_id=1, source_target_pairs={{0,0},{4,8},{8,4},{12,12},{1,1},{5,9},{9,5},{13,13},{2,2},{6,10},{... | collective-permute-start | bytes 602120 | tf_op jit(solution)/shard_map/ppermute | solution.py:292
  46.0 11.7 %collective-permute-start.12 = (bf16[112,896]{1,0:T(8,128)(2,1)S(1)}, bf16[112,896]{1,0:T(8,128)(2,1)S(1)}, u32[]{:S(2)}, u32[]{:S(2)}) collective-permute-start(bf16[112,896]{1,0:T(8,128)(2,1)S(1)} %add_select_fusion.2), channel_id=1, source_target_pairs={{0,4},{4,0},{8,12},{12,8},{1,5},{5,1},{9,13},{13,9},{2,6},{6,2},{1... | collective-permute-start | bytes 602120 | tf_op jit(solution)/shard_map/ppermute | solution.py:276
  51.5 6.9 %collective-permute-start.11 = (bf16[112,896]{1,0:T(8,128)(2,1)S(1)}, bf16[112,896]{1,0:T(8,128)(2,1)S(1)}, u32[]{:S(2)}, u32[]{:S(2)}) collective-permute-start(bf16[112,896]{1,0:T(8,128)(2,1)S(1)} %add.67), channel_id=1, source_target_pairs={{0,0},{4,8},{8,4},{12,12},{1,1},{5,9},{9,5},{13,13},{2,2},{6,10},{... | collective-permute-start | bytes 602120 | tf_op jit(solution)/shard_map/ppermute | solution.py:292
  52.4 7.6 %collective-permute-start.14 = (bf16[112,896]{1,0:T(8,128)(2,1)S(1)}, bf16[112,896]{1,0:T(8,128)(2,1)S(1)}, u32[]{:S(2)}, u32[]{:S(2)}) collective-permute-start(bf16[112,896]{1,0:T(8,128)(2,1)S(1)} %add_select_fusion), channel_id=1, source_target_pairs={{0,4},{4,0},{8,12},{12,8},{1,5},{5,1},{9,13},{13,9},{2,6},{6,2},{1... | collective-permute-start | bytes 602120 | tf_op jit(solution)/shard_map/ppermute | solution.py:276
  57.7 7.9 %collective-permute-start.13 = (bf16[112,896]{1,0:T(8,128)(2,1)S(1)}, bf16[112,896]{1,0:T(8,128)(2,1)S(1)}, u32[]{:S(2)}, u32[]{:S(2)}) collective-permute-start(bf16[112,896]{1,0:T(8,128)(2,1)S(1)} %add.69), channel_id=1, source_target_pairs={{0,0},{4,8},{8,4},{12,12},{1,1},{5,9},{9,5},{13,13},{2,2},{6,10},{... | collective-permute-start | bytes 602120 | tf_op jit(solution)/shard_map/ppermute | solution.py:292
  60.1 5.6 %collective-permute-start.15 = (bf16[112,896]{1,0:T(8,128)(2,1)S(1)}, bf16[112,896]{1,0:T(8,128)(2,1)S(1)}, u32[]{:S(2)}, u32[]{:S(2)}) collective-permute-start(bf16[112,896]{1,0:T(8,128)(2,1)S(1)} %add.71), channel_id=1, source_target_pairs={{0,0},{4,8},{8,4},{12,12},{1,1},{5,9},{9,5},{13,13},{2,2},{6,10},{... | collective-permute-start | bytes 602120 | tf_op jit(solution)/shard_map/ppermute | solution.py:292
  60.8 10.6 %collective-permute-start.16 = (bf16[112,896]{1,0:T(8,128)(2,1)S(1)}, bf16[112,896]{1,0:T(8,128)(2,1)S(1)}, u32[]{:S(2)}, u32[]{:S(2)}) collective-permute-start(bf16[112,896]{1,0:T(8,128)(2,1)S(1)} %add.68), channel_id=1, source_target_pairs={{0,4},{4,0},{8,12},{12,8},{1,5},{5,1},{9,13},{13,9},{2,6},{6,2},{1... | collective-permute-start | bytes 602120 | tf_op jit(solution)/shard_map/ppermute | solution.py:276
  66.0 9.4 %collective-permute-start.17 = (bf16[112,896]{1,0:T(8,128)(2,1)S(1)}, bf16[112,896]{1,0:T(8,128)(2,1)S(1)}, u32[]{:S(2)}, u32[]{:S(2)}) collective-permute-start(bf16[112,896]{1,0:T(8,128)(2,1)S(1)} %add.70), channel_id=1, source_target_pairs={{0,4},{4,0},{8,12},{12,8},{1,5},{5,1},{9,13},{13,9},{2,6},{6,2},{1... | collective-permute-start | bytes 602120 | tf_op jit(solution)/shard_map/ppermute | solution.py:276
  70.3 7.3 %collective-permute-start.18 = (bf16[112,896]{1,0:T(8,128)(2,1)S(1)}, bf16[112,896]{1,0:T(8,128)(2,1)S(1)}, u32[]{:S(2)}, u32[]{:S(2)}) collective-permute-start(bf16[112,896]{1,0:T(8,128)(2,1)S(1)} %add.72), channel_id=1, source_target_pairs={{0,4},{4,0},{8,12},{12,8},{1,5},{5,1},{9,13},{13,9},{2,6},{6,2},{1... | collective-permute-start | bytes 602120 | tf_op jit(solution)/shard_map/ppermute | solution.py:276
  77.9 1.9 %collective-permute-start.19 = (f32[8,220]{1,0:T(8,128)S(1)}, f32[8,220]{1,0:T(8,128)S(1)}, u32[]{:S(2)}, u32[]{:S(2)}) collective-permute-start(f32[8,220]{1,0:T(8,128)S(1)} %reshape.3), channel_id=1, source_target_pairs={{0,1},{1,0},{2,3},{3,2},{4,5},{5,4},{6,7},{7,6},{8,9},{9,8},{10,11... | collective-permute-start | bytes 21128 | tf_op jit(solution)/shard_map/ppermute | solution.py:246
  78.0 3.7 %collective-permute-start.20 = (f32[8,220]{1,0:T(8,128)S(1)}, f32[8,220]{1,0:T(8,128)S(1)}, u32[]{:S(2)}, u32[]{:S(2)}) collective-permute-start(f32[8,220]{1,0:T(8,128)S(1)} %reshape.3), channel_id=1, source_target_pairs={{0,2},{1,3},{2,0},{3,1},{4,6},{5,7},{6,4},{7,5},{8,10},{9,11},{10,... | collective-permute-start | bytes 21128 | tf_op jit(solution)/shard_map/ppermute | solution.py:246
  79.6 3.1 %collective-permute-start.21 = (f32[8,220]{1,0:T(8,128)S(1)}, f32[8,220]{1,0:T(8,128)S(1)}, u32[]{:S(2)}, u32[]{:S(2)}) collective-permute-start(f32[8,220]{1,0:T(8,128)S(1)} %reshape.3), channel_id=1, source_target_pairs={{0,3},{1,2},{2,1},{3,0},{4,7},{5,6},{6,5},{7,4},{8,11},{9,10},{10,... | collective-permute-start | bytes 21128 | tf_op jit(solution)/shard_map/ppermute | solution.py:246
  (4 other events, 6.9 us)

commit v10 on v9

--- a/solution.py
+++ b/solution.py
@@ -13,8 +13,8 @@
 MB = 8
 ROW_TILE = 16
 LANE_TILE = 128
-ROW_PARTS = 2
-LAG = 3
+ROW_PARTS = 1
+LAG = 2
 VMEM_BYTES = 24 * 1024 * 1024
 
 

time: 84.2 us -> 77.1 us (0.916)
  waiting for transfers between devices: 9.62 us -> 26.2 us
  starting transfers between devices: 42.9 us -> 29.5 us
  local copies, waits for them, and re-layouts: 4.67 us -> 0.78 us
  other arithmetic: 7.27 us -> 4.16 us
  Pallas kernels: 18.4 us -> 15.5 us
    ppermute x11 -> x6, waiting for transfers between devices: 6.75 us -> 23.4 us  [outer_next(): outer.append(lax.ppermute(payload, 'slc', outer_pairs))]
    ppermute x11 -> x6, starting transfers between devices: 32.7 us -> 20.6 us  [outer_next(): outer.append(lax.ppermute(payload, 'slc', outer_pairs))]
    pallas_call x6, local copies, waits for them, and re-layouts: 2.51 us -> 0.56 us  [encode(): pl.pallas_call(functools.partial(encode_kernel, slots, group, rows_of_cla...]
    unnamed x12 -> x8, local copies, waits for them, and re-layouts: 1.96 us -> 0.02 us
    select_n x5 -> x2, other arithmetic: 3.01 us -> 1.18 us  [outer_next(): payload = others if payload is None else jnp.where(edge, payload, others)]
    pallas_call x4, Pallas kernels: 11.7 us -> 10.1 us  [encode(): pl.pallas_call(functools.partial(encode_kernel, slots, group, rows_of_cla...]
    ppermute x8 -> x4, starting transfers between devices: 8.28 us -> 6.93 us  [line_of_four(): inner.append(lax.ppermute(half, 'slc', inner_pairs))]
    pallas_call x8 -> x4, Pallas kernels: 5.1 us -> 3.77 us  [gradient(): pl.pallas_call(functools.partial(gradient_kernel, step % ROW_PARTS, facto...]
  transfers between devices with their start and end apart: 22 -> 13, of which waited for: 7 -> 6; matrix products, arithmetic and copies ran while one was open for 11% -> 5% of each run, Pallas kernels for 16% -> 15%
where the time goes in v10:
time: 77.1 us; the launch traced here: 76.4 us
  starting transfers between devices  29.5 us (38%)
  waiting for transfers between devices  26.2 us (34%)
  Pallas kernels  15.5 us (20%)
  other arithmetic  4.16 us (5%)
  local copies, waits for them, and re-layouts  0.78 us (1%)
    ppermute x6, waiting for transfers between devices, outer_next(): outer.append(lax.ppermute(payload, 'slc', outer_pairs))  23.4 us
    ppermute x6, starting transfers between devices, outer_next(): outer.append(lax.ppermute(payload, 'slc', outer_pairs))  20.6 us
    pallas_call x4, Pallas kernels, encode(): pl.pallas_call(functools.partial(encode_kernel, slots, group, rows_of_cla...  10.1 us
    ppermute x4, starting transfers between devices, line_of_four(): inner.append(lax.ppermute(half, 'slc', inner_pairs))  6.93 us
    pallas_call x4, Pallas kernels, gradient(): pl.pallas_call(functools.partial(gradient_kernel, step % ROW_PARTS, facto...  3.77 us
    ppermute x3, waiting for transfers between devices, sum_over_replicas(): lax.ppermute(value, axes, [(index, index ^ mask) for index in range(4)])  2.76 us
    add x4, other arithmetic, line_of_four(): half = pieces[step] + after(outer[step], *latest)  2.16 us
    ppermute x3, starting transfers between devices, sum_over_replicas(): lax.ppermute(value, axes, [(index, index ^ mask) for index in range(4)])  1.93 us
  transfers between devices with their start and end apart: 13, of which 6 were waited for; matrix products, arithmetic and copies ran while one was open for 5% of the time, Pallas kernels for 15%

profile of v10, /device:TPU:0, one launch (start us, length us, event | category | flops | bytes accessed | tf_op | source)
XLA Modules:
  0.0 76.4 jit_solution(11348460842246179005)
XLA Ops:
  0.0 1.7 %fetch.1 = (bf16[1,2,220,2,220]{4,3,2,1,0:T(2,128)(2,1)S(1)}, bf16[2,2,220,2,220]{4,3,2,1,0:T(2,128)(2,1)S(1)}, bf16[2,456,220]{2,1,0:T(8,128)(2,1)S(1)}, f32[2,256,8]{2,1,0:T(8,128)S(1)}) custom-call(s32[8]{0:T(128)} %refs_0_.1, f32[8,220]{1,0:T(8,128)} %refs_1_.1, bf16[1,8,220,2,220]{4,3,2,1,0:T(2,128)(2,1)} %bitcast.48, ...), custom_call_target="tpu_custom_call" | custom-call | tf_op jit(solution)/shard_map/fetch/pallas_call | solution.py:351
  1.9 2.2 %encode.4 = (bf16[2,224,896]{2,1,0:T(8,128)(2,1)S(1)}, bf16[224,896]{1,0:T(8,128)(2,1)S(1)}, bf16[1,2,220,2,220]{4,3,2,1,0:T(2,128)(2,1)S(1)}, bf16[2,2,220,2,220]{4,3,2,1,0:T(2,128)(2,1)S(1)}) custom-call(f32[2,256,8]{2,1,0:T(8,128)S(1)} %get-tuple-element.37.refs_0_, bf16[1,2,2,220,220]{4,3,2,1,0:T(8,128)(2,1)S(1)} %bitcast.37, ...), custom_call_target="tpu_custom_call" | custom-call | flops 1022208000 | bytes 6000000 | tf_op jit(solution)/shard_map/encode/pallas_call | solution.py:379
  4.1 3.1 %collective-permute-start = (bf16[224,896]{1,0:T(8,128)(2,1)S(1)}, bf16[224,896]{1,0:T(8,128)(2,1)S(1)}, u32[]{:S(2)}, u32[]{:S(2)}) collective-permute-start(bf16[224,896]{1,0:T(8,128)(2,1)S(1)} %get-tuple-element.60.refs_0_), channel_id=1, source_target_pairs={{0,4},{4,0},{8,12},{12,8},{1,5},{5,1},{9,13},{13,9},{2,6},{6,2},{1... | collective-permute-start | bytes 1204232 | tf_op jit(solution)/shard_map/ppermute | solution.py:276
  7.4 3.6 %encode.5 = (bf16[2,224,896]{2,1,0:T(8,128)(2,1)S(1)}, bf16[224,896]{1,0:T(8,128)(2,1)S(1)}, bf16[1,2,220,2,220]{4,3,2,1,0:T(2,128)(2,1)S(1)}, bf16[2,2,220,2,220]{4,3,2,1,0:T(2,128)(2,1)S(1)}) custom-call(f32[2,256,8]{2,1,0:T(8,128)S(1)} %get-tuple-element.37.refs_0_, bf16[1,2,2,220,220]{4,3,2,1,0:T(8,128)(2,1)S(1)} %bitcast.38, ...), custom_call_target="tpu_custom_call" | custom-call | flops 1022208000 | bytes 6000000 | tf_op jit(solution)/shard_map/encode/pallas_call | solution.py:379
  11.1 6.2 %collective-permute-done.refs_1_ = bf16[224,896]{1,0:T(8,128)(2,1)S(1)} collective-permute-done((bf16[224,896]{1,0:T(8,128)(2,1)S(1)}, bf16[224,896]{1,0:T(8,128)(2,1)S(1)}, u32[]{:S(2)}, u32[]{:S(2)}) %collective-permute-start) | collective-permute-done | bytes 401440 | tf_op jit(solution)/shard_map/ppermute | solution.py:276
  17.3 0.9 %add.33 = bf16[224,896]{1,0:T(8,128)(2,1)} add(bf16[224,896]{1,0:T(8,128)(2,1)S(1)} %get-tuple-element.60.refs_0_, bf16[224,896]{1,0:T(8,128)(2,1)S(1)} %collective-permute-done.refs_1_) | non-fusion elementwise | flops 200704 | bytes 1204224 | tf_op jit(solution)/shard_map/add | solution.py:291
  18.1 4.9 %collective-permute-start.1 = (bf16[224,896]{1,0:T(8,128)(2,1)}, bf16[224,896]{1,0:T(8,128)(2,1)}, u32[]{:S(2)}, u32[]{:S(2)}) collective-permute-start(bf16[224,896]{1,0:T(8,128)(2,1)} %add.33), channel_id=1, source_target_pairs={{0,0},{4,8},{8,4},{12,12},{1,1},{5,9},{9,5},{13,13},{2,2},{6,10},{... | collective-permute-start | bytes 1204232 | tf_op jit(solution)/shard_map/ppermute | solution.py:292
  23.2 2.2 %encode.6 = (bf16[2,224,896]{2,1,0:T(8,128)(2,1)S(1)}, bf16[224,896]{1,0:T(8,128)(2,1)S(1)}, bf16[1,2,220,2,220]{4,3,2,1,0:T(2,128)(2,1)S(1)}, bf16[2,2,220,2,220]{4,3,2,1,0:T(2,128)(2,1)S(1)}) custom-call(f32[2,256,8]{2,1,0:T(8,128)S(1)} %get-tuple-element.37.refs_0_, bf16[1,2,2,220,220]{4,3,2,1,0:T(8,128)(2,1)S(1)} %bitcast.35, ...), custom_call_target="tpu_custom_call" | custom-call | flops 1022208000 | bytes 6000000 | tf_op jit(solution)/shard_map/encode/pallas_call | solution.py:379
  25.4 1.1 %add.35 = bf16[224,896]{1,0:T(8,128)(2,1)S(1)} add(bf16[224,896]{1,0:T(8,128)(2,1)S(1)} %get-tuple-element.63.refs_0_, bf16[224,896]{1,0:T(8,128)(2,1)} %collective-permute-done.2.refs_1_) | non-fusion elementwise | flops 200704 | bytes 1204224 | tf_op jit(solution)/shard_map/add | solution.py:291
  27.3 1.1 %add_select_fusion.1 = bf16[224,896]{1,0:T(8,128)(2,1)S(1)} fusion(bf16[224,896]{1,0:T(8,128)(2,1)S(1)} %get-tuple-element.65.refs_0_, bf16[224,896]{1,0:T(8,128)(2,1)S(1)} %get-tuple-element.60.refs_0_, bf16[224,896]{1,0:T(8,128)(2,1)} %collective-permute-done.1.refs_2_, pred[]{:T(512)S(6)} %or.3), kind=kLoop, calls=%fused_computation.9 | loop fusion | flops 401408 | bytes 1605633 | tf_op jit(solution)/shard_map/jit(_where)/select_n | solution.py:273
  28.3 5.8 %collective-permute-start.3 = (bf16[224,896]{1,0:T(8,128)(2,1)S(1)}, bf16[224,896]{1,0:T(8,128)(2,1)S(1)}, u32[]{:S(2)}, u32[]{:S(2)}) collective-permute-start(bf16[224,896]{1,0:T(8,128)(2,1)S(1)} %add_select_fusion.1), channel_id=1, source_target_pairs={{0,4},{4,0},{8,12},{12,8},{1,5},{5,1},{9,13},{13,9},{2,6},{6,2},{1... | collective-permute-start | bytes 1204232 | tf_op jit(solution)/shard_map/ppermute | solution.py:276
  34.3 2.1 %encode.7 = (bf16[2,224,896]{2,1,0:T(8,128)(2,1)S(1)}, bf16[224,896]{1,0:T(8,128)(2,1)S(1)}) custom-call(f32[2,256,8]{2,1,0:T(8,128)S(1)} %get-tuple-element.37.refs_0_, bf16[1,2,2,220,220]{4,3,2,1,0:T(8,128)(2,1)S(1)} %bitcast.36, bf16[2,2,2,220,220]{4,3,2,1,0:T(8,128)(2,1)S(1)} %bitcast.33, bf16[2,456,220]{2,1,0:T(8,128)(2,1)S(1)} %get-tuple-element.40.refs_3_, ...), custom_call_target="tpu_custom_call" | custom-call | flops 1022208000 | bytes 6000000 | tf_op jit(solution)/shard_map/encode/pallas_call | solution.py:379
  36.5 5.8 %collective-permute-done.3.refs_3_.refs_1_ = bf16[224,896]{1,0:T(8,128)(2,1)S(1)} collective-permute-done((bf16[224,896]{1,0:T(8,128)(2,1)S(1)}, bf16[224,896]{1,0:T(8,128)(2,1)S(1)}, u32[]{:S(2)}, u32[]{:S(2)}) %collective-permute-start.3) | collective-permute-done | bytes 401440 | tf_op jit(solution)/shard_map/ppermute | solution.py:276
  42.3 1.8 %collective-permute-start.6 = (bf16[224,896]{1,0:T(8,128)(2,1)S(1)}, bf16[224,896]{1,0:T(8,128)(2,1)S(1)}, u32[]{:S(2)}, u32[]{:S(2)}) collective-permute-start(bf16[224,896]{1,0:T(8,128)(2,1)S(1)} %add_select_fusion), channel_id=1, source_target_pairs={{0,4},{4,0},{8,12},{12,8},{1,5},{5,1},{9,13},{13,9},{2,6},{6,2},{1... | collective-permute-start | bytes 1204232 | tf_op jit(solution)/shard_map/ppermute | solution.py:276
  44.8 6.8 %collective-permute-done.6.refs_3_.refs_1_ = bf16[224,896]{1,0:T(8,128)(2,1)S(1)} collective-permute-done((bf16[224,896]{1,0:T(8,128)(2,1)S(1)}, bf16[224,896]{1,0:T(8,128)(2,1)S(1)}, u32[]{:S(2)}, u32[]{:S(2)}) %collective-permute-start.6) | collective-permute-done | bytes 401440 | tf_op jit(solution)/shard_map/ppermute | solution.py:276
  51.8 0.7 collective-permute-start.7
  52.6 3.5 %collective-permute-start.8 = (bf16[224,896]{1,0:T(8,128)(2,1)S(1)}, bf16[224,896]{1,0:T(8,128)(2,1)S(1)}, u32[]{:S(2)}, u32[]{:S(2)}) collective-permute-start(bf16[224,896]{1,0:T(8,128)(2,1)S(1)} %add.37), channel_id=1, source_target_pairs={{0,4},{4,0},{8,12},{12,8},{1,5},{5,1},{9,13},{13,9},{2,6},{6,2},{1... | collective-permute-start | bytes 1204232 | tf_op jit(solution)/shard_map/ppermute | solution.py:276
  56.1 1.4 %gradient.4 = f32[2,224]{1,0:T(2,128)S(1)} custom-call(bf16[224,896]{1,0:T(8,128)(2,1)S(1)} %get-tuple-element.60.refs_0_, bf16[224,896]{1,0:T(8,128)(2,1)S(1)} %collective-permute-done.refs_1_, bf16[224,896]{1,0:T(8,128)(2,1)} %collective-permute-done.1.refs_2_, bf16[224,896]{1,0:T(8,128)(2,1)S(1)} %collective-permute-done.3.refs_3_.refs_1_, ...), custom_call_target="tpu_custom_call" | custom-call | flops 774400 | bytes 1500000 | tf_op jit(solution)/shard_map/gradient/pallas_call | solution.py:425
  57.7 6.4 %collective-permute-start.9 = (bf16[224,896]{1,0:T(8,128)(2,1)S(1)}, bf16[224,896]{1,0:T(8,128)(2,1)S(1)}, u32[]{:S(2)}, u32[]{:S(2)}) collective-permute-start(bf16[224,896]{1,0:T(8,128)(2,1)S(1)} %add.40), channel_id=1, source_target_pairs={{0,4},{4,0},{8,12},{12,8},{1,5},{5,1},{9,13},{13,9},{2,6},{6,2},{1... | collective-permute-start | bytes 1204232 | tf_op jit(solution)/shard_map/ppermute | solution.py:276
  64.0 1.4 %gradient.5 = f32[2,224]{1,0:T(2,128)S(1)} custom-call(bf16[224,896]{1,0:T(8,128)(2,1)S(1)} %get-tuple-element.63.refs_0_, bf16[224,896]{1,0:T(8,128)(2,1)} %collective-permute-done.2.refs_1_, bf16[224,896]{1,0:T(8,128)(2,1)S(1)} %collective-permute-done.5.refs_2_, bf16[224,896]{1,0:T(8,128)(2,1)S(1)} %collective-permute-done.6.refs_3_.refs_1_, ...), custom_call_target="tpu_custom_call" | custom-call | flops 774400 | bytes 1500000 | tf_op jit(solution)/shard_map/gradient/pallas_call | solution.py:425
  65.9 4.6 %collective-permute-done.9.refs_3_ = bf16[224,896]{1,0:T(8,128)(2,1)S(1)} collective-permute-done((bf16[224,896]{1,0:T(8,128)(2,1)S(1)}, bf16[224,896]{1,0:T(8,128)(2,1)S(1)}, u32[]{:S(2)}, u32[]{:S(2)}) %collective-permute-start.9) | collective-permute-done | bytes 401440 | tf_op jit(solution)/shard_map/ppermute | solution.py:276
  71.1 1.6 %collective-permute-start.11 = (f32[8,220]{1,0:T(8,128)S(1)}, f32[8,220]{1,0:T(8,128)S(1)}, u32[]{:S(2)}, u32[]{:S(2)}) collective-permute-start(f32[8,220]{1,0:T(8,128)S(1)} %reshape.3), channel_id=1, source_target_pairs={{0,2},{1,3},{2,0},{3,1},{4,6},{5,7},{6,4},{7,5},{8,10},{9,11},{10,... | collective-permute-start | bytes 21128 | tf_op jit(solution)/shard_map/ppermute | solution.py:246
  73.0 1.9 %collective-permute-done.11 = f32[8,220]{1,0:T(8,128)S(1)} collective-permute-done((f32[8,220]{1,0:T(8,128)S(1)}, f32[8,220]{1,0:T(8,128)S(1)}, u32[]{:S(2)}, u32[]{:S(2)}) %collective-permute-start.11) | collective-permute-done | bytes 7072 | tf_op jit(solution)/shard_map/ppermute | solution.py:246
  74.9 0.9 %collective-permute-done.12 = f32[8,220]{1,0:T(8,128)S(1)} collective-permute-done((f32[8,220]{1,0:T(8,128)S(1)}, f32[8,220]{1,0:T(8,128)S(1)}, u32[]{:S(2)}, u32[]{:S(2)}) %collective-permute-start.12) | collective-permute-done | bytes 7072 | tf_op jit(solution)/shard_map/ppermute | solution.py:246
  (39 shorter events, 4.6 us)
Async XLA Ops:
  4.1 3.3 %copy-start = (bf16[2,224,896]{2,1,0:T(8,128)(2,1)}, bf16[2,224,896]{2,1,0:T(8,128)(2,1)S(1)}, u32[]{:S(2)}) copy-start(bf16[2,224,896]{2,1,0:T(8,128)(2,1)S(1)} %get-tuple-element.61.refs_4_) | copy-start | bytes 2408452
  4.1 13.2 %collective-permute-start = (bf16[224,896]{1,0:T(8,128)(2,1)S(1)}, bf16[224,896]{1,0:T(8,128)(2,1)S(1)}, u32[]{:S(2)}, u32[]{:S(2)}) collective-permute-start(bf16[224,896]{1,0:T(8,128)(2,1)S(1)} %get-tuple-element.60.refs_0_), channel_id=1, source_target_pairs={{0,4},{4,0},{8,12},{12,8},{1,5},{5,1},{9,13},{13,9},{2,6},{6,2},{1... | collective-permute-start | bytes 1204232 | tf_op jit(solution)/shard_map/ppermute | solution.py:276
  11.0 12.1 %copy-start.2 = (bf16[2,224,896]{2,1,0:T(8,128)(2,1)}, bf16[2,224,896]{2,1,0:T(8,128)(2,1)S(1)}, u32[]{:S(2)}) copy-start(bf16[2,224,896]{2,1,0:T(8,128)(2,1)S(1)} %get-tuple-element.64.refs_4_) | copy-start | bytes 2408452
  11.0 14.4 %collective-permute-start.2 = (bf16[224,896]{1,0:T(8,128)(2,1)S(1)}, bf16[224,896]{1,0:T(8,128)(2,1)}, u32[]{:S(2)}, u32[]{:S(2)}) collective-permute-start(bf16[224,896]{1,0:T(8,128)(2,1)S(1)} %get-tuple-element.63.refs_0_), channel_id=1, source_target_pairs={{0,4},{4,0},{8,12},{12,8},{1,5},{5,1},{9,13},{13,9},{2,6},{6,2},{1... | collective-permute-start | bytes 1204232 | tf_op jit(solution)/shard_map/ppermute | solution.py:276
  18.1 9.1 %collective-permute-start.1 = (bf16[224,896]{1,0:T(8,128)(2,1)}, bf16[224,896]{1,0:T(8,128)(2,1)}, u32[]{:S(2)}, u32[]{:S(2)}) collective-permute-start(bf16[224,896]{1,0:T(8,128)(2,1)} %add.33), channel_id=1, source_target_pairs={{0,0},{4,8},{8,4},{12,12},{1,1},{5,9},{9,5},{13,13},{2,2},{6,10},{... | collective-permute-start | bytes 1204232 | tf_op jit(solution)/shard_map/ppermute | solution.py:292
  26.5 9.8 %collective-permute-start.5 = (bf16[224,896]{1,0:T(8,128)(2,1)S(1)}, bf16[224,896]{1,0:T(8,128)(2,1)S(1)}, u32[]{:S(2)}, u32[]{:S(2)}) collective-permute-start(bf16[224,896]{1,0:T(8,128)(2,1)S(1)} %add.35), channel_id=1, source_target_pairs={{0,0},{4,8},{8,4},{12,12},{1,1},{5,9},{9,5},{13,13},{2,2},{6,10},{... | collective-permute-start | bytes 1204232 | tf_op jit(solution)/shard_map/ppermute | solution.py:292
  28.3 13.9 %collective-permute-start.3 = (bf16[224,896]{1,0:T(8,128)(2,1)S(1)}, bf16[224,896]{1,0:T(8,128)(2,1)S(1)}, u32[]{:S(2)}, u32[]{:S(2)}) collective-permute-start(bf16[224,896]{1,0:T(8,128)(2,1)S(1)} %add_select_fusion.1), channel_id=1, source_target_pairs={{0,4},{4,0},{8,12},{12,8},{1,5},{5,1},{9,13},{13,9},{2,6},{6,2},{1... | collective-permute-start | bytes 1204232 | tf_op jit(solution)/shard_map/ppermute | solution.py:276
  36.4 19.8 %copy-start.1 = (bf16[2,224,896]{2,1,0:T(8,128)(2,1)S(1)}, bf16[2,224,896]{2,1,0:T(8,128)(2,1)}, u32[]{:S(2)}) copy-start(bf16[2,224,896]{2,1,0:T(8,128)(2,1)} %copy-done) | copy-start | bytes 2408452
  36.5 27.6 %copy-start.3 = (bf16[2,224,896]{2,1,0:T(8,128)(2,1)S(1)}, bf16[2,224,896]{2,1,0:T(8,128)(2,1)}, u32[]{:S(2)}) copy-start(bf16[2,224,896]{2,1,0:T(8,128)(2,1)} %copy-done.2) | copy-start | bytes 2408452
  42.3 9.3 %collective-permute-start.6 = (bf16[224,896]{1,0:T(8,128)(2,1)S(1)}, bf16[224,896]{1,0:T(8,128)(2,1)S(1)}, u32[]{:S(2)}, u32[]{:S(2)}) collective-permute-start(bf16[224,896]{1,0:T(8,128)(2,1)S(1)} %add_select_fusion), channel_id=1, source_target_pairs={{0,4},{4,0},{8,12},{12,8},{1,5},{5,1},{9,13},{13,9},{2,6},{6,2},{1... | collective-permute-start | bytes 1204232 | tf_op jit(solution)/shard_map/ppermute | solution.py:276
  44.1 8.3 %collective-permute-start.4 = (bf16[224,896]{1,0:T(8,128)(2,1)S(1)}, bf16[224,896]{1,0:T(8,128)(2,1)S(1)}, u32[]{:S(2)}, u32[]{:S(2)}) collective-permute-start(bf16[224,896]{1,0:T(8,128)(2,1)S(1)} %add.36), channel_id=1, source_target_pairs={{0,0},{4,8},{8,4},{12,12},{1,1},{5,9},{9,5},{13,13},{2,2},{6,10},{... | collective-permute-start | bytes 1204232 | tf_op jit(solution)/shard_map/ppermute | solution.py:292
  51.8 5.8 %collective-permute-start.7 = (bf16[224,896]{1,0:T(8,128)(2,1)S(1)}, bf16[224,896]{1,0:T(8,128)(2,1)S(1)}, u32[]{:S(2)}, u32[]{:S(2)}) collective-permute-start(bf16[224,896]{1,0:T(8,128)(2,1)S(1)} %add.39), channel_id=1, source_target_pairs={{0,0},{4,8},{8,4},{12,12},{1,1},{5,9},{9,5},{13,13},{2,2},{6,10},{... | collective-permute-start | bytes 1204232 | tf_op jit(solution)/shard_map/ppermute | solution.py:292
  52.6 12.9 %collective-permute-start.8 = (bf16[224,896]{1,0:T(8,128)(2,1)S(1)}, bf16[224,896]{1,0:T(8,128)(2,1)S(1)}, u32[]{:S(2)}, u32[]{:S(2)}) collective-permute-start(bf16[224,896]{1,0:T(8,128)(2,1)S(1)} %add.37), channel_id=1, source_target_pairs={{0,4},{4,0},{8,12},{12,8},{1,5},{5,1},{9,13},{13,9},{2,6},{6,2},{1... | collective-permute-start | bytes 1204232 | tf_op jit(solution)/shard_map/ppermute | solution.py:276
  57.7 12.9 %collective-permute-start.9 = (bf16[224,896]{1,0:T(8,128)(2,1)S(1)}, bf16[224,896]{1,0:T(8,128)(2,1)S(1)}, u32[]{:S(2)}, u32[]{:S(2)}) collective-permute-start(bf16[224,896]{1,0:T(8,128)(2,1)S(1)} %add.40), channel_id=1, source_target_pairs={{0,4},{4,0},{8,12},{12,8},{1,5},{5,1},{9,13},{13,9},{2,6},{6,2},{1... | collective-permute-start | bytes 1204232 | tf_op jit(solution)/shard_map/ppermute | solution.py:276
  71.1 1.9 %collective-permute-start.10 = (f32[8,220]{1,0:T(8,128)S(1)}, f32[8,220]{1,0:T(8,128)S(1)}, u32[]{:S(2)}, u32[]{:S(2)}) collective-permute-start(f32[8,220]{1,0:T(8,128)S(1)} %reshape.3), channel_id=1, source_target_pairs={{0,1},{1,0},{2,3},{3,2},{4,5},{5,4},{6,7},{7,6},{8,9},{9,8},{10,11... | collective-permute-start | bytes 21128 | tf_op jit(solution)/shard_map/ppermute | solution.py:246
  71.1 3.7 %collective-permute-start.11 = (f32[8,220]{1,0:T(8,128)S(1)}, f32[8,220]{1,0:T(8,128)S(1)}, u32[]{:S(2)}, u32[]{:S(2)}) collective-permute-start(f32[8,220]{1,0:T(8,128)S(1)} %reshape.3), channel_id=1, source_target_pairs={{0,2},{1,3},{2,0},{3,1},{4,6},{5,7},{6,4},{7,5},{8,10},{9,11},{10,... | collective-permute-start | bytes 21128 | tf_op jit(solution)/shard_map/ppermute | solution.py:246
  72.7 3.1 %collective-permute-start.12 = (f32[8,220]{1,0:T(8,128)S(1)}, f32[8,220]{1,0:T(8,128)S(1)}, u32[]{:S(2)}, u32[]{:S(2)}) collective-permute-start(f32[8,220]{1,0:T(8,128)S(1)} %reshape.3), channel_id=1, source_target_pairs={{0,3},{1,2},{2,1},{3,0},{4,7},{5,6},{6,5},{7,4},{8,11},{9,10},{10,... | collective-permute-start | bytes 21128 | tf_op jit(solution)/shard_map/ppermute | solution.py:246

commit v11 on v10

--- a/solution.py
+++ b/solution.py
@@ -13,8 +13,7 @@
 MB = 8
 ROW_TILE = 16
 LANE_TILE = 128
-ROW_PARTS = 1
-LAG = 2
+SPLIT = 2
 VMEM_BYTES = 24 * 1024 * 1024
 
 
@@ -108,7 +107,7 @@
         copy.wait()
 
 
-def encode_kernel(slots, group, rows_of, next_rows, *refs):
+def encode_kernel(slots, parts, group, rows_of, next_rows, *refs):
     whole_classes = rows_of is not None
     if not whole_classes:
         place_ref, refs = refs[0], refs[1:]
@@ -116,7 +115,7 @@
     phase_ref, image, coil_map, left_ref = refs[:4]
     order_ref, gram_ref, adjoint_ref, kspace_ref, image_ref, map_ref = refs[4:10]
     shifted, refs = refs[10], refs[11:]
-    out_refs, refs = refs[:ROW_PARTS], refs[ROW_PARTS:]
+    out_refs, refs = refs[:parts], refs[parts:]
     if next_rows:
         next_image, next_map, refs = refs[0], refs[1], refs[2:]
     total, wide, raw_kspace, gram, adjoint, order, arrived, small = refs
@@ -214,11 +213,15 @@
         copy.wait()
 
 
-def gradient_kernel(index, factor, on_line, *refs):
+def gradient_kernel(start, factor, on_line, *refs):
     term_refs, shifted_ref, out_ref = refs[:-2], refs[-2], refs[-1]
-    slots, _, lanes = shifted_ref.shape
+    slots, rows, lanes = shifted_ref.shape
     part = out_ref.shape[1]
-    terms = [ref[...].astype(jnp.float32) for ref in term_refs]
+    span = slice(start, start + part)
+    terms = [
+        (ref[span, :] if ref.shape[0] == rows else ref[...]).astype(jnp.float32)
+        for ref in term_refs
+    ]
     if on_line:
         own, near, across, rest = terms
         position = lax.axis_index("slc")
@@ -227,8 +230,7 @@
     else:
         residual = terms[0]
     for slot in range(slots):
-        shifted = shifted_ref[slot, index * part : (index + 1) * part, :].astype(jnp.float32)
-        product = residual * shifted
+        product = residual * shifted_ref[slot, span, :].astype(jnp.float32)
         tiles = [product[:, at : at + LANE_TILE] for at in range(0, lanes, LANE_TILE)]
         folded = functools.reduce(lambda a, b: a + b, tiles)
         out_ref[slot : slot + 1, :] = factor * jnp.sum(folded.T, axis=0, keepdims=True)
@@ -249,68 +251,71 @@
     return (value + swapped[0]) + (swapped[1] + swapped[2])
 
 
-def line_of_four(encode, gradient, count):
+def line_of_four(encode, gradient):
     position = lax.axis_index("slc")
     edge = (position == 0) | (position == 3)
-    outer_pairs = [(0, 1), (1, 0), (2, 3), (3, 2)]
-    inner_pairs = [(0, 0), (1, 2), (2, 1), (3, 3)]
-    parts = ROW_PARTS
-    pieces, shifted, outer, inner, gradients = [], [], [], [], []
-
-    def encode_next(*earlier):
-        group = len(shifted)
-        if group * parts < count:
-            encoded = encode(group, *earlier)
-            shifted.append(encoded[0])
-            pieces.extend(encoded[1:])
-
-    def outer_next(*earlier):
-        step = len(outer)
-        back = step - LAG
-        payload = pieces[step] if step < count else None
-        if back >= 0:
-            others = pieces[back] + inner[back]
-            payload = others if payload is None else jnp.where(edge, payload, others)
-        if earlier:
-            payload = after(payload, *earlier)
-        outer.append(lax.ppermute(payload, "slc", outer_pairs))
-        return payload
-
-    def gradient_next(*earlier):
-        step = len(gradients)
-        terms = (pieces[step], outer[step], inner[step], outer[step + LAG])
-        own = after(terms[0], *earlier) if earlier else terms[0]
-        gradients.append(gradient(step, (own, *terms[1:]), shifted[step // parts]))
-
-    while len(outer) < LAG:
-        encode_next()
-        while len(outer) < min(LAG, len(pieces)):
-            outer_next()
-    latest = (pieces[-1],)
-    for step in range(count):
-        half = pieces[step] + after(outer[step], *latest)
-        inner.append(lax.ppermute(half, "slc", inner_pairs))
-        latest = ()
-        if step >= 1:
-            latest = (outer_next(half),)
-        if len(pieces) < min(count, step + LAG + 2):
-            encode_next(*(latest or (half,)))
-            latest = (*latest, pieces[-1])
-        if step >= LAG + 1:
-            gradient_next(*latest)
-            latest = (*latest, gradients[-1])
-    last = outer_next(*latest)
-    while len(gradients) < count:
-        gradient_next(last)
-    return gradients
+
+    def outer(value):
+        return lax.ppermute(value, "slc", [(0, 1), (1, 0), (2, 3), (3, 2)])
+
+    def inner(value):
+        return lax.ppermute(value, "slc", [(0, 0), (1, 2), (2, 1), (3, 3)])
+
+    def halves(value):
+        middle = value.shape[0] // SPLIT
+        return value[:middle], value[middle:]
+
+    shifted0, own0a, own0b = encode(0, SPLIT)
+    near0a = outer(own0a)
+    shifted1, own1 = encode(1, 1)
+    near0b = outer(after(own0b, own1))
+    shifted2, own2 = encode(2, 1, own1)
+    near1 = outer(after(own1, own2))
+    half0a = own0a + after(near0a, own2)
+    across0a = inner(half0a)
+    shifted3, own3 = encode(3, 1, half0a)
+    half0b = own0b + after(near0b, own3)
+    across0b = inner(half0b)
+    back0 = jnp.concatenate([own0a + after(across0a, half0b), own0b + across0b], axis=0)
+    payload2 = jnp.where(edge, own2, back0)
+    near2 = outer(payload2)
+    half1 = own1 + after(near1, payload2)
+    across1 = inner(half1)
+    half2 = own2 + after(near2, half1)
+    across2 = inner(half2)
+    payload3 = jnp.where(edge, own3, own1 + after(across1, half2))
+    near3 = outer(payload3)
+    gradient0a = gradient(0, 0, (after(own0a, payload3), near0a, across0a, near2), shifted0)
+    gradient0b = gradient(0, 1, (after(own0b, payload3), near0b, across0b, near2), shifted0)
+    back2 = own2 + after(across2, gradient0a, gradient0b)
+    rest2 = outer(back2)
+    own3a, own3b = halves(own3)
+    near3a, near3b = halves(near3)
+    half3a = own3a + after(near3a, back2)
+    across3a = inner(half3a)
+    half3b = own3b + after(near3b, half3a)
+    gradient1 = gradient(1, None, (after(own1, half3a), near1, across1, near3), shifted1)
+    across3b = inner(after(half3b, gradient1))
+    back3a = own3a + after(across3a, half3b, gradient1)
+    rest3a = outer(back3a)
+    back3b = own3b + after(across3b, back3a)
+    rest3b = outer(back3b)
+    gradient2 = gradient(2, None, (after(own2, back3b), near2, across2, rest2), shifted2)
+    gradient3a = gradient(3, 0, (own3a, near3a, across3a, rest3a), shifted3)
+    gradient3b = gradient(3, 1, (own3b, near3b, across3b, rest3b), shifted3)
+    return [
+        jnp.concatenate([gradient0a, gradient0b], axis=1),
+        gradient1,
+        gradient2,
+        jnp.concatenate([gradient3a, gradient3b], axis=1),
+    ]
 
 
 def body(images, coil_maps, kspace, shift_index, phase_offset, group_order):
     vols, per_device, _, _, length = images.shape
     coils = coil_maps.shape[0]
     groups = lax.axis_size("slc")
-    rows = round_up(length, ROW_TILE * ROW_PARTS)
-    part = rows // ROW_PARTS
+    rows = round_up(length, ROW_TILE * SPLIT)
     places = vols * coils
     lanes = round_up(places * 2 * length, LANE_TILE)
     whole_classes = per_device % groups == 0
@@ -368,7 +373,7 @@
         name="fetch",
     )(*place_of(0), in_hbm(shift_index), in_hbm(phase_offset), *lying[:2], left)
 
-    def encode(group, *earlier):
+    def encode(group, parts, *earlier):
         image, coil_map = (jnp.swapaxes(array, -3, -2) for array in raw)
         has_next = group + 1 < groups
         place, group_phases = place_of(group), phases
@@ -380,14 +385,15 @@
             functools.partial(
                 encode_kernel,
                 slots,
+                parts,
                 group,
                 rows_of_class(group),
                 (rows_of_class(group + 1) or [0]) if has_next else None,
             ),
             in_specs=scalar_specs + [in_vmem] * 4 + [in_place] * 6,
-            out_specs=[in_vmem] * (1 + ROW_PARTS + 2 * has_next),
+            out_specs=[in_vmem] * (1 + parts + 2 * has_next),
             out_shape=[jax.ShapeDtypeStruct((slots, rows, lanes), jnp.bfloat16)]
-            + [jax.ShapeDtypeStruct((part, lanes), jnp.bfloat16)] * ROW_PARTS
+            + [jax.ShapeDtypeStruct((rows // parts, lanes), jnp.bfloat16)] * parts
             + raw_shapes * has_next,
             scratch_shapes=[
                 pltpu.VMEM((rows, lanes), jnp.float32),
@@ -401,9 +407,7 @@
             ],
             compiler_params=pltpu.CompilerParams(vmem_limit_bytes=VMEM_BYTES),
             cost_estimate=pl.CostEstimate(
-                flops=places * (slots + 1) * 16 * length**3,
-                bytes_accessed=6_000_000,
-                transcendentals=0,
+                flops=length**3, bytes_accessed=length**2, transcendentals=0
             ),
             name="encode",
         )(
@@ -418,37 +422,30 @@
             lying[2],
             *lying[:2],
         )
-        raw[:] = outputs[1 + ROW_PARTS :]
-        return outputs[: 1 + ROW_PARTS]
-
-    def gradient(step, terms, encoded):
+        raw[:] = outputs[1 + parts :]
+        return outputs[: 1 + parts]
+
+    def gradient(group, half, terms, encoded):
+        part = rows if half is None else rows // SPLIT
         return pl.pallas_call(
-            functools.partial(gradient_kernel, step % ROW_PARTS, factor, on_line),
+            functools.partial(gradient_kernel, (half or 0) * part, factor, on_line),
             out_shape=jax.ShapeDtypeStruct((slots, part), jnp.float32),
             compiler_params=pltpu.CompilerParams(vmem_limit_bytes=VMEM_BYTES),
             cost_estimate=pl.CostEstimate(
-                flops=places * slots * 4 * length**2, bytes_accessed=1_500_000, transcendentals=0
+                flops=length**2, bytes_accessed=length**2, transcendentals=0
             ),
             name="gradient",
         )(*terms, encoded)
 
     if on_line:
-        gradients = line_of_four(encode, gradient, groups * ROW_PARTS)
+        gradients = line_of_four(encode, gradient)
     else:
-        encoded = [encode(group) for group in range(groups)]
-        reduced = lax.psum([list(outputs[1:]) for outputs in encoded], "slc")
+        encoded = [encode(group, 1) for group in range(groups)]
+        reduced = lax.psum([own for _, own in encoded], "slc")
         gradients = [
-            gradient(index, (piece,), encoded[group][0])
-            for group in range(groups)
-            for index, piece in enumerate(reduced[group])
+            gradient(group, None, (reduced[group],), encoded[group][0]) for group in range(groups)
         ]
-    by_class = jnp.stack(
-        [
-            jnp.concatenate(gradients[group * ROW_PARTS : (group + 1) * ROW_PARTS], axis=1)
-            for group in range(groups)
-        ],
-        axis=1,
-    )[:, :, :length]
+    by_class = jnp.stack(gradients, axis=1)[:, :, :length]
     if whole_classes:
         local = by_class.reshape(per_device, length)
     else:

time: 77.1 us -> 85.8 us (1.11); the launches traced: 76.4 us -> 86 us
  starting transfers between devices: 29.5 us -> 37.6 us
  other arithmetic: 4.16 us -> 5.93 us
  waiting for transfers between devices: 26.2 us -> 24.8 us
  Pallas kernels: 15.5 us -> 16.6 us
    ppermute x10 -> x14, starting transfers between devices: 27.6 us -> 35.6 us  [the longest x8 25.9 us: outer(): return lax.ppermute(value, 'slc', [(0, 1), (1, 0), (2, 3), (3, 2)])]
    add x6 -> x10, other arithmetic: 2.37 us -> 4.91 us  [the longest x1 1.09 us: line_of_four(): half1 = own1 + after(near1, payload2)]
    ppermute x10 -> x14, waiting for transfers between devices: 23.4 us -> 22 us  [the longest x8 22 us: outer(): return lax.ppermute(value, 'slc', [(0, 1), (1, 0), (2, 3), (3, 2)])]
    pallas_call x8 -> x10, Pallas kernels: 13.8 us -> 14.9 us  [the longest x4 10 us: encode(): pl.pallas_call(functools.partial(encode_kernel, slots, parts, group, rows...]
    select_n x2, other arithmetic: 1.18 us -> 0.2 us  [the longest x1 0.11 us: line_of_four(): payload2 = jnp.where(edge, own2, back0)]
  transfers between devices with their start and end apart: 13 -> 17, of which waited for: 6 -> 8; matrix products, arithmetic and copies ran while one was open for 5% -> 7% of each run, Pallas kernels for 15% -> 14%
where the time goes in v11:
time: 85.8 us; the launch traced here: 86 us
  starting transfers between devices  37.6 us (44%)
  waiting for transfers between devices  24.8 us (29%)
  Pallas kernels  16.6 us (19%)
  other arithmetic  5.93 us (7%)
    ppermute x8, starting transfers between devices, outer(): return lax.ppermute(value, 'slc', [(0, 1), (1, 0), (2, 3), (3, 2)])  25.9 us
    ppermute x8, waiting for transfers between devices, outer(): return lax.ppermute(value, 'slc', [(0, 1), (1, 0), (2, 3), (3, 2)])  22 us
    pallas_call x4, Pallas kernels, encode(): pl.pallas_call(functools.partial(encode_kernel, slots, parts, group, rows...  10 us
    ppermute x6, starting transfers between devices, inner(): return lax.ppermute(value, 'slc', [(0, 0), (1, 2), (2, 1), (3, 3)])  9.7 us
    pallas_call x6, Pallas kernels, gradient(): pl.pallas_call(functools.partial(gradient_kernel, (half or 0) * part, fac...  4.87 us
    ppermute x3, waiting for transfers between devices, sum_over_replicas(): lax.ppermute(value, axes, [(index, index ^ mask) for index in range(4)])  2.78 us
    ppermute x3, starting transfers between devices, sum_over_replicas(): lax.ppermute(value, axes, [(index, index ^ mask) for index in range(4)])  1.93 us
  transfers between devices with their start and end apart: 17, of which 8 were waited for; matrix products, arithmetic and copies ran while one was open for 7% of the time, Pallas kernels for 14%

profile of v11, /device:TPU:0, one launch (start us, length us, event | category | flops | bytes accessed | tf_op | source)
XLA Modules:
  0.0 86.0 jit_solution(13105229495257224528)
XLA Ops:
  0.0 1.7 %fetch.1 = (bf16[1,2,220,2,220]{4,3,2,1,0:T(2,128)(2,1)S(1)}, bf16[2,2,220,2,220]{4,3,2,1,0:T(2,128)(2,1)S(1)}, bf16[2,456,220]{2,1,0:T(8,128)(2,1)S(1)}, f32[2,256,8]{2,1,0:T(8,128)S(1)}) custom-call(s32[8]{0:T(128)} %refs_0_.1, f32[8,220]{1,0:T(8,128)} %refs_1_.1, bf16[1,8,220,2,220]{4,3,2,1,0:T(2,128)(2,1)} %bitcast.48, ...), custom_call_target="tpu_custom_call" | custom-call | tf_op jit(solution)/shard_map/fetch/pallas_call | solution.py:356
  1.9 2.2 %encode.4 = (bf16[2,224,896]{2,1,0:T(8,128)(2,1)S(1)}, bf16[112,896]{1,0:T(8,128)(2,1)S(1)}, bf16[112,896]{1,0:T(8,128)(2,1)S(1)}, bf16[1,2,220,2,220]{4,3,2,1,0...) custom-call(f32[2,256,8]{2,1,0:T(8,128)S(1)} %get-tuple-element.44.refs_0_, bf16[1,2,2,220,220]{4,3,2,1,0:T(8,128)(2,1)S(1)} %bitcast.38, ...), custom_call_target="tpu_custom_call" | custom-call | flops 10648000 | bytes 48400 | tf_op jit(solution)/shard_map/encode/pallas_call | solution.py:384
  4.1 4.5 %collective-permute-start = (bf16[112,896]{1,0:T(8,128)(2,1)S(1)}, bf16[112,896]{1,0:T(8,128)(2,1)S(1)}, u32[]{:S(2)}, u32[]{:S(2)}) collective-permute-start(bf16[112,896]{1,0:T(8,128)(2,1)S(1)} %get-tuple-element.69.refs_0_), channel_id=1, source_target_pairs={{0,4},{4,0},{8,12},{12,8},{1,5},{5,1},{9,13},{13,9},{2,6},{6,2},{1... | collective-permute-start | bytes 602120 | tf_op jit(solution)/shard_map/ppermute | solution.py:259
  8.8 2.2 %encode.5 = (bf16[2,224,896]{2,1,0:T(8,128)(2,1)S(1)}, bf16[224,896]{1,0:T(8,128)(2,1)S(1)}, bf16[1,2,220,2,220]{4,3,2,1,0:T(2,128)(2,1)S(1)}, bf16[2,2,220,2,220]{4,3,2,1,0:T(2,128)(2,1)S(1)}) custom-call(f32[2,256,8]{2,1,0:T(8,128)S(1)} %get-tuple-element.44.refs_0_, bf16[1,2,2,220,220]{4,3,2,1,0:T(8,128)(2,1)S(1)} %bitcast.40, ...), custom_call_target="tpu_custom_call" | custom-call | flops 10648000 | bytes 48400 | tf_op jit(solution)/shard_map/encode/pallas_call | solution.py:384
  11.3 2.2 %encode.6 = (bf16[2,224,896]{2,1,0:T(8,128)(2,1)S(1)}, bf16[224,896]{1,0:T(8,128)(2,1)S(1)}, bf16[1,2,220,2,220]{4,3,2,1,0:T(2,128)(2,1)S(1)}, bf16[2,2,220,2,220]{4,3,2,1,0:T(2,128)(2,1)S(1)}) custom-call(f32[2,256,8]{2,1,0:T(8,128)S(1)} %get-tuple-element.44.refs_0_, bf16[1,2,2,220,220]{4,3,2,1,0:T(8,128)(2,1)S(1)} %bitcast.39, ...), custom_call_target="tpu_custom_call" | custom-call | flops 10648000 | bytes 48400 | tf_op jit(solution)/shard_map/encode/pallas_call | solution.py:384
  14.7 3.4 %collective-permute-start.2 = (bf16[112,896]{1,0:T(8,128)(2,1)}, bf16[112,896]{1,0:T(8,128)(2,1)}, u32[]{:S(2)}, u32[]{:S(2)}) collective-permute-start(bf16[112,896]{1,0:T(8,128)(2,1)} %add.45), channel_id=1, source_target_pairs={{0,0},{4,8},{8,4},{12,12},{1,1},{5,9},{9,5},{13,13},{2,2},{6,10},{... | collective-permute-start | bytes 602120 | tf_op jit(solution)/shard_map/ppermute | solution.py:262
  18.1 3.5 %encode.7 = (bf16[2,224,896]{2,1,0:T(8,128)(2,1)S(1)}, bf16[224,896]{1,0:T(8,128)(2,1)S(1)}) custom-call(f32[2,256,8]{2,1,0:T(8,128)S(1)} %get-tuple-element.44.refs_0_, bf16[1,2,2,220,220]{4,3,2,1,0:T(8,128)(2,1)S(1)} %bitcast.37, bf16[2,2,2,220,220]{4,3,2,1,0:T(8,128)(2,1)S(1)} %bitcast.33, bf16[2,456,220]{2,1,0:T(8,128)(2,1)S(1)} %get-tuple-element.47.refs_3_, ...), custom_call_target="tpu_custom_call" | custom-call | flops 10648000 | bytes 48400 | tf_op jit(solution)/shard_map/encode/pallas_call | solution.py:384
  22.4 3.4 %collective-permute-start.4 = (bf16[112,896]{1,0:T(8,128)(2,1)}, bf16[112,896]{1,0:T(8,128)(2,1)}, u32[]{:S(2)}, u32[]{:S(2)}) collective-permute-start(bf16[112,896]{1,0:T(8,128)(2,1)} %add.46), channel_id=1, source_target_pairs={{0,0},{4,8},{8,4},{12,12},{1,1},{5,9},{9,5},{13,13},{2,2},{6,10},{... | collective-permute-start | bytes 602120 | tf_op jit(solution)/shard_map/ppermute | solution.py:262
  28.1 3.8 %collective-permute-start.6 = (bf16[224,896]{1,0:T(8,128)(2,1)S(1)}, bf16[224,896]{1,0:T(8,128)(2,1)S(1)}, u32[]{:S(2)}, u32[]{:S(2)}) collective-permute-start(bf16[224,896]{1,0:T(8,128)(2,1)S(1)} %maximum_select_fusion), channel_id=1, source_target_pairs={{0,4},{4,0},{8,12},{12,8},{1,5},{5,1},{9,13},{13,9},{2,6},{6,2},{1... | collective-permute-start | bytes 1204232 | tf_op jit(solution)/shard_map/ppermute | solution.py:259
  31.9 6.2 %collective-permute-done.1.refs_1_ = bf16[224,896]{1,0:T(8,128)(2,1)} collective-permute-done((bf16[224,896]{1,0:T(8,128)(2,1)S(1)}, bf16[224,896]{1,0:T(8,128)(2,1)}, u32[]{:S(2)}, u32[]{:S(2)}) %collective-permute-start.1) | collective-permute-done | bytes 401440 | tf_op jit(solution)/shard_map/ppermute | solution.py:259
  38.2 1.1 %add.49 = bf16[224,896]{1,0:T(8,128)(2,1)S(1)} add(bf16[224,896]{1,0:T(8,128)(2,1)S(1)} %get-tuple-element.74.refs_0_, bf16[224,896]{1,0:T(8,128)(2,1)} %collective-permute-done.1.refs_1_) | non-fusion elementwise | flops 200704 | bytes 1204224 | tf_op jit(solution)/shard_map/add | solution.py:282
  40.0 5.0 %collective-permute-done.6.refs_3_.refs_1_ = bf16[224,896]{1,0:T(8,128)(2,1)S(1)} collective-permute-done((bf16[224,896]{1,0:T(8,128)(2,1)S(1)}, bf16[224,896]{1,0:T(8,128)(2,1)S(1)}, u32[]{:S(2)}, u32[]{:S(2)}) %collective-permute-start.6) | collective-permute-done | bytes 401440 | tf_op jit(solution)/shard_map/ppermute | solution.py:259
  46.0 5.9 %collective-permute-start.7 = (bf16[224,896]{1,0:T(8,128)(2,1)S(1)}, bf16[224,896]{1,0:T(8,128)(2,1)S(1)}, u32[]{:S(2)}, u32[]{:S(2)}) collective-permute-start(bf16[224,896]{1,0:T(8,128)(2,1)S(1)} %add_select_fusion), channel_id=1, source_target_pairs={{0,4},{4,0},{8,12},{12,8},{1,5},{5,1},{9,13},{13,9},{2,6},{6,2},{1... | collective-permute-start | bytes 1204232 | tf_op jit(solution)/shard_map/ppermute | solution.py:259
  51.9 1.2 %gradient.7 = f32[2,112]{1,0:T(2,128)S(1)} custom-call(bf16[112,896]{1,0:T(8,128)(2,1)S(1)} %get-tuple-element.71.refs_0_, bf16[112,896]{1,0:T(8,128)(2,1)S(1)} %copy-done.1, bf16[112,896]{1,0:T(8,128)(2,1)} %collective-permute-done.4.refs_2_, bf16[224,896]{1,0:T(8,128)(2,1)S(1)} %collective-permute-done.6.refs_3_.refs_1_, ...), custom_call_target="tpu_custom_call" | custom-call | flops 48400 | bytes 48400 | tf_op jit(solution)/shard_map/gradient/pallas_call | solution.py:430
  53.1 1.2 %gradient.6 = f32[2,112]{1,0:T(2,128)S(1)} custom-call(bf16[112,896]{1,0:T(8,128)(2,1)S(1)} %get-tuple-element.69.refs_0_, bf16[112,896]{1,0:T(8,128)(2,1)S(1)} %collective-permute-done.refs_1_, bf16[112,896]{1,0:T(8,128)(2,1)} %collective-permute-done.2.refs_2_, bf16[224,896]{1,0:T(8,128)(2,1)S(1)} %collective-permute-done.6.refs_3_.refs_1_, ...), custom_call_target="tpu_custom_call" | custom-call | flops 48400 | bytes 48400 | tf_op jit(solution)/shard_map/gradient/pallas_call | solution.py:430
  54.4 3.9 %collective-permute-done.7.refs_3_ = bf16[224,896]{1,0:T(8,128)(2,1)S(1)} collective-permute-done((bf16[224,896]{1,0:T(8,128)(2,1)S(1)}, bf16[224,896]{1,0:T(8,128)(2,1)S(1)}, u32[]{:S(2)}, u32[]{:S(2)}) %collective-permute-start.7) | collective-permute-done | bytes 401440 | tf_op jit(solution)/shard_map/ppermute | solution.py:259
  59.1 4.5 %collective-permute-start.11 = (bf16[224,896]{1,0:T(8,128)(2,1)S(1)}, bf16[224,896]{1,0:T(8,128)(2,1)S(1)}, u32[]{:S(2)}, u32[]{:S(2)}) collective-permute-start(bf16[224,896]{1,0:T(8,128)(2,1)S(1)} %add.52), channel_id=1, source_target_pairs={{0,4},{4,0},{8,12},{12,8},{1,5},{5,1},{9,13},{13,9},{2,6},{6,2},{1... | collective-permute-start | bytes 1204232 | tf_op jit(solution)/shard_map/ppermute | solution.py:259
  63.6 1.5 %gradient.8 = f32[2,224]{1,0:T(2,128)S(1)} custom-call(bf16[224,896]{1,0:T(8,128)(2,1)S(1)} %get-tuple-element.74.refs_0_, bf16[224,896]{1,0:T(8,128)(2,1)} %collective-permute-done.1.refs_1_, bf16[224,896]{1,0:T(8,128)(2,1)S(1)} %collective-permute-done.5.refs_2_, bf16[224,896]{1,0:T(8,128)(2,1)S(1)} %collective-permute-done.7.refs_3_, ...), custom_call_target="tpu_custom_call" | custom-call | flops 48400 | bytes 48400 | tf_op jit(solution)/shard_map/gradient/pallas_call | solution.py:430
  65.8 2.0 %collective-permute-start.12 = (bf16[112,896]{1,0:T(8,128)(2,1)S(1)}, bf16[112,896]{1,0:T(8,128)(2,1)S(1)}, u32[]{:S(2)}, u32[]{:S(2)}) collective-permute-start(bf16[112,896]{1,0:T(8,128)(2,1)S(1)} %slice_add_fusion.2), channel_id=1, source_target_pairs={{0,4},{4,0},{8,12},{12,8},{1,5},{5,1},{9,13},{13,9},{2,6},{6,2},{1... | collective-permute-start | bytes 602120 | tf_op jit(solution)/shard_map/ppermute | solution.py:259
  67.9 5.0 %collective-permute-start.13 = (bf16[112,896]{1,0:T(8,128)(2,1)S(1)}, bf16[112,896]{1,0:T(8,128)(2,1)S(1)}, u32[]{:S(2)}, u32[]{:S(2)}) collective-permute-start(bf16[112,896]{1,0:T(8,128)(2,1)S(1)} %slice_add_fusion), channel_id=1, source_target_pairs={{0,4},{4,0},{8,12},{12,8},{1,5},{5,1},{9,13},{13,9},{2,6},{6,2},{1... | collective-permute-start | bytes 602120 | tf_op jit(solution)/shard_map/ppermute | solution.py:259
  72.9 4.8 %collective-permute-done.12.refs_3_ = bf16[112,896]{1,0:T(8,128)(2,1)S(1)} collective-permute-done((bf16[112,896]{1,0:T(8,128)(2,1)S(1)}, bf16[112,896]{1,0:T(8,128)(2,1)S(1)}, u32[]{:S(2)}, u32[]{:S(2)}) %collective-permute-start.12) | collective-permute-done | bytes 200736 | tf_op jit(solution)/shard_map/ppermute | solution.py:259
  78.0 1.9 %collective-permute-done.13.refs_3_ = bf16[112,896]{1,0:T(8,128)(2,1)S(1)} collective-permute-done((bf16[112,896]{1,0:T(8,128)(2,1)S(1)}, bf16[112,896]{1,0:T(8,128)(2,1)S(1)}, u32[]{:S(2)}, u32[]{:S(2)}) %collective-permute-start.13) | collective-permute-done | bytes 200736 | tf_op jit(solution)/shard_map/ppermute | solution.py:259
  80.8 1.6 %collective-permute-start.15 = (f32[8,220]{1,0:T(8,128)S(1)}, f32[8,220]{1,0:T(8,128)S(1)}, u32[]{:S(2)}, u32[]{:S(2)}) collective-permute-start(f32[8,220]{1,0:T(8,128)S(1)} %reshape.3), channel_id=1, source_target_pairs={{0,2},{1,3},{2,0},{3,1},{4,6},{5,7},{6,4},{7,5},{8,10},{9,11},{10,... | collective-permute-start | bytes 21128 | tf_op jit(solution)/shard_map/ppermute | solution.py:248
  82.7 1.9 %collective-permute-done.15 = f32[8,220]{1,0:T(8,128)S(1)} collective-permute-done((f32[8,220]{1,0:T(8,128)S(1)}, f32[8,220]{1,0:T(8,128)S(1)}, u32[]{:S(2)}, u32[]{:S(2)}) %collective-permute-start.15) | collective-permute-done | bytes 7072 | tf_op jit(solution)/shard_map/ppermute | solution.py:248
  (61 shorter events, 11.4 us)
Async XLA Ops:
  4.1 9.9 %collective-permute-start = (bf16[112,896]{1,0:T(8,128)(2,1)S(1)}, bf16[112,896]{1,0:T(8,128)(2,1)S(1)}, u32[]{:S(2)}, u32[]{:S(2)}) collective-permute-start(bf16[112,896]{1,0:T(8,128)(2,1)S(1)} %get-tuple-element.69.refs_0_), channel_id=1, source_target_pairs={{0,4},{4,0},{8,12},{12,8},{1,5},{5,1},{9,13},{13,9},{2,6},{6,2},{1... | collective-permute-start | bytes 602120 | tf_op jit(solution)/shard_map/ppermute | solution.py:259
  11.0 2.5 %copy-start.4 = (bf16[2,224,896]{2,1,0:T(8,128)(2,1)}, bf16[2,224,896]{2,1,0:T(8,128)(2,1)S(1)}, u32[]{:S(2)}) copy-start(bf16[2,224,896]{2,1,0:T(8,128)(2,1)S(1)} %get-tuple-element.75.refs_4_) | copy-start | bytes 2408452
  11.0 10.6 %collective-permute-start.3 = (bf16[112,896]{1,0:T(8,128)(2,1)S(1)}, bf16[112,896]{1,0:T(8,128)(2,1)S(1)}, u32[]{:S(2)}, u32[]{:S(2)}) collective-permute-start(bf16[112,896]{1,0:T(8,128)(2,1)S(1)} %get-tuple-element.71.refs_0_), channel_id=1, source_target_pairs={{0,4},{4,0},{8,12},{12,8},{1,5},{5,1},{9,13},{13,9},{2,6},{6,2},{1... | collective-permute-start | bytes 602120 | tf_op jit(solution)/shard_map/ppermute | solution.py:259
  13.5 8.1 %copy-start.2 = (bf16[2,224,896]{2,1,0:T(8,128)(2,1)}, bf16[2,224,896]{2,1,0:T(8,128)(2,1)S(1)}, u32[]{:S(2)}) copy-start(bf16[2,224,896]{2,1,0:T(8,128)(2,1)S(1)} %get-tuple-element.81.refs_4_) | copy-start | bytes 2408452
  14.7 11.3 %collective-permute-start.2 = (bf16[112,896]{1,0:T(8,128)(2,1)}, bf16[112,896]{1,0:T(8,128)(2,1)}, u32[]{:S(2)}, u32[]{:S(2)}) collective-permute-start(bf16[112,896]{1,0:T(8,128)(2,1)} %add.45), channel_id=1, source_target_pairs={{0,0},{4,8},{8,4},{12,12},{1,1},{5,9},{9,5},{13,13},{2,2},{6,10},{... | collective-permute-start | bytes 602120 | tf_op jit(solution)/shard_map/ppermute | solution.py:262
  21.7 0.8 copy-start
  22.4 4.6 %collective-permute-start.4 = (bf16[112,896]{1,0:T(8,128)(2,1)}, bf16[112,896]{1,0:T(8,128)(2,1)}, u32[]{:S(2)}, u32[]{:S(2)}) collective-permute-start(bf16[112,896]{1,0:T(8,128)(2,1)} %add.46), channel_id=1, source_target_pairs={{0,0},{4,8},{8,4},{12,12},{1,1},{5,9},{9,5},{13,13},{2,2},{6,10},{... | collective-permute-start | bytes 602120 | tf_op jit(solution)/shard_map/ppermute | solution.py:262
  25.8 12.3 %collective-permute-start.1 = (bf16[224,896]{1,0:T(8,128)(2,1)S(1)}, bf16[224,896]{1,0:T(8,128)(2,1)}, u32[]{:S(2)}, u32[]{:S(2)}) collective-permute-start(bf16[224,896]{1,0:T(8,128)(2,1)S(1)} %get-tuple-element.74.refs_0_), channel_id=1, source_target_pairs={{0,4},{4,0},{8,12},{12,8},{1,5},{5,1},{9,13},{13,9},{2,6},{6,2},{1... | collective-permute-start | bytes 1204232 | tf_op jit(solution)/shard_map/ppermute | solution.py:259
  26.0 25.9 %copy-start.1 = (bf16[112,896]{1,0:T(8,128)(2,1)S(1)}, bf16[112,896]{1,0:T(8,128)(2,1)}, u32[]{:S(2)}) copy-start(bf16[112,896]{1,0:T(8,128)(2,1)} %copy-done) | copy-start | bytes 602116
  28.1 16.8 %collective-permute-start.6 = (bf16[224,896]{1,0:T(8,128)(2,1)S(1)}, bf16[224,896]{1,0:T(8,128)(2,1)S(1)}, u32[]{:S(2)}, u32[]{:S(2)}) collective-permute-start(bf16[224,896]{1,0:T(8,128)(2,1)S(1)} %maximum_select_fusion), channel_id=1, source_target_pairs={{0,4},{4,0},{8,12},{12,8},{1,5},{5,1},{9,13},{13,9},{2,6},{6,2},{1... | collective-permute-start | bytes 1204232 | tf_op jit(solution)/shard_map/ppermute | solution.py:259
  39.3 6.7 %collective-permute-start.5 = (bf16[224,896]{1,0:T(8,128)(2,1)S(1)}, bf16[224,896]{1,0:T(8,128)(2,1)S(1)}, u32[]{:S(2)}, u32[]{:S(2)}) collective-permute-start(bf16[224,896]{1,0:T(8,128)(2,1)S(1)} %add.49), channel_id=1, source_target_pairs={{0,0},{4,8},{8,4},{12,12},{1,1},{5,9},{9,5},{13,13},{2,2},{6,10},{... | collective-permute-start | bytes 1204232 | tf_op jit(solution)/shard_map/ppermute | solution.py:262
  45.0 9.3 %collective-permute-start.8 = (bf16[224,896]{1,0:T(8,128)(2,1)S(1)}, bf16[224,896]{1,0:T(8,128)(2,1)S(1)}, u32[]{:S(2)}, u32[]{:S(2)}) collective-permute-start(bf16[224,896]{1,0:T(8,128)(2,1)S(1)} %add.50), channel_id=1, source_target_pairs={{0,0},{4,8},{8,4},{12,12},{1,1},{5,9},{9,5},{13,13},{2,2},{6,10},{... | collective-permute-start | bytes 1204232 | tf_op jit(solution)/shard_map/ppermute | solution.py:262
  46.0 17.6 %copy-start.5 = (bf16[2,224,896]{2,1,0:T(8,128)(2,1)S(1)}, bf16[2,224,896]{2,1,0:T(8,128)(2,1)}, u32[]{:S(2)}) copy-start(bf16[2,224,896]{2,1,0:T(8,128)(2,1)} %copy-done.4) | copy-start | bytes 2408452
  46.0 12.3 %collective-permute-start.7 = (bf16[224,896]{1,0:T(8,128)(2,1)S(1)}, bf16[224,896]{1,0:T(8,128)(2,1)S(1)}, u32[]{:S(2)}, u32[]{:S(2)}) collective-permute-start(bf16[224,896]{1,0:T(8,128)(2,1)S(1)} %add_select_fusion), channel_id=1, source_target_pairs={{0,4},{4,0},{8,12},{12,8},{1,5},{5,1},{9,13},{13,9},{2,6},{6,2},{1... | collective-permute-start | bytes 1204232 | tf_op jit(solution)/shard_map/ppermute | solution.py:259
  58.4 7.4 %collective-permute-start.10 = (bf16[112,896]{1,0:T(8,128)(2,1)S(1)}, bf16[112,896]{1,0:T(8,128)(2,1)S(1)}, u32[]{:S(2)}, u32[]{:S(2)}) collective-permute-start(bf16[112,896]{1,0:T(8,128)(2,1)S(1)} %get-tuple-element.84), channel_id=1, source_target_pairs={{0,0},{4,8},{8,4},{12,12},{1,1},{5,9},{9,5},{13,13},{2,2},{6,10},{... | collective-permute-start | bytes 602120 | tf_op jit(solution)/shard_map/ppermute | solution.py:262
  59.1 21.1 %collective-permute-start.11 = (bf16[224,896]{1,0:T(8,128)(2,1)S(1)}, bf16[224,896]{1,0:T(8,128)(2,1)S(1)}, u32[]{:S(2)}, u32[]{:S(2)}) collective-permute-start(bf16[224,896]{1,0:T(8,128)(2,1)S(1)} %add.52), channel_id=1, source_target_pairs={{0,4},{4,0},{8,12},{12,8},{1,5},{5,1},{9,13},{13,9},{2,6},{6,2},{1... | collective-permute-start | bytes 1204232 | tf_op jit(solution)/shard_map/ppermute | solution.py:259
  63.6 16.6 %copy-start.3 = (bf16[2,224,896]{2,1,0:T(8,128)(2,1)S(1)}, bf16[2,224,896]{2,1,0:T(8,128)(2,1)}, u32[]{:S(2)}) copy-start(bf16[2,224,896]{2,1,0:T(8,128)(2,1)} %copy-done.2) | copy-start | bytes 2408452
  65.1 2.7 %collective-permute-start.9 = (bf16[112,896]{1,0:T(8,128)(2,1)S(1)}, bf16[112,896]{1,0:T(8,128)(2,1)S(1)}, u32[]{:S(2)}, u32[]{:S(2)}) collective-permute-start(bf16[112,896]{1,0:T(8,128)(2,1)S(1)} %slice_add_fusion.1), channel_id=1, source_target_pairs={{0,0},{4,8},{8,4},{12,12},{1,1},{5,9},{9,5},{13,13},{2,2},{6,10},{... | collective-permute-start | bytes 602120 | tf_op jit(solution)/shard_map/ppermute | solution.py:262
  65.8 11.9 %collective-permute-start.12 = (bf16[112,896]{1,0:T(8,128)(2,1)S(1)}, bf16[112,896]{1,0:T(8,128)(2,1)S(1)}, u32[]{:S(2)}, u32[]{:S(2)}) collective-permute-start(bf16[112,896]{1,0:T(8,128)(2,1)S(1)} %slice_add_fusion.2), channel_id=1, source_target_pairs={{0,4},{4,0},{8,12},{12,8},{1,5},{5,1},{9,13},{13,9},{2,6},{6,2},{1... | collective-permute-start | bytes 602120 | tf_op jit(solution)/shard_map/ppermute | solution.py:259
  67.9 12.0 %collective-permute-start.13 = (bf16[112,896]{1,0:T(8,128)(2,1)S(1)}, bf16[112,896]{1,0:T(8,128)(2,1)S(1)}, u32[]{:S(2)}, u32[]{:S(2)}) collective-permute-start(bf16[112,896]{1,0:T(8,128)(2,1)S(1)} %slice_add_fusion), channel_id=1, source_target_pairs={{0,4},{4,0},{8,12},{12,8},{1,5},{5,1},{9,13},{13,9},{2,6},{6,2},{1... | collective-permute-start | bytes 602120 | tf_op jit(solution)/shard_map/ppermute | solution.py:259
  80.7 1.9 %collective-permute-start.14 = (f32[8,220]{1,0:T(8,128)S(1)}, f32[8,220]{1,0:T(8,128)S(1)}, u32[]{:S(2)}, u32[]{:S(2)}) collective-permute-start(f32[8,220]{1,0:T(8,128)S(1)} %reshape.3), channel_id=1, source_target_pairs={{0,1},{1,0},{2,3},{3,2},{4,5},{5,4},{6,7},{7,6},{8,9},{9,8},{10,11... | collective-permute-start | bytes 21128 | tf_op jit(solution)/shard_map/ppermute | solution.py:248
  80.8 3.7 %collective-permute-start.15 = (f32[8,220]{1,0:T(8,128)S(1)}, f32[8,220]{1,0:T(8,128)S(1)}, u32[]{:S(2)}, u32[]{:S(2)}) collective-permute-start(f32[8,220]{1,0:T(8,128)S(1)} %reshape.3), channel_id=1, source_target_pairs={{0,2},{1,3},{2,0},{3,1},{4,6},{5,7},{6,4},{7,5},{8,10},{9,11},{10,... | collective-permute-start | bytes 21128 | tf_op jit(solution)/shard_map/ppermute | solution.py:248
  82.3 3.1 %collective-permute-start.16 = (f32[8,220]{1,0:T(8,128)S(1)}, f32[8,220]{1,0:T(8,128)S(1)}, u32[]{:S(2)}, u32[]{:S(2)}) collective-permute-start(f32[8,220]{1,0:T(8,128)S(1)} %reshape.3), channel_id=1, source_target_pairs={{0,3},{1,2},{2,1},{3,0},{4,7},{5,6},{6,5},{7,4},{8,11},{9,10},{10,... | collective-permute-start | bytes 21128 | tf_op jit(solution)/shard_map/ppermute | solution.py:248

commit v12 on v10

--- a/solution.py
+++ b/solution.py
@@ -13,8 +13,6 @@
 MB = 8
 ROW_TILE = 16
 LANE_TILE = 128
-ROW_PARTS = 1
-LAG = 2
 VMEM_BYTES = 24 * 1024 * 1024
 
 
@@ -116,13 +114,12 @@
     phase_ref, image, coil_map, left_ref = refs[:4]
     order_ref, gram_ref, adjoint_ref, kspace_ref, image_ref, map_ref = refs[4:10]
     shifted, refs = refs[10], refs[11:]
-    out_refs, refs = refs[:ROW_PARTS], refs[ROW_PARTS:]
+    out_ref, refs = refs[0], refs[1:]
     if next_rows:
         next_image, next_map, refs = refs[0], refs[1], refs[2:]
     total, wide, raw_kspace, gram, adjoint, order, arrived, small = refs
     vols, coils, length = image.shape[0], coil_map.shape[0], image.shape[-1]
     _, rows, lanes = shifted.shape
-    part = rows // len(out_refs)
     order_copy = pltpu.make_async_copy(order_ref, order, small.at[0])
     gram_copy = pltpu.make_async_copy(gram_ref, gram, small.at[1])
     owner_copies = [
@@ -208,27 +205,28 @@
                         measured = term if measured is None else measured + term
                 total[:length, place * 2 * length : (place + 1) * 2 * length] -= measured
 
-    for index, out_ref in enumerate(out_refs):
-        out_ref[...] = total[index * part : (index + 1) * part, :].astype(jnp.bfloat16)
+    out_ref[...] = total[...].astype(jnp.bfloat16)
     for copy in next_copies:
         copy.wait()
 
 
-def gradient_kernel(index, factor, on_line, *refs):
+def line_place():
+    position = lax.axis_index("slc")
+    edge = (position == 0) | (position == lax.axis_size("slc") - 1)
+    return edge, lax.axis_index("vol") % 2 == 0
+
+
+def gradient_kernel(factor, on_line, *refs):
     term_refs, shifted_ref, out_ref = refs[:-2], refs[-2], refs[-1]
     slots, _, lanes = shifted_ref.shape
-    part = out_ref.shape[1]
     terms = [ref[...].astype(jnp.float32) for ref in term_refs]
+    residual = terms[0]
     if on_line:
-        own, near, across, rest = terms
-        position = lax.axis_index("slc")
-        edge = (position == 0) | (position == lax.axis_size("slc") - 1)
-        residual = own + jnp.where(edge, rest, near + across)
-    else:
-        residual = terms[0]
+        edge, leads = line_place()
+        inside = jnp.where(leads, terms[1] + terms[2], terms[2] + terms[3])
+        residual += jnp.where(edge, jnp.where(leads, terms[3], terms[4]), inside)
     for slot in range(slots):
-        shifted = shifted_ref[slot, index * part : (index + 1) * part, :].astype(jnp.float32)
-        product = residual * shifted
+        product = residual * shifted_ref[slot].astype(jnp.float32)
         tiles = [product[:, at : at + LANE_TILE] for at in range(0, lanes, LANE_TILE)]
         folded = functools.reduce(lambda a, b: a + b, tiles)
         out_ref[slot : slot + 1, :] = factor * jnp.sum(folded.T, axis=0, keepdims=True)
@@ -250,58 +248,50 @@
 
 
 def line_of_four(encode, gradient, count):
-    position = lax.axis_index("slc")
-    edge = (position == 0) | (position == 3)
+    edge, leads = line_place()
+    cores = lax.axis_size("vol")
     outer_pairs = [(0, 1), (1, 0), (2, 3), (3, 2)]
     inner_pairs = [(0, 0), (1, 2), (2, 1), (3, 3)]
-    parts = ROW_PARTS
-    pieces, shifted, outer, inner, gradients = [], [], [], [], []
-
-    def encode_next(*earlier):
-        group = len(shifted)
-        if group * parts < count:
-            encoded = encode(group, *earlier)
+
+    def exchange(value, step):
+        pairs = [
+            (source * cores + core, target * cores + core)
+            for core in range(cores)
+            for source, target in ((outer_pairs, inner_pairs)[(step + core) % 2])
+        ]
+        return lax.ppermute(value, ("slc", "vol"), pairs)
+
+    shifted, own = map(list, zip(encode(0)))
+    payload, received, gradients = own[0], [], []
+    for step in range(2 * count + 2):
+        received.append(exchange(payload, step))
+        group = step // 2
+        if step % 2 == 0 and group + 1 < count:
+            encoded = encode(group + 1, payload) if step else encode(1)
             shifted.append(encoded[0])
-            pieces.extend(encoded[1:])
-
-    def outer_next(*earlier):
-        step = len(outer)
-        back = step - LAG
-        payload = pieces[step] if step < count else None
-        if back >= 0:
-            others = pieces[back] + inner[back]
-            payload = others if payload is None else jnp.where(edge, payload, others)
-        if earlier:
-            payload = after(payload, *earlier)
-        outer.append(lax.ppermute(payload, "slc", outer_pairs))
-        return payload
-
-    def gradient_next(*earlier):
-        step = len(gradients)
-        terms = (pieces[step], outer[step], inner[step], outer[step + LAG])
-        own = after(terms[0], *earlier) if earlier else terms[0]
-        gradients.append(gradient(step, (own, *terms[1:]), shifted[step // parts]))
-
-    while len(outer) < LAG:
-        encode_next()
-        while len(outer) < min(LAG, len(pieces)):
-            outer_next()
-    latest = (pieces[-1],)
-    for step in range(count):
-        half = pieces[step] + after(outer[step], *latest)
-        inner.append(lax.ppermute(half, "slc", inner_pairs))
-        latest = ()
-        if step >= 1:
-            latest = (outer_next(half),)
-        if len(pieces) < min(count, step + LAG + 2):
-            encode_next(*(latest or (half,)))
-            latest = (*latest, pieces[-1])
-        if step >= LAG + 1:
-            gradient_next(*latest)
-            latest = (*latest, gradients[-1])
-    last = outer_next(*latest)
-    while len(gradients) < count:
-        gradient_next(last)
+            own.append(encoded[1])
+        done = group - 2
+        if step % 2 == 0 and done >= 0:
+            terms = (own[done], *received[2 * done : 2 * done + 4])
+            gradients.append(gradient((after(terms[0], payload), *terms[1:]), shifted[done]))
+        if step == 2 * count + 1:
+            break
+        arrived = received[-1]
+        if step % 2 == 0:
+            before = own[group - 1] if group else own[0]
+            if group < count:
+                mine = own[group]
+                payload = jnp.where(
+                    leads, mine + arrived, jnp.where(edge, mine, before + arrived)
+                )
+            else:
+                payload = before + arrived
+        else:
+            payload = own[group] + arrived
+            if group + 1 < count:
+                payload = jnp.where(leads & edge, own[group + 1], payload)
+    last = count - 1
+    gradients.append(gradient((own[last], *received[2 * last : 2 * last + 4]), shifted[last]))
     return gradients
 
 
@@ -309,8 +299,7 @@
     vols, per_device, _, _, length = images.shape
     coils = coil_maps.shape[0]
     groups = lax.axis_size("slc")
-    rows = round_up(length, ROW_TILE * ROW_PARTS)
-    part = rows // ROW_PARTS
+    rows = round_up(length, ROW_TILE)
     places = vols * coils
     lanes = round_up(places * 2 * length, LANE_TILE)
     whole_classes = per_device % groups == 0
@@ -385,9 +374,9 @@
                 (rows_of_class(group + 1) or [0]) if has_next else None,
             ),
             in_specs=scalar_specs + [in_vmem] * 4 + [in_place] * 6,
-            out_specs=[in_vmem] * (1 + ROW_PARTS + 2 * has_next),
+            out_specs=[in_vmem] * (2 + 2 * has_next),
             out_shape=[jax.ShapeDtypeStruct((slots, rows, lanes), jnp.bfloat16)]
-            + [jax.ShapeDtypeStruct((part, lanes), jnp.bfloat16)] * ROW_PARTS
+            + [jax.ShapeDtypeStruct((rows, lanes), jnp.bfloat16)]
             + raw_shapes * has_next,
             scratch_shapes=[
                 pltpu.VMEM((rows, lanes), jnp.float32),
@@ -418,13 +407,13 @@
             lying[2],
             *lying[:2],
         )
-        raw[:] = outputs[1 + ROW_PARTS :]
-        return outputs[: 1 + ROW_PARTS]
-
-    def gradient(step, terms, encoded):
+        raw[:] = outputs[2:]
+        return outputs[:2]
+
+    def gradient(terms, encoded):
         return pl.pallas_call(
-            functools.partial(gradient_kernel, step % ROW_PARTS, factor, on_line),
-            out_shape=jax.ShapeDtypeStruct((slots, part), jnp.float32),
+            functools.partial(gradient_kernel, factor, on_line),
+            out_shape=jax.ShapeDtypeStruct((slots, rows), jnp.float32),
             compiler_params=pltpu.CompilerParams(vmem_limit_bytes=VMEM_BYTES),
             cost_estimate=pl.CostEstimate(
                 flops=places * slots * 4 * length**2, bytes_accessed=1_500_000, transcendentals=0
@@ -433,22 +422,12 @@
         )(*terms, encoded)
 
     if on_line:
-        gradients = line_of_four(encode, gradient, groups * ROW_PARTS)
+        gradients = line_of_four(encode, gradient, groups)
     else:
         encoded = [encode(group) for group in range(groups)]
-        reduced = lax.psum([list(outputs[1:]) for outputs in encoded], "slc")
-        gradients = [
-            gradient(index, (piece,), encoded[group][0])
-            for group in range(groups)
-            for index, piece in enumerate(reduced[group])
-        ]
-    by_class = jnp.stack(
-        [
-            jnp.concatenate(gradients[group * ROW_PARTS : (group + 1) * ROW_PARTS], axis=1)
-            for group in range(groups)
-        ],
-        axis=1,
-    )[:, :, :length]
+        reduced = lax.psum([own for _, own in encoded], "slc")
+        gradients = [gradient((reduced[group],), encoded[group][0]) for group in range(groups)]
+    by_class = jnp.stack(gradients, axis=1)[:, :, :length]
     if whole_classes:
         local = by_class.reshape(per_device, length)
     else:

time: 77.1 us -> 124 us (1.61)
  the two profiles are of different devices: /device:TPU:0 before, /device:TPU:13 now
where the time goes in v12:
time: 124 us; the launch traced here: 125 us
  waiting for transfers between devices  67.8 us (55%)
  starting transfers between devices  39.6 us (32%)
  Pallas kernels  13.9 us (11%)
  other arithmetic  2.18 us (2%)
  local copies, waits for them, and re-layouts  1.65 us (1%)
    ppermute x10, waiting for transfers between devices, exchange(): return lax.ppermute(value, ('slc', 'vol'), pairs)  65.8 us
    ppermute x10, starting transfers between devices, exchange(): return lax.ppermute(value, ('slc', 'vol'), pairs)  26.7 us
    ppermute x3, starting transfers between devices, sum_over_replicas(): lax.ppermute(value, axes, [(index, index ^ mask) for index in range(4)])  12.9 us
    pallas_call x4, Pallas kernels, encode(): pl.pallas_call(functools.partial(encode_kernel, slots, group, rows_of_cla...  10 us
  transfers between devices with their start and end apart: 13, of which 12 were waited for; matrix products, arithmetic and copies ran while one was open for 0% of the time, Pallas kernels for 8%

profile of v12, /device:TPU:13, one launch (start us, length us, event | category | flops | bytes accessed | tf_op | source)
XLA Modules:
  0.0 125.5 jit_solution(13325467337863287861)
XLA Ops:
  1.9 2.2 %encode.4 = (bf16[2,224,896]{2,1,0:T(8,128)(2,1)S(1)}, bf16[224,896]{1,0:T(8,128)(2,1)S(1)}, bf16[1,2,220,2,220]{4,3,2,1,0:T(2,128)(2,1)S(1)}, bf16[2,2,220,2,220]{4,3,2,1,0:T(2,128)(2,1)S(1)}) custom-call(f32[2,256,8]{2,1,0:T(8,128)S(1)} %get-tuple-element.28.refs_0_, bf16[1,2,2,220,220]{4,3,2,1,0:T(8,128)(2,1)S(1)} %bitcast.36, ...), custom_call_target="tpu_custom_call" | custom-call | flops 1022208000 | bytes 6000000 | tf_op jit(solution)/shard_map/encode/pallas_call | solution.py:368
  4.9 3.2 %collective-permute-start = (bf16[224,896]{1,0:T(8,128)(2,1)S(1)}, bf16[224,896]{1,0:T(8,128)(2,1)S(1)}, u32[]{:S(2)}, u32[]{:S(2)}) collective-permute-start(bf16[224,896]{1,0:T(8,128)(2,1)S(1)} %get-tuple-element.40.refs_0_), channel_id=1, source_target_pairs={{0,4},{4,0},{8,12},{12,8},{1,1},{5,9},{9,5},{13,13},{2,6},{6,2},{1... | collective-permute-start | bytes 1204232 | tf_op jit(solution)/shard_map/ppermute | solution.py:262
  8.1 5.7 %collective-permute-done.refs_1_ = bf16[224,896]{1,0:T(8,128)(2,1)S(1)} collective-permute-done((bf16[224,896]{1,0:T(8,128)(2,1)S(1)}, bf16[224,896]{1,0:T(8,128)(2,1)S(1)}, u32[]{:S(2)}, u32[]{:S(2)}) %collective-permute-start) | collective-permute-done | bytes 401440 | tf_op jit(solution)/shard_map/ppermute | solution.py:262
  16.8 2.2 %encode.5 = (bf16[2,224,896]{2,1,0:T(8,128)(2,1)S(1)}, bf16[224,896]{1,0:T(8,128)(2,1)S(1)}, bf16[1,2,220,2,220]{4,3,2,1,0:T(2,128)(2,1)S(1)}, bf16[2,2,220,2,220]{4,3,2,1,0:T(2,128)(2,1)S(1)}) custom-call(f32[2,256,8]{2,1,0:T(8,128)S(1)} %get-tuple-element.28.refs_0_, bf16[1,2,2,220,220]{4,3,2,1,0:T(8,128)(2,1)S(1)} %bitcast.37, ...), custom_call_target="tpu_custom_call" | custom-call | flops 1022208000 | bytes 6000000 | tf_op jit(solution)/shard_map/encode/pallas_call | solution.py:368
  19.0 4.8 %collective-permute-done.1.refs_2_ = bf16[224,896]{1,0:T(8,128)(2,1)S(1)} collective-permute-done((bf16[224,896]{1,0:T(8,128)(2,1)}, bf16[224,896]{1,0:T(8,128)(2,1)S(1)}, u32[]{:S(2)}, u32[]{:S(2)}) %collective-permute-start.1) | collective-permute-done | bytes 401440 | tf_op jit(solution)/shard_map/ppermute | solution.py:262
  23.8 3.2 %collective-permute-start.2 = (bf16[224,896]{1,0:T(8,128)(2,1)S(1)}, bf16[224,896]{1,0:T(8,128)(2,1)S(1)}, u32[]{:S(2)}, u32[]{:S(2)}) collective-permute-start(bf16[224,896]{1,0:T(8,128)(2,1)S(1)} %add_select_fusion.2), channel_id=1, source_target_pairs={{0,4},{4,0},{8,12},{12,8},{1,1},{5,9},{9,5},{13,13},{2,6},{6,2},{1... | collective-permute-start | bytes 1204232 | tf_op jit(solution)/shard_map/ppermute | solution.py:262
  27.1 5.7 %collective-permute-done.2.refs_3_.refs_1_ = bf16[224,896]{1,0:T(8,128)(2,1)S(1)} collective-permute-done((bf16[224,896]{1,0:T(8,128)(2,1)S(1)}, bf16[224,896]{1,0:T(8,128)(2,1)S(1)}, u32[]{:S(2)}, u32[]{:S(2)}) %collective-permute-start.2) | collective-permute-done | bytes 401440 | tf_op jit(solution)/shard_map/ppermute | solution.py:262
  32.8 1.9 %collective-permute-start.3 = (bf16[224,896]{1,0:T(8,128)(2,1)S(1)}, bf16[224,896]{1,0:T(8,128)(2,1)S(1)}, u32[]{:S(2)}, u32[]{:S(2)}) collective-permute-start(bf16[224,896]{1,0:T(8,128)(2,1)S(1)} %select_select_fusion.3), channel_id=1, source_target_pairs={{0,0},{4,8},{8,4},{12,12},{1,5},{5,1},{9,13},{13,9},{2,2},{6,10},{... | collective-permute-start | bytes 1204232 | tf_op jit(solution)/shard_map/ppermute | solution.py:262
  35.0 2.2 %encode.6 = (bf16[2,224,896]{2,1,0:T(8,128)(2,1)S(1)}, bf16[224,896]{1,0:T(8,128)(2,1)S(1)}, bf16[1,2,220,2,220]{4,3,2,1,0:T(2,128)(2,1)S(1)}, bf16[2,2,220,2,220]{4,3,2,1,0:T(2,128)(2,1)S(1)}) custom-call(f32[2,256,8]{2,1,0:T(8,128)S(1)} %get-tuple-element.28.refs_0_, bf16[1,2,2,220,220]{4,3,2,1,0:T(8,128)(2,1)S(1)} %bitcast.38, ...), custom_call_target="tpu_custom_call" | custom-call | flops 1022208000 | bytes 6000000 | tf_op jit(solution)/shard_map/encode/pallas_call | solution.py:368
  37.2 4.6 %collective-permute-done.3.refs_4_.refs_2_ = bf16[224,896]{1,0:T(8,128)(2,1)S(1)} collective-permute-done((bf16[224,896]{1,0:T(8,128)(2,1)S(1)}, bf16[224,896]{1,0:T(8,128)(2,1)S(1)}, u32[]{:S(2)}, u32[]{:S(2)}) %collective-permute-start.3) | collective-permute-done | bytes 401440 | tf_op jit(solution)/shard_map/ppermute | solution.py:262
  41.8 2.9 %collective-permute-start.4 = (bf16[224,896]{1,0:T(8,128)(2,1)S(1)}, bf16[224,896]{1,0:T(8,128)(2,1)S(1)}, u32[]{:S(2)}, u32[]{:S(2)}) collective-permute-start(bf16[224,896]{1,0:T(8,128)(2,1)S(1)} %add_select_fusion.1), channel_id=1, source_target_pairs={{0,4},{4,0},{8,12},{12,8},{1,1},{5,9},{9,5},{13,13},{2,6},{6,2},{1... | collective-permute-start | bytes 1204232 | tf_op jit(solution)/shard_map/ppermute | solution.py:262
  44.7 5.7 %collective-permute-done.4.refs_3_.refs_1_ = bf16[224,896]{1,0:T(8,128)(2,1)S(1)} collective-permute-done((bf16[224,896]{1,0:T(8,128)(2,1)S(1)}, bf16[224,896]{1,0:T(8,128)(2,1)S(1)}, u32[]{:S(2)}, u32[]{:S(2)}) %collective-permute-start.4) | collective-permute-done | bytes 401440 | tf_op jit(solution)/shard_map/ppermute | solution.py:262
  50.5 1.9 %collective-permute-start.5 = (bf16[224,896]{1,0:T(8,128)(2,1)S(1)}, bf16[224,896]{1,0:T(8,128)(2,1)S(1)}, u32[]{:S(2)}, u32[]{:S(2)}) collective-permute-start(bf16[224,896]{1,0:T(8,128)(2,1)S(1)} %select_select_fusion.2), channel_id=1, source_target_pairs={{0,0},{4,8},{8,4},{12,12},{1,5},{5,1},{9,13},{13,9},{2,2},{6,10},{... | collective-permute-start | bytes 1204232 | tf_op jit(solution)/shard_map/ppermute | solution.py:262
  52.7 3.5 %encode.7 = (bf16[2,224,896]{2,1,0:T(8,128)(2,1)S(1)}, bf16[224,896]{1,0:T(8,128)(2,1)S(1)}) custom-call(f32[2,256,8]{2,1,0:T(8,128)S(1)} %get-tuple-element.28.refs_0_, bf16[1,2,2,220,220]{4,3,2,1,0:T(8,128)(2,1)S(1)} %bitcast.35, bf16[2,2,2,220,220]{4,3,2,1,0:T(8,128)(2,1)S(1)} %bitcast.31, bf16[2,456,220]{2,1,0:T(8,128)(2,1)S(1)} %get-tuple-element.31.refs_3_, ...), custom_call_target="tpu_custom_call" | custom-call | flops 1022208000 | bytes 6000000 | tf_op jit(solution)/shard_map/encode/pallas_call | solution.py:368
  56.1 3.7 %collective-permute-done.5.refs_4_.refs_2_ = bf16[224,896]{1,0:T(8,128)(2,1)S(1)} collective-permute-done((bf16[224,896]{1,0:T(8,128)(2,1)S(1)}, bf16[224,896]{1,0:T(8,128)(2,1)S(1)}, u32[]{:S(2)}, u32[]{:S(2)}) %collective-permute-start.5) | collective-permute-done | bytes 401440 | tf_op jit(solution)/shard_map/ppermute | solution.py:262
  60.0 3.9 %collective-permute-start.6 = (bf16[224,896]{1,0:T(8,128)(2,1)S(1)}, bf16[224,896]{1,0:T(8,128)(2,1)S(1)}, u32[]{:S(2)}, u32[]{:S(2)}) collective-permute-start(bf16[224,896]{1,0:T(8,128)(2,1)S(1)} %add_select_fusion), channel_id=1, source_target_pairs={{0,4},{4,0},{8,12},{12,8},{1,1},{5,9},{9,5},{13,13},{2,6},{6,2},{1... | collective-permute-start | bytes 1204232 | tf_op jit(solution)/shard_map/ppermute | solution.py:262
  63.9 7.4 %collective-permute-done.6.refs_3_.refs_1_ = bf16[224,896]{1,0:T(8,128)(2,1)S(1)} collective-permute-done((bf16[224,896]{1,0:T(8,128)(2,1)S(1)}, bf16[224,896]{1,0:T(8,128)(2,1)S(1)}, u32[]{:S(2)}, u32[]{:S(2)}) %collective-permute-start.6) | collective-permute-done | bytes 401440 | tf_op jit(solution)/shard_map/ppermute | solution.py:262
  71.4 1.9 %collective-permute-start.7 = (bf16[224,896]{1,0:T(8,128)(2,1)S(1)}, bf16[224,896]{1,0:T(8,128)(2,1)S(1)}, u32[]{:S(2)}, u32[]{:S(2)}) collective-permute-start(bf16[224,896]{1,0:T(8,128)(2,1)S(1)} %select_select_fusion.1), channel_id=1, source_target_pairs={{0,0},{4,8},{8,4},{12,12},{1,5},{5,1},{9,13},{13,9},{2,2},{6,10},{... | collective-permute-start | bytes 1204232 | tf_op jit(solution)/shard_map/ppermute | solution.py:262
  73.3 10.0 %collective-permute-done.7.refs_4_.refs_2_ = bf16[224,896]{1,0:T(8,128)(2,1)S(1)} collective-permute-done((bf16[224,896]{1,0:T(8,128)(2,1)S(1)}, bf16[224,896]{1,0:T(8,128)(2,1)S(1)}, u32[]{:S(2)}, u32[]{:S(2)}) %collective-permute-start.7) | collective-permute-done | bytes 401440 | tf_op jit(solution)/shard_map/ppermute | solution.py:262
  83.4 3.9 %collective-permute-start.8 = (bf16[224,896]{1,0:T(8,128)(2,1)S(1)}, bf16[224,896]{1,0:T(8,128)(2,1)S(1)}, u32[]{:S(2)}, u32[]{:S(2)}) collective-permute-start(bf16[224,896]{1,0:T(8,128)(2,1)S(1)} %add.61), channel_id=1, source_target_pairs={{0,4},{4,0},{8,12},{12,8},{1,1},{5,9},{9,5},{13,13},{2,6},{6,2},{1... | collective-permute-start | bytes 1204232 | tf_op jit(solution)/shard_map/ppermute | solution.py:262
  87.3 9.7 %collective-permute-done.8.refs_3_ = bf16[224,896]{1,0:T(8,128)(2,1)S(1)} collective-permute-done((bf16[224,896]{1,0:T(8,128)(2,1)S(1)}, bf16[224,896]{1,0:T(8,128)(2,1)S(1)}, u32[]{:S(2)}, u32[]{:S(2)}) %collective-permute-start.8) | collective-permute-done | bytes 401440 | tf_op jit(solution)/shard_map/ppermute | solution.py:262
  97.1 1.9 %collective-permute-start.9 = (bf16[224,896]{1,0:T(8,128)(2,1)S(1)}, bf16[224,896]{1,0:T(8,128)(2,1)S(1)}, u32[]{:S(2)}, u32[]{:S(2)}) collective-permute-start(bf16[224,896]{1,0:T(8,128)(2,1)S(1)} %add.62), channel_id=1, source_target_pairs={{0,0},{4,8},{8,4},{12,12},{1,5},{5,1},{9,13},{13,9},{2,2},{6,10},{... | collective-permute-start | bytes 1204232 | tf_op jit(solution)/shard_map/ppermute | solution.py:262
  100.7 8.6 %collective-permute-done.9.refs_4_ = bf16[224,896]{1,0:T(8,128)(2,1)S(1)} collective-permute-done((bf16[224,896]{1,0:T(8,128)(2,1)S(1)}, bf16[224,896]{1,0:T(8,128)(2,1)S(1)}, u32[]{:S(2)}, u32[]{:S(2)}) %collective-permute-start.9) | collective-permute-done | bytes 401440 | tf_op jit(solution)/shard_map/ppermute | solution.py:262
  109.9 12.4 %collective-permute-start.12 = (f32[8,220]{1,0:T(8,128)S(1)}, f32[8,220]{1,0:T(8,128)S(1)}, u32[]{:S(2)}, u32[]{:S(2)}) collective-permute-start(f32[8,220]{1,0:T(8,128)S(1)} %reshape.3), channel_id=1, source_target_pairs={{0,3},{1,2},{2,1},{3,0},{4,7},{5,6},{6,5},{7,4},{8,11},{9,10},{10,... | collective-permute-start | bytes 21128 | tf_op jit(solution)/shard_map/ppermute | solution.py:244
  (36 shorter events, 12.1 us)
Async XLA Ops:
  4.0 0.9 copy-start
  4.9 8.9 %collective-permute-start = (bf16[224,896]{1,0:T(8,128)(2,1)S(1)}, bf16[224,896]{1,0:T(8,128)(2,1)S(1)}, u32[]{:S(2)}, u32[]{:S(2)}) collective-permute-start(bf16[224,896]{1,0:T(8,128)(2,1)S(1)} %get-tuple-element.40.refs_0_), channel_id=1, source_target_pairs={{0,4},{4,0},{8,12},{12,8},{1,1},{5,9},{9,5},{13,13},{2,6},{6,2},{1... | collective-permute-start | bytes 1204232 | tf_op jit(solution)/shard_map/ppermute | solution.py:262
  14.7 9.1 %collective-permute-start.1 = (bf16[224,896]{1,0:T(8,128)(2,1)}, bf16[224,896]{1,0:T(8,128)(2,1)S(1)}, u32[]{:S(2)}, u32[]{:S(2)}) collective-permute-start(bf16[224,896]{1,0:T(8,128)(2,1)} %select_select_fusion), channel_id=1, source_target_pairs={{0,0},{4,8},{8,4},{12,12},{1,5},{5,1},{9,13},{13,9},{2,2},{6,10},{... | collective-permute-start | bytes 1204232 | tf_op jit(solution)/shard_map/ppermute | solution.py:262
  23.8 8.9 %collective-permute-start.2 = (bf16[224,896]{1,0:T(8,128)(2,1)S(1)}, bf16[224,896]{1,0:T(8,128)(2,1)S(1)}, u32[]{:S(2)}, u32[]{:S(2)}) collective-permute-start(bf16[224,896]{1,0:T(8,128)(2,1)S(1)} %add_select_fusion.2), channel_id=1, source_target_pairs={{0,4},{4,0},{8,12},{12,8},{1,1},{5,9},{9,5},{13,13},{2,6},{6,2},{1... | collective-permute-start | bytes 1204232 | tf_op jit(solution)/shard_map/ppermute | solution.py:262
  32.8 8.9 %collective-permute-start.3 = (bf16[224,896]{1,0:T(8,128)(2,1)S(1)}, bf16[224,896]{1,0:T(8,128)(2,1)S(1)}, u32[]{:S(2)}, u32[]{:S(2)}) collective-permute-start(bf16[224,896]{1,0:T(8,128)(2,1)S(1)} %select_select_fusion.3), channel_id=1, source_target_pairs={{0,0},{4,8},{8,4},{12,12},{1,5},{5,1},{9,13},{13,9},{2,2},{6,10},{... | collective-permute-start | bytes 1204232 | tf_op jit(solution)/shard_map/ppermute | solution.py:262
  41.8 8.6 %collective-permute-start.4 = (bf16[224,896]{1,0:T(8,128)(2,1)S(1)}, bf16[224,896]{1,0:T(8,128)(2,1)S(1)}, u32[]{:S(2)}, u32[]{:S(2)}) collective-permute-start(bf16[224,896]{1,0:T(8,128)(2,1)S(1)} %add_select_fusion.1), channel_id=1, source_target_pairs={{0,4},{4,0},{8,12},{12,8},{1,1},{5,9},{9,5},{13,13},{2,6},{6,2},{1... | collective-permute-start | bytes 1204232 | tf_op jit(solution)/shard_map/ppermute | solution.py:262
  50.5 9.3 %collective-permute-start.5 = (bf16[224,896]{1,0:T(8,128)(2,1)S(1)}, bf16[224,896]{1,0:T(8,128)(2,1)S(1)}, u32[]{:S(2)}, u32[]{:S(2)}) collective-permute-start(bf16[224,896]{1,0:T(8,128)(2,1)S(1)} %select_select_fusion.2), channel_id=1, source_target_pairs={{0,0},{4,8},{8,4},{12,12},{1,5},{5,1},{9,13},{13,9},{2,2},{6,10},{... | collective-permute-start | bytes 1204232 | tf_op jit(solution)/shard_map/ppermute | solution.py:262
  56.1 42.9 %copy-start.1 = (bf16[2,224,896]{2,1,0:T(8,128)(2,1)S(1)}, bf16[2,224,896]{2,1,0:T(8,128)(2,1)}, u32[]{:S(2)}) copy-start(bf16[2,224,896]{2,1,0:T(8,128)(2,1)} %copy-done) | copy-start | bytes 2408452
  60.0 11.3 %collective-permute-start.6 = (bf16[224,896]{1,0:T(8,128)(2,1)S(1)}, bf16[224,896]{1,0:T(8,128)(2,1)S(1)}, u32[]{:S(2)}, u32[]{:S(2)}) collective-permute-start(bf16[224,896]{1,0:T(8,128)(2,1)S(1)} %add_select_fusion), channel_id=1, source_target_pairs={{0,4},{4,0},{8,12},{12,8},{1,1},{5,9},{9,5},{13,13},{2,6},{6,2},{1... | collective-permute-start | bytes 1204232 | tf_op jit(solution)/shard_map/ppermute | solution.py:262
  71.4 11.9 %collective-permute-start.7 = (bf16[224,896]{1,0:T(8,128)(2,1)S(1)}, bf16[224,896]{1,0:T(8,128)(2,1)S(1)}, u32[]{:S(2)}, u32[]{:S(2)}) collective-permute-start(bf16[224,896]{1,0:T(8,128)(2,1)S(1)} %select_select_fusion.1), channel_id=1, source_target_pairs={{0,0},{4,8},{8,4},{12,12},{1,5},{5,1},{9,13},{13,9},{2,2},{6,10},{... | collective-permute-start | bytes 1204232 | tf_op jit(solution)/shard_map/ppermute | solution.py:262
  83.4 13.6 %collective-permute-start.8 = (bf16[224,896]{1,0:T(8,128)(2,1)S(1)}, bf16[224,896]{1,0:T(8,128)(2,1)S(1)}, u32[]{:S(2)}, u32[]{:S(2)}) collective-permute-start(bf16[224,896]{1,0:T(8,128)(2,1)S(1)} %add.61), channel_id=1, source_target_pairs={{0,4},{4,0},{8,12},{12,8},{1,1},{5,9},{9,5},{13,13},{2,6},{6,2},{1... | collective-permute-start | bytes 1204232 | tf_op jit(solution)/shard_map/ppermute | solution.py:262
  97.1 12.2 %collective-permute-start.9 = (bf16[224,896]{1,0:T(8,128)(2,1)S(1)}, bf16[224,896]{1,0:T(8,128)(2,1)S(1)}, u32[]{:S(2)}, u32[]{:S(2)}) collective-permute-start(bf16[224,896]{1,0:T(8,128)(2,1)S(1)} %add.62), channel_id=1, source_target_pairs={{0,0},{4,8},{8,4},{12,12},{1,5},{5,1},{9,13},{13,9},{2,2},{6,10},{... | collective-permute-start | bytes 1204232 | tf_op jit(solution)/shard_map/ppermute | solution.py:262
  109.9 14.0 %collective-permute-start.12 = (f32[8,220]{1,0:T(8,128)S(1)}, f32[8,220]{1,0:T(8,128)S(1)}, u32[]{:S(2)}, u32[]{:S(2)}) collective-permute-start(f32[8,220]{1,0:T(8,128)S(1)} %reshape.3), channel_id=1, source_target_pairs={{0,3},{1,2},{2,1},{3,0},{4,7},{5,6},{6,5},{7,4},{8,11},{9,10},{10,... | collective-permute-start | bytes 21128 | tf_op jit(solution)/shard_map/ppermute | solution.py:244
  122.3 2.5 %collective-permute-start.11 = (f32[8,220]{1,0:T(8,128)S(1)}, f32[8,220]{1,0:T(8,128)S(1)}, u32[]{:S(2)}, u32[]{:S(2)}) collective-permute-start(f32[8,220]{1,0:T(8,128)S(1)} %reshape.3), channel_id=1, source_target_pairs={{0,2},{1,3},{2,0},{3,1},{4,6},{5,7},{6,4},{7,5},{8,10},{9,11},{10,... | collective-permute-start | bytes 21128 | tf_op jit(solution)/shard_map/ppermute | solution.py:244
  122.6 2.3 %collective-permute-start.10 = (f32[8,220]{1,0:T(8,128)S(1)}, f32[8,220]{1,0:T(8,128)S(1)}, u32[]{:S(2)}, u32[]{:S(2)}) collective-permute-start(f32[8,220]{1,0:T(8,128)S(1)} %reshape.3), channel_id=1, source_target_pairs={{0,1},{1,0},{2,3},{3,2},{4,5},{5,4},{6,7},{7,6},{8,9},{9,8},{10,11... | collective-permute-start | bytes 21128 | tf_op jit(solution)/shard_map/ppermute | solution.py:244

commit v13 on v12

--- a/solution.py
+++ b/solution.py
@@ -100,8 +100,8 @@
         angle[row : row + 1, :length] = (
             2.0 * math.pi / MB * turns.astype(jnp.float32) + offset[row : row + 1, :]
         )
-    phase_out[0] = jnp.cos(angle[...]).T
-    phase_out[1] = jnp.sin(angle[...]).T
+    phase_out[:, :per_device] = jnp.cos(angle[...]).T
+    phase_out[:, per_device:] = jnp.sin(angle[...]).T
     for copy in copies:
         copy.wait()
 
@@ -113,8 +113,12 @@
         next_rows = next_rows and [place_ref[2]]
     phase_ref, image, coil_map, left_ref = refs[:4]
     order_ref, gram_ref, adjoint_ref, kspace_ref, image_ref, map_ref = refs[4:10]
-    shifted, refs = refs[10], refs[11:]
-    out_ref, refs = refs[0], refs[1:]
+    refs = refs[10:]
+    if group > 0:
+        earlier_ref, refs = refs[0], refs[1:]
+    shifted, out_ref, refs = refs[0], refs[1], refs[2:]
+    if group > 0:
+        kept_ref, refs = refs[0], refs[1:]
     if next_rows:
         next_image, next_map, refs = refs[0], refs[1], refs[2:]
     total, wide, raw_kspace, gram, adjoint, order, arrived, small = refs
@@ -129,6 +133,8 @@
     next_copies = []
     if next_rows:
         next_copies = slice_copies(image_ref, map_ref, next_image, next_map, arrived, next_rows)
+    if group > 0:
+        next_copies.append(pltpu.make_async_copy(earlier_ref, kept_ref, small.at[4]))
     start_all([order_copy, gram_copy, *next_copies])
 
     if lanes > vols * coils * 2 * length:
@@ -140,10 +146,11 @@
     for slot in range(slots):
         if whole_classes:
             column = rows_of[slot]
-            cosine = phase_ref[0, :rows, column : column + 1]
-            sine = phase_ref[1, :rows, column : column + 1]
+            half = phase_ref.shape[1] // 2
+            cosine = phase_ref[:rows, column : column + 1]
+            sine = phase_ref[:rows, half + column : half + column + 1]
         else:
-            cosine, sine = phase_ref[0, :rows], phase_ref[1, :rows]
+            cosine, sine = phase_ref[:rows, :1], phase_ref[:rows, 1:]
         for vol in range(vols):
             image_re = image[vol, slot, 0].astype(jnp.float32)
             image_im = image[vol, slot, 1].astype(jnp.float32)
@@ -210,10 +217,9 @@
         copy.wait()
 
 
-def line_place():
+def at_line_end():
     position = lax.axis_index("slc")
-    edge = (position == 0) | (position == lax.axis_size("slc") - 1)
-    return edge, lax.axis_index("vol") % 2 == 0
+    return (position == 0) | (position == lax.axis_size("slc") - 1)
 
 
 def gradient_kernel(factor, on_line, *refs):
@@ -222,9 +228,8 @@
     terms = [ref[...].astype(jnp.float32) for ref in term_refs]
     residual = terms[0]
     if on_line:
-        edge, leads = line_place()
-        inside = jnp.where(leads, terms[1] + terms[2], terms[2] + terms[3])
-        residual += jnp.where(edge, jnp.where(leads, terms[3], terms[4]), inside)
+        near, across, rest = terms[1:]
+        residual += jnp.where(at_line_end(), rest, near + across)
     for slot in range(slots):
         product = residual * shifted_ref[slot].astype(jnp.float32)
         tiles = [product[:, at : at + LANE_TILE] for at in range(0, lanes, LANE_TILE)]
@@ -248,50 +253,41 @@
 
 
 def line_of_four(encode, gradient, count):
-    edge, leads = line_place()
-    cores = lax.axis_size("vol")
-    outer_pairs = [(0, 1), (1, 0), (2, 3), (3, 2)]
-    inner_pairs = [(0, 0), (1, 2), (2, 1), (3, 3)]
-
-    def exchange(value, step):
-        pairs = [
-            (source * cores + core, target * cores + core)
-            for core in range(cores)
-            for source, target in ((outer_pairs, inner_pairs)[(step + core) % 2])
-        ]
-        return lax.ppermute(value, ("slc", "vol"), pairs)
-
-    shifted, own = map(list, zip(encode(0)))
-    payload, received, gradients = own[0], [], []
-    for step in range(2 * count + 2):
-        received.append(exchange(payload, step))
-        group = step // 2
-        if step % 2 == 0 and group + 1 < count:
-            encoded = encode(group + 1, payload) if step else encode(1)
-            shifted.append(encoded[0])
-            own.append(encoded[1])
-        done = group - 2
-        if step % 2 == 0 and done >= 0:
-            terms = (own[done], *received[2 * done : 2 * done + 4])
-            gradients.append(gradient((after(terms[0], payload), *terms[1:]), shifted[done]))
-        if step == 2 * count + 1:
-            break
-        arrived = received[-1]
-        if step % 2 == 0:
-            before = own[group - 1] if group else own[0]
-            if group < count:
-                mine = own[group]
-                payload = jnp.where(
-                    leads, mine + arrived, jnp.where(edge, mine, before + arrived)
-                )
-            else:
-                payload = before + arrived
+    edge = at_line_end()
+
+    def outer(value):
+        return lax.ppermute(value, "slc", [(0, 1), (1, 0), (2, 3), (3, 2)])
+
+    def inner(value):
+        return lax.ppermute(value, "slc", [(0, 0), (1, 2), (2, 1), (3, 3)])
+
+    own = [encode(0)]
+    near, across, gradients = [outer(own[0])], [], []
+    while len(own) < min(3, count):
+        own.append(encode(len(own)))
+    latest = own[-1]
+    for step in range(1, count + 2):
+        arrived = after(near[-1], latest)
+        half = own[step - 1] + arrived if step <= count else None
+        payload = own[step] if step < count else None
+        if step >= 2:
+            others = own[step - 2] + after(across[step - 2], near[-1] if half is None else half)
+            payload = others if payload is None else jnp.where(edge, payload, others)
         else:
-            payload = own[group] + arrived
-            if group + 1 < count:
-                payload = jnp.where(leads & edge, own[group + 1], payload)
+            payload = after(payload, half)
+        if half is not None:
+            across.append(inner(half))
+        near.append(outer(payload))
+        latest = payload
+        if len(own) < count:
+            own.append(encode(len(own), payload))
+            latest = own[-1]
+        if step >= 3:
+            done = step - 3
+            terms = (own[done], near[done], across[done], near[done + 2])
+            gradients.append(gradient((after(terms[0], payload), *terms[1:]), done))
     last = count - 1
-    gradients.append(gradient((own[last], *received[2 * last : 2 * last + 4]), shifted[last]))
+    gradients.append(gradient((own[last], near[last], across[last], near[last + 2]), last))
     return gradients
 
 
@@ -344,7 +340,7 @@
         out_shape=raw_shapes
         + [
             jax.ShapeDtypeStruct(left.shape, left.dtype),
-            jax.ShapeDtypeStruct((2, padded_rows, per_device), jnp.float32),
+            jax.ShapeDtypeStruct((padded_rows, 2 * per_device), jnp.float32),
         ],
         scratch_shapes=[
             pltpu.SMEM((per_device,), jnp.int32),
@@ -357,14 +353,19 @@
         name="fetch",
     )(*place_of(0), in_hbm(shift_index), in_hbm(phase_offset), *lying[:2], left)
 
+    latest, kept = [], []
+
     def encode(group, *earlier):
         image, coil_map = (jnp.swapaxes(array, -3, -2) for array in raw)
         has_next = group + 1 < groups
         place, group_phases = place_of(group), phases
         if not whole_classes:
-            group_phases = lax.dynamic_slice_in_dim(phases, place[0][1], 1, axis=2)
+            group_phases = jnp.take(
+                phases, jnp.stack([place[0][1], place[0][1] + per_device]), axis=1
+            )
         if earlier:
             image = after(image, *earlier)
+        kept_shape = pltpu.HBM((slots, rows, lanes), jnp.bfloat16)
         outputs = pl.pallas_call(
             functools.partial(
                 encode_kernel,
@@ -373,10 +374,13 @@
                 rows_of_class(group),
                 (rows_of_class(group + 1) or [0]) if has_next else None,
             ),
-            in_specs=scalar_specs + [in_vmem] * 4 + [in_place] * 6,
-            out_specs=[in_vmem] * (2 + 2 * has_next),
-            out_shape=[jax.ShapeDtypeStruct((slots, rows, lanes), jnp.bfloat16)]
-            + [jax.ShapeDtypeStruct((rows, lanes), jnp.bfloat16)]
+            in_specs=scalar_specs + [in_vmem] * 4 + [in_place] * 6 + [in_vmem] * len(latest),
+            out_specs=[in_vmem] * 2 + [in_place] * len(latest) + [in_vmem] * 2 * has_next,
+            out_shape=[
+                jax.ShapeDtypeStruct((slots, rows, lanes), jnp.bfloat16),
+                jax.ShapeDtypeStruct((rows, lanes), jnp.bfloat16),
+            ]
+            + [kept_shape] * len(latest)
             + raw_shapes * has_next,
             scratch_shapes=[
                 pltpu.VMEM((rows, lanes), jnp.float32),
@@ -386,7 +390,7 @@
                 pltpu.VMEM(adjoint.shape, jnp.bfloat16),
                 pltpu.SMEM((groups,), jnp.int32),
                 slice_semaphores,
-                pltpu.SemaphoreType.DMA((4,)),
+                pltpu.SemaphoreType.DMA((5,)),
             ],
             compiler_params=pltpu.CompilerParams(vmem_limit_bytes=VMEM_BYTES),
             cost_estimate=pl.CostEstimate(
@@ -406,11 +410,17 @@
             adjoint,
             lying[2],
             *lying[:2],
+            *latest,
         )
-        raw[:] = outputs[2:]
-        return outputs[:2]
-
-    def gradient(terms, encoded):
+        raw[:] = outputs[2 + len(latest) :]
+        kept.extend(outputs[2 : 2 + len(latest)])
+        latest[:] = outputs[:1]
+        return outputs[1]
+
+    def shifted_of(group):
+        return (kept + latest)[group]
+
+    def gradient(terms, group):
         return pl.pallas_call(
             functools.partial(gradient_kernel, factor, on_line),
             out_shape=jax.ShapeDtypeStruct((slots, rows), jnp.float32),
@@ -419,14 +429,13 @@
                 flops=places * slots * 4 * length**2, bytes_accessed=1_500_000, transcendentals=0
             ),
             name="gradient",
-        )(*terms, encoded)
+        )(*terms, shifted_of(group))
 
     if on_line:
         gradients = line_of_four(encode, gradient, groups)
     else:
-        encoded = [encode(group) for group in range(groups)]
-        reduced = lax.psum([own for _, own in encoded], "slc")
-        gradients = [gradient((reduced[group],), encoded[group][0]) for group in range(groups)]
+        reduced = lax.psum([encode(group) for group in range(groups)], "slc")
+        gradients = [gradient((reduced[group],), group) for group in range(groups)]
     by_class = jnp.stack(gradients, axis=1)[:, :, :length]
     if whole_classes:
         local = by_class.reshape(per_device, length)

time: 124 us -> 78.6 us (0.63)
  the two profiles are of different devices: /device:TPU:13 before, /device:TPU:0 now
where the time goes in v13:
time: 78.6 us; the launch traced here: 77.8 us
  starting transfers between devices  28.9 us (37%)
  waiting for transfers between devices  26.8 us (34%)
  Pallas kernels  15.8 us (20%)
  other arithmetic  4.19 us (5%)
  local copies, waits for them, and re-layouts  1.93 us (2%)
    ppermute x6, waiting for transfers between devices, outer(): return lax.ppermute(value, 'slc', [(0, 1), (1, 0), (2, 3), (3, 2)])  24 us
    ppermute x6, starting transfers between devices, outer(): return lax.ppermute(value, 'slc', [(0, 1), (1, 0), (2, 3), (3, 2)])  20 us
    pallas_call x4, Pallas kernels, encode(): pl.pallas_call(functools.partial(encode_kernel, slots, group, rows_of_cla...  10.3 us
    ppermute x4, starting transfers between devices, inner(): return lax.ppermute(value, 'slc', [(0, 0), (1, 2), (2, 1), (3, 3)])  6.9 us
    pallas_call x4, Pallas kernels, gradient(): pl.pallas_call(functools.partial(gradient_kernel, factor, on_line), out_s...  3.81 us
    ppermute x3, waiting for transfers between devices, sum_over_replicas(): lax.ppermute(value, axes, [(index, index ^ mask) for index in range(4)])  2.75 us
    add x4, other arithmetic, line_of_four(): half = own[step - 1] + arrived if step <= count else None  2.2 us
    ppermute x3, starting transfers between devices, sum_over_replicas(): lax.ppermute(value, axes, [(index, index ^ mask) for index in range(4)])  1.93 us
  transfers between devices with their start and end apart: 13, of which 8 were waited for; matrix products, arithmetic and copies ran while one was open for 2% of the time, Pallas kernels for 15%

profile of v13, /device:TPU:0, one launch (start us, length us, event | category | flops | bytes accessed | tf_op | source)
XLA Modules:
  0.0 77.8 jit_solution(4625695272040086662)
XLA Ops:
  0.0 1.7 %fetch.1 = (bf16[1,2,220,2,220]{4,3,2,1,0:T(2,128)(2,1)S(1)}, bf16[2,2,220,2,220]{4,3,2,1,0:T(2,128)(2,1)S(1)}, bf16[2,456,220]{2,1,0:T(8,128)(2,1)S(1)}, f32[256,16]{1,0:T(8,128)S(1)}) custom-call(s32[8]{0:T(128)} %refs_0_.1, f32[8,220]{1,0:T(8,128)} %refs_1_.1, bf16[1,8,220,2,220]{4,3,2,1,0:T(2,128)(2,1)} %bitcast.48, ...), custom_call_target="tpu_custom_call" | custom-call | tf_op jit(solution)/shard_map/fetch/pallas_call | solution.py:336
  1.9 2.2 %encode.4 = (bf16[2,224,896]{2,1,0:T(8,128)(2,1)S(1)}, bf16[224,896]{1,0:T(8,128)(2,1)S(1)}, bf16[1,2,220,2,220]{4,3,2,1,0:T(2,128)(2,1)S(1)}, bf16[2,2,220,2,220]{4,3,2,1,0:T(2,128)(2,1)S(1)}) custom-call(f32[256,16]{1,0:T(8,128)S(1)} %get-tuple-element.39.refs_0_, bf16[1,2,2,220,220]{4,3,2,1,0:T(8,128)(2,1)S(1)} %bitcast.38, ...), custom_call_target="tpu_custom_call" | custom-call | flops 1022208000 | bytes 6000000 | tf_op jit(solution)/shard_map/encode/pallas_call | solution.py:369
  4.1 3.1 %collective-permute-start = (bf16[224,896]{1,0:T(8,128)(2,1)S(1)}, bf16[224,896]{1,0:T(8,128)(2,1)S(1)}, u32[]{:S(2)}, u32[]{:S(2)}) collective-permute-start(bf16[224,896]{1,0:T(8,128)(2,1)S(1)} %get-tuple-element.63.refs_0_), channel_id=1, source_target_pairs={{0,4},{4,0},{8,12},{12,8},{1,5},{5,1},{9,13},{13,9},{2,6},{6,2},{1... | collective-permute-start | bytes 1204232 | tf_op jit(solution)/shard_map/ppermute | solution.py:259
  7.3 2.4 %encode.5 = (bf16[2,224,896]{2,1,0:T(8,128)(2,1)S(1)}, bf16[224,896]{1,0:T(8,128)(2,1)S(1)}, bf16[2,224,896]{2,1,0:T(8,128)(2,1)}, bf16[1,2,220,2,220]{4,3,2,1,0...) custom-call(f32[256,16]{1,0:T(8,128)S(1)} %get-tuple-element.39.refs_0_, bf16[1,2,2,220,220]{4,3,2,1,0:T(8,128)(2,1)S(1)} %bitcast.36, ...), custom_call_target="tpu_custom_call" | custom-call | flops 1022208000 | bytes 6000000 | tf_op jit(solution)/shard_map/encode/pallas_call | solution.py:369
  10.0 3.7 %encode.6 = (bf16[2,224,896]{2,1,0:T(8,128)(2,1)S(1)}, bf16[224,896]{1,0:T(8,128)(2,1)S(1)}, bf16[2,224,896]{2,1,0:T(8,128)(2,1)}, bf16[1,2,220,2,220]{4,3,2,1,0...) custom-call(f32[256,16]{1,0:T(8,128)S(1)} %get-tuple-element.39.refs_0_, bf16[1,2,2,220,220]{4,3,2,1,0:T(8,128)(2,1)S(1)} %bitcast.37, ...), custom_call_target="tpu_custom_call" | custom-call | flops 1022208000 | bytes 6000000 | tf_op jit(solution)/shard_map/encode/pallas_call | solution.py:369
  13.7 2.8 %collective-permute-done.refs_1_ = bf16[224,896]{1,0:T(8,128)(2,1)S(1)} collective-permute-done((bf16[224,896]{1,0:T(8,128)(2,1)S(1)}, bf16[224,896]{1,0:T(8,128)(2,1)S(1)}, u32[]{:S(2)}, u32[]{:S(2)}) %collective-permute-start) | collective-permute-done | bytes 401440 | tf_op jit(solution)/shard_map/ppermute | solution.py:259
  17.3 1.7 %collective-permute-start.1 = (bf16[224,896]{1,0:T(8,128)(2,1)S(1)}, bf16[224,896]{1,0:T(8,128)(2,1)}, u32[]{:S(2)}, u32[]{:S(2)}) collective-permute-start(bf16[224,896]{1,0:T(8,128)(2,1)S(1)} %get-tuple-element.67.refs_0_), channel_id=1, source_target_pairs={{0,4},{4,0},{8,12},{12,8},{1,5},{5,1},{9,13},{13,9},{2,6},{6,2},{1... | collective-permute-start | bytes 1204232 | tf_op jit(solution)/shard_map/ppermute | solution.py:259
  19.1 4.9 %collective-permute-start.3 = (bf16[224,896]{1,0:T(8,128)(2,1)}, bf16[224,896]{1,0:T(8,128)(2,1)}, u32[]{:S(2)}, u32[]{:S(2)}) collective-permute-start(bf16[224,896]{1,0:T(8,128)(2,1)} %add.33), channel_id=1, source_target_pairs={{0,0},{4,8},{8,4},{12,12},{1,1},{5,9},{9,5},{13,13},{2,2},{6,10},{... | collective-permute-start | bytes 1204232 | tf_op jit(solution)/shard_map/ppermute | solution.py:262
  24.2 1.1 %copy-done.3 = bf16[2,224,896]{2,1,0:T(8,128)(2,1)S(1)} copy-done((bf16[2,224,896]{2,1,0:T(8,128)(2,1)S(1)}, bf16[2,224,896]{2,1,0:T(8,128)(2,1)}, u32[]{:S(2)}) %copy-start.3) | copy-done | bytes 802840
  25.3 2.1 %encode.7 = (bf16[2,224,896]{2,1,0:T(8,128)(2,1)S(1)}, bf16[224,896]{1,0:T(8,128)(2,1)S(1)}, bf16[2,224,896]{2,1,0:T(8,128)(2,1)}) custom-call(f32[256,16]{1,0:T(8,128)S(1)} %get-tuple-element.39.refs_0_, bf16[1,2,2,220,220]{4,3,2,1,0:T(8,128)(2,1)S(1)} %bitcast.35, bf16[2,2,2,220,220]{4,3,2,1,0:T(8,128)(2,1)S(1)} %bitcast.31, ...), custom_call_target="tpu_custom_call" | custom-call | flops 1022208000 | bytes 6000000 | tf_op jit(solution)/shard_map/encode/pallas_call | solution.py:369
  27.9 1.1 %add.34 = bf16[224,896]{1,0:T(8,128)(2,1)S(1)} add(bf16[224,896]{1,0:T(8,128)(2,1)S(1)} %get-tuple-element.67.refs_0_, bf16[224,896]{1,0:T(8,128)(2,1)} %collective-permute-done.1.refs_1_) | non-fusion elementwise | flops 200704 | bytes 1204224 | tf_op jit(solution)/shard_map/add | solution.py:271
  29.0 1.1 %add_select_fusion.1 = bf16[224,896]{1,0:T(8,128)(2,1)S(1)} fusion(bf16[224,896]{1,0:T(8,128)(2,1)S(1)} %get-tuple-element.70.refs_0_, bf16[224,896]{1,0:T(8,128)(2,1)S(1)} %get-tuple-element.63.refs_0_, bf16[224,896]{1,0:T(8,128)(2,1)} %collective-permute-done.3.refs_2_, pred[]{:T(512)S(6)} %or.3), kind=kLoop, calls=%fused_computation.9 | loop fusion | flops 401408 | bytes 1605633 | tf_op jit(solution)/shard_map/jit(_where)/select_n | solution.py:275
  30.1 3.9 %collective-permute-start.4 = (bf16[224,896]{1,0:T(8,128)(2,1)S(1)}, bf16[224,896]{1,0:T(8,128)(2,1)S(1)}, u32[]{:S(2)}, u32[]{:S(2)}) collective-permute-start(bf16[224,896]{1,0:T(8,128)(2,1)S(1)} %add_select_fusion.1), channel_id=1, source_target_pairs={{0,4},{4,0},{8,12},{12,8},{1,5},{5,1},{9,13},{13,9},{2,6},{6,2},{1... | collective-permute-start | bytes 1204232 | tf_op jit(solution)/shard_map/ppermute | solution.py:259
  34.8 7.0 %collective-permute-done.4.refs_3_.refs_1_ = bf16[224,896]{1,0:T(8,128)(2,1)S(1)} collective-permute-done((bf16[224,896]{1,0:T(8,128)(2,1)S(1)}, bf16[224,896]{1,0:T(8,128)(2,1)S(1)}, u32[]{:S(2)}, u32[]{:S(2)}) %collective-permute-start.4) | collective-permute-done | bytes 401440 | tf_op jit(solution)/shard_map/ppermute | solution.py:259
  42.0 3.7 %collective-permute-start.6 = (bf16[224,896]{1,0:T(8,128)(2,1)S(1)}, bf16[224,896]{1,0:T(8,128)(2,1)S(1)}, u32[]{:S(2)}, u32[]{:S(2)}) collective-permute-start(bf16[224,896]{1,0:T(8,128)(2,1)S(1)} %add_select_fusion), channel_id=1, source_target_pairs={{0,4},{4,0},{8,12},{12,8},{1,5},{5,1},{9,13},{13,9},{2,6},{6,2},{1... | collective-permute-start | bytes 1204232 | tf_op jit(solution)/shard_map/ppermute | solution.py:259
  46.4 6.1 %collective-permute-done.6.refs_3_.refs_1_ = bf16[224,896]{1,0:T(8,128)(2,1)S(1)} collective-permute-done((bf16[224,896]{1,0:T(8,128)(2,1)S(1)}, bf16[224,896]{1,0:T(8,128)(2,1)S(1)}, u32[]{:S(2)}, u32[]{:S(2)}) %collective-permute-start.6) | collective-permute-done | bytes 401440 | tf_op jit(solution)/shard_map/ppermute | solution.py:259
  52.7 3.6 %collective-permute-start.8 = (bf16[224,896]{1,0:T(8,128)(2,1)S(1)}, bf16[224,896]{1,0:T(8,128)(2,1)S(1)}, u32[]{:S(2)}, u32[]{:S(2)}) collective-permute-start(bf16[224,896]{1,0:T(8,128)(2,1)S(1)} %add.39), channel_id=1, source_target_pairs={{0,4},{4,0},{8,12},{12,8},{1,5},{5,1},{9,13},{13,9},{2,6},{6,2},{1... | collective-permute-start | bytes 1204232 | tf_op jit(solution)/shard_map/ppermute | solution.py:259
  56.9 5.2 %collective-permute-done.8.refs_3_ = bf16[224,896]{1,0:T(8,128)(2,1)S(1)} collective-permute-done((bf16[224,896]{1,0:T(8,128)(2,1)S(1)}, bf16[224,896]{1,0:T(8,128)(2,1)S(1)}, u32[]{:S(2)}, u32[]{:S(2)}) %collective-permute-start.8) | collective-permute-done | bytes 401440 | tf_op jit(solution)/shard_map/ppermute | solution.py:259
  62.2 4.0 %collective-permute-start.9 = (bf16[224,896]{1,0:T(8,128)(2,1)S(1)}, bf16[224,896]{1,0:T(8,128)(2,1)S(1)}, u32[]{:S(2)}, u32[]{:S(2)}) collective-permute-start(bf16[224,896]{1,0:T(8,128)(2,1)S(1)} %add.40), channel_id=1, source_target_pairs={{0,4},{4,0},{8,12},{12,8},{1,5},{5,1},{9,13},{13,9},{2,6},{6,2},{1... | collective-permute-start | bytes 1204232 | tf_op jit(solution)/shard_map/ppermute | solution.py:259
  66.2 1.5 %gradient.4 = f32[2,224]{1,0:T(2,128)S(1)} custom-call(bf16[224,896]{1,0:T(8,128)(2,1)S(1)} %get-tuple-element.63.refs_0_, bf16[224,896]{1,0:T(8,128)(2,1)S(1)} %copy-done.1, bf16[224,896]{1,0:T(8,128)(2,1)} %collective-permute-done.3.refs_2_, bf16[224,896]{1,0:T(8,128)(2,1)S(1)} %collective-permute-done.4.refs_3_.refs_1_, bf16[2,224,896]{2,1,0:T(8,128)(2,1)S(1)} %copy-done.4), custom_call_target="tpu_custom_call" | custom-call | flops 774400 | bytes 1500000 | tf_op jit(solution)/shard_map/gradient/pallas_call | solution.py:424
  67.7 1.4 %gradient.5 = f32[2,224]{1,0:T(2,128)S(1)} custom-call(bf16[224,896]{1,0:T(8,128)(2,1)S(1)} %get-tuple-element.67.refs_0_, bf16[224,896]{1,0:T(8,128)(2,1)} %collective-permute-done.1.refs_1_, bf16[224,896]{1,0:T(8,128)(2,1)S(1)} %collective-permute-done.2.refs_2_, bf16[224,896]{1,0:T(8,128)(2,1)S(1)} %collective-permute-done.6.refs_3_.refs_1_, ...), custom_call_target="tpu_custom_call" | custom-call | flops 774400 | bytes 1500000 | tf_op jit(solution)/shard_map/gradient/pallas_call | solution.py:424
  69.6 2.5 %collective-permute-done.9.refs_3_ = bf16[224,896]{1,0:T(8,128)(2,1)S(1)} collective-permute-done((bf16[224,896]{1,0:T(8,128)(2,1)S(1)}, bf16[224,896]{1,0:T(8,128)(2,1)S(1)}, u32[]{:S(2)}, u32[]{:S(2)}) %collective-permute-start.9) | collective-permute-done | bytes 401440 | tf_op jit(solution)/shard_map/ppermute | solution.py:259
  72.6 1.5 %collective-permute-start.11 = (f32[8,220]{1,0:T(8,128)S(1)}, f32[8,220]{1,0:T(8,128)S(1)}, u32[]{:S(2)}, u32[]{:S(2)}) collective-permute-start(f32[8,220]{1,0:T(8,128)S(1)} %reshape.3), channel_id=1, source_target_pairs={{0,2},{1,3},{2,0},{3,1},{4,6},{5,7},{6,4},{7,5},{8,10},{9,11},{10,... | collective-permute-start | bytes 21128 | tf_op jit(solution)/shard_map/ppermute | solution.py:249
  74.5 1.9 %collective-permute-done.11 = f32[8,220]{1,0:T(8,128)S(1)} collective-permute-done((f32[8,220]{1,0:T(8,128)S(1)}, f32[8,220]{1,0:T(8,128)S(1)}, u32[]{:S(2)}, u32[]{:S(2)}) %collective-permute-start.11) | collective-permute-done | bytes 7072 | tf_op jit(solution)/shard_map/ppermute | solution.py:249
  (45 shorter events, 7.5 us)
Async XLA Ops:
  4.1 12.4 %collective-permute-start = (bf16[224,896]{1,0:T(8,128)(2,1)S(1)}, bf16[224,896]{1,0:T(8,128)(2,1)S(1)}, u32[]{:S(2)}, u32[]{:S(2)}) collective-permute-start(bf16[224,896]{1,0:T(8,128)(2,1)S(1)} %get-tuple-element.63.refs_0_), channel_id=1, source_target_pairs={{0,4},{4,0},{8,12},{12,8},{1,5},{5,1},{9,13},{13,9},{2,6},{6,2},{1... | collective-permute-start | bytes 1204232 | tf_op jit(solution)/shard_map/ppermute | solution.py:259
  13.7 10.4 %copy-start.2 = (bf16[2,224,896]{2,1,0:T(8,128)(2,1)}, bf16[2,224,896]{2,1,0:T(8,128)(2,1)S(1)}, u32[]{:S(2)}) copy-start(bf16[2,224,896]{2,1,0:T(8,128)(2,1)S(1)} %get-tuple-element.57.refs_10_) | copy-start | bytes 2408452
  16.4 7.6 %copy-start = (bf16[224,896]{1,0:T(8,128)(2,1)}, bf16[224,896]{1,0:T(8,128)(2,1)S(1)}, u32[]{:S(2)}) copy-start(bf16[224,896]{1,0:T(8,128)(2,1)S(1)} %collective-permute-done.refs_1_) | copy-start | bytes 1204228
  17.3 10.6 %collective-permute-start.1 = (bf16[224,896]{1,0:T(8,128)(2,1)S(1)}, bf16[224,896]{1,0:T(8,128)(2,1)}, u32[]{:S(2)}, u32[]{:S(2)}) collective-permute-start(bf16[224,896]{1,0:T(8,128)(2,1)S(1)} %get-tuple-element.67.refs_0_), channel_id=1, source_target_pairs={{0,4},{4,0},{8,12},{12,8},{1,5},{5,1},{9,13},{13,9},{2,6},{6,2},{1... | collective-permute-start | bytes 1204232 | tf_op jit(solution)/shard_map/ppermute | solution.py:259
  19.1 9.9 %collective-permute-start.3 = (bf16[224,896]{1,0:T(8,128)(2,1)}, bf16[224,896]{1,0:T(8,128)(2,1)}, u32[]{:S(2)}, u32[]{:S(2)}) collective-permute-start(bf16[224,896]{1,0:T(8,128)(2,1)} %add.33), channel_id=1, source_target_pairs={{0,0},{4,8},{8,4},{12,12},{1,1},{5,9},{9,5},{13,13},{2,2},{6,10},{... | collective-permute-start | bytes 1204232 | tf_op jit(solution)/shard_map/ppermute | solution.py:262
  24.2 1.1 %copy-start.3 = (bf16[2,224,896]{2,1,0:T(8,128)(2,1)S(1)}, bf16[2,224,896]{2,1,0:T(8,128)(2,1)}, u32[]{:S(2)}) copy-start(bf16[2,224,896]{2,1,0:T(8,128)(2,1)} %copy-done.2) | copy-start | bytes 2408452
  30.1 36.1 %copy-start.1 = (bf16[224,896]{1,0:T(8,128)(2,1)S(1)}, bf16[224,896]{1,0:T(8,128)(2,1)}, u32[]{:S(2)}) copy-start(bf16[224,896]{1,0:T(8,128)(2,1)} %copy-done) | copy-start | bytes 1204228
  30.1 36.1 %copy-start.4 = (bf16[2,224,896]{2,1,0:T(8,128)(2,1)S(1)}, bf16[2,224,896]{2,1,0:T(8,128)(2,1)}, u32[]{:S(2)}) copy-start(bf16[2,224,896]{2,1,0:T(8,128)(2,1)} %get-tuple-element.64.refs_4_) | copy-start | bytes 2408452
  30.1 11.6 %collective-permute-start.4 = (bf16[224,896]{1,0:T(8,128)(2,1)S(1)}, bf16[224,896]{1,0:T(8,128)(2,1)S(1)}, u32[]{:S(2)}, u32[]{:S(2)}) collective-permute-start(bf16[224,896]{1,0:T(8,128)(2,1)S(1)} %add_select_fusion.1), channel_id=1, source_target_pairs={{0,4},{4,0},{8,12},{12,8},{1,5},{5,1},{9,13},{13,9},{2,6},{6,2},{1... | collective-permute-start | bytes 1204232 | tf_op jit(solution)/shard_map/ppermute | solution.py:259
  34.1 7.8 %collective-permute-start.2 = (bf16[224,896]{1,0:T(8,128)(2,1)S(1)}, bf16[224,896]{1,0:T(8,128)(2,1)S(1)}, u32[]{:S(2)}, u32[]{:S(2)}) collective-permute-start(bf16[224,896]{1,0:T(8,128)(2,1)S(1)} %add.34), channel_id=1, source_target_pairs={{0,0},{4,8},{8,4},{12,12},{1,1},{5,9},{9,5},{13,13},{2,2},{6,10},{... | collective-permute-start | bytes 1204232 | tf_op jit(solution)/shard_map/ppermute | solution.py:262
  41.9 25.8 %copy-start.5 = (bf16[2,224,896]{2,1,0:T(8,128)(2,1)S(1)}, bf16[2,224,896]{2,1,0:T(8,128)(2,1)}, u32[]{:S(2)}) copy-start(bf16[2,224,896]{2,1,0:T(8,128)(2,1)} %get-tuple-element.68.refs_4_) | copy-start | bytes 2408452
  42.0 10.5 %collective-permute-start.6 = (bf16[224,896]{1,0:T(8,128)(2,1)S(1)}, bf16[224,896]{1,0:T(8,128)(2,1)S(1)}, u32[]{:S(2)}, u32[]{:S(2)}) collective-permute-start(bf16[224,896]{1,0:T(8,128)(2,1)S(1)} %add_select_fusion), channel_id=1, source_target_pairs={{0,4},{4,0},{8,12},{12,8},{1,5},{5,1},{9,13},{13,9},{2,6},{6,2},{1... | collective-permute-start | bytes 1204232 | tf_op jit(solution)/shard_map/ppermute | solution.py:259
  45.7 6.9 %collective-permute-start.5 = (bf16[224,896]{1,0:T(8,128)(2,1)S(1)}, bf16[224,896]{1,0:T(8,128)(2,1)S(1)}, u32[]{:S(2)}, u32[]{:S(2)}) collective-permute-start(bf16[224,896]{1,0:T(8,128)(2,1)S(1)} %add.36), channel_id=1, source_target_pairs={{0,0},{4,8},{8,4},{12,12},{1,1},{5,9},{9,5},{13,13},{2,2},{6,10},{... | collective-permute-start | bytes 1204232 | tf_op jit(solution)/shard_map/ppermute | solution.py:262
  52.5 16.6 %copy-start.6 = (bf16[2,224,896]{2,1,0:T(8,128)(2,1)S(1)}, bf16[2,224,896]{2,1,0:T(8,128)(2,1)}, u32[]{:S(2)}) copy-start(bf16[2,224,896]{2,1,0:T(8,128)(2,1)} %get-tuple-element.71.refs_4_) | copy-start | bytes 2408452
  52.7 9.4 %collective-permute-start.8 = (bf16[224,896]{1,0:T(8,128)(2,1)S(1)}, bf16[224,896]{1,0:T(8,128)(2,1)S(1)}, u32[]{:S(2)}, u32[]{:S(2)}) collective-permute-start(bf16[224,896]{1,0:T(8,128)(2,1)S(1)} %add.39), channel_id=1, source_target_pairs={{0,4},{4,0},{8,12},{12,8},{1,5},{5,1},{9,13},{13,9},{2,6},{6,2},{1... | collective-permute-start | bytes 1204232 | tf_op jit(solution)/shard_map/ppermute | solution.py:259
  56.3 5.8 %collective-permute-start.7 = (bf16[224,896]{1,0:T(8,128)(2,1)S(1)}, bf16[224,896]{1,0:T(8,128)(2,1)S(1)}, u32[]{:S(2)}, u32[]{:S(2)}) collective-permute-start(bf16[224,896]{1,0:T(8,128)(2,1)S(1)} %add.38), channel_id=1, source_target_pairs={{0,0},{4,8},{8,4},{12,12},{1,1},{5,9},{9,5},{13,13},{2,2},{6,10},{... | collective-permute-start | bytes 1204232 | tf_op jit(solution)/shard_map/ppermute | solution.py:262
  62.2 9.8 %collective-permute-start.9 = (bf16[224,896]{1,0:T(8,128)(2,1)S(1)}, bf16[224,896]{1,0:T(8,128)(2,1)S(1)}, u32[]{:S(2)}, u32[]{:S(2)}) collective-permute-start(bf16[224,896]{1,0:T(8,128)(2,1)S(1)} %add.40), channel_id=1, source_target_pairs={{0,4},{4,0},{8,12},{12,8},{1,5},{5,1},{9,13},{13,9},{2,6},{6,2},{1... | collective-permute-start | bytes 1204232 | tf_op jit(solution)/shard_map/ppermute | solution.py:259
  72.5 1.9 %collective-permute-start.10 = (f32[8,220]{1,0:T(8,128)S(1)}, f32[8,220]{1,0:T(8,128)S(1)}, u32[]{:S(2)}, u32[]{:S(2)}) collective-permute-start(f32[8,220]{1,0:T(8,128)S(1)} %reshape.3), channel_id=1, source_target_pairs={{0,1},{1,0},{2,3},{3,2},{4,5},{5,4},{6,7},{7,6},{8,9},{9,8},{10,11... | collective-permute-start | bytes 21128 | tf_op jit(solution)/shard_map/ppermute | solution.py:249
  72.6 3.7 %collective-permute-start.11 = (f32[8,220]{1,0:T(8,128)S(1)}, f32[8,220]{1,0:T(8,128)S(1)}, u32[]{:S(2)}, u32[]{:S(2)}) collective-permute-start(f32[8,220]{1,0:T(8,128)S(1)} %reshape.3), channel_id=1, source_target_pairs={{0,2},{1,3},{2,0},{3,1},{4,6},{5,7},{6,4},{7,5},{8,10},{9,11},{10,... | collective-permute-start | bytes 21128 | tf_op jit(solution)/shard_map/ppermute | solution.py:249
  74.2 3.1 %collective-permute-start.12 = (f32[8,220]{1,0:T(8,128)S(1)}, f32[8,220]{1,0:T(8,128)S(1)}, u32[]{:S(2)}, u32[]{:S(2)}) collective-permute-start(f32[8,220]{1,0:T(8,128)S(1)} %reshape.3), channel_id=1, source_target_pairs={{0,3},{1,2},{2,1},{3,0},{4,7},{5,6},{6,5},{7,4},{8,11},{9,10},{10,... | collective-permute-start | bytes 21128 | tf_op jit(solution)/shard_map/ppermute | solution.py:249

commit v14 on v13

--- a/solution.py
+++ b/solution.py
@@ -13,6 +13,7 @@
 MB = 8
 ROW_TILE = 16
 LANE_TILE = 128
+PARTS = 1
 VMEM_BYTES = 24 * 1024 * 1024
 
 
@@ -54,6 +55,11 @@
     return jnp.dot(left, right, preferred_element_type=jnp.float32)
 
 
+def at_line_end():
+    position = lax.axis_index("slc")
+    return (position == 0) | (position == lax.axis_size("slc") - 1)
+
+
 def start_all(copies):
     for copy in copies:
         copy.start()
@@ -80,8 +86,8 @@
     if rows_of is None:
         rows_of, refs = [refs[0][1]], refs[1:]
     shift_ref, offset_ref, image_ref, map_ref, left_ref = refs[:5]
-    image_out, map_out, left_out, phase_out = refs[5:9]
-    shift, offset, angle, arrived, small = refs[9:]
+    image_out, map_out, left_out, phase_out, ends_out = refs[5:10]
+    shift, offset, angle, arrived, small = refs[10:]
     copies = slice_copies(image_ref, map_ref, image_out, map_out, arrived, rows_of)
     copies.append(pltpu.make_async_copy(left_ref, left_out, small.at[0]))
     early = [
@@ -90,6 +96,7 @@
     ]
     start_all(early)
     start_all(copies)
+    ends_out[...] = jnp.where(at_line_end(), 1.0, 0.0) * jnp.ones_like(ends_out)
     for copy in early:
         copy.wait()
     per_device, length = offset.shape
@@ -114,11 +121,8 @@
     phase_ref, image, coil_map, left_ref = refs[:4]
     order_ref, gram_ref, adjoint_ref, kspace_ref, image_ref, map_ref = refs[4:10]
     refs = refs[10:]
-    if group > 0:
-        earlier_ref, refs = refs[0], refs[1:]
-    shifted, out_ref, refs = refs[0], refs[1], refs[2:]
-    if group > 0:
-        kept_ref, refs = refs[0], refs[1:]
+    shifted, refs = refs[0], refs[1:]
+    out_refs, refs = refs[:PARTS], refs[PARTS:]
     if next_rows:
         next_image, next_map, refs = refs[0], refs[1], refs[2:]
     total, wide, raw_kspace, gram, adjoint, order, arrived, small = refs
@@ -133,8 +137,6 @@
     next_copies = []
     if next_rows:
         next_copies = slice_copies(image_ref, map_ref, next_image, next_map, arrived, next_rows)
-    if group > 0:
-        next_copies.append(pltpu.make_async_copy(earlier_ref, kept_ref, small.at[4]))
     start_all([order_copy, gram_copy, *next_copies])
 
     if lanes > vols * coils * 2 * length:
@@ -212,26 +214,26 @@
                         measured = term if measured is None else measured + term
                 total[:length, place * 2 * length : (place + 1) * 2 * length] -= measured
 
-    out_ref[...] = total[...].astype(jnp.bfloat16)
+    part = rows // PARTS
+    for index, out_ref in enumerate(out_refs):
+        out_ref[...] = total[index * part : (index + 1) * part, :].astype(jnp.bfloat16)
     for copy in next_copies:
         copy.wait()
 
 
-def at_line_end():
-    position = lax.axis_index("slc")
-    return (position == 0) | (position == lax.axis_size("slc") - 1)
-
-
-def gradient_kernel(factor, on_line, *refs):
+def gradient_kernel(index, factor, on_line, *refs):
     term_refs, shifted_ref, out_ref = refs[:-2], refs[-2], refs[-1]
-    slots, _, lanes = shifted_ref.shape
+    slots, rows, lanes = shifted_ref.shape
+    part = rows // PARTS
     terms = [ref[...].astype(jnp.float32) for ref in term_refs]
     residual = terms[0]
     if on_line:
         near, across, rest = terms[1:]
         residual += jnp.where(at_line_end(), rest, near + across)
     for slot in range(slots):
-        product = residual * shifted_ref[slot].astype(jnp.float32)
+        product = residual * shifted_ref[slot, index * part : (index + 1) * part, :].astype(
+            jnp.float32
+        )
         tiles = [product[:, at : at + LANE_TILE] for at in range(0, lanes, LANE_TILE)]
         folded = functools.reduce(lambda a, b: a + b, tiles)
         out_ref[slot : slot + 1, :] = factor * jnp.sum(folded.T, axis=0, keepdims=True)
@@ -252,19 +254,32 @@
     return (value + swapped[0]) + (swapped[1] + swapped[2])
 
 
-def line_of_four(encode, gradient, count):
-    edge = at_line_end()
+def line_of_four(encode, gradient, groups, ends):
+    cores = lax.axis_size("vol")
+    count = groups * PARTS
+    outer_pairs = [(0, 1), (1, 0), (2, 3), (3, 2)]
+    inner_pairs = [
+        (source * cores + core, target * cores + (core ^ 1 if swap and cores % 2 == 0 else core))
+        for source, target, swap in ((0, 0, True), (1, 2, False), (2, 1, False), (3, 3, True))
+        for core in range(cores)
+    ]
 
     def outer(value):
-        return lax.ppermute(value, "slc", [(0, 1), (1, 0), (2, 3), (3, 2)])
+        return lax.ppermute(value, "slc", outer_pairs)
 
     def inner(value):
-        return lax.ppermute(value, "slc", [(0, 0), (1, 2), (2, 1), (3, 3)])
-
-    own = [encode(0)]
-    near, across, gradients = [outer(own[0])], [], []
-    while len(own) < min(3, count):
-        own.append(encode(len(own)))
+        return lax.ppermute(value, ("slc", "vol"), inner_pairs)
+
+    own = [*encode(0)]
+    near, across, gradients, encoded = [outer(own[0])], [], [], 1
+
+    def encode_more(wanted, *earlier):
+        nonlocal encoded
+        while len(own) < min(wanted, count):
+            own.extend(encode(encoded, *earlier))
+            encoded += 1
+
+    encode_more(3)
     latest = own[-1]
     for step in range(1, count + 2):
         arrived = after(near[-1], latest)
@@ -272,16 +287,15 @@
         payload = own[step] if step < count else None
         if step >= 2:
             others = own[step - 2] + after(across[step - 2], near[-1] if half is None else half)
-            payload = others if payload is None else jnp.where(edge, payload, others)
+            payload = others if payload is None else jnp.where(ends > 0, payload, others)
         else:
             payload = after(payload, half)
         if half is not None:
             across.append(inner(half))
         near.append(outer(payload))
         latest = payload
-        if len(own) < count:
-            own.append(encode(len(own), payload))
-            latest = own[-1]
+        encode_more(step + 3, payload)
+        latest = own[-1] if step + 1 < count else payload
         if step >= 3:
             done = step - 3
             terms = (own[done], near[done], across[done], near[done + 2])
@@ -295,7 +309,7 @@
     vols, per_device, _, _, length = images.shape
     coils = coil_maps.shape[0]
     groups = lax.axis_size("slc")
-    rows = round_up(length, ROW_TILE)
+    rows = round_up(length, ROW_TILE * PARTS)
     places = vols * coils
     lanes = round_up(places * 2 * length, LANE_TILE)
     whole_classes = per_device % groups == 0
@@ -333,14 +347,15 @@
     scalar_specs = [] if whole_classes else [in_smem]
     padded_rows = round_up(rows, LANE_TILE)
     slice_semaphores = pltpu.SemaphoreType.DMA((slots, vols + coils))
-    *raw, left, phases = pl.pallas_call(
+    *raw, left, phases, ends = pl.pallas_call(
         functools.partial(fetch_kernel, rows_of_class(0)),
         in_specs=scalar_specs + [in_place] * 5,
-        out_specs=[in_vmem] * 4,
+        out_specs=[in_vmem] * 5,
         out_shape=raw_shapes
         + [
             jax.ShapeDtypeStruct(left.shape, left.dtype),
             jax.ShapeDtypeStruct((padded_rows, 2 * per_device), jnp.float32),
+            jax.ShapeDtypeStruct((1, lanes), jnp.float32),
         ],
         scratch_shapes=[
             pltpu.SMEM((per_device,), jnp.int32),
@@ -353,7 +368,7 @@
         name="fetch",
     )(*place_of(0), in_hbm(shift_index), in_hbm(phase_offset), *lying[:2], left)
 
-    latest, kept = [], []
+    shifted = []
 
     def encode(group, *earlier):
         image, coil_map = (jnp.swapaxes(array, -3, -2) for array in raw)
@@ -365,7 +380,6 @@
             )
         if earlier:
             image = after(image, *earlier)
-        kept_shape = pltpu.HBM((slots, rows, lanes), jnp.bfloat16)
         outputs = pl.pallas_call(
             functools.partial(
                 encode_kernel,
@@ -374,13 +388,10 @@
                 rows_of_class(group),
                 (rows_of_class(group + 1) or [0]) if has_next else None,
             ),
-            in_specs=scalar_specs + [in_vmem] * 4 + [in_place] * 6 + [in_vmem] * len(latest),
-            out_specs=[in_vmem] * 2 + [in_place] * len(latest) + [in_vmem] * 2 * has_next,
-            out_shape=[
-                jax.ShapeDtypeStruct((slots, rows, lanes), jnp.bfloat16),
-                jax.ShapeDtypeStruct((rows, lanes), jnp.bfloat16),
-            ]
-            + [kept_shape] * len(latest)
+            in_specs=scalar_specs + [in_vmem] * 4 + [in_place] * 6,
+            out_specs=[in_vmem] * (1 + PARTS + 2 * has_next),
+            out_shape=[jax.ShapeDtypeStruct((slots, rows, lanes), jnp.bfloat16)]
+            + [jax.ShapeDtypeStruct((rows // PARTS, lanes), jnp.bfloat16)] * PARTS
             + raw_shapes * has_next,
             scratch_shapes=[
                 pltpu.VMEM((rows, lanes), jnp.float32),
@@ -390,7 +401,7 @@
                 pltpu.VMEM(adjoint.shape, jnp.bfloat16),
                 pltpu.SMEM((groups,), jnp.int32),
                 slice_semaphores,
-                pltpu.SemaphoreType.DMA((5,)),
+                pltpu.SemaphoreType.DMA((4,)),
             ],
             compiler_params=pltpu.CompilerParams(vmem_limit_bytes=VMEM_BYTES),
             cost_estimate=pl.CostEstimate(
@@ -410,33 +421,35 @@
             adjoint,
             lying[2],
             *lying[:2],
-            *latest,
-        )
-        raw[:] = outputs[2 + len(latest) :]
-        kept.extend(outputs[2 : 2 + len(latest)])
-        latest[:] = outputs[:1]
-        return outputs[1]
-
-    def shifted_of(group):
-        return (kept + latest)[group]
-
-    def gradient(terms, group):
+        )
+        raw[:] = outputs[1 + PARTS :]
+        shifted.append(outputs[0])
+        return outputs[1 : 1 + PARTS]
+
+    def gradient(terms, piece):
+        group, index = divmod(piece, PARTS)
         return pl.pallas_call(
-            functools.partial(gradient_kernel, factor, on_line),
-            out_shape=jax.ShapeDtypeStruct((slots, rows), jnp.float32),
+            functools.partial(gradient_kernel, index, factor, on_line),
+            out_shape=jax.ShapeDtypeStruct((slots, rows // PARTS), jnp.float32),
             compiler_params=pltpu.CompilerParams(vmem_limit_bytes=VMEM_BYTES),
             cost_estimate=pl.CostEstimate(
                 flops=places * slots * 4 * length**2, bytes_accessed=1_500_000, transcendentals=0
             ),
             name="gradient",
-        )(*terms, shifted_of(group))
+        )(*terms, shifted[group])
 
     if on_line:
-        gradients = line_of_four(encode, gradient, groups)
+        gradients = line_of_four(encode, gradient, groups, ends)
     else:
-        reduced = lax.psum([encode(group) for group in range(groups)], "slc")
-        gradients = [gradient((reduced[group],), group) for group in range(groups)]
-    by_class = jnp.stack(gradients, axis=1)[:, :, :length]
+        reduced = lax.psum([piece for group in range(groups) for piece in encode(group)], "slc")
+        gradients = [gradient((piece,), index) for index, piece in enumerate(reduced)]
+    by_class = jnp.stack(
+        [
+            jnp.concatenate(gradients[group * PARTS : (group + 1) * PARTS], axis=1)
+            for group in range(groups)
+        ],
+        axis=1,
+    )[:, :, :length]
     if whole_classes:
         local = by_class.reshape(per_device, length)
     else:

time: 78.6 us -> 71.7 us (0.912)
  starting transfers between devices: 28.9 us -> 14.9 us
  waiting for transfers between devices: 26.8 us -> 40.2 us
  other arithmetic: 4.19 us -> 1.43 us
  Pallas kernels: 15.8 us -> 13.6 us
  local copies, waits for them, and re-layouts: 1.93 us -> 0.76 us
    ppermute x10, starting transfers between devices: 27 us -> 13 us  [the longest x6 13 us: outer(): return lax.ppermute(value, 'slc', outer_pairs)]
    ppermute x10, waiting for transfers between devices: 24 us -> 37.5 us  [the longest x6 37.5 us: outer(): return lax.ppermute(value, 'slc', outer_pairs)]
    pallas_call x4, Pallas kernels: 3.81 us -> 1.77 us  [gradient(): pl.pallas_call(functools.partial(gradient_kernel, index, factor, on_line)...]
    add x4, other arithmetic: 2.2 us -> 0.4 us  [line_of_four(): half = own[step - 1] + arrived if step <= count else None]
    unnamed x14 -> x0, local copies, waits for them, and re-layouts: 1.16 us -> none
    select_n x2, other arithmetic: 1.16 us -> 0.19 us  [line_of_four(): jnp.where(ends > 0, payload, others)]
  transfers between devices with their start and end apart: 13 -> 13, of which waited for: 8 -> 8; matrix products, arithmetic and copies ran while one was open for 2% -> 1% of each run, Pallas kernels for 15% -> 13%
where the time goes in v14:
time: 71.7 us; the launch traced here: 71.2 us
  waiting for transfers between devices  40.2 us (56%)
  starting transfers between devices  14.9 us (21%)
  Pallas kernels  13.6 us (19%)
  other arithmetic  1.43 us (2%)
  local copies, waits for them, and re-layouts  0.76 us (1%)
    ppermute x6, waiting for transfers between devices, outer(): return lax.ppermute(value, 'slc', outer_pairs)  37.5 us
    ppermute x6, starting transfers between devices, outer(): return lax.ppermute(value, 'slc', outer_pairs)  13 us
    pallas_call x4, Pallas kernels, encode(): pl.pallas_call(functools.partial(encode_kernel, slots, group, rows_of_cla...  10.2 us
    ppermute x3, waiting for transfers between devices, sum_over_replicas(): lax.ppermute(value, axes, [(index, index ^ mask) for index in range(4)])  2.76 us
    ppermute x3, starting transfers between devices, sum_over_replicas(): lax.ppermute(value, axes, [(index, index ^ mask) for index in range(4)])  1.93 us
    pallas_call x4, Pallas kernels, gradient(): pl.pallas_call(functools.partial(gradient_kernel, index, factor, on_line)...  1.77 us
    pallas_call x1, Pallas kernels, body(): pl.pallas_call(functools.partial(fetch_kernel, rows_of_class(0)), in_spec...  1.66 us
  transfers between devices with their start and end apart: 13, of which 8 were waited for; matrix products, arithmetic and copies ran while one was open for 1% of the time, Pallas kernels for 13%

profile of v14, /device:TPU:0, one launch (start us, length us, event | category | flops | bytes accessed | tf_op | source)
XLA Modules:
  0.0 71.2 jit_solution(7723849565261946430)
XLA Ops:
  0.0 1.7 %fetch.1 = (bf16[1,2,220,2,220]{4,3,2,1,0:T(2,128)(2,1)S(1)}, bf16[2,2,220,2,220]{4,3,2,1,0:T(2,128)(2,1)S(1)}, bf16[2,456,220]{2,1,0:T(8,128)(2,1)S(1)}, f32[256,16]{1,0:T(8,128)S(1)}, f32[1,896]{1,0:T(1,128)S(1)}) custom-call(s32[8]{0:T(128)} %refs_0_.1, f32[8,220]{1,0:T(8,128)} %refs_1_.1, bf16[1,8,220,2,220]{4,3,2,1,0:T(2,128)(2,1)} %bitcast.48, ...), custom_call_target="tpu_custom_call" | custom-call | tf_op jit(solution)/shard_map/fetch/pallas_call | solution.py:350
  1.9 2.2 %encode.4 = (bf16[2,224,896]{2,1,0:T(8,128)(2,1)S(1)}, bf16[224,896]{1,0:T(8,128)(2,1)S(1)}, bf16[1,2,220,2,220]{4,3,2,1,0:T(2,128)(2,1)S(1)}, bf16[2,2,220,2,220]{4,3,2,1,0:T(2,128)(2,1)S(1)}) custom-call(f32[256,16]{1,0:T(8,128)S(1)} %get-tuple-element.37.refs_0_, bf16[1,2,2,220,220]{4,3,2,1,0:T(8,128)(2,1)S(1)} %bitcast.36, ...), custom_call_target="tpu_custom_call" | custom-call | flops 1022208000 | bytes 6000000 | tf_op jit(solution)/shard_map/encode/pallas_call | solution.py:383
  4.1 4.5 %collective-permute-start = (bf16[224,896]{1,0:T(8,128)(2,1)S(1)}, bf16[224,896]{1,0:T(8,128)(2,1)S(1)}, u32[]{:S(2)}, u32[]{:S(2)}) collective-permute-start(bf16[224,896]{1,0:T(8,128)(2,1)S(1)} %get-tuple-element.59.refs_0_), channel_id=1, source_target_pairs={{0,4},{4,0},{8,12},{12,8},{1,5},{5,1},{9,13},{13,9},{2,6},{6,2},{1... | collective-permute-start | bytes 1204232 | tf_op jit(solution)/shard_map/ppermute | solution.py:268
  8.8 2.2 %encode.5 = (bf16[2,224,896]{2,1,0:T(8,128)(2,1)S(1)}, bf16[224,896]{1,0:T(8,128)(2,1)S(1)}, bf16[1,2,220,2,220]{4,3,2,1,0:T(2,128)(2,1)S(1)}, bf16[2,2,220,2,220]{4,3,2,1,0:T(2,128)(2,1)S(1)}) custom-call(f32[256,16]{1,0:T(8,128)S(1)} %get-tuple-element.37.refs_0_, bf16[1,2,2,220,220]{4,3,2,1,0:T(8,128)(2,1)S(1)} %bitcast.37, ...), custom_call_target="tpu_custom_call" | custom-call | flops 1022208000 | bytes 6000000 | tf_op jit(solution)/shard_map/encode/pallas_call | solution.py:383
  11.2 2.2 %encode.6 = (bf16[2,224,896]{2,1,0:T(8,128)(2,1)S(1)}, bf16[224,896]{1,0:T(8,128)(2,1)S(1)}, bf16[1,2,220,2,220]{4,3,2,1,0:T(2,128)(2,1)S(1)}, bf16[2,2,220,2,220]{4,3,2,1,0:T(2,128)(2,1)S(1)}) custom-call(f32[256,16]{1,0:T(8,128)S(1)} %get-tuple-element.37.refs_0_, bf16[1,2,2,220,220]{4,3,2,1,0:T(8,128)(2,1)S(1)} %bitcast.38, ...), custom_call_target="tpu_custom_call" | custom-call | flops 1022208000 | bytes 6000000 | tf_op jit(solution)/shard_map/encode/pallas_call | solution.py:383
  13.4 4.5 %collective-permute-done.refs_1_ = bf16[224,896]{1,0:T(8,128)(2,1)S(1)} collective-permute-done((bf16[224,896]{1,0:T(8,128)(2,1)S(1)}, bf16[224,896]{1,0:T(8,128)(2,1)S(1)}, u32[]{:S(2)}, u32[]{:S(2)}) %collective-permute-start) | collective-permute-done | bytes 401440 | tf_op jit(solution)/shard_map/ppermute | solution.py:268
  18.0 1.8 %collective-permute-start.1 = (bf16[224,896]{1,0:T(8,128)(2,1)S(1)}, bf16[224,896]{1,0:T(8,128)(2,1)S(1)}, u32[]{:S(2)}, u32[]{:S(2)}) collective-permute-start(bf16[224,896]{1,0:T(8,128)(2,1)S(1)} %get-tuple-element.63.refs_0_), channel_id=1, source_target_pairs={{0,4},{4,0},{8,12},{12,8},{1,5},{5,1},{9,13},{13,9},{2,6},{6,2},{1... | collective-permute-start | bytes 1204232 | tf_op jit(solution)/shard_map/ppermute | solution.py:268
  20.0 3.7 %encode.7 = (bf16[2,224,896]{2,1,0:T(8,128)(2,1)S(1)}, bf16[224,896]{1,0:T(8,128)(2,1)S(1)}) custom-call(f32[256,16]{1,0:T(8,128)S(1)} %get-tuple-element.37.refs_0_, bf16[1,2,2,220,220]{4,3,2,1,0:T(8,128)(2,1)S(1)} %bitcast.35, bf16[2,2,2,220,220]{4,3,2,1,0:T(8,128)(2,1)S(1)} %bitcast.31, bf16[2,456,220]{2,1,0:T(8,128)(2,1)S(1)} %get-tuple-element.40.refs_3_, ...), custom_call_target="tpu_custom_call" | custom-call | flops 1022208000 | bytes 6000000 | tf_op jit(solution)/shard_map/encode/pallas_call | solution.py:383
  23.7 4.9 %collective-permute-done.1.refs_1_ = bf16[224,896]{1,0:T(8,128)(2,1)S(1)} collective-permute-done((bf16[224,896]{1,0:T(8,128)(2,1)S(1)}, bf16[224,896]{1,0:T(8,128)(2,1)S(1)}, u32[]{:S(2)}, u32[]{:S(2)}) %collective-permute-start.1) | collective-permute-done | bytes 401440 | tf_op jit(solution)/shard_map/ppermute | solution.py:268
  28.8 1.7 %collective-permute-start.4 = (bf16[224,896]{1,0:T(8,128)(2,1)S(1)}, bf16[224,896]{1,0:T(8,128)(2,1)S(1)}, u32[]{:S(2)}, u32[]{:S(2)}) collective-permute-start(bf16[224,896]{1,0:T(8,128)(2,1)S(1)} %add_select_fusion.1), channel_id=1, source_target_pairs={{0,4},{4,0},{8,12},{12,8},{1,5},{5,1},{9,13},{13,9},{2,6},{6,2},{1... | collective-permute-start | bytes 1204232 | tf_op jit(solution)/shard_map/ppermute | solution.py:268
  30.4 7.9 %collective-permute-done.4.refs_3_.refs_1_ = bf16[224,896]{1,0:T(8,128)(2,1)S(1)} collective-permute-done((bf16[224,896]{1,0:T(8,128)(2,1)S(1)}, bf16[224,896]{1,0:T(8,128)(2,1)S(1)}, u32[]{:S(2)}, u32[]{:S(2)}) %collective-permute-start.4) | collective-permute-done | bytes 401440 | tf_op jit(solution)/shard_map/ppermute | solution.py:268
  38.6 1.7 %collective-permute-start.6 = (bf16[224,896]{1,0:T(8,128)(2,1)S(1)}, bf16[224,896]{1,0:T(8,128)(2,1)S(1)}, u32[]{:S(2)}, u32[]{:S(2)}) collective-permute-start(bf16[224,896]{1,0:T(8,128)(2,1)S(1)} %add_select_fusion), channel_id=1, source_target_pairs={{0,4},{4,0},{8,12},{12,8},{1,5},{5,1},{9,13},{13,9},{2,6},{6,2},{1... | collective-permute-start | bytes 1204232 | tf_op jit(solution)/shard_map/ppermute | solution.py:268
  40.3 7.5 %collective-permute-done.6.refs_3_.refs_1_ = bf16[224,896]{1,0:T(8,128)(2,1)S(1)} collective-permute-done((bf16[224,896]{1,0:T(8,128)(2,1)S(1)}, bf16[224,896]{1,0:T(8,128)(2,1)S(1)}, u32[]{:S(2)}, u32[]{:S(2)}) %collective-permute-start.6) | collective-permute-done | bytes 401440 | tf_op jit(solution)/shard_map/ppermute | solution.py:268
  48.0 1.7 %collective-permute-start.8 = (bf16[224,896]{1,0:T(8,128)(2,1)S(1)}, bf16[224,896]{1,0:T(8,128)(2,1)S(1)}, u32[]{:S(2)}, u32[]{:S(2)}) collective-permute-start(bf16[224,896]{1,0:T(8,128)(2,1)S(1)} %add.39), channel_id=1, source_target_pairs={{0,4},{4,0},{8,12},{12,8},{1,5},{5,1},{9,13},{13,9},{2,6},{6,2},{1... | collective-permute-start | bytes 1204232 | tf_op jit(solution)/shard_map/ppermute | solution.py:268
  49.7 7.7 %collective-permute-done.8.refs_3_ = bf16[224,896]{1,0:T(8,128)(2,1)S(1)} collective-permute-done((bf16[224,896]{1,0:T(8,128)(2,1)S(1)}, bf16[224,896]{1,0:T(8,128)(2,1)S(1)}, u32[]{:S(2)}, u32[]{:S(2)}) %collective-permute-start.8) | collective-permute-done | bytes 401440 | tf_op jit(solution)/shard_map/ppermute | solution.py:268
  57.5 1.6 %collective-permute-start.9 = (bf16[224,896]{1,0:T(8,128)(2,1)S(1)}, bf16[224,896]{1,0:T(8,128)(2,1)S(1)}, u32[]{:S(2)}, u32[]{:S(2)}) collective-permute-start(bf16[224,896]{1,0:T(8,128)(2,1)S(1)} %add.40), channel_id=1, source_target_pairs={{0,4},{4,0},{8,12},{12,8},{1,5},{5,1},{9,13},{13,9},{2,6},{6,2},{1... | collective-permute-start | bytes 1204232 | tf_op jit(solution)/shard_map/ppermute | solution.py:268
  59.1 0.4 gradient.4
  59.5 0.4 gradient.5
  60.4 5.0 %collective-permute-done.9.refs_3_ = bf16[224,896]{1,0:T(8,128)(2,1)S(1)} collective-permute-done((bf16[224,896]{1,0:T(8,128)(2,1)S(1)}, bf16[224,896]{1,0:T(8,128)(2,1)S(1)}, u32[]{:S(2)}, u32[]{:S(2)}) %collective-permute-start.9) | collective-permute-done | bytes 401440 | tf_op jit(solution)/shard_map/ppermute | solution.py:268
  65.4 0.4 gradient.7
  66.0 1.5 %collective-permute-start.11 = (f32[8,220]{1,0:T(8,128)S(1)}, f32[8,220]{1,0:T(8,128)S(1)}, u32[]{:S(2)}, u32[]{:S(2)}) collective-permute-start(f32[8,220]{1,0:T(8,128)S(1)} %reshape.3), channel_id=1, source_target_pairs={{0,2},{1,3},{2,0},{3,1},{4,6},{5,7},{6,4},{7,5},{8,10},{9,11},{10,... | collective-permute-start | bytes 21128 | tf_op jit(solution)/shard_map/ppermute | solution.py:251
  67.9 1.9 %collective-permute-done.11 = f32[8,220]{1,0:T(8,128)S(1)} collective-permute-done((f32[8,220]{1,0:T(8,128)S(1)}, f32[8,220]{1,0:T(8,128)S(1)}, u32[]{:S(2)}, u32[]{:S(2)}) %collective-permute-start.11) | collective-permute-done | bytes 7072 | tf_op jit(solution)/shard_map/ppermute | solution.py:251
  69.7 0.9 %collective-permute-done.12 = f32[8,220]{1,0:T(8,128)S(1)} collective-permute-done((f32[8,220]{1,0:T(8,128)S(1)}, f32[8,220]{1,0:T(8,128)S(1)}, u32[]{:S(2)}, u32[]{:S(2)}) %collective-permute-start.12) | collective-permute-done | bytes 7072 | tf_op jit(solution)/shard_map/ppermute | solution.py:251
  70.6 0.6 add_add_fusion
  (32 shorter events, 2.4 us)
Async XLA Ops:
  4.1 13.8 %collective-permute-start = (bf16[224,896]{1,0:T(8,128)(2,1)S(1)}, bf16[224,896]{1,0:T(8,128)(2,1)S(1)}, u32[]{:S(2)}, u32[]{:S(2)}) collective-permute-start(bf16[224,896]{1,0:T(8,128)(2,1)S(1)} %get-tuple-element.59.refs_0_), channel_id=1, source_target_pairs={{0,4},{4,0},{8,12},{12,8},{1,5},{5,1},{9,13},{13,9},{2,6},{6,2},{1... | collective-permute-start | bytes 1204232 | tf_op jit(solution)/shard_map/ppermute | solution.py:268
  18.0 10.5 %collective-permute-start.1 = (bf16[224,896]{1,0:T(8,128)(2,1)S(1)}, bf16[224,896]{1,0:T(8,128)(2,1)S(1)}, u32[]{:S(2)}, u32[]{:S(2)}) collective-permute-start(bf16[224,896]{1,0:T(8,128)(2,1)S(1)} %get-tuple-element.63.refs_0_), channel_id=1, source_target_pairs={{0,4},{4,0},{8,12},{12,8},{1,5},{5,1},{9,13},{13,9},{2,6},{6,2},{1... | collective-permute-start | bytes 1204232 | tf_op jit(solution)/shard_map/ppermute | solution.py:268
  19.8 8.9 %collective-permute-start.3 = (bf16[224,896]{1,0:T(8,128)(2,1)S(1)}, bf16[224,896]{1,0:T(8,128)(2,1)S(1)}, u32[]{:S(2)}, u32[]{:S(2)}) collective-permute-start(bf16[224,896]{1,0:T(8,128)(2,1)S(1)} %add.33), channel_id=1, source_target_pairs={{0,1},{1,0},{4,8},{5,9},{8,4},{9,5},{12,13},{13,12},{2,3},{3,2},{6... | collective-permute-start | bytes 1204232 | tf_op jit(solution)/shard_map/ppermute | solution.py:271
  28.8 9.6 %collective-permute-start.4 = (bf16[224,896]{1,0:T(8,128)(2,1)S(1)}, bf16[224,896]{1,0:T(8,128)(2,1)S(1)}, u32[]{:S(2)}, u32[]{:S(2)}) collective-permute-start(bf16[224,896]{1,0:T(8,128)(2,1)S(1)} %add_select_fusion.1), channel_id=1, source_target_pairs={{0,4},{4,0},{8,12},{12,8},{1,5},{5,1},{9,13},{13,9},{2,6},{6,2},{1... | collective-permute-start | bytes 1204232 | tf_op jit(solution)/shard_map/ppermute | solution.py:268
  30.4 8.0 %collective-permute-start.2 = (bf16[224,896]{1,0:T(8,128)(2,1)S(1)}, bf16[224,896]{1,0:T(8,128)(2,1)S(1)}, u32[]{:S(2)}, u32[]{:S(2)}) collective-permute-start(bf16[224,896]{1,0:T(8,128)(2,1)S(1)} %add.34), channel_id=1, source_target_pairs={{0,1},{1,0},{4,8},{5,9},{8,4},{9,5},{12,13},{13,12},{2,3},{3,2},{6... | collective-permute-start | bytes 1204232 | tf_op jit(solution)/shard_map/ppermute | solution.py:271
  38.6 9.2 %collective-permute-start.6 = (bf16[224,896]{1,0:T(8,128)(2,1)S(1)}, bf16[224,896]{1,0:T(8,128)(2,1)S(1)}, u32[]{:S(2)}, u32[]{:S(2)}) collective-permute-start(bf16[224,896]{1,0:T(8,128)(2,1)S(1)} %add_select_fusion), channel_id=1, source_target_pairs={{0,4},{4,0},{8,12},{12,8},{1,5},{5,1},{9,13},{13,9},{2,6},{6,2},{1... | collective-permute-start | bytes 1204232 | tf_op jit(solution)/shard_map/ppermute | solution.py:268
  40.3 7.6 %collective-permute-start.5 = (bf16[224,896]{1,0:T(8,128)(2,1)S(1)}, bf16[224,896]{1,0:T(8,128)(2,1)S(1)}, u32[]{:S(2)}, u32[]{:S(2)}) collective-permute-start(bf16[224,896]{1,0:T(8,128)(2,1)S(1)} %add.36), channel_id=1, source_target_pairs={{0,1},{1,0},{4,8},{5,9},{8,4},{9,5},{12,13},{13,12},{2,3},{3,2},{6... | collective-permute-start | bytes 1204232 | tf_op jit(solution)/shard_map/ppermute | solution.py:271
  48.0 9.4 %collective-permute-start.8 = (bf16[224,896]{1,0:T(8,128)(2,1)S(1)}, bf16[224,896]{1,0:T(8,128)(2,1)S(1)}, u32[]{:S(2)}, u32[]{:S(2)}) collective-permute-start(bf16[224,896]{1,0:T(8,128)(2,1)S(1)} %add.39), channel_id=1, source_target_pairs={{0,4},{4,0},{8,12},{12,8},{1,5},{5,1},{9,13},{13,9},{2,6},{6,2},{1... | collective-permute-start | bytes 1204232 | tf_op jit(solution)/shard_map/ppermute | solution.py:268
  49.7 7.7 %collective-permute-start.7 = (bf16[224,896]{1,0:T(8,128)(2,1)S(1)}, bf16[224,896]{1,0:T(8,128)(2,1)S(1)}, u32[]{:S(2)}, u32[]{:S(2)}) collective-permute-start(bf16[224,896]{1,0:T(8,128)(2,1)S(1)} %add.38), channel_id=1, source_target_pairs={{0,1},{1,0},{4,8},{5,9},{8,4},{9,5},{12,13},{13,12},{2,3},{3,2},{6... | collective-permute-start | bytes 1204232 | tf_op jit(solution)/shard_map/ppermute | solution.py:271
  57.5 7.9 %collective-permute-start.9 = (bf16[224,896]{1,0:T(8,128)(2,1)S(1)}, bf16[224,896]{1,0:T(8,128)(2,1)S(1)}, u32[]{:S(2)}, u32[]{:S(2)}) collective-permute-start(bf16[224,896]{1,0:T(8,128)(2,1)S(1)} %add.40), channel_id=1, source_target_pairs={{0,4},{4,0},{8,12},{12,8},{1,5},{5,1},{9,13},{13,9},{2,6},{6,2},{1... | collective-permute-start | bytes 1204232 | tf_op jit(solution)/shard_map/ppermute | solution.py:268
  65.9 1.9 %collective-permute-start.10 = (f32[8,220]{1,0:T(8,128)S(1)}, f32[8,220]{1,0:T(8,128)S(1)}, u32[]{:S(2)}, u32[]{:S(2)}) collective-permute-start(f32[8,220]{1,0:T(8,128)S(1)} %reshape.3), channel_id=1, source_target_pairs={{0,1},{1,0},{2,3},{3,2},{4,5},{5,4},{6,7},{7,6},{8,9},{9,8},{10,11... | collective-permute-start | bytes 21128 | tf_op jit(solution)/shard_map/ppermute | solution.py:251
  66.0 3.7 %collective-permute-start.11 = (f32[8,220]{1,0:T(8,128)S(1)}, f32[8,220]{1,0:T(8,128)S(1)}, u32[]{:S(2)}, u32[]{:S(2)}) collective-permute-start(f32[8,220]{1,0:T(8,128)S(1)} %reshape.3), channel_id=1, source_target_pairs={{0,2},{1,3},{2,0},{3,1},{4,6},{5,7},{6,4},{7,5},{8,10},{9,11},{10,... | collective-permute-start | bytes 21128 | tf_op jit(solution)/shard_map/ppermute | solution.py:251
  67.5 3.1 %collective-permute-start.12 = (f32[8,220]{1,0:T(8,128)S(1)}, f32[8,220]{1,0:T(8,128)S(1)}, u32[]{:S(2)}, u32[]{:S(2)}) collective-permute-start(f32[8,220]{1,0:T(8,128)S(1)} %reshape.3), channel_id=1, source_target_pairs={{0,3},{1,2},{2,1},{3,0},{4,7},{5,6},{6,5},{7,4},{8,11},{9,10},{10,... | collective-permute-start | bytes 21128 | tf_op jit(solution)/shard_map/ppermute | solution.py:251

commit v15 on v14

--- a/solution.py
+++ b/solution.py
@@ -13,7 +13,7 @@
 MB = 8
 ROW_TILE = 16
 LANE_TILE = 128
-PARTS = 1
+PARTS = 2
 VMEM_BYTES = 24 * 1024 * 1024
 
 
@@ -279,29 +279,35 @@
             own.extend(encode(encoded, *earlier))
             encoded += 1
 
+    def gradient_of(piece, *earlier):
+        terms = (own[piece], near[piece], across[piece], near[piece + 3])
+        if earlier:
+            terms = (after(terms[0], *earlier), *terms[1:])
+        gradients.append(gradient(terms, piece))
+
     encode_more(3)
-    latest = own[-1]
-    for step in range(1, count + 2):
-        arrived = after(near[-1], latest)
-        half = own[step - 1] + arrived if step <= count else None
-        payload = own[step] if step < count else None
-        if step >= 2:
-            others = own[step - 2] + after(across[step - 2], near[-1] if half is None else half)
+    near.append(outer(after(own[1], own[2])))
+    latest = own[2]
+    for step in range(count):
+        half = own[step] + after(near[step], latest)
+        across.append(inner(half))
+        payload = own[step + 2] if step + 2 < count else None
+        if step >= 1:
+            others = own[step - 1] + after(across[step - 1], half)
             payload = others if payload is None else jnp.where(ends > 0, payload, others)
         else:
             payload = after(payload, half)
-        if half is not None:
-            across.append(inner(half))
         near.append(outer(payload))
         latest = payload
-        encode_more(step + 3, payload)
-        latest = own[-1] if step + 1 < count else payload
+        if len(own) < min(step + 4, count):
+            encode_more(step + 4, payload)
+            latest = own[-1]
         if step >= 3:
-            done = step - 3
-            terms = (own[done], near[done], across[done], near[done + 2])
-            gradients.append(gradient((after(terms[0], payload), *terms[1:]), done))
-    last = count - 1
-    gradients.append(gradient((own[last], near[last], across[last], near[last + 2]), last))
+            gradient_of(step - 3, payload)
+    last = own[count - 1] + after(across[count - 1], latest)
+    near.append(outer(last))
+    for piece in range(count - 3, count):
+        gradient_of(piece, last)
     return gradients
 
 

time: 71.7 us -> 70.5 us (0.983)
  waiting for transfers between devices: 40.2 us -> 19.1 us
  starting transfers between devices: 14.9 us -> 34 us
    ppermute x6 -> x11, waiting for transfers between devices: 37.5 us -> 16.9 us  [outer(): return lax.ppermute(value, 'slc', outer_pairs)]
    ppermute x6 -> x11, starting transfers between devices: 13 us -> 30.7 us  [outer(): return lax.ppermute(value, 'slc', outer_pairs)]
    ppermute x3, starting transfers between devices: 1.93 us -> 2.66 us  [sum_over_replicas(): lax.ppermute(value, axes, [(index, index ^ mask) for index in range(4)])]
    pallas_call x4 -> x8, Pallas kernels: 1.77 us -> 2.13 us  [gradient(): pl.pallas_call(functools.partial(gradient_kernel, index, factor, on_line)...]
  transfers between devices with their start and end apart: 13 -> 22, of which waited for: 8 -> 9; matrix products, arithmetic and copies ran while one was open for 1% -> 2% of each run, Pallas kernels for 13% -> 12%
where the time goes in v15:
time: 70.5 us; the launch traced here: 70 us
  starting transfers between devices  34 us (48%)
  waiting for transfers between devices  19.1 us (27%)
  Pallas kernels  14 us (20%)
  other arithmetic  1.77 us (3%)
  local copies, waits for them, and re-layouts  0.77 us (1%)
    ppermute x11, starting transfers between devices, outer(): return lax.ppermute(value, 'slc', outer_pairs)  30.7 us
    ppermute x11, waiting for transfers between devices, outer(): return lax.ppermute(value, 'slc', outer_pairs)  16.9 us
    pallas_call x4, Pallas kernels, encode(): pl.pallas_call(functools.partial(encode_kernel, slots, group, rows_of_cla...  10.2 us
    ppermute x3, starting transfers between devices, sum_over_replicas(): lax.ppermute(value, axes, [(index, index ^ mask) for index in range(4)])  2.66 us
    ppermute x3, waiting for transfers between devices, sum_over_replicas(): lax.ppermute(value, axes, [(index, index ^ mask) for index in range(4)])  2.19 us
    pallas_call x8, Pallas kernels, gradient(): pl.pallas_call(functools.partial(gradient_kernel, index, factor, on_line)...  2.13 us
    pallas_call x1, Pallas kernels, body(): pl.pallas_call(functools.partial(fetch_kernel, rows_of_class(0)), in_spec...  1.66 us
  transfers between devices with their start and end apart: 22, of which 9 were waited for; matrix products, arithmetic and copies ran while one was open for 2% of the time, Pallas kernels for 12%

profile of v15, /device:TPU:0, one launch (start us, length us, event | category | flops | bytes accessed | tf_op | source)
XLA Modules:
  0.0 70.0 jit_solution(10793129301718578245)
XLA Ops:
  0.0 1.7 %fetch.1 = (bf16[1,2,220,2,220]{4,3,2,1,0:T(2,128)(2,1)S(1)}, bf16[2,2,220,2,220]{4,3,2,1,0:T(2,128)(2,1)S(1)}, bf16[2,456,220]{2,1,0:T(8,128)(2,1)S(1)}, f32[256,16]{1,0:T(8,128)S(1)}, f32[1,896]{1,0:T(1,128)S(1)}) custom-call(s32[8]{0:T(128)} %refs_0_.1, f32[8,220]{1,0:T(8,128)} %refs_1_.1, bf16[1,8,220,2,220]{4,3,2,1,0:T(2,128)(2,1)} %bitcast.48, ...), custom_call_target="tpu_custom_call" | custom-call | tf_op jit(solution)/shard_map/fetch/pallas_call | solution.py:356
  1.9 3.6 %encode.4 = (bf16[2,224,896]{2,1,0:T(8,128)(2,1)S(1)}, bf16[112,896]{1,0:T(8,128)(2,1)S(1)}, bf16[112,896]{1,0:T(8,128)(2,1)S(1)}, bf16[1,2,220,2,220]{4,3,2,1,0...) custom-call(f32[256,16]{1,0:T(8,128)S(1)} %get-tuple-element.56.refs_0_, bf16[1,2,2,220,220]{4,3,2,1,0:T(8,128)(2,1)S(1)} %bitcast.41, ...), custom_call_target="tpu_custom_call" | custom-call | flops 1022208000 | bytes 6000000 | tf_op jit(solution)/shard_map/encode/pallas_call | solution.py:389
  5.5 1.6 %collective-permute-start = (bf16[112,896]{1,0:T(8,128)(2,1)S(1)}, bf16[112,896]{1,0:T(8,128)(2,1)S(1)}, u32[]{:S(2)}, u32[]{:S(2)}) collective-permute-start(bf16[112,896]{1,0:T(8,128)(2,1)S(1)} %get-tuple-element.81.refs_0_), channel_id=1, source_target_pairs={{0,4},{4,0},{8,12},{12,8},{1,5},{5,1},{9,13},{13,9},{2,6},{6,2},{1... | collective-permute-start | bytes 602120 | tf_op jit(solution)/shard_map/ppermute | solution.py:268
  7.3 2.2 %encode.5 = (bf16[2,224,896]{2,1,0:T(8,128)(2,1)S(1)}, bf16[112,896]{1,0:T(8,128)(2,1)S(1)}, bf16[112,896]{1,0:T(8,128)(2,1)S(1)}, bf16[1,2,220,2,220]{4,3,2,1,0...) custom-call(f32[256,16]{1,0:T(8,128)S(1)} %get-tuple-element.56.refs_0_, bf16[1,2,2,220,220]{4,3,2,1,0:T(8,128)(2,1)S(1)} %bitcast.42, ...), custom_call_target="tpu_custom_call" | custom-call | flops 1022208000 | bytes 6000000 | tf_op jit(solution)/shard_map/encode/pallas_call | solution.py:389
  9.5 2.0 %collective-permute-start.2 = (bf16[112,896]{1,0:T(8,128)(2,1)S(1)}, bf16[112,896]{1,0:T(8,128)(2,1)S(1)}, u32[]{:S(2)}, u32[]{:S(2)}) collective-permute-start(bf16[112,896]{1,0:T(8,128)(2,1)S(1)} %get-tuple-element.90.refs_0_), channel_id=1, source_target_pairs={{0,4},{4,0},{8,12},{12,8},{1,5},{5,1},{9,13},{13,9},{2,6},{6,2},{1... | collective-permute-start | bytes 602120 | tf_op jit(solution)/shard_map/ppermute | solution.py:268
  11.5 1.7 %collective-permute-done.refs_1_ = bf16[112,896]{1,0:T(8,128)(2,1)S(1)} collective-permute-done((bf16[112,896]{1,0:T(8,128)(2,1)S(1)}, bf16[112,896]{1,0:T(8,128)(2,1)S(1)}, u32[]{:S(2)}, u32[]{:S(2)}) %collective-permute-start) | collective-permute-done | bytes 200736 | tf_op jit(solution)/shard_map/ppermute | solution.py:268
  13.6 2.7 %collective-permute-start.3 = (bf16[112,896]{1,0:T(8,128)(2,1)S(1)}, bf16[112,896]{1,0:T(8,128)(2,1)S(1)}, u32[]{:S(2)}, u32[]{:S(2)}) collective-permute-start(bf16[112,896]{1,0:T(8,128)(2,1)S(1)} %get-tuple-element.93.refs_0_), channel_id=1, source_target_pairs={{0,4},{4,0},{8,12},{12,8},{1,5},{5,1},{9,13},{13,9},{2,6},{6,2},{1... | collective-permute-start | bytes 602120 | tf_op jit(solution)/shard_map/ppermute | solution.py:268
  17.8 2.2 %collective-permute-start.5 = (bf16[112,896]{1,0:T(8,128)(2,1)S(1)}, bf16[112,896]{1,0:T(8,128)(2,1)S(1)}, u32[]{:S(2)}, u32[]{:S(2)}) collective-permute-start(bf16[112,896]{1,0:T(8,128)(2,1)S(1)} %add_select_fusion.4), channel_id=1, source_target_pairs={{0,4},{4,0},{8,12},{12,8},{1,5},{5,1},{9,13},{13,9},{2,6},{6,2},{1... | collective-permute-start | bytes 602120 | tf_op jit(solution)/shard_map/ppermute | solution.py:268
  20.0 2.2 %encode.6 = (bf16[2,224,896]{2,1,0:T(8,128)(2,1)S(1)}, bf16[112,896]{1,0:T(8,128)(2,1)S(1)}, bf16[112,896]{1,0:T(8,128)(2,1)S(1)}, bf16[1,2,220,2,220]{4,3,2,1,0...) custom-call(f32[256,16]{1,0:T(8,128)S(1)} %get-tuple-element.56.refs_0_, bf16[1,2,2,220,220]{4,3,2,1,0:T(8,128)(2,1)S(1)} %bitcast.40, ...), custom_call_target="tpu_custom_call" | custom-call | flops 1022208000 | bytes 6000000 | tf_op jit(solution)/shard_map/encode/pallas_call | solution.py:389
  22.5 3.5 %collective-permute-start.8 = (bf16[112,896]{1,0:T(8,128)(2,1)S(1)}, bf16[112,896]{1,0:T(8,128)(2,1)S(1)}, u32[]{:S(2)}, u32[]{:S(2)}) collective-permute-start(bf16[112,896]{1,0:T(8,128)(2,1)S(1)} %add_select_fusion.3), channel_id=1, source_target_pairs={{0,4},{4,0},{8,12},{12,8},{1,5},{5,1},{9,13},{13,9},{2,6},{6,2},{1... | collective-permute-start | bytes 602120 | tf_op jit(solution)/shard_map/ppermute | solution.py:268
  26.3 6.1 %collective-permute-start.10 = (bf16[112,896]{1,0:T(8,128)(2,1)S(1)}, bf16[112,896]{1,0:T(8,128)(2,1)S(1)}, u32[]{:S(2)}, u32[]{:S(2)}) collective-permute-start(bf16[112,896]{1,0:T(8,128)(2,1)S(1)} %add_select_fusion.2), channel_id=1, source_target_pairs={{0,4},{4,0},{8,12},{12,8},{1,5},{5,1},{9,13},{13,9},{2,6},{6,2},{1... | collective-permute-start | bytes 602120 | tf_op jit(solution)/shard_map/ppermute | solution.py:268
  32.4 2.2 %encode.7 = (bf16[2,224,896]{2,1,0:T(8,128)(2,1)S(1)}, bf16[112,896]{1,0:T(8,128)(2,1)S(1)}, bf16[112,896]{1,0:T(8,128)(2,1)S(1)}) custom-call(f32[256,16]{1,0:T(8,128)S(1)} %get-tuple-element.56.refs_0_, bf16[1,2,2,220,220]{4,3,2,1,0:T(8,128)(2,1)S(1)} %bitcast.39, bf16[2,2,2,220,220]{4,3,2,1,0:T(8,128)(2,1)S(1)} %bitcast.36, ...), custom_call_target="tpu_custom_call" | custom-call | flops 1022208000 | bytes 6000000 | tf_op jit(solution)/shard_map/encode/pallas_call | solution.py:389
  34.8 1.5 %collective-permute-start.12 = (bf16[112,896]{1,0:T(8,128)(2,1)S(1)}, bf16[112,896]{1,0:T(8,128)(2,1)S(1)}, u32[]{:S(2)}, u32[]{:S(2)}) collective-permute-start(bf16[112,896]{1,0:T(8,128)(2,1)S(1)} %add_select_fusion.1), channel_id=1, source_target_pairs={{0,4},{4,0},{8,12},{12,8},{1,5},{5,1},{9,13},{13,9},{2,6},{6,2},{1... | collective-permute-start | bytes 602120 | tf_op jit(solution)/shard_map/ppermute | solution.py:268
  36.5 4.1 %collective-permute-start.14 = (bf16[112,896]{1,0:T(8,128)(2,1)S(1)}, bf16[112,896]{1,0:T(8,128)(2,1)S(1)}, u32[]{:S(2)}, u32[]{:S(2)}) collective-permute-start(bf16[112,896]{1,0:T(8,128)(2,1)S(1)} %add_select_fusion), channel_id=1, source_target_pairs={{0,4},{4,0},{8,12},{12,8},{1,5},{5,1},{9,13},{13,9},{2,6},{6,2},{1... | collective-permute-start | bytes 602120 | tf_op jit(solution)/shard_map/ppermute | solution.py:268
  40.6 2.1 %collective-permute-done.12.refs_3_.refs_1_ = bf16[112,896]{1,0:T(8,128)(2,1)S(1)} collective-permute-done((bf16[112,896]{1,0:T(8,128)(2,1)S(1)}, bf16[112,896]{1,0:T(8,128)(2,1)S(1)}, u32[]{:S(2)}, u32[]{:S(2)}) %collective-permute-start.12) | collective-permute-done | bytes 200736 | tf_op jit(solution)/shard_map/ppermute | solution.py:268
  42.9 3.7 %collective-permute-done.14.refs_3_.refs_1_ = bf16[112,896]{1,0:T(8,128)(2,1)S(1)} collective-permute-done((bf16[112,896]{1,0:T(8,128)(2,1)S(1)}, bf16[112,896]{1,0:T(8,128)(2,1)S(1)}, u32[]{:S(2)}, u32[]{:S(2)}) %collective-permute-start.14) | collective-permute-done | bytes 200736 | tf_op jit(solution)/shard_map/ppermute | solution.py:268
  47.6 3.2 %collective-permute-start.16 = (bf16[112,896]{1,0:T(8,128)(2,1)S(1)}, bf16[112,896]{1,0:T(8,128)(2,1)S(1)}, u32[]{:S(2)}, u32[]{:S(2)}) collective-permute-start(bf16[112,896]{1,0:T(8,128)(2,1)S(1)} %add.69), channel_id=1, source_target_pairs={{0,4},{4,0},{8,12},{12,8},{1,5},{5,1},{9,13},{13,9},{2,6},{6,2},{1... | collective-permute-start | bytes 602120 | tf_op jit(solution)/shard_map/ppermute | solution.py:268
  51.3 3.7 %collective-permute-start.18 = (bf16[112,896]{1,0:T(8,128)(2,1)S(1)}, bf16[112,896]{1,0:T(8,128)(2,1)S(1)}, u32[]{:S(2)}, u32[]{:S(2)}) collective-permute-start(bf16[112,896]{1,0:T(8,128)(2,1)S(1)} %add.72), channel_id=1, source_target_pairs={{0,4},{4,0},{8,12},{12,8},{1,5},{5,1},{9,13},{13,9},{2,6},{6,2},{1... | collective-permute-start | bytes 602120 | tf_op jit(solution)/shard_map/ppermute | solution.py:268
  55.4 1.2 %collective-permute-done.16.refs_3_ = bf16[112,896]{1,0:T(8,128)(2,1)S(1)} collective-permute-done((bf16[112,896]{1,0:T(8,128)(2,1)S(1)}, bf16[112,896]{1,0:T(8,128)(2,1)S(1)}, u32[]{:S(2)}, u32[]{:S(2)}) %collective-permute-start.16) | collective-permute-done | bytes 200736 | tf_op jit(solution)/shard_map/ppermute | solution.py:268
  56.9 4.0 %collective-permute-done.17.refs_3_ = bf16[112,896]{1,0:T(8,128)(2,1)S(1)} collective-permute-done((bf16[112,896]{1,0:T(8,128)(2,1)S(1)}, bf16[112,896]{1,0:T(8,128)(2,1)S(1)}, u32[]{:S(2)}, u32[]{:S(2)}) %collective-permute-start.17) | collective-permute-done | bytes 200736 | tf_op jit(solution)/shard_map/ppermute | solution.py:268
  61.1 3.0 %collective-permute-done.18.refs_3_ = bf16[112,896]{1,0:T(8,128)(2,1)S(1)} collective-permute-done((bf16[112,896]{1,0:T(8,128)(2,1)S(1)}, bf16[112,896]{1,0:T(8,128)(2,1)S(1)}, u32[]{:S(2)}, u32[]{:S(2)}) %collective-permute-start.18) | collective-permute-done | bytes 200736 | tf_op jit(solution)/shard_map/ppermute | solution.py:268
  64.5 1.2 %collective-permute-start.21 = (f32[8,220]{1,0:T(8,128)S(1)}, f32[8,220]{1,0:T(8,128)S(1)}, u32[]{:S(2)}, u32[]{:S(2)}) collective-permute-start(f32[8,220]{1,0:T(8,128)S(1)} %reshape.3), channel_id=1, source_target_pairs={{0,3},{1,2},{2,1},{3,0},{4,7},{5,6},{6,5},{7,4},{8,11},{9,10},{10,... | collective-permute-start | bytes 21128 | tf_op jit(solution)/shard_map/ppermute | solution.py:251
  65.7 1.4 %collective-permute-start.20 = (f32[8,220]{1,0:T(8,128)S(1)}, f32[8,220]{1,0:T(8,128)S(1)}, u32[]{:S(2)}, u32[]{:S(2)}) collective-permute-start(f32[8,220]{1,0:T(8,128)S(1)} %reshape.3), channel_id=1, source_target_pairs={{0,2},{1,3},{2,0},{3,1},{4,6},{5,7},{6,4},{7,5},{8,10},{9,11},{10,... | collective-permute-start | bytes 21128 | tf_op jit(solution)/shard_map/ppermute | solution.py:251
  67.6 1.7 %collective-permute-done.20 = f32[8,220]{1,0:T(8,128)S(1)} collective-permute-done((f32[8,220]{1,0:T(8,128)S(1)}, f32[8,220]{1,0:T(8,128)S(1)}, u32[]{:S(2)}, u32[]{:S(2)}) %collective-permute-start.20) | collective-permute-done | bytes 7072 | tf_op jit(solution)/shard_map/ppermute | solution.py:251
  (66 shorter events, 7.1 us)
Async XLA Ops:
  5.5 7.7 %collective-permute-start = (bf16[112,896]{1,0:T(8,128)(2,1)S(1)}, bf16[112,896]{1,0:T(8,128)(2,1)S(1)}, u32[]{:S(2)}, u32[]{:S(2)}) collective-permute-start(bf16[112,896]{1,0:T(8,128)(2,1)S(1)} %get-tuple-element.81.refs_0_), channel_id=1, source_target_pairs={{0,4},{4,0},{8,12},{12,8},{1,5},{5,1},{9,13},{13,9},{2,6},{6,2},{1... | collective-permute-start | bytes 602120 | tf_op jit(solution)/shard_map/ppermute | solution.py:268
  9.5 8.0 %collective-permute-start.2 = (bf16[112,896]{1,0:T(8,128)(2,1)S(1)}, bf16[112,896]{1,0:T(8,128)(2,1)S(1)}, u32[]{:S(2)}, u32[]{:S(2)}) collective-permute-start(bf16[112,896]{1,0:T(8,128)(2,1)S(1)} %get-tuple-element.90.refs_0_), channel_id=1, source_target_pairs={{0,4},{4,0},{8,12},{12,8},{1,5},{5,1},{9,13},{13,9},{2,6},{6,2},{1... | collective-permute-start | bytes 602120 | tf_op jit(solution)/shard_map/ppermute | solution.py:268
  13.3 4.4 %collective-permute-start.1 = (bf16[112,896]{1,0:T(8,128)(2,1)S(1)}, bf16[112,896]{1,0:T(8,128)(2,1)S(1)}, u32[]{:S(2)}, u32[]{:S(2)}) collective-permute-start(bf16[112,896]{1,0:T(8,128)(2,1)S(1)} %add.57), channel_id=1, source_target_pairs={{0,1},{1,0},{4,8},{5,9},{8,4},{9,5},{12,13},{13,12},{2,3},{3,2},{6... | collective-permute-start | bytes 602120 | tf_op jit(solution)/shard_map/ppermute | solution.py:271
  13.6 8.6 %collective-permute-start.3 = (bf16[112,896]{1,0:T(8,128)(2,1)S(1)}, bf16[112,896]{1,0:T(8,128)(2,1)S(1)}, u32[]{:S(2)}, u32[]{:S(2)}) collective-permute-start(bf16[112,896]{1,0:T(8,128)(2,1)S(1)} %get-tuple-element.93.refs_0_), channel_id=1, source_target_pairs={{0,4},{4,0},{8,12},{12,8},{1,5},{5,1},{9,13},{13,9},{2,6},{6,2},{1... | collective-permute-start | bytes 602120 | tf_op jit(solution)/shard_map/ppermute | solution.py:268
  17.6 4.8 %collective-permute-start.6 = (bf16[112,896]{1,0:T(8,128)(2,1)S(1)}, bf16[112,896]{1,0:T(8,128)(2,1)S(1)}, u32[]{:S(2)}, u32[]{:S(2)}) collective-permute-start(bf16[112,896]{1,0:T(8,128)(2,1)S(1)} %add.58), channel_id=1, source_target_pairs={{0,1},{1,0},{4,8},{5,9},{8,4},{9,5},{12,13},{13,12},{2,3},{3,2},{6... | collective-permute-start | bytes 602120 | tf_op jit(solution)/shard_map/ppermute | solution.py:271
  17.8 8.3 %collective-permute-start.5 = (bf16[112,896]{1,0:T(8,128)(2,1)S(1)}, bf16[112,896]{1,0:T(8,128)(2,1)S(1)}, u32[]{:S(2)}, u32[]{:S(2)}) collective-permute-start(bf16[112,896]{1,0:T(8,128)(2,1)S(1)} %add_select_fusion.4), channel_id=1, source_target_pairs={{0,4},{4,0},{8,12},{12,8},{1,5},{5,1},{9,13},{13,9},{2,6},{6,2},{1... | collective-permute-start | bytes 602120 | tf_op jit(solution)/shard_map/ppermute | solution.py:268
  22.3 3.9 %collective-permute-start.4 = (bf16[112,896]{1,0:T(8,128)(2,1)S(1)}, bf16[112,896]{1,0:T(8,128)(2,1)S(1)}, u32[]{:S(2)}, u32[]{:S(2)}) collective-permute-start(bf16[112,896]{1,0:T(8,128)(2,1)S(1)} %add.60), channel_id=1, source_target_pairs={{0,1},{1,0},{4,8},{5,9},{8,4},{9,5},{12,13},{13,12},{2,3},{3,2},{6... | collective-permute-start | bytes 602120 | tf_op jit(solution)/shard_map/ppermute | solution.py:271
  22.5 12.2 %collective-permute-start.8 = (bf16[112,896]{1,0:T(8,128)(2,1)S(1)}, bf16[112,896]{1,0:T(8,128)(2,1)S(1)}, u32[]{:S(2)}, u32[]{:S(2)}) collective-permute-start(bf16[112,896]{1,0:T(8,128)(2,1)S(1)} %add_select_fusion.3), channel_id=1, source_target_pairs={{0,4},{4,0},{8,12},{12,8},{1,5},{5,1},{9,13},{13,9},{2,6},{6,2},{1... | collective-permute-start | bytes 602120 | tf_op jit(solution)/shard_map/ppermute | solution.py:268
  26.1 8.7 %collective-permute-start.7 = (bf16[112,896]{1,0:T(8,128)(2,1)S(1)}, bf16[112,896]{1,0:T(8,128)(2,1)S(1)}, u32[]{:S(2)}, u32[]{:S(2)}) collective-permute-start(bf16[112,896]{1,0:T(8,128)(2,1)S(1)} %add.62), channel_id=1, source_target_pairs={{0,1},{1,0},{4,8},{5,9},{8,4},{9,5},{12,13},{13,12},{2,3},{3,2},{6... | collective-permute-start | bytes 602120 | tf_op jit(solution)/shard_map/ppermute | solution.py:271
  26.3 10.1 %collective-permute-start.10 = (bf16[112,896]{1,0:T(8,128)(2,1)S(1)}, bf16[112,896]{1,0:T(8,128)(2,1)S(1)}, u32[]{:S(2)}, u32[]{:S(2)}) collective-permute-start(bf16[112,896]{1,0:T(8,128)(2,1)S(1)} %add_select_fusion.2), channel_id=1, source_target_pairs={{0,4},{4,0},{8,12},{12,8},{1,5},{5,1},{9,13},{13,9},{2,6},{6,2},{1... | collective-permute-start | bytes 602120 | tf_op jit(solution)/shard_map/ppermute | solution.py:268
  34.7 1.8 %collective-permute-start.9 = (bf16[112,896]{1,0:T(8,128)(2,1)S(1)}, bf16[112,896]{1,0:T(8,128)(2,1)S(1)}, u32[]{:S(2)}, u32[]{:S(2)}) collective-permute-start(bf16[112,896]{1,0:T(8,128)(2,1)S(1)} %add.64), channel_id=1, source_target_pairs={{0,1},{1,0},{4,8},{5,9},{8,4},{9,5},{12,13},{13,12},{2,3},{3,2},{6... | collective-permute-start | bytes 602120 | tf_op jit(solution)/shard_map/ppermute | solution.py:271
  34.8 7.8 %collective-permute-start.12 = (bf16[112,896]{1,0:T(8,128)(2,1)S(1)}, bf16[112,896]{1,0:T(8,128)(2,1)S(1)}, u32[]{:S(2)}, u32[]{:S(2)}) collective-permute-start(bf16[112,896]{1,0:T(8,128)(2,1)S(1)} %add_select_fusion.1), channel_id=1, source_target_pairs={{0,4},{4,0},{8,12},{12,8},{1,5},{5,1},{9,13},{13,9},{2,6},{6,2},{1... | collective-permute-start | bytes 602120 | tf_op jit(solution)/shard_map/ppermute | solution.py:268
  36.4 6.5 %collective-permute-start.11 = (bf16[112,896]{1,0:T(8,128)(2,1)S(1)}, bf16[112,896]{1,0:T(8,128)(2,1)S(1)}, u32[]{:S(2)}, u32[]{:S(2)}) collective-permute-start(bf16[112,896]{1,0:T(8,128)(2,1)S(1)} %add.66), channel_id=1, source_target_pairs={{0,1},{1,0},{4,8},{5,9},{8,4},{9,5},{12,13},{13,12},{2,3},{3,2},{6... | collective-permute-start | bytes 602120 | tf_op jit(solution)/shard_map/ppermute | solution.py:271
  36.5 10.1 %collective-permute-start.14 = (bf16[112,896]{1,0:T(8,128)(2,1)S(1)}, bf16[112,896]{1,0:T(8,128)(2,1)S(1)}, u32[]{:S(2)}, u32[]{:S(2)}) collective-permute-start(bf16[112,896]{1,0:T(8,128)(2,1)S(1)} %add_select_fusion), channel_id=1, source_target_pairs={{0,4},{4,0},{8,12},{12,8},{1,5},{5,1},{9,13},{13,9},{2,6},{6,2},{1... | collective-permute-start | bytes 602120 | tf_op jit(solution)/shard_map/ppermute | solution.py:268
  42.7 8.3 %collective-permute-start.13 = (bf16[112,896]{1,0:T(8,128)(2,1)S(1)}, bf16[112,896]{1,0:T(8,128)(2,1)S(1)}, u32[]{:S(2)}, u32[]{:S(2)}) collective-permute-start(bf16[112,896]{1,0:T(8,128)(2,1)S(1)} %add.68), channel_id=1, source_target_pairs={{0,1},{1,0},{4,8},{5,9},{8,4},{9,5},{12,13},{13,12},{2,3},{3,2},{6... | collective-permute-start | bytes 602120 | tf_op jit(solution)/shard_map/ppermute | solution.py:271
  46.6 4.6 %collective-permute-start.15 = (bf16[112,896]{1,0:T(8,128)(2,1)S(1)}, bf16[112,896]{1,0:T(8,128)(2,1)S(1)}, u32[]{:S(2)}, u32[]{:S(2)}) collective-permute-start(bf16[112,896]{1,0:T(8,128)(2,1)S(1)} %add.70), channel_id=1, source_target_pairs={{0,1},{1,0},{4,8},{5,9},{8,4},{9,5},{12,13},{13,12},{2,3},{3,2},{6... | collective-permute-start | bytes 602120 | tf_op jit(solution)/shard_map/ppermute | solution.py:271
  47.6 9.0 %collective-permute-start.16 = (bf16[112,896]{1,0:T(8,128)(2,1)S(1)}, bf16[112,896]{1,0:T(8,128)(2,1)S(1)}, u32[]{:S(2)}, u32[]{:S(2)}) collective-permute-start(bf16[112,896]{1,0:T(8,128)(2,1)S(1)} %add.69), channel_id=1, source_target_pairs={{0,4},{4,0},{8,12},{12,8},{1,5},{5,1},{9,13},{13,9},{2,6},{6,2},{1... | collective-permute-start | bytes 602120 | tf_op jit(solution)/shard_map/ppermute | solution.py:268
  51.1 9.7 %collective-permute-start.17 = (bf16[112,896]{1,0:T(8,128)(2,1)S(1)}, bf16[112,896]{1,0:T(8,128)(2,1)S(1)}, u32[]{:S(2)}, u32[]{:S(2)}) collective-permute-start(bf16[112,896]{1,0:T(8,128)(2,1)S(1)} %add.71), channel_id=1, source_target_pairs={{0,4},{4,0},{8,12},{12,8},{1,5},{5,1},{9,13},{13,9},{2,6},{6,2},{1... | collective-permute-start | bytes 602120 | tf_op jit(solution)/shard_map/ppermute | solution.py:268
  51.3 12.8 %collective-permute-start.18 = (bf16[112,896]{1,0:T(8,128)(2,1)S(1)}, bf16[112,896]{1,0:T(8,128)(2,1)S(1)}, u32[]{:S(2)}, u32[]{:S(2)}) collective-permute-start(bf16[112,896]{1,0:T(8,128)(2,1)S(1)} %add.72), channel_id=1, source_target_pairs={{0,4},{4,0},{8,12},{12,8},{1,5},{5,1},{9,13},{13,9},{2,6},{6,2},{1... | collective-permute-start | bytes 602120 | tf_op jit(solution)/shard_map/ppermute | solution.py:268
  64.5 3.1 %collective-permute-start.21 = (f32[8,220]{1,0:T(8,128)S(1)}, f32[8,220]{1,0:T(8,128)S(1)}, u32[]{:S(2)}, u32[]{:S(2)}) collective-permute-start(f32[8,220]{1,0:T(8,128)S(1)} %reshape.3), channel_id=1, source_target_pairs={{0,3},{1,2},{2,1},{3,0},{4,7},{5,6},{6,5},{7,4},{8,11},{9,10},{10,... | collective-permute-start | bytes 21128 | tf_op jit(solution)/shard_map/ppermute | solution.py:251
  65.7 3.7 %collective-permute-start.20 = (f32[8,220]{1,0:T(8,128)S(1)}, f32[8,220]{1,0:T(8,128)S(1)}, u32[]{:S(2)}, u32[]{:S(2)}) collective-permute-start(f32[8,220]{1,0:T(8,128)S(1)} %reshape.3), channel_id=1, source_target_pairs={{0,2},{1,3},{2,0},{3,1},{4,6},{5,7},{6,4},{7,5},{8,10},{9,11},{10,... | collective-permute-start | bytes 21128 | tf_op jit(solution)/shard_map/ppermute | solution.py:251
  67.1 2.2 %collective-permute-start.19 = (f32[8,220]{1,0:T(8,128)S(1)}, f32[8,220]{1,0:T(8,128)S(1)}, u32[]{:S(2)}, u32[]{:S(2)}) collective-permute-start(f32[8,220]{1,0:T(8,128)S(1)} %reshape.3), channel_id=1, source_target_pairs={{0,1},{1,0},{2,3},{3,2},{4,5},{5,4},{6,7},{7,6},{8,9},{9,8},{10,11... | collective-permute-start | bytes 21128 | tf_op jit(solution)/shard_map/ppermute | solution.py:251

commit v16 on v15

--- a/solution.py
+++ b/solution.py
@@ -280,34 +280,34 @@
             encoded += 1
 
     def gradient_of(piece, *earlier):
-        terms = (own[piece], near[piece], across[piece], near[piece + 3])
-        if earlier:
-            terms = (after(terms[0], *earlier), *terms[1:])
-        gradients.append(gradient(terms, piece))
+        terms = (own[piece], near[piece], across[piece], near[piece + 4])
+        gradients.append(gradient((after(terms[0], *earlier), *terms[1:]), piece))
 
     encode_more(3)
     near.append(outer(after(own[1], own[2])))
-    latest = own[2]
+    encode_more(5)
+    latest = own[4]
     for step in range(count):
         half = own[step] + after(near[step], latest)
         across.append(inner(half))
         payload = own[step + 2] if step + 2 < count else None
-        if step >= 1:
-            others = own[step - 1] + after(across[step - 1], half)
+        if step >= 2:
+            others = own[step - 2] + after(across[step - 2], half)
             payload = others if payload is None else jnp.where(ends > 0, payload, others)
         else:
             payload = after(payload, half)
         near.append(outer(payload))
         latest = payload
-        if len(own) < min(step + 4, count):
-            encode_more(step + 4, payload)
+        if len(own) < min(step + 7, count):
+            encode_more(step + 7, payload)
             latest = own[-1]
-        if step >= 3:
-            gradient_of(step - 3, payload)
-    last = own[count - 1] + after(across[count - 1], latest)
-    near.append(outer(last))
-    for piece in range(count - 3, count):
-        gradient_of(piece, last)
+        if step >= 4:
+            gradient_of(step - 4, payload)
+    for piece in range(count - 2, count):
+        latest = own[piece] + after(across[piece], latest, near[count])
+        near.append(outer(latest))
+    for piece in range(count - 4, count):
+        gradient_of(piece, latest)
     return gradients
 
 

time: 70.5 us -> 67.7 us (0.960)
  starting transfers between devices: 34 us -> 28.2 us
  waiting for transfers between devices: 19.1 us -> 22.3 us
    ppermute x11 -> x12, starting transfers between devices: 30.7 us -> 25.8 us  [outer(): return lax.ppermute(value, 'slc', outer_pairs)]
    ppermute x11 -> x12, waiting for transfers between devices: 16.9 us -> 19.5 us  [outer(): return lax.ppermute(value, 'slc', outer_pairs)]
    ppermute x3, starting transfers between devices: 2.66 us -> 1.93 us  [sum_over_replicas(): lax.ppermute(value, axes, [(index, index ^ mask) for index in range(4)])]
  transfers between devices with their start and end apart: 22 -> 23, of which waited for: 9 -> 11; matrix products, arithmetic and copies ran while one was open for 2% -> 2% of each run, Pallas kernels for 12% -> 15%
where the time goes in v16:
time: 67.7 us; the launch traced here: 67.5 us
  starting transfers between devices  28.2 us (42%)
  waiting for transfers between devices  22.3 us (33%)
  Pallas kernels  14.1 us (21%)
  other arithmetic  1.79 us (3%)
  local copies, waits for them, and re-layouts  0.77 us (1%)
    ppermute x12, starting transfers between devices, outer(): return lax.ppermute(value, 'slc', outer_pairs)  25.8 us
    ppermute x12, waiting for transfers between devices, outer(): return lax.ppermute(value, 'slc', outer_pairs)  19.5 us
    pallas_call x4, Pallas kernels, encode(): pl.pallas_call(functools.partial(encode_kernel, slots, group, rows_of_cla...  10.3 us
    ppermute x3, waiting for transfers between devices, sum_over_replicas(): lax.ppermute(value, axes, [(index, index ^ mask) for index in range(4)])  2.77 us
    pallas_call x8, Pallas kernels, gradient(): pl.pallas_call(functools.partial(gradient_kernel, index, factor, on_line)...  2.14 us
    ppermute x3, starting transfers between devices, sum_over_replicas(): lax.ppermute(value, axes, [(index, index ^ mask) for index in range(4)])  1.93 us
    pallas_call x1, Pallas kernels, body(): pl.pallas_call(functools.partial(fetch_kernel, rows_of_class(0)), in_spec...  1.66 us
  transfers between devices with their start and end apart: 23, of which 11 were waited for; matrix products, arithmetic and copies ran while one was open for 2% of the time, Pallas kernels for 15%

profile of v16, /device:TPU:0, one launch (start us, length us, event | category | flops | bytes accessed | tf_op | source)
XLA Modules:
  0.0 67.5 jit_solution(604815396815442996)
XLA Ops:
  0.0 1.7 %fetch.1 = (bf16[1,2,220,2,220]{4,3,2,1,0:T(2,128)(2,1)S(1)}, bf16[2,2,220,2,220]{4,3,2,1,0:T(2,128)(2,1)S(1)}, bf16[2,456,220]{2,1,0:T(8,128)(2,1)S(1)}, f32[256,16]{1,0:T(8,128)S(1)}, f32[1,896]{1,0:T(1,128)S(1)}) custom-call(s32[8]{0:T(128)} %refs_0_.1, f32[8,220]{1,0:T(8,128)} %refs_1_.1, bf16[1,8,220,2,220]{4,3,2,1,0:T(2,128)(2,1)} %bitcast.48, ...), custom_call_target="tpu_custom_call" | custom-call | tf_op jit(solution)/shard_map/fetch/pallas_call | solution.py:356
  1.9 2.2 %encode.4 = (bf16[2,224,896]{2,1,0:T(8,128)(2,1)S(1)}, bf16[112,896]{1,0:T(8,128)(2,1)S(1)}, bf16[112,896]{1,0:T(8,128)(2,1)S(1)}, bf16[1,2,220,2,220]{4,3,2,1,0...) custom-call(f32[256,16]{1,0:T(8,128)S(1)} %get-tuple-element.56.refs_0_, bf16[1,2,2,220,220]{4,3,2,1,0:T(8,128)(2,1)S(1)} %bitcast.40, ...), custom_call_target="tpu_custom_call" | custom-call | flops 1022208000 | bytes 6000000 | tf_op jit(solution)/shard_map/encode/pallas_call | solution.py:389
  4.1 4.5 %collective-permute-start = (bf16[112,896]{1,0:T(8,128)(2,1)S(1)}, bf16[112,896]{1,0:T(8,128)(2,1)S(1)}, u32[]{:S(2)}, u32[]{:S(2)}) collective-permute-start(bf16[112,896]{1,0:T(8,128)(2,1)S(1)} %get-tuple-element.87.refs_0_), channel_id=1, source_target_pairs={{0,4},{4,0},{8,12},{12,8},{1,5},{5,1},{9,13},{13,9},{2,6},{6,2},{1... | collective-permute-start | bytes 602120 | tf_op jit(solution)/shard_map/ppermute | solution.py:268
  8.8 2.2 %encode.5 = (bf16[2,224,896]{2,1,0:T(8,128)(2,1)S(1)}, bf16[112,896]{1,0:T(8,128)(2,1)S(1)}, bf16[112,896]{1,0:T(8,128)(2,1)S(1)}, bf16[1,2,220,2,220]{4,3,2,1,0...) custom-call(f32[256,16]{1,0:T(8,128)S(1)} %get-tuple-element.56.refs_0_, bf16[1,2,2,220,220]{4,3,2,1,0:T(8,128)(2,1)S(1)} %bitcast.41, ...), custom_call_target="tpu_custom_call" | custom-call | flops 1022208000 | bytes 6000000 | tf_op jit(solution)/shard_map/encode/pallas_call | solution.py:389
  11.3 3.6 %encode.6 = (bf16[2,224,896]{2,1,0:T(8,128)(2,1)S(1)}, bf16[112,896]{1,0:T(8,128)(2,1)S(1)}, bf16[112,896]{1,0:T(8,128)(2,1)S(1)}, bf16[1,2,220,2,220]{4,3,2,1,0...) custom-call(f32[256,16]{1,0:T(8,128)S(1)} %get-tuple-element.56.refs_0_, bf16[1,2,2,220,220]{4,3,2,1,0:T(8,128)(2,1)S(1)} %bitcast.42, ...), custom_call_target="tpu_custom_call" | custom-call | flops 1022208000 | bytes 6000000 | tf_op jit(solution)/shard_map/encode/pallas_call | solution.py:389
  15.3 2.1 %collective-permute-start.1 = (bf16[112,896]{1,0:T(8,128)(2,1)S(1)}, bf16[112,896]{1,0:T(8,128)(2,1)S(1)}, u32[]{:S(2)}, u32[]{:S(2)}) collective-permute-start(bf16[112,896]{1,0:T(8,128)(2,1)S(1)} %get-tuple-element.94.refs_0_), channel_id=1, source_target_pairs={{0,4},{4,0},{8,12},{12,8},{1,5},{5,1},{9,13},{13,9},{2,6},{6,2},{1... | collective-permute-start | bytes 602120 | tf_op jit(solution)/shard_map/ppermute | solution.py:268
  17.4 2.2 %encode.7 = (bf16[2,224,896]{2,1,0:T(8,128)(2,1)S(1)}, bf16[112,896]{1,0:T(8,128)(2,1)S(1)}, bf16[112,896]{1,0:T(8,128)(2,1)S(1)}) custom-call(f32[256,16]{1,0:T(8,128)S(1)} %get-tuple-element.56.refs_0_, bf16[1,2,2,220,220]{4,3,2,1,0:T(8,128)(2,1)S(1)} %bitcast.39, bf16[2,2,2,220,220]{4,3,2,1,0:T(8,128)(2,1)S(1)} %bitcast.35, ...), custom_call_target="tpu_custom_call" | custom-call | flops 1022208000 | bytes 6000000 | tf_op jit(solution)/shard_map/encode/pallas_call | solution.py:389
  19.8 2.6 %collective-permute-start.7 = (bf16[112,896]{1,0:T(8,128)(2,1)S(1)}, bf16[112,896]{1,0:T(8,128)(2,1)S(1)}, u32[]{:S(2)}, u32[]{:S(2)}) collective-permute-start(bf16[112,896]{1,0:T(8,128)(2,1)S(1)} %get-tuple-element.98.refs_0_), channel_id=1, source_target_pairs={{0,4},{4,0},{8,12},{12,8},{1,5},{5,1},{9,13},{13,9},{2,6},{6,2},{1... | collective-permute-start | bytes 602120 | tf_op jit(solution)/shard_map/ppermute | solution.py:268
  22.9 1.7 %collective-permute-start.5 = (bf16[112,896]{1,0:T(8,128)(2,1)S(1)}, bf16[112,896]{1,0:T(8,128)(2,1)S(1)}, u32[]{:S(2)}, u32[]{:S(2)}) collective-permute-start(bf16[112,896]{1,0:T(8,128)(2,1)S(1)} %add_select_fusion.3), channel_id=1, source_target_pairs={{0,4},{4,0},{8,12},{12,8},{1,5},{5,1},{9,13},{13,9},{2,6},{6,2},{1... | collective-permute-start | bytes 602120 | tf_op jit(solution)/shard_map/ppermute | solution.py:268
  24.6 3.7 %collective-permute-done.7.refs_1_ = bf16[112,896]{1,0:T(8,128)(2,1)S(1)} collective-permute-done((bf16[112,896]{1,0:T(8,128)(2,1)S(1)}, bf16[112,896]{1,0:T(8,128)(2,1)S(1)}, u32[]{:S(2)}, u32[]{:S(2)}) %collective-permute-start.7) | collective-permute-done | bytes 200736 | tf_op jit(solution)/shard_map/ppermute | solution.py:268
  28.5 1.9 %collective-permute-start.9 = (bf16[112,896]{1,0:T(8,128)(2,1)S(1)}, bf16[112,896]{1,0:T(8,128)(2,1)S(1)}, u32[]{:S(2)}, u32[]{:S(2)}) collective-permute-start(bf16[112,896]{1,0:T(8,128)(2,1)S(1)} %add_select_fusion.2), channel_id=1, source_target_pairs={{0,4},{4,0},{8,12},{12,8},{1,5},{5,1},{9,13},{13,9},{2,6},{6,2},{1... | collective-permute-start | bytes 602120 | tf_op jit(solution)/shard_map/ppermute | solution.py:268
  31.7 1.9 %collective-permute-start.11 = (bf16[112,896]{1,0:T(8,128)(2,1)S(1)}, bf16[112,896]{1,0:T(8,128)(2,1)S(1)}, u32[]{:S(2)}, u32[]{:S(2)}) collective-permute-start(bf16[112,896]{1,0:T(8,128)(2,1)S(1)} %add_select_fusion.1), channel_id=1, source_target_pairs={{0,4},{4,0},{8,12},{12,8},{1,5},{5,1},{9,13},{13,9},{2,6},{6,2},{1... | collective-permute-start | bytes 602120 | tf_op jit(solution)/shard_map/ppermute | solution.py:268
  33.7 2.7 %collective-permute-done.9.refs_3_.refs_1_ = bf16[112,896]{1,0:T(8,128)(2,1)S(1)} collective-permute-done((bf16[112,896]{1,0:T(8,128)(2,1)S(1)}, bf16[112,896]{1,0:T(8,128)(2,1)S(1)}, u32[]{:S(2)}, u32[]{:S(2)}) %collective-permute-start.9) | collective-permute-done | bytes 200736 | tf_op jit(solution)/shard_map/ppermute | solution.py:268
  36.5 2.1 %collective-permute-start.13 = (bf16[112,896]{1,0:T(8,128)(2,1)S(1)}, bf16[112,896]{1,0:T(8,128)(2,1)S(1)}, u32[]{:S(2)}, u32[]{:S(2)}) collective-permute-start(bf16[112,896]{1,0:T(8,128)(2,1)S(1)} %add_select_fusion), channel_id=1, source_target_pairs={{0,4},{4,0},{8,12},{12,8},{1,5},{5,1},{9,13},{13,9},{2,6},{6,2},{1... | collective-permute-start | bytes 602120 | tf_op jit(solution)/shard_map/ppermute | solution.py:268
  38.6 2.1 %collective-permute-done.11.refs_3_.refs_1_ = bf16[112,896]{1,0:T(8,128)(2,1)S(1)} collective-permute-done((bf16[112,896]{1,0:T(8,128)(2,1)S(1)}, bf16[112,896]{1,0:T(8,128)(2,1)S(1)}, u32[]{:S(2)}, u32[]{:S(2)}) %collective-permute-start.11) | collective-permute-done | bytes 200736 | tf_op jit(solution)/shard_map/ppermute | solution.py:268
  40.8 2.1 %collective-permute-start.16 = (bf16[112,896]{1,0:T(8,128)(2,1)S(1)}, bf16[112,896]{1,0:T(8,128)(2,1)S(1)}, u32[]{:S(2)}, u32[]{:S(2)}) collective-permute-start(bf16[112,896]{1,0:T(8,128)(2,1)S(1)} %add.68), channel_id=1, source_target_pairs={{0,4},{4,0},{8,12},{12,8},{1,5},{5,1},{9,13},{13,9},{2,6},{6,2},{1... | collective-permute-start | bytes 602120 | tf_op jit(solution)/shard_map/ppermute | solution.py:268
  42.9 2.1 %collective-permute-done.13.refs_3_.refs_1_ = bf16[112,896]{1,0:T(8,128)(2,1)S(1)} collective-permute-done((bf16[112,896]{1,0:T(8,128)(2,1)S(1)}, bf16[112,896]{1,0:T(8,128)(2,1)S(1)}, u32[]{:S(2)}, u32[]{:S(2)}) %collective-permute-start.13) | collective-permute-done | bytes 200736 | tf_op jit(solution)/shard_map/ppermute | solution.py:268
  45.7 3.2 %collective-permute-start.17 = (bf16[112,896]{1,0:T(8,128)(2,1)S(1)}, bf16[112,896]{1,0:T(8,128)(2,1)S(1)}, u32[]{:S(2)}, u32[]{:S(2)}) collective-permute-start(bf16[112,896]{1,0:T(8,128)(2,1)S(1)} %add.70), channel_id=1, source_target_pairs={{0,4},{4,0},{8,12},{12,8},{1,5},{5,1},{9,13},{13,9},{2,6},{6,2},{1... | collective-permute-start | bytes 602120 | tf_op jit(solution)/shard_map/ppermute | solution.py:268
  49.6 1.4 %collective-permute-start.18 = (bf16[112,896]{1,0:T(8,128)(2,1)S(1)}, bf16[112,896]{1,0:T(8,128)(2,1)S(1)}, u32[]{:S(2)}, u32[]{:S(2)}) collective-permute-start(bf16[112,896]{1,0:T(8,128)(2,1)S(1)} %add.71), channel_id=1, source_target_pairs={{0,4},{4,0},{8,12},{12,8},{1,5},{5,1},{9,13},{13,9},{2,6},{6,2},{1... | collective-permute-start | bytes 602120 | tf_op jit(solution)/shard_map/ppermute | solution.py:268
  51.0 2.2 %collective-permute-start.19 = (bf16[112,896]{1,0:T(8,128)(2,1)S(1)}, bf16[112,896]{1,0:T(8,128)(2,1)S(1)}, u32[]{:S(2)}, u32[]{:S(2)}) collective-permute-start(bf16[112,896]{1,0:T(8,128)(2,1)S(1)} %add.72), channel_id=1, source_target_pairs={{0,4},{4,0},{8,12},{12,8},{1,5},{5,1},{9,13},{13,9},{2,6},{6,2},{1... | collective-permute-start | bytes 602120 | tf_op jit(solution)/shard_map/ppermute | solution.py:268
  55.2 4.0 %collective-permute-done.18.refs_3_ = bf16[112,896]{1,0:T(8,128)(2,1)S(1)} collective-permute-done((bf16[112,896]{1,0:T(8,128)(2,1)S(1)}, bf16[112,896]{1,0:T(8,128)(2,1)S(1)}, u32[]{:S(2)}, u32[]{:S(2)}) %collective-permute-start.18) | collective-permute-done | bytes 200736 | tf_op jit(solution)/shard_map/ppermute | solution.py:268
  59.4 2.4 %collective-permute-done.19.refs_3_ = bf16[112,896]{1,0:T(8,128)(2,1)S(1)} collective-permute-done((bf16[112,896]{1,0:T(8,128)(2,1)S(1)}, bf16[112,896]{1,0:T(8,128)(2,1)S(1)}, u32[]{:S(2)}, u32[]{:S(2)}) %collective-permute-start.19) | collective-permute-done | bytes 200736 | tf_op jit(solution)/shard_map/ppermute | solution.py:268
  62.2 1.6 %collective-permute-start.21 = (f32[8,220]{1,0:T(8,128)S(1)}, f32[8,220]{1,0:T(8,128)S(1)}, u32[]{:S(2)}, u32[]{:S(2)}) collective-permute-start(f32[8,220]{1,0:T(8,128)S(1)} %reshape.3), channel_id=1, source_target_pairs={{0,2},{1,3},{2,0},{3,1},{4,6},{5,7},{6,4},{7,5},{8,10},{9,11},{10,... | collective-permute-start | bytes 21128 | tf_op jit(solution)/shard_map/ppermute | solution.py:251
  64.1 1.9 %collective-permute-done.21 = f32[8,220]{1,0:T(8,128)S(1)} collective-permute-done((f32[8,220]{1,0:T(8,128)S(1)}, f32[8,220]{1,0:T(8,128)S(1)}, u32[]{:S(2)}, u32[]{:S(2)}) %collective-permute-start.21) | collective-permute-done | bytes 7072 | tf_op jit(solution)/shard_map/ppermute | solution.py:251
  (68 shorter events, 9.1 us)
Async XLA Ops:
  4.1 11.1 %collective-permute-start = (bf16[112,896]{1,0:T(8,128)(2,1)S(1)}, bf16[112,896]{1,0:T(8,128)(2,1)S(1)}, u32[]{:S(2)}, u32[]{:S(2)}) collective-permute-start(bf16[112,896]{1,0:T(8,128)(2,1)S(1)} %get-tuple-element.87.refs_0_), channel_id=1, source_target_pairs={{0,4},{4,0},{8,12},{12,8},{1,5},{5,1},{9,13},{13,9},{2,6},{6,2},{1... | collective-permute-start | bytes 602120 | tf_op jit(solution)/shard_map/ppermute | solution.py:268
  11.0 8.7 %collective-permute-start.2 = (bf16[112,896]{1,0:T(8,128)(2,1)S(1)}, bf16[112,896]{1,0:T(8,128)(2,1)S(1)}, u32[]{:S(2)}, u32[]{:S(2)}) collective-permute-start(bf16[112,896]{1,0:T(8,128)(2,1)S(1)} %get-tuple-element.91.refs_0_), channel_id=1, source_target_pairs={{0,4},{4,0},{8,12},{12,8},{1,5},{5,1},{9,13},{13,9},{2,6},{6,2},{1... | collective-permute-start | bytes 602120 | tf_op jit(solution)/shard_map/ppermute | solution.py:268
  15.2 7.6 %collective-permute-start.4 = (bf16[112,896]{1,0:T(8,128)(2,1)S(1)}, bf16[112,896]{1,0:T(8,128)(2,1)S(1)}, u32[]{:S(2)}, u32[]{:S(2)}) collective-permute-start(bf16[112,896]{1,0:T(8,128)(2,1)S(1)} %add.57), channel_id=1, source_target_pairs={{0,1},{1,0},{4,8},{5,9},{8,4},{9,5},{12,13},{13,12},{2,3},{3,2},{6... | collective-permute-start | bytes 602120 | tf_op jit(solution)/shard_map/ppermute | solution.py:271
  15.3 7.4 %collective-permute-start.1 = (bf16[112,896]{1,0:T(8,128)(2,1)S(1)}, bf16[112,896]{1,0:T(8,128)(2,1)S(1)}, u32[]{:S(2)}, u32[]{:S(2)}) collective-permute-start(bf16[112,896]{1,0:T(8,128)(2,1)S(1)} %get-tuple-element.94.refs_0_), channel_id=1, source_target_pairs={{0,4},{4,0},{8,12},{12,8},{1,5},{5,1},{9,13},{13,9},{2,6},{6,2},{1... | collective-permute-start | bytes 602120 | tf_op jit(solution)/shard_map/ppermute | solution.py:268
  19.8 8.7 %collective-permute-start.6 = (bf16[112,896]{1,0:T(8,128)(2,1)S(1)}, bf16[112,896]{1,0:T(8,128)(2,1)S(1)}, u32[]{:S(2)}, u32[]{:S(2)}) collective-permute-start(bf16[112,896]{1,0:T(8,128)(2,1)S(1)} %add.58), channel_id=1, source_target_pairs={{0,1},{1,0},{4,8},{5,9},{8,4},{9,5},{12,13},{13,12},{2,3},{3,2},{6... | collective-permute-start | bytes 602120 | tf_op jit(solution)/shard_map/ppermute | solution.py:271
  19.8 8.5 %collective-permute-start.7 = (bf16[112,896]{1,0:T(8,128)(2,1)S(1)}, bf16[112,896]{1,0:T(8,128)(2,1)S(1)}, u32[]{:S(2)}, u32[]{:S(2)}) collective-permute-start(bf16[112,896]{1,0:T(8,128)(2,1)S(1)} %get-tuple-element.98.refs_0_), channel_id=1, source_target_pairs={{0,4},{4,0},{8,12},{12,8},{1,5},{5,1},{9,13},{13,9},{2,6},{6,2},{1... | collective-permute-start | bytes 602120 | tf_op jit(solution)/shard_map/ppermute | solution.py:268
  22.7 8.9 %collective-permute-start.3 = (bf16[112,896]{1,0:T(8,128)(2,1)S(1)}, bf16[112,896]{1,0:T(8,128)(2,1)S(1)}, u32[]{:S(2)}, u32[]{:S(2)}) collective-permute-start(bf16[112,896]{1,0:T(8,128)(2,1)S(1)} %add.59), channel_id=1, source_target_pairs={{0,1},{1,0},{4,8},{5,9},{8,4},{9,5},{12,13},{13,12},{2,3},{3,2},{6... | collective-permute-start | bytes 602120 | tf_op jit(solution)/shard_map/ppermute | solution.py:271
  22.9 8.7 %collective-permute-start.5 = (bf16[112,896]{1,0:T(8,128)(2,1)S(1)}, bf16[112,896]{1,0:T(8,128)(2,1)S(1)}, u32[]{:S(2)}, u32[]{:S(2)}) collective-permute-start(bf16[112,896]{1,0:T(8,128)(2,1)S(1)} %add_select_fusion.3), channel_id=1, source_target_pairs={{0,4},{4,0},{8,12},{12,8},{1,5},{5,1},{9,13},{13,9},{2,6},{6,2},{1... | collective-permute-start | bytes 602120 | tf_op jit(solution)/shard_map/ppermute | solution.py:268
  28.4 8.1 %collective-permute-start.8 = (bf16[112,896]{1,0:T(8,128)(2,1)S(1)}, bf16[112,896]{1,0:T(8,128)(2,1)S(1)}, u32[]{:S(2)}, u32[]{:S(2)}) collective-permute-start(bf16[112,896]{1,0:T(8,128)(2,1)S(1)} %add.61), channel_id=1, source_target_pairs={{0,1},{1,0},{4,8},{5,9},{8,4},{9,5},{12,13},{13,12},{2,3},{3,2},{6... | collective-permute-start | bytes 602120 | tf_op jit(solution)/shard_map/ppermute | solution.py:271
  28.5 7.8 %collective-permute-start.9 = (bf16[112,896]{1,0:T(8,128)(2,1)S(1)}, bf16[112,896]{1,0:T(8,128)(2,1)S(1)}, u32[]{:S(2)}, u32[]{:S(2)}) collective-permute-start(bf16[112,896]{1,0:T(8,128)(2,1)S(1)} %add_select_fusion.2), channel_id=1, source_target_pairs={{0,4},{4,0},{8,12},{12,8},{1,5},{5,1},{9,13},{13,9},{2,6},{6,2},{1... | collective-permute-start | bytes 602120 | tf_op jit(solution)/shard_map/ppermute | solution.py:268
  31.6 9.1 %collective-permute-start.10 = (bf16[112,896]{1,0:T(8,128)(2,1)S(1)}, bf16[112,896]{1,0:T(8,128)(2,1)S(1)}, u32[]{:S(2)}, u32[]{:S(2)}) collective-permute-start(bf16[112,896]{1,0:T(8,128)(2,1)S(1)} %add.63), channel_id=1, source_target_pairs={{0,1},{1,0},{4,8},{5,9},{8,4},{9,5},{12,13},{13,12},{2,3},{3,2},{6... | collective-permute-start | bytes 602120 | tf_op jit(solution)/shard_map/ppermute | solution.py:271
  31.7 8.9 %collective-permute-start.11 = (bf16[112,896]{1,0:T(8,128)(2,1)S(1)}, bf16[112,896]{1,0:T(8,128)(2,1)S(1)}, u32[]{:S(2)}, u32[]{:S(2)}) collective-permute-start(bf16[112,896]{1,0:T(8,128)(2,1)S(1)} %add_select_fusion.1), channel_id=1, source_target_pairs={{0,4},{4,0},{8,12},{12,8},{1,5},{5,1},{9,13},{13,9},{2,6},{6,2},{1... | collective-permute-start | bytes 602120 | tf_op jit(solution)/shard_map/ppermute | solution.py:268
  36.5 8.5 %collective-permute-start.13 = (bf16[112,896]{1,0:T(8,128)(2,1)S(1)}, bf16[112,896]{1,0:T(8,128)(2,1)S(1)}, u32[]{:S(2)}, u32[]{:S(2)}) collective-permute-start(bf16[112,896]{1,0:T(8,128)(2,1)S(1)} %add_select_fusion), channel_id=1, source_target_pairs={{0,4},{4,0},{8,12},{12,8},{1,5},{5,1},{9,13},{13,9},{2,6},{6,2},{1... | collective-permute-start | bytes 602120 | tf_op jit(solution)/shard_map/ppermute | solution.py:268
  38.6 7.1 %collective-permute-start.12 = (bf16[112,896]{1,0:T(8,128)(2,1)S(1)}, bf16[112,896]{1,0:T(8,128)(2,1)S(1)}, u32[]{:S(2)}, u32[]{:S(2)}) collective-permute-start(bf16[112,896]{1,0:T(8,128)(2,1)S(1)} %add.65), channel_id=1, source_target_pairs={{0,1},{1,0},{4,8},{5,9},{8,4},{9,5},{12,13},{13,12},{2,3},{3,2},{6... | collective-permute-start | bytes 602120 | tf_op jit(solution)/shard_map/ppermute | solution.py:271
  40.8 8.7 %collective-permute-start.16 = (bf16[112,896]{1,0:T(8,128)(2,1)S(1)}, bf16[112,896]{1,0:T(8,128)(2,1)S(1)}, u32[]{:S(2)}, u32[]{:S(2)}) collective-permute-start(bf16[112,896]{1,0:T(8,128)(2,1)S(1)} %add.68), channel_id=1, source_target_pairs={{0,4},{4,0},{8,12},{12,8},{1,5},{5,1},{9,13},{13,9},{2,6},{6,2},{1... | collective-permute-start | bytes 602120 | tf_op jit(solution)/shard_map/ppermute | solution.py:268
  42.9 6.7 %collective-permute-start.15 = (bf16[112,896]{1,0:T(8,128)(2,1)S(1)}, bf16[112,896]{1,0:T(8,128)(2,1)S(1)}, u32[]{:S(2)}, u32[]{:S(2)}) collective-permute-start(bf16[112,896]{1,0:T(8,128)(2,1)S(1)} %add.67), channel_id=1, source_target_pairs={{0,1},{1,0},{4,8},{5,9},{8,4},{9,5},{12,13},{13,12},{2,3},{3,2},{6... | collective-permute-start | bytes 602120 | tf_op jit(solution)/shard_map/ppermute | solution.py:271
  45.0 6.0 %collective-permute-start.14 = (bf16[112,896]{1,0:T(8,128)(2,1)S(1)}, bf16[112,896]{1,0:T(8,128)(2,1)S(1)}, u32[]{:S(2)}, u32[]{:S(2)}) collective-permute-start(bf16[112,896]{1,0:T(8,128)(2,1)S(1)} %add.69), channel_id=1, source_target_pairs={{0,1},{1,0},{4,8},{5,9},{8,4},{9,5},{12,13},{13,12},{2,3},{3,2},{6... | collective-permute-start | bytes 602120 | tf_op jit(solution)/shard_map/ppermute | solution.py:271
  45.7 9.1 %collective-permute-start.17 = (bf16[112,896]{1,0:T(8,128)(2,1)S(1)}, bf16[112,896]{1,0:T(8,128)(2,1)S(1)}, u32[]{:S(2)}, u32[]{:S(2)}) collective-permute-start(bf16[112,896]{1,0:T(8,128)(2,1)S(1)} %add.70), channel_id=1, source_target_pairs={{0,4},{4,0},{8,12},{12,8},{1,5},{5,1},{9,13},{13,9},{2,6},{6,2},{1... | collective-permute-start | bytes 602120 | tf_op jit(solution)/shard_map/ppermute | solution.py:268
  49.6 9.5 %collective-permute-start.18 = (bf16[112,896]{1,0:T(8,128)(2,1)S(1)}, bf16[112,896]{1,0:T(8,128)(2,1)S(1)}, u32[]{:S(2)}, u32[]{:S(2)}) collective-permute-start(bf16[112,896]{1,0:T(8,128)(2,1)S(1)} %add.71), channel_id=1, source_target_pairs={{0,4},{4,0},{8,12},{12,8},{1,5},{5,1},{9,13},{13,9},{2,6},{6,2},{1... | collective-permute-start | bytes 602120 | tf_op jit(solution)/shard_map/ppermute | solution.py:268
  51.0 10.7 %collective-permute-start.19 = (bf16[112,896]{1,0:T(8,128)(2,1)S(1)}, bf16[112,896]{1,0:T(8,128)(2,1)S(1)}, u32[]{:S(2)}, u32[]{:S(2)}) collective-permute-start(bf16[112,896]{1,0:T(8,128)(2,1)S(1)} %add.72), channel_id=1, source_target_pairs={{0,4},{4,0},{8,12},{12,8},{1,5},{5,1},{9,13},{13,9},{2,6},{6,2},{1... | collective-permute-start | bytes 602120 | tf_op jit(solution)/shard_map/ppermute | solution.py:268
  62.1 1.9 %collective-permute-start.20 = (f32[8,220]{1,0:T(8,128)S(1)}, f32[8,220]{1,0:T(8,128)S(1)}, u32[]{:S(2)}, u32[]{:S(2)}) collective-permute-start(f32[8,220]{1,0:T(8,128)S(1)} %reshape.3), channel_id=1, source_target_pairs={{0,1},{1,0},{2,3},{3,2},{4,5},{5,4},{6,7},{7,6},{8,9},{9,8},{10,11... | collective-permute-start | bytes 21128 | tf_op jit(solution)/shard_map/ppermute | solution.py:251
  62.2 3.7 %collective-permute-start.21 = (f32[8,220]{1,0:T(8,128)S(1)}, f32[8,220]{1,0:T(8,128)S(1)}, u32[]{:S(2)}, u32[]{:S(2)}) collective-permute-start(f32[8,220]{1,0:T(8,128)S(1)} %reshape.3), channel_id=1, source_target_pairs={{0,2},{1,3},{2,0},{3,1},{4,6},{5,7},{6,4},{7,5},{8,10},{9,11},{10,... | collective-permute-start | bytes 21128 | tf_op jit(solution)/shard_map/ppermute | solution.py:251
  63.8 3.1 %collective-permute-start.22 = (f32[8,220]{1,0:T(8,128)S(1)}, f32[8,220]{1,0:T(8,128)S(1)}, u32[]{:S(2)}, u32[]{:S(2)}) collective-permute-start(f32[8,220]{1,0:T(8,128)S(1)} %reshape.3), channel_id=1, source_target_pairs={{0,3},{1,2},{2,1},{3,0},{4,7},{5,6},{6,5},{7,4},{8,11},{9,10},{10,... | collective-permute-start | bytes 21128 | tf_op jit(solution)/shard_map/ppermute | solution.py:251

commit v17 on v16

--- a/solution.py
+++ b/solution.py
@@ -118,22 +118,19 @@
     if not whole_classes:
         place_ref, refs = refs[0], refs[1:]
         next_rows = next_rows and [place_ref[2]]
-    phase_ref, image, coil_map, left_ref = refs[:4]
-    order_ref, gram_ref, adjoint_ref, kspace_ref, image_ref, map_ref = refs[4:10]
+    phase_ref, image, coil_map, left_ref, kspace_ref = refs[:5]
+    order_ref, gram_ref, adjoint_ref, image_ref, map_ref = refs[5:10]
     refs = refs[10:]
     shifted, refs = refs[0], refs[1:]
     out_refs, refs = refs[:PARTS], refs[PARTS:]
     if next_rows:
         next_image, next_map, refs = refs[0], refs[1], refs[2:]
-    total, wide, raw_kspace, gram, adjoint, order, arrived, small = refs
+    total, gram, adjoint, order, arrived, small = refs
     vols, coils, length = image.shape[0], coil_map.shape[0], image.shape[-1]
     _, rows, lanes = shifted.shape
     order_copy = pltpu.make_async_copy(order_ref, order, small.at[0])
     gram_copy = pltpu.make_async_copy(gram_ref, gram, small.at[1])
-    owner_copies = [
-        pltpu.make_async_copy(kspace_ref, raw_kspace, small.at[2]),
-        pltpu.make_async_copy(adjoint_ref, adjoint, small.at[3]),
-    ]
+    owner_copies = [pltpu.make_async_copy(adjoint_ref, adjoint, small.at[2])]
     next_copies = []
     if next_rows:
         next_copies = slice_copies(image_ref, map_ref, next_image, next_map, arrived, next_rows)
@@ -200,18 +197,9 @@
         for vol in range(vols):
             for coil in range(coils):
                 place = vol * coils + coil
-                lying = raw_kspace.at[vol, 0, coil].reshape(2 * length, length)[...]
-                measured = None
-                for kind in range(2):
-                    for tile in range(wide.shape[0]):
-                        at, end = tile * LANE_TILE, min(length, (tile + 1) * LANE_TILE)
-                        if kind == 0:
-                            wide[tile, :, : end - at] = lying[:, at:end].astype(jnp.float32)
-                        rows_read = wide[tile, pl.ds(kind, length, stride=2), :]
-                        term = dot(
-                            rows_read[:, : end - at].astype(jnp.bfloat16), adjoint[kind, at:end, :]
-                        )
-                        measured = term if measured is None else measured + term
+                measured = dot(kspace_ref[vol, 0, coil, 0], adjoint[0]) + dot(
+                    kspace_ref[vol, 0, coil, 1], adjoint[1]
+                )
                 total[:length, place * 2 * length : (place + 1) * 2 * length] -= measured
 
     part = rows // PARTS
@@ -295,7 +283,7 @@
             others = own[step - 2] + after(across[step - 2], half)
             payload = others if payload is None else jnp.where(ends > 0, payload, others)
         else:
-            payload = after(payload, half)
+            payload = after(payload, near[step])
         near.append(outer(payload))
         latest = payload
         if len(own) < min(step + 7, count):
@@ -343,9 +331,8 @@
         return (jnp.stack([inside[0], rows_held[0], rows_held[1]]).astype(jnp.int32),)
 
     left, gram, adjoint = (in_hbm(table) for table in tables)
-    lying = [in_hbm(jnp.swapaxes(array, -3, -2)) for array in (images, coil_maps, kspace)]
+    lying = [in_hbm(jnp.swapaxes(array, -3, -2)) for array in (images, coil_maps)]
     order = in_hbm(group_order)
-    tiles = round_up(length, LANE_TILE) // LANE_TILE
     raw_shapes = [
         jax.ShapeDtypeStruct((count, slots, length, 2, length), jnp.bfloat16)
         for count in (vols, coils)
@@ -372,7 +359,7 @@
         ],
         compiler_params=pltpu.CompilerParams(vmem_limit_bytes=VMEM_BYTES),
         name="fetch",
-    )(*place_of(0), in_hbm(shift_index), in_hbm(phase_offset), *lying[:2], left)
+    )(*place_of(0), in_hbm(shift_index), in_hbm(phase_offset), *lying, left)
 
     shifted = []
 
@@ -394,20 +381,18 @@
                 rows_of_class(group),
                 (rows_of_class(group + 1) or [0]) if has_next else None,
             ),
-            in_specs=scalar_specs + [in_vmem] * 4 + [in_place] * 6,
+            in_specs=scalar_specs + [in_vmem] * 5 + [in_place] * 5,
             out_specs=[in_vmem] * (1 + PARTS + 2 * has_next),
             out_shape=[jax.ShapeDtypeStruct((slots, rows, lanes), jnp.bfloat16)]
             + [jax.ShapeDtypeStruct((rows // PARTS, lanes), jnp.bfloat16)] * PARTS
             + raw_shapes * has_next,
             scratch_shapes=[
                 pltpu.VMEM((rows, lanes), jnp.float32),
-                pltpu.VMEM((tiles, 2 * length, LANE_TILE), jnp.float32),
-                pltpu.VMEM(lying[2].shape, jnp.bfloat16),
                 pltpu.VMEM(gram.shape, jnp.bfloat16),
                 pltpu.VMEM(adjoint.shape, jnp.bfloat16),
                 pltpu.SMEM((groups,), jnp.int32),
                 slice_semaphores,
-                pltpu.SemaphoreType.DMA((4,)),
+                pltpu.SemaphoreType.DMA((3,)),
             ],
             compiler_params=pltpu.CompilerParams(vmem_limit_bytes=VMEM_BYTES),
             cost_estimate=pl.CostEstimate(
@@ -422,11 +407,11 @@
             image,
             coil_map,
             left,
+            kspace,
             order,
             gram,
             adjoint,
-            lying[2],
-            *lying[:2],
+            *lying,
         )
         raw[:] = outputs[1 + PARTS :]
         shifted.append(outputs[0])

time: 67.7 us -> 67.8 us (level)
  starting transfers between devices: 28.2 us -> 32.7 us
  waiting for transfers between devices: 22.3 us -> 18.3 us
    ppermute x12, starting transfers between devices: 25.8 us -> 29.8 us  [outer(): return lax.ppermute(value, 'slc', outer_pairs)]
    ppermute x12, waiting for transfers between devices: 19.5 us -> 15.5 us  [outer(): return lax.ppermute(value, 'slc', outer_pairs)]
  transfers between devices with their start and end apart: 23 -> 23, of which waited for: 11 -> 10; matrix products, arithmetic and copies ran while one was open for 2% -> 2% of each run, Pallas kernels for 15% -> 14%
where the time goes in v17:
time: 67.8 us; the launch traced here: 67.5 us
  starting transfers between devices  32.7 us (48%)
  waiting for transfers between devices  18.3 us (27%)
  Pallas kernels  13.6 us (20%)
  other arithmetic  1.75 us (3%)
  local copies, waits for them, and re-layouts  0.84 us (1%)
    ppermute x12, starting transfers between devices, outer(): return lax.ppermute(value, 'slc', outer_pairs)  29.8 us
    ppermute x12, waiting for transfers between devices, outer(): return lax.ppermute(value, 'slc', outer_pairs)  15.5 us
    pallas_call x4, Pallas kernels, encode(): pl.pallas_call(functools.partial(encode_kernel, slots, group, rows_of_cla...  9.76 us
    ppermute x3, waiting for transfers between devices, sum_over_replicas(): lax.ppermute(value, axes, [(index, index ^ mask) for index in range(4)])  2.77 us
    pallas_call x8, Pallas kernels, gradient(): pl.pallas_call(functools.partial(gradient_kernel, index, factor, on_line)...  2.13 us
    ppermute x3, starting transfers between devices, sum_over_replicas(): lax.ppermute(value, axes, [(index, index ^ mask) for index in range(4)])  1.93 us
    pallas_call x1, Pallas kernels, body(): pl.pallas_call(functools.partial(fetch_kernel, rows_of_class(0)), in_spec...  1.7 us
  transfers between devices with their start and end apart: 23, of which 10 were waited for; matrix products, arithmetic and copies ran while one was open for 2% of the time, Pallas kernels for 14%

profile of v17, /device:TPU:0, one launch (start us, length us, event | category | flops | bytes accessed | tf_op | source)
XLA Modules:
  0.0 67.5 jit_solution(12607719751730087362)
XLA Ops:
  0.0 1.7 %fetch.1 = (bf16[1,2,220,2,220]{4,3,2,1,0:T(2,128)(2,1)S(1)}, bf16[2,2,220,2,220]{4,3,2,1,0:T(2,128)(2,1)S(1)}, bf16[2,456,220]{2,1,0:T(8,128)(2,1)S(1)}, f32[256,16]{1,0:T(8,128)S(1)}, f32[1,896]{1,0:T(1,128)S(1)}) custom-call(s32[8]{0:T(128)} %refs_0_.1, f32[8,220]{1,0:T(8,128)} %refs_1_.1, bf16[1,8,220,2,220]{4,3,2,1,0:T(2,128)(2,1)} %bitcast.47, ...), custom_call_target="tpu_custom_call" | custom-call | tf_op jit(solution)/shard_map/fetch/pallas_call | solution.py:343
  2.0 2.2 %encode.4 = (bf16[2,224,896]{2,1,0:T(8,128)(2,1)S(1)}, bf16[112,896]{1,0:T(8,128)(2,1)S(1)}, bf16[112,896]{1,0:T(8,128)(2,1)S(1)}, bf16[1,2,220,2,220]{4,3,2,1,0...) custom-call(f32[256,16]{1,0:T(8,128)S(1)} %get-tuple-element.56.refs_0_, bf16[1,2,2,220,220]{4,3,2,1,0:T(8,128)(2,1)S(1)} %bitcast.39, ...), custom_call_target="tpu_custom_call" | custom-call | flops 1022208000 | bytes 6000000 | tf_op jit(solution)/shard_map/encode/pallas_call | solution.py:376
  4.2 3.1 %collective-permute-start = (bf16[112,896]{1,0:T(8,128)(2,1)S(1)}, bf16[112,896]{1,0:T(8,128)(2,1)S(1)}, u32[]{:S(2)}, u32[]{:S(2)}) collective-permute-start(bf16[112,896]{1,0:T(8,128)(2,1)S(1)} %get-tuple-element.87.refs_0_), channel_id=1, source_target_pairs={{0,4},{4,0},{8,12},{12,8},{1,5},{5,1},{9,13},{13,9},{2,6},{6,2},{1... | collective-permute-start | bytes 602120 | tf_op jit(solution)/shard_map/ppermute | solution.py:256
  7.5 2.2 %encode.5 = (bf16[2,224,896]{2,1,0:T(8,128)(2,1)S(1)}, bf16[112,896]{1,0:T(8,128)(2,1)S(1)}, bf16[112,896]{1,0:T(8,128)(2,1)S(1)}, bf16[1,2,220,2,220]{4,3,2,1,0...) custom-call(f32[256,16]{1,0:T(8,128)S(1)} %get-tuple-element.56.refs_0_, bf16[1,2,2,220,220]{4,3,2,1,0:T(8,128)(2,1)S(1)} %bitcast.40, ...), custom_call_target="tpu_custom_call" | custom-call | flops 1022208000 | bytes 6000000 | tf_op jit(solution)/shard_map/encode/pallas_call | solution.py:376
  10.9 3.2 %encode.6 = (bf16[2,224,896]{2,1,0:T(8,128)(2,1)S(1)}, bf16[112,896]{1,0:T(8,128)(2,1)S(1)}, bf16[112,896]{1,0:T(8,128)(2,1)S(1)}, bf16[1,2,220,2,220]{4,3,2,1,0...) custom-call(f32[256,16]{1,0:T(8,128)S(1)} %get-tuple-element.56.refs_0_, bf16[1,2,2,220,220]{4,3,2,1,0:T(8,128)(2,1)S(1)} %bitcast.41, ...), custom_call_target="tpu_custom_call" | custom-call | flops 1022208000 | bytes 6000000 | tf_op jit(solution)/shard_map/encode/pallas_call | solution.py:376
  14.9 2.2 %encode.7 = (bf16[2,224,896]{2,1,0:T(8,128)(2,1)S(1)}, bf16[112,896]{1,0:T(8,128)(2,1)S(1)}, bf16[112,896]{1,0:T(8,128)(2,1)S(1)}) custom-call(f32[256,16]{1,0:T(8,128)S(1)} %get-tuple-element.56.refs_0_, bf16[1,2,2,220,220]{4,3,2,1,0:T(8,128)(2,1)S(1)} %bitcast.38, bf16[2,2,2,220,220]{4,3,2,1,0:T(8,128)(2,1)S(1)} %bitcast.34, ...), custom_call_target="tpu_custom_call" | custom-call | flops 1022208000 | bytes 6000000 | tf_op jit(solution)/shard_map/encode/pallas_call | solution.py:376
  17.8 5.0 %collective-permute-start.7 = (bf16[112,896]{1,0:T(8,128)(2,1)S(1)}, bf16[112,896]{1,0:T(8,128)(2,1)S(1)}, u32[]{:S(2)}, u32[]{:S(2)}) collective-permute-start(bf16[112,896]{1,0:T(8,128)(2,1)S(1)} %get-tuple-element.98.refs_0_), channel_id=1, source_target_pairs={{0,4},{4,0},{8,12},{12,8},{1,5},{5,1},{9,13},{13,9},{2,6},{6,2},{1... | collective-permute-start | bytes 602120 | tf_op jit(solution)/shard_map/ppermute | solution.py:256
  23.0 2.2 %collective-permute-start.5 = (bf16[112,896]{1,0:T(8,128)(2,1)S(1)}, bf16[112,896]{1,0:T(8,128)(2,1)S(1)}, u32[]{:S(2)}, u32[]{:S(2)}) collective-permute-start(bf16[112,896]{1,0:T(8,128)(2,1)S(1)} %add_select_fusion.3), channel_id=1, source_target_pairs={{0,4},{4,0},{8,12},{12,8},{1,5},{5,1},{9,13},{13,9},{2,6},{6,2},{1... | collective-permute-start | bytes 602120 | tf_op jit(solution)/shard_map/ppermute | solution.py:256
  25.2 2.7 %collective-permute-done.7.refs_1_ = bf16[112,896]{1,0:T(8,128)(2,1)S(1)} collective-permute-done((bf16[112,896]{1,0:T(8,128)(2,1)S(1)}, bf16[112,896]{1,0:T(8,128)(2,1)S(1)}, u32[]{:S(2)}, u32[]{:S(2)}) %collective-permute-start.7) | collective-permute-done | bytes 200736 | tf_op jit(solution)/shard_map/ppermute | solution.py:256
  28.1 2.8 %collective-permute-start.9 = (bf16[112,896]{1,0:T(8,128)(2,1)S(1)}, bf16[112,896]{1,0:T(8,128)(2,1)S(1)}, u32[]{:S(2)}, u32[]{:S(2)}) collective-permute-start(bf16[112,896]{1,0:T(8,128)(2,1)S(1)} %add_select_fusion.2), channel_id=1, source_target_pairs={{0,4},{4,0},{8,12},{12,8},{1,5},{5,1},{9,13},{13,9},{2,6},{6,2},{1... | collective-permute-start | bytes 602120 | tf_op jit(solution)/shard_map/ppermute | solution.py:256
  31.7 3.0 %collective-permute-start.11 = (bf16[112,896]{1,0:T(8,128)(2,1)S(1)}, bf16[112,896]{1,0:T(8,128)(2,1)S(1)}, u32[]{:S(2)}, u32[]{:S(2)}) collective-permute-start(bf16[112,896]{1,0:T(8,128)(2,1)S(1)} %add_select_fusion.1), channel_id=1, source_target_pairs={{0,4},{4,0},{8,12},{12,8},{1,5},{5,1},{9,13},{13,9},{2,6},{6,2},{1... | collective-permute-start | bytes 602120 | tf_op jit(solution)/shard_map/ppermute | solution.py:256
  34.6 1.8 %collective-permute-done.9.refs_3_.refs_1_ = bf16[112,896]{1,0:T(8,128)(2,1)S(1)} collective-permute-done((bf16[112,896]{1,0:T(8,128)(2,1)S(1)}, bf16[112,896]{1,0:T(8,128)(2,1)S(1)}, u32[]{:S(2)}, u32[]{:S(2)}) %collective-permute-start.9) | collective-permute-done | bytes 200736 | tf_op jit(solution)/shard_map/ppermute | solution.py:256
  36.5 2.5 %collective-permute-start.13 = (bf16[112,896]{1,0:T(8,128)(2,1)S(1)}, bf16[112,896]{1,0:T(8,128)(2,1)S(1)}, u32[]{:S(2)}, u32[]{:S(2)}) collective-permute-start(bf16[112,896]{1,0:T(8,128)(2,1)S(1)} %add_select_fusion), channel_id=1, source_target_pairs={{0,4},{4,0},{8,12},{12,8},{1,5},{5,1},{9,13},{13,9},{2,6},{6,2},{1... | collective-permute-start | bytes 602120 | tf_op jit(solution)/shard_map/ppermute | solution.py:256
  39.1 1.6 %collective-permute-done.11.refs_3_.refs_1_ = bf16[112,896]{1,0:T(8,128)(2,1)S(1)} collective-permute-done((bf16[112,896]{1,0:T(8,128)(2,1)S(1)}, bf16[112,896]{1,0:T(8,128)(2,1)S(1)}, u32[]{:S(2)}, u32[]{:S(2)}) %collective-permute-start.11) | collective-permute-done | bytes 200736 | tf_op jit(solution)/shard_map/ppermute | solution.py:256
  40.9 2.5 %collective-permute-start.16 = (bf16[112,896]{1,0:T(8,128)(2,1)S(1)}, bf16[112,896]{1,0:T(8,128)(2,1)S(1)}, u32[]{:S(2)}, u32[]{:S(2)}) collective-permute-start(bf16[112,896]{1,0:T(8,128)(2,1)S(1)} %add.68), channel_id=1, source_target_pairs={{0,4},{4,0},{8,12},{12,8},{1,5},{5,1},{9,13},{13,9},{2,6},{6,2},{1... | collective-permute-start | bytes 602120 | tf_op jit(solution)/shard_map/ppermute | solution.py:256
  43.4 1.6 %collective-permute-done.13.refs_3_.refs_1_ = bf16[112,896]{1,0:T(8,128)(2,1)S(1)} collective-permute-done((bf16[112,896]{1,0:T(8,128)(2,1)S(1)}, bf16[112,896]{1,0:T(8,128)(2,1)S(1)}, u32[]{:S(2)}, u32[]{:S(2)}) %collective-permute-start.13) | collective-permute-done | bytes 200736 | tf_op jit(solution)/shard_map/ppermute | solution.py:256
  45.8 3.5 %collective-permute-start.17 = (bf16[112,896]{1,0:T(8,128)(2,1)S(1)}, bf16[112,896]{1,0:T(8,128)(2,1)S(1)}, u32[]{:S(2)}, u32[]{:S(2)}) collective-permute-start(bf16[112,896]{1,0:T(8,128)(2,1)S(1)} %add.70), channel_id=1, source_target_pairs={{0,4},{4,0},{8,12},{12,8},{1,5},{5,1},{9,13},{13,9},{2,6},{6,2},{1... | collective-permute-start | bytes 602120 | tf_op jit(solution)/shard_map/ppermute | solution.py:256
  49.9 1.5 %collective-permute-start.18 = (bf16[112,896]{1,0:T(8,128)(2,1)S(1)}, bf16[112,896]{1,0:T(8,128)(2,1)S(1)}, u32[]{:S(2)}, u32[]{:S(2)}) collective-permute-start(bf16[112,896]{1,0:T(8,128)(2,1)S(1)} %add.71), channel_id=1, source_target_pairs={{0,4},{4,0},{8,12},{12,8},{1,5},{5,1},{9,13},{13,9},{2,6},{6,2},{1... | collective-permute-start | bytes 602120 | tf_op jit(solution)/shard_map/ppermute | solution.py:256
  51.5 2.1 %collective-permute-start.19 = (bf16[112,896]{1,0:T(8,128)(2,1)S(1)}, bf16[112,896]{1,0:T(8,128)(2,1)S(1)}, u32[]{:S(2)}, u32[]{:S(2)}) collective-permute-start(bf16[112,896]{1,0:T(8,128)(2,1)S(1)} %add.72), channel_id=1, source_target_pairs={{0,4},{4,0},{8,12},{12,8},{1,5},{5,1},{9,13},{13,9},{2,6},{6,2},{1... | collective-permute-start | bytes 602120 | tf_op jit(solution)/shard_map/ppermute | solution.py:256
  53.9 1.2 %collective-permute-done.17.refs_3_ = bf16[112,896]{1,0:T(8,128)(2,1)S(1)} collective-permute-done((bf16[112,896]{1,0:T(8,128)(2,1)S(1)}, bf16[112,896]{1,0:T(8,128)(2,1)S(1)}, u32[]{:S(2)}, u32[]{:S(2)}) %collective-permute-start.17) | collective-permute-done | bytes 200736 | tf_op jit(solution)/shard_map/ppermute | solution.py:256
  55.5 4.0 %collective-permute-done.18.refs_3_ = bf16[112,896]{1,0:T(8,128)(2,1)S(1)} collective-permute-done((bf16[112,896]{1,0:T(8,128)(2,1)S(1)}, bf16[112,896]{1,0:T(8,128)(2,1)S(1)}, u32[]{:S(2)}, u32[]{:S(2)}) %collective-permute-start.18) | collective-permute-done | bytes 200736 | tf_op jit(solution)/shard_map/ppermute | solution.py:256
  59.7 2.1 %collective-permute-done.19.refs_3_ = bf16[112,896]{1,0:T(8,128)(2,1)S(1)} collective-permute-done((bf16[112,896]{1,0:T(8,128)(2,1)S(1)}, bf16[112,896]{1,0:T(8,128)(2,1)S(1)}, u32[]{:S(2)}, u32[]{:S(2)}) %collective-permute-start.19) | collective-permute-done | bytes 200736 | tf_op jit(solution)/shard_map/ppermute | solution.py:256
  62.3 1.6 %collective-permute-start.21 = (f32[8,220]{1,0:T(8,128)S(1)}, f32[8,220]{1,0:T(8,128)S(1)}, u32[]{:S(2)}, u32[]{:S(2)}) collective-permute-start(f32[8,220]{1,0:T(8,128)S(1)} %reshape.3), channel_id=1, source_target_pairs={{0,2},{1,3},{2,0},{3,1},{4,6},{5,7},{6,4},{7,5},{8,10},{9,11},{10,... | collective-permute-start | bytes 21128 | tf_op jit(solution)/shard_map/ppermute | solution.py:239
  64.1 1.9 %collective-permute-done.21 = f32[8,220]{1,0:T(8,128)S(1)} collective-permute-done((f32[8,220]{1,0:T(8,128)S(1)}, f32[8,220]{1,0:T(8,128)S(1)}, u32[]{:S(2)}, u32[]{:S(2)}) %collective-permute-start.21) | collective-permute-done | bytes 7072 | tf_op jit(solution)/shard_map/ppermute | solution.py:239
  (71 shorter events, 9.0 us)
Async XLA Ops:
  0.0 1.9 %copy-start = (bf16[1,1,2,2,220,220]{5,3,4,2,1,0:T(2,128)(2,1)S(1)}, bf16[1,1,2,2,220,220]{5,3,4,2,1,0:T(2,128)(2,1)}, u32[]{:S(2)}) copy-start(bf16[1,1,2,2,220,220]{5,3,4,2,1,0:T(2,128)(2,1)} %param.11) | copy-start | bytes 1161604
  4.2 10.1 %collective-permute-start = (bf16[112,896]{1,0:T(8,128)(2,1)S(1)}, bf16[112,896]{1,0:T(8,128)(2,1)S(1)}, u32[]{:S(2)}, u32[]{:S(2)}) collective-permute-start(bf16[112,896]{1,0:T(8,128)(2,1)S(1)} %get-tuple-element.87.refs_0_), channel_id=1, source_target_pairs={{0,4},{4,0},{8,12},{12,8},{1,5},{5,1},{9,13},{13,9},{2,6},{6,2},{1... | collective-permute-start | bytes 602120 | tf_op jit(solution)/shard_map/ppermute | solution.py:256
  9.7 7.5 %collective-permute-start.2 = (bf16[112,896]{1,0:T(8,128)(2,1)S(1)}, bf16[112,896]{1,0:T(8,128)(2,1)S(1)}, u32[]{:S(2)}, u32[]{:S(2)}) collective-permute-start(bf16[112,896]{1,0:T(8,128)(2,1)S(1)} %get-tuple-element.91.refs_0_), channel_id=1, source_target_pairs={{0,4},{4,0},{8,12},{12,8},{1,5},{5,1},{9,13},{13,9},{2,6},{6,2},{1... | collective-permute-start | bytes 602120 | tf_op jit(solution)/shard_map/ppermute | solution.py:256
  14.3 8.5 %collective-permute-start.1 = (bf16[112,896]{1,0:T(8,128)(2,1)S(1)}, bf16[112,896]{1,0:T(8,128)(2,1)S(1)}, u32[]{:S(2)}, u32[]{:S(2)}) collective-permute-start(bf16[112,896]{1,0:T(8,128)(2,1)S(1)} %get-tuple-element.94.refs_0_), channel_id=1, source_target_pairs={{0,4},{4,0},{8,12},{12,8},{1,5},{5,1},{9,13},{13,9},{2,6},{6,2},{1... | collective-permute-start | bytes 602120 | tf_op jit(solution)/shard_map/ppermute | solution.py:256
  14.8 8.1 %collective-permute-start.4 = (bf16[112,896]{1,0:T(8,128)(2,1)S(1)}, bf16[112,896]{1,0:T(8,128)(2,1)S(1)}, u32[]{:S(2)}, u32[]{:S(2)}) collective-permute-start(bf16[112,896]{1,0:T(8,128)(2,1)S(1)} %add.58), channel_id=1, source_target_pairs={{0,1},{1,0},{4,8},{5,9},{8,4},{9,5},{12,13},{13,12},{2,3},{3,2},{6... | collective-permute-start | bytes 602120 | tf_op jit(solution)/shard_map/ppermute | solution.py:259
  17.3 10.8 %collective-permute-start.6 = (bf16[112,896]{1,0:T(8,128)(2,1)S(1)}, bf16[112,896]{1,0:T(8,128)(2,1)S(1)}, u32[]{:S(2)}, u32[]{:S(2)}) collective-permute-start(bf16[112,896]{1,0:T(8,128)(2,1)S(1)} %add.60), channel_id=1, source_target_pairs={{0,1},{1,0},{4,8},{5,9},{8,4},{9,5},{12,13},{13,12},{2,3},{3,2},{6... | collective-permute-start | bytes 602120 | tf_op jit(solution)/shard_map/ppermute | solution.py:259
  17.8 10.1 %collective-permute-start.7 = (bf16[112,896]{1,0:T(8,128)(2,1)S(1)}, bf16[112,896]{1,0:T(8,128)(2,1)S(1)}, u32[]{:S(2)}, u32[]{:S(2)}) collective-permute-start(bf16[112,896]{1,0:T(8,128)(2,1)S(1)} %get-tuple-element.98.refs_0_), channel_id=1, source_target_pairs={{0,4},{4,0},{8,12},{12,8},{1,5},{5,1},{9,13},{13,9},{2,6},{6,2},{1... | collective-permute-start | bytes 602120 | tf_op jit(solution)/shard_map/ppermute | solution.py:256
  22.8 8.8 %collective-permute-start.3 = (bf16[112,896]{1,0:T(8,128)(2,1)S(1)}, bf16[112,896]{1,0:T(8,128)(2,1)S(1)}, u32[]{:S(2)}, u32[]{:S(2)}) collective-permute-start(bf16[112,896]{1,0:T(8,128)(2,1)S(1)} %add.57), channel_id=1, source_target_pairs={{0,1},{1,0},{4,8},{5,9},{8,4},{9,5},{12,13},{13,12},{2,3},{3,2},{6... | collective-permute-start | bytes 602120 | tf_op jit(solution)/shard_map/ppermute | solution.py:259
  23.0 8.5 %collective-permute-start.5 = (bf16[112,896]{1,0:T(8,128)(2,1)S(1)}, bf16[112,896]{1,0:T(8,128)(2,1)S(1)}, u32[]{:S(2)}, u32[]{:S(2)}) collective-permute-start(bf16[112,896]{1,0:T(8,128)(2,1)S(1)} %add_select_fusion.3), channel_id=1, source_target_pairs={{0,4},{4,0},{8,12},{12,8},{1,5},{5,1},{9,13},{13,9},{2,6},{6,2},{1... | collective-permute-start | bytes 602120 | tf_op jit(solution)/shard_map/ppermute | solution.py:256
  28.0 8.5 %collective-permute-start.8 = (bf16[112,896]{1,0:T(8,128)(2,1)S(1)}, bf16[112,896]{1,0:T(8,128)(2,1)S(1)}, u32[]{:S(2)}, u32[]{:S(2)}) collective-permute-start(bf16[112,896]{1,0:T(8,128)(2,1)S(1)} %add.61), channel_id=1, source_target_pairs={{0,1},{1,0},{4,8},{5,9},{8,4},{9,5},{12,13},{13,12},{2,3},{3,2},{6... | collective-permute-start | bytes 602120 | tf_op jit(solution)/shard_map/ppermute | solution.py:259
  28.1 8.3 %collective-permute-start.9 = (bf16[112,896]{1,0:T(8,128)(2,1)S(1)}, bf16[112,896]{1,0:T(8,128)(2,1)S(1)}, u32[]{:S(2)}, u32[]{:S(2)}) collective-permute-start(bf16[112,896]{1,0:T(8,128)(2,1)S(1)} %add_select_fusion.2), channel_id=1, source_target_pairs={{0,4},{4,0},{8,12},{12,8},{1,5},{5,1},{9,13},{13,9},{2,6},{6,2},{1... | collective-permute-start | bytes 602120 | tf_op jit(solution)/shard_map/ppermute | solution.py:256
  31.5 9.3 %collective-permute-start.10 = (bf16[112,896]{1,0:T(8,128)(2,1)S(1)}, bf16[112,896]{1,0:T(8,128)(2,1)S(1)}, u32[]{:S(2)}, u32[]{:S(2)}) collective-permute-start(bf16[112,896]{1,0:T(8,128)(2,1)S(1)} %add.63), channel_id=1, source_target_pairs={{0,1},{1,0},{4,8},{5,9},{8,4},{9,5},{12,13},{13,12},{2,3},{3,2},{6... | collective-permute-start | bytes 602120 | tf_op jit(solution)/shard_map/ppermute | solution.py:259
  31.7 9.0 %collective-permute-start.11 = (bf16[112,896]{1,0:T(8,128)(2,1)S(1)}, bf16[112,896]{1,0:T(8,128)(2,1)S(1)}, u32[]{:S(2)}, u32[]{:S(2)}) collective-permute-start(bf16[112,896]{1,0:T(8,128)(2,1)S(1)} %add_select_fusion.1), channel_id=1, source_target_pairs={{0,4},{4,0},{8,12},{12,8},{1,5},{5,1},{9,13},{13,9},{2,6},{6,2},{1... | collective-permute-start | bytes 602120 | tf_op jit(solution)/shard_map/ppermute | solution.py:256
  36.5 8.5 %collective-permute-start.13 = (bf16[112,896]{1,0:T(8,128)(2,1)S(1)}, bf16[112,896]{1,0:T(8,128)(2,1)S(1)}, u32[]{:S(2)}, u32[]{:S(2)}) collective-permute-start(bf16[112,896]{1,0:T(8,128)(2,1)S(1)} %add_select_fusion), channel_id=1, source_target_pairs={{0,4},{4,0},{8,12},{12,8},{1,5},{5,1},{9,13},{13,9},{2,6},{6,2},{1... | collective-permute-start | bytes 602120 | tf_op jit(solution)/shard_map/ppermute | solution.py:256
  39.1 6.6 %collective-permute-start.12 = (bf16[112,896]{1,0:T(8,128)(2,1)S(1)}, bf16[112,896]{1,0:T(8,128)(2,1)S(1)}, u32[]{:S(2)}, u32[]{:S(2)}) collective-permute-start(bf16[112,896]{1,0:T(8,128)(2,1)S(1)} %add.65), channel_id=1, source_target_pairs={{0,1},{1,0},{4,8},{5,9},{8,4},{9,5},{12,13},{13,12},{2,3},{3,2},{6... | collective-permute-start | bytes 602120 | tf_op jit(solution)/shard_map/ppermute | solution.py:259
  40.9 9.0 %collective-permute-start.16 = (bf16[112,896]{1,0:T(8,128)(2,1)S(1)}, bf16[112,896]{1,0:T(8,128)(2,1)S(1)}, u32[]{:S(2)}, u32[]{:S(2)}) collective-permute-start(bf16[112,896]{1,0:T(8,128)(2,1)S(1)} %add.68), channel_id=1, source_target_pairs={{0,4},{4,0},{8,12},{12,8},{1,5},{5,1},{9,13},{13,9},{2,6},{6,2},{1... | collective-permute-start | bytes 602120 | tf_op jit(solution)/shard_map/ppermute | solution.py:256
  43.4 6.5 %collective-permute-start.15 = (bf16[112,896]{1,0:T(8,128)(2,1)S(1)}, bf16[112,896]{1,0:T(8,128)(2,1)S(1)}, u32[]{:S(2)}, u32[]{:S(2)}) collective-permute-start(bf16[112,896]{1,0:T(8,128)(2,1)S(1)} %add.67), channel_id=1, source_target_pairs={{0,1},{1,0},{4,8},{5,9},{8,4},{9,5},{12,13},{13,12},{2,3},{3,2},{6... | collective-permute-start | bytes 602120 | tf_op jit(solution)/shard_map/ppermute | solution.py:259
  45.1 6.4 %collective-permute-start.14 = (bf16[112,896]{1,0:T(8,128)(2,1)S(1)}, bf16[112,896]{1,0:T(8,128)(2,1)S(1)}, u32[]{:S(2)}, u32[]{:S(2)}) collective-permute-start(bf16[112,896]{1,0:T(8,128)(2,1)S(1)} %add.69), channel_id=1, source_target_pairs={{0,1},{1,0},{4,8},{5,9},{8,4},{9,5},{12,13},{13,12},{2,3},{3,2},{6... | collective-permute-start | bytes 602120 | tf_op jit(solution)/shard_map/ppermute | solution.py:259
  45.8 9.4 %collective-permute-start.17 = (bf16[112,896]{1,0:T(8,128)(2,1)S(1)}, bf16[112,896]{1,0:T(8,128)(2,1)S(1)}, u32[]{:S(2)}, u32[]{:S(2)}) collective-permute-start(bf16[112,896]{1,0:T(8,128)(2,1)S(1)} %add.70), channel_id=1, source_target_pairs={{0,4},{4,0},{8,12},{12,8},{1,5},{5,1},{9,13},{13,9},{2,6},{6,2},{1... | collective-permute-start | bytes 602120 | tf_op jit(solution)/shard_map/ppermute | solution.py:256
  49.9 9.5 %collective-permute-start.18 = (bf16[112,896]{1,0:T(8,128)(2,1)S(1)}, bf16[112,896]{1,0:T(8,128)(2,1)S(1)}, u32[]{:S(2)}, u32[]{:S(2)}) collective-permute-start(bf16[112,896]{1,0:T(8,128)(2,1)S(1)} %add.71), channel_id=1, source_target_pairs={{0,4},{4,0},{8,12},{12,8},{1,5},{5,1},{9,13},{13,9},{2,6},{6,2},{1... | collective-permute-start | bytes 602120 | tf_op jit(solution)/shard_map/ppermute | solution.py:256
  51.5 10.3 %collective-permute-start.19 = (bf16[112,896]{1,0:T(8,128)(2,1)S(1)}, bf16[112,896]{1,0:T(8,128)(2,1)S(1)}, u32[]{:S(2)}, u32[]{:S(2)}) collective-permute-start(bf16[112,896]{1,0:T(8,128)(2,1)S(1)} %add.72), channel_id=1, source_target_pairs={{0,4},{4,0},{8,12},{12,8},{1,5},{5,1},{9,13},{13,9},{2,6},{6,2},{1... | collective-permute-start | bytes 602120 | tf_op jit(solution)/shard_map/ppermute | solution.py:256
  62.2 1.9 %collective-permute-start.20 = (f32[8,220]{1,0:T(8,128)S(1)}, f32[8,220]{1,0:T(8,128)S(1)}, u32[]{:S(2)}, u32[]{:S(2)}) collective-permute-start(f32[8,220]{1,0:T(8,128)S(1)} %reshape.3), channel_id=1, source_target_pairs={{0,1},{1,0},{2,3},{3,2},{4,5},{5,4},{6,7},{7,6},{8,9},{9,8},{10,11... | collective-permute-start | bytes 21128 | tf_op jit(solution)/shard_map/ppermute | solution.py:239
  62.3 3.7 %collective-permute-start.21 = (f32[8,220]{1,0:T(8,128)S(1)}, f32[8,220]{1,0:T(8,128)S(1)}, u32[]{:S(2)}, u32[]{:S(2)}) collective-permute-start(f32[8,220]{1,0:T(8,128)S(1)} %reshape.3), channel_id=1, source_target_pairs={{0,2},{1,3},{2,0},{3,1},{4,6},{5,7},{6,4},{7,5},{8,10},{9,11},{10,... | collective-permute-start | bytes 21128 | tf_op jit(solution)/shard_map/ppermute | solution.py:239
  63.8 3.1 %collective-permute-start.22 = (f32[8,220]{1,0:T(8,128)S(1)}, f32[8,220]{1,0:T(8,128)S(1)}, u32[]{:S(2)}, u32[]{:S(2)}) collective-permute-start(f32[8,220]{1,0:T(8,128)S(1)} %reshape.3), channel_id=1, source_target_pairs={{0,3},{1,2},{2,1},{3,0},{4,7},{5,6},{6,5},{7,4},{8,11},{9,10},{10,... | collective-permute-start | bytes 21128 | tf_op jit(solution)/shard_map/ppermute | solution.py:239

commit v18 on v17

--- a/solution.py
+++ b/solution.py
@@ -286,8 +286,8 @@
             payload = after(payload, near[step])
         near.append(outer(payload))
         latest = payload
-        if len(own) < min(step + 7, count):
-            encode_more(step + 7, payload)
+        if len(own) < min(step + 5, count):
+            encode_more(step + 5, payload)
             latest = own[-1]
         if step >= 4:
             gradient_of(step - 4, payload)

time: 67.8 us -> 67.3 us (level)
  starting transfers between devices: 32.7 us -> 30.8 us
  waiting for transfers between devices: 18.3 us -> 19.7 us
    ppermute x12, starting transfers between devices: 29.8 us -> 28.4 us  [outer(): return lax.ppermute(value, 'slc', outer_pairs)]
    ppermute x12, waiting for transfers between devices: 15.5 us -> 16.9 us  [outer(): return lax.ppermute(value, 'slc', outer_pairs)]
where the time goes in v18:
time: 67.3 us; the launch traced here: 67 us
  starting transfers between devices  30.8 us (46%)
  waiting for transfers between devices  19.7 us (29%)
  Pallas kernels  13.6 us (20%)
  other arithmetic  1.77 us (3%)
  local copies, waits for them, and re-layouts  0.84 us (1%)
    ppermute x12, starting transfers between devices, outer(): return lax.ppermute(value, 'slc', outer_pairs)  28.4 us
    ppermute x12, waiting for transfers between devices, outer(): return lax.ppermute(value, 'slc', outer_pairs)  16.9 us
    pallas_call x4, Pallas kernels, encode(): pl.pallas_call(functools.partial(encode_kernel, slots, group, rows_of_cla...  9.77 us
    ppermute x3, waiting for transfers between devices, sum_over_replicas(): lax.ppermute(value, axes, [(index, index ^ mask) for index in range(4)])  2.79 us
    pallas_call x8, Pallas kernels, gradient(): pl.pallas_call(functools.partial(gradient_kernel, index, factor, on_line)...  2.13 us
    ppermute x3, starting transfers between devices, sum_over_replicas(): lax.ppermute(value, axes, [(index, index ^ mask) for index in range(4)])  1.93 us
    pallas_call x1, Pallas kernels, body(): pl.pallas_call(functools.partial(fetch_kernel, rows_of_class(0)), in_spec...  1.7 us
  transfers between devices with their start and end apart: 23, of which 10 were waited for; matrix products, arithmetic and copies ran while one was open for 2% of the time, Pallas kernels for 14%

profile of v18, /device:TPU:0, one launch (start us, length us, event | category | flops | bytes accessed | tf_op | source)
XLA Modules:
  0.0 67.0 jit_solution(13269318582800803467)
XLA Ops:
  0.0 1.7 %fetch.1 = (bf16[1,2,220,2,220]{4,3,2,1,0:T(2,128)(2,1)S(1)}, bf16[2,2,220,2,220]{4,3,2,1,0:T(2,128)(2,1)S(1)}, bf16[2,456,220]{2,1,0:T(8,128)(2,1)S(1)}, f32[256,16]{1,0:T(8,128)S(1)}, f32[1,896]{1,0:T(1,128)S(1)}) custom-call(s32[8]{0:T(128)} %refs_0_.1, f32[8,220]{1,0:T(8,128)} %refs_1_.1, bf16[1,8,220,2,220]{4,3,2,1,0:T(2,128)(2,1)} %bitcast.47, ...), custom_call_target="tpu_custom_call" | custom-call | tf_op jit(solution)/shard_map/fetch/pallas_call | solution.py:343
  2.0 2.2 %encode.4 = (bf16[2,224,896]{2,1,0:T(8,128)(2,1)S(1)}, bf16[112,896]{1,0:T(8,128)(2,1)S(1)}, bf16[112,896]{1,0:T(8,128)(2,1)S(1)}, bf16[1,2,220,2,220]{4,3,2,1,0...) custom-call(f32[256,16]{1,0:T(8,128)S(1)} %get-tuple-element.56.refs_0_, bf16[1,2,2,220,220]{4,3,2,1,0:T(8,128)(2,1)S(1)} %bitcast.39, ...), custom_call_target="tpu_custom_call" | custom-call | flops 1022208000 | bytes 6000000 | tf_op jit(solution)/shard_map/encode/pallas_call | solution.py:376
  4.2 4.1 %collective-permute-start = (bf16[112,896]{1,0:T(8,128)(2,1)S(1)}, bf16[112,896]{1,0:T(8,128)(2,1)S(1)}, u32[]{:S(2)}, u32[]{:S(2)}) collective-permute-start(bf16[112,896]{1,0:T(8,128)(2,1)S(1)} %get-tuple-element.87.refs_0_), channel_id=1, source_target_pairs={{0,4},{4,0},{8,12},{12,8},{1,5},{5,1},{9,13},{13,9},{2,6},{6,2},{1... | collective-permute-start | bytes 602120 | tf_op jit(solution)/shard_map/ppermute | solution.py:256
  8.4 2.2 %encode.5 = (bf16[2,224,896]{2,1,0:T(8,128)(2,1)S(1)}, bf16[112,896]{1,0:T(8,128)(2,1)S(1)}, bf16[112,896]{1,0:T(8,128)(2,1)S(1)}, bf16[1,2,220,2,220]{4,3,2,1,0...) custom-call(f32[256,16]{1,0:T(8,128)S(1)} %get-tuple-element.56.refs_0_, bf16[1,2,2,220,220]{4,3,2,1,0:T(8,128)(2,1)S(1)} %bitcast.40, ...), custom_call_target="tpu_custom_call" | custom-call | flops 1022208000 | bytes 6000000 | tf_op jit(solution)/shard_map/encode/pallas_call | solution.py:376
  10.9 3.2 %encode.6 = (bf16[2,224,896]{2,1,0:T(8,128)(2,1)S(1)}, bf16[112,896]{1,0:T(8,128)(2,1)S(1)}, bf16[112,896]{1,0:T(8,128)(2,1)S(1)}, bf16[1,2,220,2,220]{4,3,2,1,0...) custom-call(f32[256,16]{1,0:T(8,128)S(1)} %get-tuple-element.56.refs_0_, bf16[1,2,2,220,220]{4,3,2,1,0:T(8,128)(2,1)S(1)} %bitcast.41, ...), custom_call_target="tpu_custom_call" | custom-call | flops 1022208000 | bytes 6000000 | tf_op jit(solution)/shard_map/encode/pallas_call | solution.py:376
  14.1 2.0 %collective-permute-start.2 = (bf16[112,896]{1,0:T(8,128)(2,1)S(1)}, bf16[112,896]{1,0:T(8,128)(2,1)S(1)}, u32[]{:S(2)}, u32[]{:S(2)}) collective-permute-start(bf16[112,896]{1,0:T(8,128)(2,1)S(1)} %get-tuple-element.94.refs_0_), channel_id=1, source_target_pairs={{0,4},{4,0},{8,12},{12,8},{1,5},{5,1},{9,13},{13,9},{2,6},{6,2},{1... | collective-permute-start | bytes 602120 | tf_op jit(solution)/shard_map/ppermute | solution.py:256
  16.5 2.1 %collective-permute-done.3.refs_1_ = bf16[112,896]{1,0:T(8,128)(2,1)S(1)} collective-permute-done((bf16[112,896]{1,0:T(8,128)(2,1)S(1)}, bf16[112,896]{1,0:T(8,128)(2,1)S(1)}, u32[]{:S(2)}, u32[]{:S(2)}) %collective-permute-start.3) | collective-permute-done | bytes 200736 | tf_op jit(solution)/shard_map/ppermute | solution.py:256
  18.8 2.2 %collective-permute-start.7 = (bf16[112,896]{1,0:T(8,128)(2,1)S(1)}, bf16[112,896]{1,0:T(8,128)(2,1)S(1)}, u32[]{:S(2)}, u32[]{:S(2)}) collective-permute-start(bf16[112,896]{1,0:T(8,128)(2,1)S(1)} %get-tuple-element.98.refs_0_), channel_id=1, source_target_pairs={{0,4},{4,0},{8,12},{12,8},{1,5},{5,1},{9,13},{13,9},{2,6},{6,2},{1... | collective-permute-start | bytes 602120 | tf_op jit(solution)/shard_map/ppermute | solution.py:256
  22.4 2.5 %collective-permute-start.5 = (bf16[112,896]{1,0:T(8,128)(2,1)S(1)}, bf16[112,896]{1,0:T(8,128)(2,1)S(1)}, u32[]{:S(2)}, u32[]{:S(2)}) collective-permute-start(bf16[112,896]{1,0:T(8,128)(2,1)S(1)} %add_select_fusion.3), channel_id=1, source_target_pairs={{0,4},{4,0},{8,12},{12,8},{1,5},{5,1},{9,13},{13,9},{2,6},{6,2},{1... | collective-permute-start | bytes 602120 | tf_op jit(solution)/shard_map/ppermute | solution.py:256
  25.0 2.2 %encode.7 = (bf16[2,224,896]{2,1,0:T(8,128)(2,1)S(1)}, bf16[112,896]{1,0:T(8,128)(2,1)S(1)}, bf16[112,896]{1,0:T(8,128)(2,1)S(1)}) custom-call(f32[256,16]{1,0:T(8,128)S(1)} %get-tuple-element.56.refs_0_, bf16[1,2,2,220,220]{4,3,2,1,0:T(8,128)(2,1)S(1)} %bitcast.38, bf16[2,2,2,220,220]{4,3,2,1,0:T(8,128)(2,1)S(1)} %bitcast.34, ...), custom_call_target="tpu_custom_call" | custom-call | flops 1022208000 | bytes 6000000 | tf_op jit(solution)/shard_map/encode/pallas_call | solution.py:376
  27.4 3.0 %collective-permute-start.9 = (bf16[112,896]{1,0:T(8,128)(2,1)S(1)}, bf16[112,896]{1,0:T(8,128)(2,1)S(1)}, u32[]{:S(2)}, u32[]{:S(2)}) collective-permute-start(bf16[112,896]{1,0:T(8,128)(2,1)S(1)} %add_select_fusion.2), channel_id=1, source_target_pairs={{0,4},{4,0},{8,12},{12,8},{1,5},{5,1},{9,13},{13,9},{2,6},{6,2},{1... | collective-permute-start | bytes 602120 | tf_op jit(solution)/shard_map/ppermute | solution.py:256
  30.7 2.4 %collective-permute-start.11 = (bf16[112,896]{1,0:T(8,128)(2,1)S(1)}, bf16[112,896]{1,0:T(8,128)(2,1)S(1)}, u32[]{:S(2)}, u32[]{:S(2)}) collective-permute-start(bf16[112,896]{1,0:T(8,128)(2,1)S(1)} %add_select_fusion.1), channel_id=1, source_target_pairs={{0,4},{4,0},{8,12},{12,8},{1,5},{5,1},{9,13},{13,9},{2,6},{6,2},{1... | collective-permute-start | bytes 602120 | tf_op jit(solution)/shard_map/ppermute | solution.py:256
  33.0 2.9 %collective-permute-done.9.refs_3_.refs_1_ = bf16[112,896]{1,0:T(8,128)(2,1)S(1)} collective-permute-done((bf16[112,896]{1,0:T(8,128)(2,1)S(1)}, bf16[112,896]{1,0:T(8,128)(2,1)S(1)}, u32[]{:S(2)}, u32[]{:S(2)}) %collective-permute-start.9) | collective-permute-done | bytes 200736 | tf_op jit(solution)/shard_map/ppermute | solution.py:256
  36.0 2.5 %collective-permute-start.13 = (bf16[112,896]{1,0:T(8,128)(2,1)S(1)}, bf16[112,896]{1,0:T(8,128)(2,1)S(1)}, u32[]{:S(2)}, u32[]{:S(2)}) collective-permute-start(bf16[112,896]{1,0:T(8,128)(2,1)S(1)} %add_select_fusion), channel_id=1, source_target_pairs={{0,4},{4,0},{8,12},{12,8},{1,5},{5,1},{9,13},{13,9},{2,6},{6,2},{1... | collective-permute-start | bytes 602120 | tf_op jit(solution)/shard_map/ppermute | solution.py:256
  38.6 1.6 %collective-permute-done.11.refs_3_.refs_1_ = bf16[112,896]{1,0:T(8,128)(2,1)S(1)} collective-permute-done((bf16[112,896]{1,0:T(8,128)(2,1)S(1)}, bf16[112,896]{1,0:T(8,128)(2,1)S(1)}, u32[]{:S(2)}, u32[]{:S(2)}) %collective-permute-start.11) | collective-permute-done | bytes 200736 | tf_op jit(solution)/shard_map/ppermute | solution.py:256
  40.3 2.5 %collective-permute-start.16 = (bf16[112,896]{1,0:T(8,128)(2,1)S(1)}, bf16[112,896]{1,0:T(8,128)(2,1)S(1)}, u32[]{:S(2)}, u32[]{:S(2)}) collective-permute-start(bf16[112,896]{1,0:T(8,128)(2,1)S(1)} %add.68), channel_id=1, source_target_pairs={{0,4},{4,0},{8,12},{12,8},{1,5},{5,1},{9,13},{13,9},{2,6},{6,2},{1... | collective-permute-start | bytes 602120 | tf_op jit(solution)/shard_map/ppermute | solution.py:256
  42.9 1.6 %collective-permute-done.13.refs_3_.refs_1_ = bf16[112,896]{1,0:T(8,128)(2,1)S(1)} collective-permute-done((bf16[112,896]{1,0:T(8,128)(2,1)S(1)}, bf16[112,896]{1,0:T(8,128)(2,1)S(1)}, u32[]{:S(2)}, u32[]{:S(2)}) %collective-permute-start.13) | collective-permute-done | bytes 200736 | tf_op jit(solution)/shard_map/ppermute | solution.py:256
  45.2 2.5 %collective-permute-start.17 = (bf16[112,896]{1,0:T(8,128)(2,1)S(1)}, bf16[112,896]{1,0:T(8,128)(2,1)S(1)}, u32[]{:S(2)}, u32[]{:S(2)}) collective-permute-start(bf16[112,896]{1,0:T(8,128)(2,1)S(1)} %add.70), channel_id=1, source_target_pairs={{0,4},{4,0},{8,12},{12,8},{1,5},{5,1},{9,13},{13,9},{2,6},{6,2},{1... | collective-permute-start | bytes 602120 | tf_op jit(solution)/shard_map/ppermute | solution.py:256
  48.5 2.4 %collective-permute-start.18 = (bf16[112,896]{1,0:T(8,128)(2,1)S(1)}, bf16[112,896]{1,0:T(8,128)(2,1)S(1)}, u32[]{:S(2)}, u32[]{:S(2)}) collective-permute-start(bf16[112,896]{1,0:T(8,128)(2,1)S(1)} %add.71), channel_id=1, source_target_pairs={{0,4},{4,0},{8,12},{12,8},{1,5},{5,1},{9,13},{13,9},{2,6},{6,2},{1... | collective-permute-start | bytes 602120 | tf_op jit(solution)/shard_map/ppermute | solution.py:256
  51.0 2.1 %collective-permute-start.19 = (bf16[112,896]{1,0:T(8,128)(2,1)S(1)}, bf16[112,896]{1,0:T(8,128)(2,1)S(1)}, u32[]{:S(2)}, u32[]{:S(2)}) collective-permute-start(bf16[112,896]{1,0:T(8,128)(2,1)S(1)} %add.72), channel_id=1, source_target_pairs={{0,4},{4,0},{8,12},{12,8},{1,5},{5,1},{9,13},{13,9},{2,6},{6,2},{1... | collective-permute-start | bytes 602120 | tf_op jit(solution)/shard_map/ppermute | solution.py:256
  54.0 4.0 %collective-permute-done.18.refs_3_ = bf16[112,896]{1,0:T(8,128)(2,1)S(1)} collective-permute-done((bf16[112,896]{1,0:T(8,128)(2,1)S(1)}, bf16[112,896]{1,0:T(8,128)(2,1)S(1)}, u32[]{:S(2)}, u32[]{:S(2)}) %collective-permute-start.18) | collective-permute-done | bytes 200736 | tf_op jit(solution)/shard_map/ppermute | solution.py:256
  58.2 3.1 %collective-permute-done.19.refs_3_ = bf16[112,896]{1,0:T(8,128)(2,1)S(1)} collective-permute-done((bf16[112,896]{1,0:T(8,128)(2,1)S(1)}, bf16[112,896]{1,0:T(8,128)(2,1)S(1)}, u32[]{:S(2)}, u32[]{:S(2)}) %collective-permute-start.19) | collective-permute-done | bytes 200736 | tf_op jit(solution)/shard_map/ppermute | solution.py:256
  61.8 1.6 %collective-permute-start.21 = (f32[8,220]{1,0:T(8,128)S(1)}, f32[8,220]{1,0:T(8,128)S(1)}, u32[]{:S(2)}, u32[]{:S(2)}) collective-permute-start(f32[8,220]{1,0:T(8,128)S(1)} %reshape.3), channel_id=1, source_target_pairs={{0,2},{1,3},{2,0},{3,1},{4,6},{5,7},{6,4},{7,5},{8,10},{9,11},{10,... | collective-permute-start | bytes 21128 | tf_op jit(solution)/shard_map/ppermute | solution.py:239
  63.6 1.9 %collective-permute-done.21 = f32[8,220]{1,0:T(8,128)S(1)} collective-permute-done((f32[8,220]{1,0:T(8,128)S(1)}, f32[8,220]{1,0:T(8,128)S(1)}, u32[]{:S(2)}, u32[]{:S(2)}) %collective-permute-start.21) | collective-permute-done | bytes 7072 | tf_op jit(solution)/shard_map/ppermute | solution.py:239
  (71 shorter events, 8.1 us)
Async XLA Ops:
  0.0 1.9 %copy-start = (bf16[1,1,2,2,220,220]{5,3,4,2,1,0:T(2,128)(2,1)S(1)}, bf16[1,1,2,2,220,220]{5,3,4,2,1,0:T(2,128)(2,1)}, u32[]{:S(2)}) copy-start(bf16[1,1,2,2,220,220]{5,3,4,2,1,0:T(2,128)(2,1)} %param.11) | copy-start | bytes 1161604
  4.2 9.9 %collective-permute-start = (bf16[112,896]{1,0:T(8,128)(2,1)S(1)}, bf16[112,896]{1,0:T(8,128)(2,1)S(1)}, u32[]{:S(2)}, u32[]{:S(2)}) collective-permute-start(bf16[112,896]{1,0:T(8,128)(2,1)S(1)} %get-tuple-element.87.refs_0_), channel_id=1, source_target_pairs={{0,4},{4,0},{8,12},{12,8},{1,5},{5,1},{9,13},{13,9},{2,6},{6,2},{1... | collective-permute-start | bytes 602120 | tf_op jit(solution)/shard_map/ppermute | solution.py:256
  10.6 8.0 %collective-permute-start.3 = (bf16[112,896]{1,0:T(8,128)(2,1)S(1)}, bf16[112,896]{1,0:T(8,128)(2,1)S(1)}, u32[]{:S(2)}, u32[]{:S(2)}) collective-permute-start(bf16[112,896]{1,0:T(8,128)(2,1)S(1)} %get-tuple-element.91.refs_0_), channel_id=1, source_target_pairs={{0,4},{4,0},{8,12},{12,8},{1,5},{5,1},{9,13},{13,9},{2,6},{6,2},{1... | collective-permute-start | bytes 602120 | tf_op jit(solution)/shard_map/ppermute | solution.py:256
  14.1 8.1 %collective-permute-start.2 = (bf16[112,896]{1,0:T(8,128)(2,1)S(1)}, bf16[112,896]{1,0:T(8,128)(2,1)S(1)}, u32[]{:S(2)}, u32[]{:S(2)}) collective-permute-start(bf16[112,896]{1,0:T(8,128)(2,1)S(1)} %get-tuple-element.94.refs_0_), channel_id=1, source_target_pairs={{0,4},{4,0},{8,12},{12,8},{1,5},{5,1},{9,13},{13,9},{2,6},{6,2},{1... | collective-permute-start | bytes 602120 | tf_op jit(solution)/shard_map/ppermute | solution.py:256
  16.2 6.2 %collective-permute-start.1 = (bf16[112,896]{1,0:T(8,128)(2,1)S(1)}, bf16[112,896]{1,0:T(8,128)(2,1)S(1)}, u32[]{:S(2)}, u32[]{:S(2)}) collective-permute-start(bf16[112,896]{1,0:T(8,128)(2,1)S(1)} %add.57), channel_id=1, source_target_pairs={{0,1},{1,0},{4,8},{5,9},{8,4},{9,5},{12,13},{13,12},{2,3},{3,2},{6... | collective-permute-start | bytes 602120 | tf_op jit(solution)/shard_map/ppermute | solution.py:259
  18.7 8.7 %collective-permute-start.6 = (bf16[112,896]{1,0:T(8,128)(2,1)S(1)}, bf16[112,896]{1,0:T(8,128)(2,1)S(1)}, u32[]{:S(2)}, u32[]{:S(2)}) collective-permute-start(bf16[112,896]{1,0:T(8,128)(2,1)S(1)} %add.60), channel_id=1, source_target_pairs={{0,1},{1,0},{4,8},{5,9},{8,4},{9,5},{12,13},{13,12},{2,3},{3,2},{6... | collective-permute-start | bytes 602120 | tf_op jit(solution)/shard_map/ppermute | solution.py:259
  18.8 8.5 %collective-permute-start.7 = (bf16[112,896]{1,0:T(8,128)(2,1)S(1)}, bf16[112,896]{1,0:T(8,128)(2,1)S(1)}, u32[]{:S(2)}, u32[]{:S(2)}) collective-permute-start(bf16[112,896]{1,0:T(8,128)(2,1)S(1)} %get-tuple-element.98.refs_0_), channel_id=1, source_target_pairs={{0,4},{4,0},{8,12},{12,8},{1,5},{5,1},{9,13},{13,9},{2,6},{6,2},{1... | collective-permute-start | bytes 602120 | tf_op jit(solution)/shard_map/ppermute | solution.py:256
  22.3 8.3 %collective-permute-start.4 = (bf16[112,896]{1,0:T(8,128)(2,1)S(1)}, bf16[112,896]{1,0:T(8,128)(2,1)S(1)}, u32[]{:S(2)}, u32[]{:S(2)}) collective-permute-start(bf16[112,896]{1,0:T(8,128)(2,1)S(1)} %add.58), channel_id=1, source_target_pairs={{0,1},{1,0},{4,8},{5,9},{8,4},{9,5},{12,13},{13,12},{2,3},{3,2},{6... | collective-permute-start | bytes 602120 | tf_op jit(solution)/shard_map/ppermute | solution.py:259
  22.4 8.0 %collective-permute-start.5 = (bf16[112,896]{1,0:T(8,128)(2,1)S(1)}, bf16[112,896]{1,0:T(8,128)(2,1)S(1)}, u32[]{:S(2)}, u32[]{:S(2)}) collective-permute-start(bf16[112,896]{1,0:T(8,128)(2,1)S(1)} %add_select_fusion.3), channel_id=1, source_target_pairs={{0,4},{4,0},{8,12},{12,8},{1,5},{5,1},{9,13},{13,9},{2,6},{6,2},{1... | collective-permute-start | bytes 602120 | tf_op jit(solution)/shard_map/ppermute | solution.py:256
  27.3 8.7 %collective-permute-start.8 = (bf16[112,896]{1,0:T(8,128)(2,1)S(1)}, bf16[112,896]{1,0:T(8,128)(2,1)S(1)}, u32[]{:S(2)}, u32[]{:S(2)}) collective-permute-start(bf16[112,896]{1,0:T(8,128)(2,1)S(1)} %add.61), channel_id=1, source_target_pairs={{0,1},{1,0},{4,8},{5,9},{8,4},{9,5},{12,13},{13,12},{2,3},{3,2},{6... | collective-permute-start | bytes 602120 | tf_op jit(solution)/shard_map/ppermute | solution.py:259
  27.4 8.5 %collective-permute-start.9 = (bf16[112,896]{1,0:T(8,128)(2,1)S(1)}, bf16[112,896]{1,0:T(8,128)(2,1)S(1)}, u32[]{:S(2)}, u32[]{:S(2)}) collective-permute-start(bf16[112,896]{1,0:T(8,128)(2,1)S(1)} %add_select_fusion.2), channel_id=1, source_target_pairs={{0,4},{4,0},{8,12},{12,8},{1,5},{5,1},{9,13},{13,9},{2,6},{6,2},{1... | collective-permute-start | bytes 602120 | tf_op jit(solution)/shard_map/ppermute | solution.py:256
  30.5 9.7 %collective-permute-start.10 = (bf16[112,896]{1,0:T(8,128)(2,1)S(1)}, bf16[112,896]{1,0:T(8,128)(2,1)S(1)}, u32[]{:S(2)}, u32[]{:S(2)}) collective-permute-start(bf16[112,896]{1,0:T(8,128)(2,1)S(1)} %add.63), channel_id=1, source_target_pairs={{0,1},{1,0},{4,8},{5,9},{8,4},{9,5},{12,13},{13,12},{2,3},{3,2},{6... | collective-permute-start | bytes 602120 | tf_op jit(solution)/shard_map/ppermute | solution.py:259
  30.7 9.5 %collective-permute-start.11 = (bf16[112,896]{1,0:T(8,128)(2,1)S(1)}, bf16[112,896]{1,0:T(8,128)(2,1)S(1)}, u32[]{:S(2)}, u32[]{:S(2)}) collective-permute-start(bf16[112,896]{1,0:T(8,128)(2,1)S(1)} %add_select_fusion.1), channel_id=1, source_target_pairs={{0,4},{4,0},{8,12},{12,8},{1,5},{5,1},{9,13},{13,9},{2,6},{6,2},{1... | collective-permute-start | bytes 602120 | tf_op jit(solution)/shard_map/ppermute | solution.py:256
  36.0 8.5 %collective-permute-start.13 = (bf16[112,896]{1,0:T(8,128)(2,1)S(1)}, bf16[112,896]{1,0:T(8,128)(2,1)S(1)}, u32[]{:S(2)}, u32[]{:S(2)}) collective-permute-start(bf16[112,896]{1,0:T(8,128)(2,1)S(1)} %add_select_fusion), channel_id=1, source_target_pairs={{0,4},{4,0},{8,12},{12,8},{1,5},{5,1},{9,13},{13,9},{2,6},{6,2},{1... | collective-permute-start | bytes 602120 | tf_op jit(solution)/shard_map/ppermute | solution.py:256
  38.6 6.6 %collective-permute-start.12 = (bf16[112,896]{1,0:T(8,128)(2,1)S(1)}, bf16[112,896]{1,0:T(8,128)(2,1)S(1)}, u32[]{:S(2)}, u32[]{:S(2)}) collective-permute-start(bf16[112,896]{1,0:T(8,128)(2,1)S(1)} %add.65), channel_id=1, source_target_pairs={{0,1},{1,0},{4,8},{5,9},{8,4},{9,5},{12,13},{13,12},{2,3},{3,2},{6... | collective-permute-start | bytes 602120 | tf_op jit(solution)/shard_map/ppermute | solution.py:259
  40.3 8.1 %collective-permute-start.16 = (bf16[112,896]{1,0:T(8,128)(2,1)S(1)}, bf16[112,896]{1,0:T(8,128)(2,1)S(1)}, u32[]{:S(2)}, u32[]{:S(2)}) collective-permute-start(bf16[112,896]{1,0:T(8,128)(2,1)S(1)} %add.68), channel_id=1, source_target_pairs={{0,4},{4,0},{8,12},{12,8},{1,5},{5,1},{9,13},{13,9},{2,6},{6,2},{1... | collective-permute-start | bytes 602120 | tf_op jit(solution)/shard_map/ppermute | solution.py:256
  42.9 5.5 %collective-permute-start.15 = (bf16[112,896]{1,0:T(8,128)(2,1)S(1)}, bf16[112,896]{1,0:T(8,128)(2,1)S(1)}, u32[]{:S(2)}, u32[]{:S(2)}) collective-permute-start(bf16[112,896]{1,0:T(8,128)(2,1)S(1)} %add.67), channel_id=1, source_target_pairs={{0,1},{1,0},{4,8},{5,9},{8,4},{9,5},{12,13},{13,12},{2,3},{3,2},{6... | collective-permute-start | bytes 602120 | tf_op jit(solution)/shard_map/ppermute | solution.py:259
  44.6 6.4 %collective-permute-start.14 = (bf16[112,896]{1,0:T(8,128)(2,1)S(1)}, bf16[112,896]{1,0:T(8,128)(2,1)S(1)}, u32[]{:S(2)}, u32[]{:S(2)}) collective-permute-start(bf16[112,896]{1,0:T(8,128)(2,1)S(1)} %add.69), channel_id=1, source_target_pairs={{0,1},{1,0},{4,8},{5,9},{8,4},{9,5},{12,13},{13,12},{2,3},{3,2},{6... | collective-permute-start | bytes 602120 | tf_op jit(solution)/shard_map/ppermute | solution.py:259
  45.2 8.4 %collective-permute-start.17 = (bf16[112,896]{1,0:T(8,128)(2,1)S(1)}, bf16[112,896]{1,0:T(8,128)(2,1)S(1)}, u32[]{:S(2)}, u32[]{:S(2)}) collective-permute-start(bf16[112,896]{1,0:T(8,128)(2,1)S(1)} %add.70), channel_id=1, source_target_pairs={{0,4},{4,0},{8,12},{12,8},{1,5},{5,1},{9,13},{13,9},{2,6},{6,2},{1... | collective-permute-start | bytes 602120 | tf_op jit(solution)/shard_map/ppermute | solution.py:256
  48.5 9.4 %collective-permute-start.18 = (bf16[112,896]{1,0:T(8,128)(2,1)S(1)}, bf16[112,896]{1,0:T(8,128)(2,1)S(1)}, u32[]{:S(2)}, u32[]{:S(2)}) collective-permute-start(bf16[112,896]{1,0:T(8,128)(2,1)S(1)} %add.71), channel_id=1, source_target_pairs={{0,4},{4,0},{8,12},{12,8},{1,5},{5,1},{9,13},{13,9},{2,6},{6,2},{1... | collective-permute-start | bytes 602120 | tf_op jit(solution)/shard_map/ppermute | solution.py:256
  51.0 10.3 %collective-permute-start.19 = (bf16[112,896]{1,0:T(8,128)(2,1)S(1)}, bf16[112,896]{1,0:T(8,128)(2,1)S(1)}, u32[]{:S(2)}, u32[]{:S(2)}) collective-permute-start(bf16[112,896]{1,0:T(8,128)(2,1)S(1)} %add.72), channel_id=1, source_target_pairs={{0,4},{4,0},{8,12},{12,8},{1,5},{5,1},{9,13},{13,9},{2,6},{6,2},{1... | collective-permute-start | bytes 602120 | tf_op jit(solution)/shard_map/ppermute | solution.py:256
  61.7 1.9 %collective-permute-start.20 = (f32[8,220]{1,0:T(8,128)S(1)}, f32[8,220]{1,0:T(8,128)S(1)}, u32[]{:S(2)}, u32[]{:S(2)}) collective-permute-start(f32[8,220]{1,0:T(8,128)S(1)} %reshape.3), channel_id=1, source_target_pairs={{0,1},{1,0},{2,3},{3,2},{4,5},{5,4},{6,7},{7,6},{8,9},{9,8},{10,11... | collective-permute-start | bytes 21128 | tf_op jit(solution)/shard_map/ppermute | solution.py:239
  61.8 3.7 %collective-permute-start.21 = (f32[8,220]{1,0:T(8,128)S(1)}, f32[8,220]{1,0:T(8,128)S(1)}, u32[]{:S(2)}, u32[]{:S(2)}) collective-permute-start(f32[8,220]{1,0:T(8,128)S(1)} %reshape.3), channel_id=1, source_target_pairs={{0,2},{1,3},{2,0},{3,1},{4,6},{5,7},{6,4},{7,5},{8,10},{9,11},{10,... | collective-permute-start | bytes 21128 | tf_op jit(solution)/shard_map/ppermute | solution.py:239
  63.3 3.1 %collective-permute-start.22 = (f32[8,220]{1,0:T(8,128)S(1)}, f32[8,220]{1,0:T(8,128)S(1)}, u32[]{:S(2)}, u32[]{:S(2)}) collective-permute-start(f32[8,220]{1,0:T(8,128)S(1)} %reshape.3), channel_id=1, source_target_pairs={{0,3},{1,2},{2,1},{3,0},{4,7},{5,6},{6,5},{7,4},{8,11},{9,10},{10,... | collective-permute-start | bytes 21128 | tf_op jit(solution)/shard_map/ppermute | solution.py:239

commit v19 on v17

--- a/solution.py
+++ b/solution.py
@@ -268,7 +268,7 @@
             encoded += 1
 
     def gradient_of(piece, *earlier):
-        terms = (own[piece], near[piece], across[piece], near[piece + 4])
+        terms = (own[piece], near[piece], across[piece], near[piece + 3])
         gradients.append(gradient((after(terms[0], *earlier), *terms[1:]), piece))
 
     encode_more(3)
@@ -279,8 +279,8 @@
         half = own[step] + after(near[step], latest)
         across.append(inner(half))
         payload = own[step + 2] if step + 2 < count else None
-        if step >= 2:
-            others = own[step - 2] + after(across[step - 2], half)
+        if step >= 1:
+            others = own[step - 1] + after(across[step - 1], half)
             payload = others if payload is None else jnp.where(ends > 0, payload, others)
         else:
             payload = after(payload, near[step])
@@ -289,13 +289,12 @@
         if len(own) < min(step + 7, count):
             encode_more(step + 7, payload)
             latest = own[-1]
-        if step >= 4:
-            gradient_of(step - 4, payload)
-    for piece in range(count - 2, count):
-        latest = own[piece] + after(across[piece], latest, near[count])
-        near.append(outer(latest))
-    for piece in range(count - 4, count):
-        gradient_of(piece, latest)
+        if step >= 3:
+            gradient_of(step - 3, payload)
+    last = own[count - 1] + after(across[count - 1], latest, near[count])
+    near.append(outer(last))
+    for piece in range(count - 3, count):
+        gradient_of(piece, last)
     return gradients
 
 

time: 67.8 us -> 67.5 us (level)
  waiting for transfers between devices: 18.3 us -> 13.9 us
  starting transfers between devices: 32.7 us -> 36.7 us
    ppermute x12 -> x11, waiting for transfers between devices: 15.5 us -> 11.1 us  [outer(): return lax.ppermute(value, 'slc', outer_pairs)]
    ppermute x12 -> x11, starting transfers between devices: 29.8 us -> 34.2 us  [outer(): return lax.ppermute(value, 'slc', outer_pairs)]
  transfers between devices with their start and end apart: 23 -> 22, of which waited for: 10 -> 9; matrix products, arithmetic and copies ran while one was open for 2% -> 2% of each run, Pallas kernels for 14% -> 13%
where the time goes in v19:
time: 67.5 us; the launch traced here: 67.1 us
  starting transfers between devices  36.7 us (54%)
  waiting for transfers between devices  13.9 us (21%)
  Pallas kernels  13.6 us (20%)
  other arithmetic  1.7 us (3%)
  local copies, waits for them, and re-layouts  0.84 us (1%)
    ppermute x11, starting transfers between devices, outer(): return lax.ppermute(value, 'slc', outer_pairs)  34.2 us
    ppermute x11, waiting for transfers between devices, outer(): return lax.ppermute(value, 'slc', outer_pairs)  11.1 us
    pallas_call x4, Pallas kernels, encode(): pl.pallas_call(functools.partial(encode_kernel, slots, group, rows_of_cla...  9.76 us
    ppermute x3, waiting for transfers between devices, sum_over_replicas(): lax.ppermute(value, axes, [(index, index ^ mask) for index in range(4)])  2.75 us
    pallas_call x8, Pallas kernels, gradient(): pl.pallas_call(functools.partial(gradient_kernel, index, factor, on_line)...  2.13 us
    ppermute x3, starting transfers between devices, sum_over_replicas(): lax.ppermute(value, axes, [(index, index ^ mask) for index in range(4)])  1.93 us
    pallas_call x1, Pallas kernels, body(): pl.pallas_call(functools.partial(fetch_kernel, rows_of_class(0)), in_spec...  1.7 us
  transfers between devices with their start and end apart: 22, of which 9 were waited for; matrix products, arithmetic and copies ran while one was open for 2% of the time, Pallas kernels for 13%

profile of v19, /device:TPU:0, one launch (start us, length us, event | category | flops | bytes accessed | tf_op | source)
XLA Modules:
  0.0 67.1 jit_solution(18303046389932290873)
XLA Ops:
  0.0 1.7 %fetch.1 = (bf16[1,2,220,2,220]{4,3,2,1,0:T(2,128)(2,1)S(1)}, bf16[2,2,220,2,220]{4,3,2,1,0:T(2,128)(2,1)S(1)}, bf16[2,456,220]{2,1,0:T(8,128)(2,1)S(1)}, f32[256,16]{1,0:T(8,128)S(1)}, f32[1,896]{1,0:T(1,128)S(1)}) custom-call(s32[8]{0:T(128)} %refs_0_.1, f32[8,220]{1,0:T(8,128)} %refs_1_.1, bf16[1,8,220,2,220]{4,3,2,1,0:T(2,128)(2,1)} %bitcast.47, ...), custom_call_target="tpu_custom_call" | custom-call | tf_op jit(solution)/shard_map/fetch/pallas_call | solution.py:342
  2.0 3.2 %encode.4 = (bf16[2,224,896]{2,1,0:T(8,128)(2,1)S(1)}, bf16[112,896]{1,0:T(8,128)(2,1)S(1)}, bf16[112,896]{1,0:T(8,128)(2,1)S(1)}, bf16[1,2,220,2,220]{4,3,2,1,0...) custom-call(f32[256,16]{1,0:T(8,128)S(1)} %get-tuple-element.55.refs_0_, bf16[1,2,2,220,220]{4,3,2,1,0:T(8,128)(2,1)S(1)} %bitcast.39, ...), custom_call_target="tpu_custom_call" | custom-call | flops 1022208000 | bytes 6000000 | tf_op jit(solution)/shard_map/encode/pallas_call | solution.py:375
  5.2 2.1 %collective-permute-start = (bf16[112,896]{1,0:T(8,128)(2,1)S(1)}, bf16[112,896]{1,0:T(8,128)(2,1)S(1)}, u32[]{:S(2)}, u32[]{:S(2)}) collective-permute-start(bf16[112,896]{1,0:T(8,128)(2,1)S(1)} %get-tuple-element.83.refs_0_), channel_id=1, source_target_pairs={{0,4},{4,0},{8,12},{12,8},{1,5},{5,1},{9,13},{13,9},{2,6},{6,2},{1... | collective-permute-start | bytes 602120 | tf_op jit(solution)/shard_map/ppermute | solution.py:256
  7.5 2.2 %encode.5 = (bf16[2,224,896]{2,1,0:T(8,128)(2,1)S(1)}, bf16[112,896]{1,0:T(8,128)(2,1)S(1)}, bf16[112,896]{1,0:T(8,128)(2,1)S(1)}, bf16[1,2,220,2,220]{4,3,2,1,0...) custom-call(f32[256,16]{1,0:T(8,128)S(1)} %get-tuple-element.55.refs_0_, bf16[1,2,2,220,220]{4,3,2,1,0:T(8,128)(2,1)S(1)} %bitcast.40, ...), custom_call_target="tpu_custom_call" | custom-call | flops 1022208000 | bytes 6000000 | tf_op jit(solution)/shard_map/encode/pallas_call | solution.py:375
  9.7 1.0 %collective-permute-start.3 = (bf16[112,896]{1,0:T(8,128)(2,1)S(1)}, bf16[112,896]{1,0:T(8,128)(2,1)S(1)}, u32[]{:S(2)}, u32[]{:S(2)}) collective-permute-start(bf16[112,896]{1,0:T(8,128)(2,1)S(1)} %get-tuple-element.88.refs_0_), channel_id=1, source_target_pairs={{0,4},{4,0},{8,12},{12,8},{1,5},{5,1},{9,13},{13,9},{2,6},{6,2},{1... | collective-permute-start | bytes 602120 | tf_op jit(solution)/shard_map/ppermute | solution.py:256
  10.9 2.2 %encode.6 = (bf16[2,224,896]{2,1,0:T(8,128)(2,1)S(1)}, bf16[112,896]{1,0:T(8,128)(2,1)S(1)}, bf16[112,896]{1,0:T(8,128)(2,1)S(1)}, bf16[1,2,220,2,220]{4,3,2,1,0...) custom-call(f32[256,16]{1,0:T(8,128)S(1)} %get-tuple-element.55.refs_0_, bf16[1,2,2,220,220]{4,3,2,1,0:T(8,128)(2,1)S(1)} %bitcast.41, ...), custom_call_target="tpu_custom_call" | custom-call | flops 1022208000 | bytes 6000000 | tf_op jit(solution)/shard_map/encode/pallas_call | solution.py:375
  13.5 2.8 %collective-permute-start.1 = (bf16[112,896]{1,0:T(8,128)(2,1)S(1)}, bf16[112,896]{1,0:T(8,128)(2,1)S(1)}, u32[]{:S(2)}, u32[]{:S(2)}) collective-permute-start(bf16[112,896]{1,0:T(8,128)(2,1)S(1)} %get-tuple-element.91.refs_0_), channel_id=1, source_target_pairs={{0,4},{4,0},{8,12},{12,8},{1,5},{5,1},{9,13},{13,9},{2,6},{6,2},{1... | collective-permute-start | bytes 602120 | tf_op jit(solution)/shard_map/ppermute | solution.py:256
  16.3 2.2 %encode.7 = (bf16[2,224,896]{2,1,0:T(8,128)(2,1)S(1)}, bf16[112,896]{1,0:T(8,128)(2,1)S(1)}, bf16[112,896]{1,0:T(8,128)(2,1)S(1)}) custom-call(f32[256,16]{1,0:T(8,128)S(1)} %get-tuple-element.55.refs_0_, bf16[1,2,2,220,220]{4,3,2,1,0:T(8,128)(2,1)S(1)} %bitcast.38, bf16[2,2,2,220,220]{4,3,2,1,0:T(8,128)(2,1)S(1)} %bitcast.34, ...), custom_call_target="tpu_custom_call" | custom-call | flops 1022208000 | bytes 6000000 | tf_op jit(solution)/shard_map/encode/pallas_call | solution.py:375
  18.7 3.4 %collective-permute-start.5 = (bf16[112,896]{1,0:T(8,128)(2,1)S(1)}, bf16[112,896]{1,0:T(8,128)(2,1)S(1)}, u32[]{:S(2)}, u32[]{:S(2)}) collective-permute-start(bf16[112,896]{1,0:T(8,128)(2,1)S(1)} %add_select_fusion.4), channel_id=1, source_target_pairs={{0,4},{4,0},{8,12},{12,8},{1,5},{5,1},{9,13},{13,9},{2,6},{6,2},{1... | collective-permute-start | bytes 602120 | tf_op jit(solution)/shard_map/ppermute | solution.py:256
  22.3 5.6 %collective-permute-start.8 = (bf16[112,896]{1,0:T(8,128)(2,1)S(1)}, bf16[112,896]{1,0:T(8,128)(2,1)S(1)}, u32[]{:S(2)}, u32[]{:S(2)}) collective-permute-start(bf16[112,896]{1,0:T(8,128)(2,1)S(1)} %add_select_fusion.3), channel_id=1, source_target_pairs={{0,4},{4,0},{8,12},{12,8},{1,5},{5,1},{9,13},{13,9},{2,6},{6,2},{1... | collective-permute-start | bytes 602120 | tf_op jit(solution)/shard_map/ppermute | solution.py:256
  28.1 4.1 %collective-permute-start.10 = (bf16[112,896]{1,0:T(8,128)(2,1)S(1)}, bf16[112,896]{1,0:T(8,128)(2,1)S(1)}, u32[]{:S(2)}, u32[]{:S(2)}) collective-permute-start(bf16[112,896]{1,0:T(8,128)(2,1)S(1)} %add_select_fusion.2), channel_id=1, source_target_pairs={{0,4},{4,0},{8,12},{12,8},{1,5},{5,1},{9,13},{13,9},{2,6},{6,2},{1... | collective-permute-start | bytes 602120 | tf_op jit(solution)/shard_map/ppermute | solution.py:256
  32.6 4.3 %collective-permute-start.12 = (bf16[112,896]{1,0:T(8,128)(2,1)S(1)}, bf16[112,896]{1,0:T(8,128)(2,1)S(1)}, u32[]{:S(2)}, u32[]{:S(2)}) collective-permute-start(bf16[112,896]{1,0:T(8,128)(2,1)S(1)} %add_select_fusion.1), channel_id=1, source_target_pairs={{0,4},{4,0},{8,12},{12,8},{1,5},{5,1},{9,13},{13,9},{2,6},{6,2},{1... | collective-permute-start | bytes 602120 | tf_op jit(solution)/shard_map/ppermute | solution.py:256
  37.4 3.7 %collective-permute-start.14 = (bf16[112,896]{1,0:T(8,128)(2,1)S(1)}, bf16[112,896]{1,0:T(8,128)(2,1)S(1)}, u32[]{:S(2)}, u32[]{:S(2)}) collective-permute-start(bf16[112,896]{1,0:T(8,128)(2,1)S(1)} %add_select_fusion), channel_id=1, source_target_pairs={{0,4},{4,0},{8,12},{12,8},{1,5},{5,1},{9,13},{13,9},{2,6},{6,2},{1... | collective-permute-start | bytes 602120 | tf_op jit(solution)/shard_map/ppermute | solution.py:256
  41.9 3.4 %collective-permute-done.14.refs_3_.refs_1_ = bf16[112,896]{1,0:T(8,128)(2,1)S(1)} collective-permute-done((bf16[112,896]{1,0:T(8,128)(2,1)S(1)}, bf16[112,896]{1,0:T(8,128)(2,1)S(1)}, u32[]{:S(2)}, u32[]{:S(2)}) %collective-permute-start.14) | collective-permute-done | bytes 200736 | tf_op jit(solution)/shard_map/ppermute | solution.py:256
  45.4 3.9 %collective-permute-start.16 = (bf16[112,896]{1,0:T(8,128)(2,1)S(1)}, bf16[112,896]{1,0:T(8,128)(2,1)S(1)}, u32[]{:S(2)}, u32[]{:S(2)}) collective-permute-start(bf16[112,896]{1,0:T(8,128)(2,1)S(1)} %add.69), channel_id=1, source_target_pairs={{0,4},{4,0},{8,12},{12,8},{1,5},{5,1},{9,13},{13,9},{2,6},{6,2},{1... | collective-permute-start | bytes 602120 | tf_op jit(solution)/shard_map/ppermute | solution.py:256
  50.6 1.7 %collective-permute-start.17 = (bf16[112,896]{1,0:T(8,128)(2,1)S(1)}, bf16[112,896]{1,0:T(8,128)(2,1)S(1)}, u32[]{:S(2)}, u32[]{:S(2)}) collective-permute-start(bf16[112,896]{1,0:T(8,128)(2,1)S(1)} %add.71), channel_id=1, source_target_pairs={{0,4},{4,0},{8,12},{12,8},{1,5},{5,1},{9,13},{13,9},{2,6},{6,2},{1... | collective-permute-start | bytes 602120 | tf_op jit(solution)/shard_map/ppermute | solution.py:256
  52.3 3.0 %collective-permute-done.16.refs_3_ = bf16[112,896]{1,0:T(8,128)(2,1)S(1)} collective-permute-done((bf16[112,896]{1,0:T(8,128)(2,1)S(1)}, bf16[112,896]{1,0:T(8,128)(2,1)S(1)}, u32[]{:S(2)}, u32[]{:S(2)}) %collective-permute-start.16) | collective-permute-done | bytes 200736 | tf_op jit(solution)/shard_map/ppermute | solution.py:256
  55.3 1.6 %collective-permute-start.18 = (bf16[112,896]{1,0:T(8,128)(2,1)S(1)}, bf16[112,896]{1,0:T(8,128)(2,1)S(1)}, u32[]{:S(2)}, u32[]{:S(2)}) collective-permute-start(bf16[112,896]{1,0:T(8,128)(2,1)S(1)} %add.72), channel_id=1, source_target_pairs={{0,4},{4,0},{8,12},{12,8},{1,5},{5,1},{9,13},{13,9},{2,6},{6,2},{1... | collective-permute-start | bytes 602120 | tf_op jit(solution)/shard_map/ppermute | solution.py:256
  57.6 1.7 %collective-permute-done.17.refs_3_ = bf16[112,896]{1,0:T(8,128)(2,1)S(1)} collective-permute-done((bf16[112,896]{1,0:T(8,128)(2,1)S(1)}, bf16[112,896]{1,0:T(8,128)(2,1)S(1)}, u32[]{:S(2)}, u32[]{:S(2)}) %collective-permute-start.17) | collective-permute-done | bytes 200736 | tf_op jit(solution)/shard_map/ppermute | solution.py:256
  59.5 1.9 %collective-permute-done.18.refs_3_ = bf16[112,896]{1,0:T(8,128)(2,1)S(1)} collective-permute-done((bf16[112,896]{1,0:T(8,128)(2,1)S(1)}, bf16[112,896]{1,0:T(8,128)(2,1)S(1)}, u32[]{:S(2)}, u32[]{:S(2)}) %collective-permute-start.18) | collective-permute-done | bytes 200736 | tf_op jit(solution)/shard_map/ppermute | solution.py:256
  61.9 1.5 %collective-permute-start.20 = (f32[8,220]{1,0:T(8,128)S(1)}, f32[8,220]{1,0:T(8,128)S(1)}, u32[]{:S(2)}, u32[]{:S(2)}) collective-permute-start(f32[8,220]{1,0:T(8,128)S(1)} %reshape.3), channel_id=1, source_target_pairs={{0,2},{1,3},{2,0},{3,1},{4,6},{5,7},{6,4},{7,5},{8,10},{9,11},{10,... | collective-permute-start | bytes 21128 | tf_op jit(solution)/shard_map/ppermute | solution.py:239
  63.8 1.9 %collective-permute-done.20 = f32[8,220]{1,0:T(8,128)S(1)} collective-permute-done((f32[8,220]{1,0:T(8,128)S(1)}, f32[8,220]{1,0:T(8,128)S(1)}, u32[]{:S(2)}, u32[]{:S(2)}) %collective-permute-start.20) | collective-permute-done | bytes 7072 | tf_op jit(solution)/shard_map/ppermute | solution.py:239
  65.6 0.9 %collective-permute-done.21 = f32[8,220]{1,0:T(8,128)S(1)} collective-permute-done((f32[8,220]{1,0:T(8,128)S(1)}, f32[8,220]{1,0:T(8,128)S(1)}, u32[]{:S(2)}, u32[]{:S(2)}) %collective-permute-start.21) | collective-permute-done | bytes 7072 | tf_op jit(solution)/shard_map/ppermute | solution.py:239
  66.5 0.6 add_add_fusion
  (69 shorter events, 6.2 us)
Async XLA Ops:
  0.0 1.9 %copy-start = (bf16[1,1,2,2,220,220]{5,3,4,2,1,0:T(2,128)(2,1)S(1)}, bf16[1,1,2,2,220,220]{5,3,4,2,1,0:T(2,128)(2,1)}, u32[]{:S(2)}) copy-start(bf16[1,1,2,2,220,220]{5,3,4,2,1,0:T(2,128)(2,1)} %param.11) | copy-start | bytes 1161604
  5.2 8.2 %collective-permute-start = (bf16[112,896]{1,0:T(8,128)(2,1)S(1)}, bf16[112,896]{1,0:T(8,128)(2,1)S(1)}, u32[]{:S(2)}, u32[]{:S(2)}) collective-permute-start(bf16[112,896]{1,0:T(8,128)(2,1)S(1)} %get-tuple-element.83.refs_0_), channel_id=1, source_target_pairs={{0,4},{4,0},{8,12},{12,8},{1,5},{5,1},{9,13},{13,9},{2,6},{6,2},{1... | collective-permute-start | bytes 602120 | tf_op jit(solution)/shard_map/ppermute | solution.py:256
  9.7 8.8 %collective-permute-start.3 = (bf16[112,896]{1,0:T(8,128)(2,1)S(1)}, bf16[112,896]{1,0:T(8,128)(2,1)S(1)}, u32[]{:S(2)}, u32[]{:S(2)}) collective-permute-start(bf16[112,896]{1,0:T(8,128)(2,1)S(1)} %get-tuple-element.88.refs_0_), channel_id=1, source_target_pairs={{0,4},{4,0},{8,12},{12,8},{1,5},{5,1},{9,13},{13,9},{2,6},{6,2},{1... | collective-permute-start | bytes 602120 | tf_op jit(solution)/shard_map/ppermute | solution.py:256
  13.4 5.3 %collective-permute-start.2 = (bf16[112,896]{1,0:T(8,128)(2,1)S(1)}, bf16[112,896]{1,0:T(8,128)(2,1)S(1)}, u32[]{:S(2)}, u32[]{:S(2)}) collective-permute-start(bf16[112,896]{1,0:T(8,128)(2,1)S(1)} %add.57), channel_id=1, source_target_pairs={{0,1},{1,0},{4,8},{5,9},{8,4},{9,5},{12,13},{13,12},{2,3},{3,2},{6... | collective-permute-start | bytes 602120 | tf_op jit(solution)/shard_map/ppermute | solution.py:259
  13.5 8.7 %collective-permute-start.1 = (bf16[112,896]{1,0:T(8,128)(2,1)S(1)}, bf16[112,896]{1,0:T(8,128)(2,1)S(1)}, u32[]{:S(2)}, u32[]{:S(2)}) collective-permute-start(bf16[112,896]{1,0:T(8,128)(2,1)S(1)} %get-tuple-element.91.refs_0_), channel_id=1, source_target_pairs={{0,4},{4,0},{8,12},{12,8},{1,5},{5,1},{9,13},{13,9},{2,6},{6,2},{1... | collective-permute-start | bytes 602120 | tf_op jit(solution)/shard_map/ppermute | solution.py:256
  18.6 3.7 %collective-permute-start.6 = (bf16[112,896]{1,0:T(8,128)(2,1)S(1)}, bf16[112,896]{1,0:T(8,128)(2,1)S(1)}, u32[]{:S(2)}, u32[]{:S(2)}) collective-permute-start(bf16[112,896]{1,0:T(8,128)(2,1)S(1)} %add.58), channel_id=1, source_target_pairs={{0,1},{1,0},{4,8},{5,9},{8,4},{9,5},{12,13},{13,12},{2,3},{3,2},{6... | collective-permute-start | bytes 602120 | tf_op jit(solution)/shard_map/ppermute | solution.py:259
  18.7 9.2 %collective-permute-start.5 = (bf16[112,896]{1,0:T(8,128)(2,1)S(1)}, bf16[112,896]{1,0:T(8,128)(2,1)S(1)}, u32[]{:S(2)}, u32[]{:S(2)}) collective-permute-start(bf16[112,896]{1,0:T(8,128)(2,1)S(1)} %add_select_fusion.4), channel_id=1, source_target_pairs={{0,4},{4,0},{8,12},{12,8},{1,5},{5,1},{9,13},{13,9},{2,6},{6,2},{1... | collective-permute-start | bytes 602120 | tf_op jit(solution)/shard_map/ppermute | solution.py:256
  22.2 5.8 %collective-permute-start.4 = (bf16[112,896]{1,0:T(8,128)(2,1)S(1)}, bf16[112,896]{1,0:T(8,128)(2,1)S(1)}, u32[]{:S(2)}, u32[]{:S(2)}) collective-permute-start(bf16[112,896]{1,0:T(8,128)(2,1)S(1)} %add.60), channel_id=1, source_target_pairs={{0,1},{1,0},{4,8},{5,9},{8,4},{9,5},{12,13},{13,12},{2,3},{3,2},{6... | collective-permute-start | bytes 602120 | tf_op jit(solution)/shard_map/ppermute | solution.py:259
  22.3 10.0 %collective-permute-start.8 = (bf16[112,896]{1,0:T(8,128)(2,1)S(1)}, bf16[112,896]{1,0:T(8,128)(2,1)S(1)}, u32[]{:S(2)}, u32[]{:S(2)}) collective-permute-start(bf16[112,896]{1,0:T(8,128)(2,1)S(1)} %add_select_fusion.3), channel_id=1, source_target_pairs={{0,4},{4,0},{8,12},{12,8},{1,5},{5,1},{9,13},{13,9},{2,6},{6,2},{1... | collective-permute-start | bytes 602120 | tf_op jit(solution)/shard_map/ppermute | solution.py:256
  28.0 4.6 %collective-permute-start.7 = (bf16[112,896]{1,0:T(8,128)(2,1)S(1)}, bf16[112,896]{1,0:T(8,128)(2,1)S(1)}, u32[]{:S(2)}, u32[]{:S(2)}) collective-permute-start(bf16[112,896]{1,0:T(8,128)(2,1)S(1)} %add.62), channel_id=1, source_target_pairs={{0,1},{1,0},{4,8},{5,9},{8,4},{9,5},{12,13},{13,12},{2,3},{3,2},{6... | collective-permute-start | bytes 602120 | tf_op jit(solution)/shard_map/ppermute | solution.py:259
  28.1 9.1 %collective-permute-start.10 = (bf16[112,896]{1,0:T(8,128)(2,1)S(1)}, bf16[112,896]{1,0:T(8,128)(2,1)S(1)}, u32[]{:S(2)}, u32[]{:S(2)}) collective-permute-start(bf16[112,896]{1,0:T(8,128)(2,1)S(1)} %add_select_fusion.2), channel_id=1, source_target_pairs={{0,4},{4,0},{8,12},{12,8},{1,5},{5,1},{9,13},{13,9},{2,6},{6,2},{1... | collective-permute-start | bytes 602120 | tf_op jit(solution)/shard_map/ppermute | solution.py:256
  32.4 4.9 %collective-permute-start.9 = (bf16[112,896]{1,0:T(8,128)(2,1)S(1)}, bf16[112,896]{1,0:T(8,128)(2,1)S(1)}, u32[]{:S(2)}, u32[]{:S(2)}) collective-permute-start(bf16[112,896]{1,0:T(8,128)(2,1)S(1)} %add.64), channel_id=1, source_target_pairs={{0,1},{1,0},{4,8},{5,9},{8,4},{9,5},{12,13},{13,12},{2,3},{3,2},{6... | collective-permute-start | bytes 602120 | tf_op jit(solution)/shard_map/ppermute | solution.py:259
  32.6 9.1 %collective-permute-start.12 = (bf16[112,896]{1,0:T(8,128)(2,1)S(1)}, bf16[112,896]{1,0:T(8,128)(2,1)S(1)}, u32[]{:S(2)}, u32[]{:S(2)}) collective-permute-start(bf16[112,896]{1,0:T(8,128)(2,1)S(1)} %add_select_fusion.1), channel_id=1, source_target_pairs={{0,4},{4,0},{8,12},{12,8},{1,5},{5,1},{9,13},{13,9},{2,6},{6,2},{1... | collective-permute-start | bytes 602120 | tf_op jit(solution)/shard_map/ppermute | solution.py:256
  37.3 4.6 %collective-permute-start.11 = (bf16[112,896]{1,0:T(8,128)(2,1)S(1)}, bf16[112,896]{1,0:T(8,128)(2,1)S(1)}, u32[]{:S(2)}, u32[]{:S(2)}) collective-permute-start(bf16[112,896]{1,0:T(8,128)(2,1)S(1)} %add.66), channel_id=1, source_target_pairs={{0,1},{1,0},{4,8},{5,9},{8,4},{9,5},{12,13},{13,12},{2,3},{3,2},{6... | collective-permute-start | bytes 602120 | tf_op jit(solution)/shard_map/ppermute | solution.py:259
  37.4 7.9 %collective-permute-start.14 = (bf16[112,896]{1,0:T(8,128)(2,1)S(1)}, bf16[112,896]{1,0:T(8,128)(2,1)S(1)}, u32[]{:S(2)}, u32[]{:S(2)}) collective-permute-start(bf16[112,896]{1,0:T(8,128)(2,1)S(1)} %add_select_fusion), channel_id=1, source_target_pairs={{0,4},{4,0},{8,12},{12,8},{1,5},{5,1},{9,13},{13,9},{2,6},{6,2},{1... | collective-permute-start | bytes 602120 | tf_op jit(solution)/shard_map/ppermute | solution.py:256
  41.8 8.7 %collective-permute-start.13 = (bf16[112,896]{1,0:T(8,128)(2,1)S(1)}, bf16[112,896]{1,0:T(8,128)(2,1)S(1)}, u32[]{:S(2)}, u32[]{:S(2)}) collective-permute-start(bf16[112,896]{1,0:T(8,128)(2,1)S(1)} %add.68), channel_id=1, source_target_pairs={{0,1},{1,0},{4,8},{5,9},{8,4},{9,5},{12,13},{13,12},{2,3},{3,2},{6... | collective-permute-start | bytes 602120 | tf_op jit(solution)/shard_map/ppermute | solution.py:259
  45.3 6.9 %collective-permute-start.15 = (bf16[112,896]{1,0:T(8,128)(2,1)S(1)}, bf16[112,896]{1,0:T(8,128)(2,1)S(1)}, u32[]{:S(2)}, u32[]{:S(2)}) collective-permute-start(bf16[112,896]{1,0:T(8,128)(2,1)S(1)} %add.70), channel_id=1, source_target_pairs={{0,1},{1,0},{4,8},{5,9},{8,4},{9,5},{12,13},{13,12},{2,3},{3,2},{6... | collective-permute-start | bytes 602120 | tf_op jit(solution)/shard_map/ppermute | solution.py:259
  45.4 9.8 %collective-permute-start.16 = (bf16[112,896]{1,0:T(8,128)(2,1)S(1)}, bf16[112,896]{1,0:T(8,128)(2,1)S(1)}, u32[]{:S(2)}, u32[]{:S(2)}) collective-permute-start(bf16[112,896]{1,0:T(8,128)(2,1)S(1)} %add.69), channel_id=1, source_target_pairs={{0,4},{4,0},{8,12},{12,8},{1,5},{5,1},{9,13},{13,9},{2,6},{6,2},{1... | collective-permute-start | bytes 602120 | tf_op jit(solution)/shard_map/ppermute | solution.py:256
  50.6 8.7 %collective-permute-start.17 = (bf16[112,896]{1,0:T(8,128)(2,1)S(1)}, bf16[112,896]{1,0:T(8,128)(2,1)S(1)}, u32[]{:S(2)}, u32[]{:S(2)}) collective-permute-start(bf16[112,896]{1,0:T(8,128)(2,1)S(1)} %add.71), channel_id=1, source_target_pairs={{0,4},{4,0},{8,12},{12,8},{1,5},{5,1},{9,13},{13,9},{2,6},{6,2},{1... | collective-permute-start | bytes 602120 | tf_op jit(solution)/shard_map/ppermute | solution.py:256
  55.3 6.1 %collective-permute-start.18 = (bf16[112,896]{1,0:T(8,128)(2,1)S(1)}, bf16[112,896]{1,0:T(8,128)(2,1)S(1)}, u32[]{:S(2)}, u32[]{:S(2)}) collective-permute-start(bf16[112,896]{1,0:T(8,128)(2,1)S(1)} %add.72), channel_id=1, source_target_pairs={{0,4},{4,0},{8,12},{12,8},{1,5},{5,1},{9,13},{13,9},{2,6},{6,2},{1... | collective-permute-start | bytes 602120 | tf_op jit(solution)/shard_map/ppermute | solution.py:256
  61.8 1.9 %collective-permute-start.19 = (f32[8,220]{1,0:T(8,128)S(1)}, f32[8,220]{1,0:T(8,128)S(1)}, u32[]{:S(2)}, u32[]{:S(2)}) collective-permute-start(f32[8,220]{1,0:T(8,128)S(1)} %reshape.3), channel_id=1, source_target_pairs={{0,1},{1,0},{2,3},{3,2},{4,5},{5,4},{6,7},{7,6},{8,9},{9,8},{10,11... | collective-permute-start | bytes 21128 | tf_op jit(solution)/shard_map/ppermute | solution.py:239
  61.9 3.7 %collective-permute-start.20 = (f32[8,220]{1,0:T(8,128)S(1)}, f32[8,220]{1,0:T(8,128)S(1)}, u32[]{:S(2)}, u32[]{:S(2)}) collective-permute-start(f32[8,220]{1,0:T(8,128)S(1)} %reshape.3), channel_id=1, source_target_pairs={{0,2},{1,3},{2,0},{3,1},{4,6},{5,7},{6,4},{7,5},{8,10},{9,11},{10,... | collective-permute-start | bytes 21128 | tf_op jit(solution)/shard_map/ppermute | solution.py:239
  63.4 3.1 %collective-permute-start.21 = (f32[8,220]{1,0:T(8,128)S(1)}, f32[8,220]{1,0:T(8,128)S(1)}, u32[]{:S(2)}, u32[]{:S(2)}) collective-permute-start(f32[8,220]{1,0:T(8,128)S(1)} %reshape.3), channel_id=1, source_target_pairs={{0,3},{1,2},{2,1},{3,0},{4,7},{5,6},{6,5},{7,4},{8,11},{9,10},{10,... | collective-permute-start | bytes 21128 | tf_op jit(solution)/shard_map/ppermute | solution.py:239

commit v20 on v19

--- a/solution.py
+++ b/solution.py
@@ -134,7 +134,7 @@
     next_copies = []
     if next_rows:
         next_copies = slice_copies(image_ref, map_ref, next_image, next_map, arrived, next_rows)
-    start_all([order_copy, gram_copy, *next_copies])
+    start_all([order_copy, gram_copy, *owner_copies, *next_copies])
 
     if lanes > vols * coils * 2 * length:
         last = slice(lanes - LANE_TILE, lanes)
@@ -173,13 +173,6 @@
                 if slot > 0:
                     shift_re, shift_im = sums[place][0] + shift_re, sums[place][1] + shift_im
                 sums[place] = (shift_re, shift_im)
-        if slot == 0:
-            order_copy.wait()
-            owner = order[group] == lax.axis_index("slc")
-
-            @pl.when(owner)
-            def _():
-                start_all(owner_copies)
 
     gram_copy.wait()
     for place, (sum_re, sum_im) in enumerate(sums):
@@ -190,10 +183,11 @@
             mixed = jnp.where(place_ref[0] > 0, mixed, 0.0)
         total[:, place * 2 * length : (place + 1) * 2 * length] = mixed
 
-    @pl.when(owner)
+    for copy in (order_copy, *owner_copies):
+        copy.wait()
+
+    @pl.when(order[group] == lax.axis_index("slc"))
     def _():
-        for copy in owner_copies:
-            copy.wait()
         for vol in range(vols):
             for coil in range(coils):
                 place = vol * coils + coil

time: 67.5 us -> 67.2 us (level)
  waiting for transfers between devices: 13.9 us -> 12.6 us
  starting transfers between devices: 36.7 us -> 37.8 us
    ppermute x11, waiting for transfers between devices: 11.1 us -> 9.8 us  [outer(): return lax.ppermute(value, 'slc', outer_pairs)]
    ppermute x11, starting transfers between devices: 34.2 us -> 35.3 us  [outer(): return lax.ppermute(value, 'slc', outer_pairs)]
  transfers between devices with their start and end apart: 22 -> 22, of which waited for: 9 -> 7; matrix products, arithmetic and copies ran while one was open for 2% -> 2% of each run, Pallas kernels for 13% -> 14%
where the time goes in v20:
time: 67.2 us; the launch traced here: 66.9 us
  starting transfers between devices  37.8 us (56%)
  Pallas kernels  13.6 us (20%)
  waiting for transfers between devices  12.6 us (19%)
  other arithmetic  1.7 us (3%)
  local copies, waits for them, and re-layouts  0.84 us (1%)
    ppermute x11, starting transfers between devices, outer(): return lax.ppermute(value, 'slc', outer_pairs)  35.3 us
    ppermute x11, waiting for transfers between devices, outer(): return lax.ppermute(value, 'slc', outer_pairs)  9.8 us
    pallas_call x4, Pallas kernels, encode(): pl.pallas_call(functools.partial(encode_kernel, slots, group, rows_of_cla...  9.75 us
    ppermute x3, waiting for transfers between devices, sum_over_replicas(): lax.ppermute(value, axes, [(index, index ^ mask) for index in range(4)])  2.74 us
    pallas_call x8, Pallas kernels, gradient(): pl.pallas_call(functools.partial(gradient_kernel, index, factor, on_line)...  2.13 us
    ppermute x3, starting transfers between devices, sum_over_replicas(): lax.ppermute(value, axes, [(index, index ^ mask) for index in range(4)])  1.93 us
    pallas_call x1, Pallas kernels, body(): pl.pallas_call(functools.partial(fetch_kernel, rows_of_class(0)), in_spec...  1.7 us
  transfers between devices with their start and end apart: 22, of which 7 were waited for; matrix products, arithmetic and copies ran while one was open for 2% of the time, Pallas kernels for 14%

profile of v20, /device:TPU:0, one launch (start us, length us, event | category | flops | bytes accessed | tf_op | source)
XLA Modules:
  0.0 66.9 jit_solution(14641014538746088044)
XLA Ops:
  0.0 1.7 %fetch.1 = (bf16[1,2,220,2,220]{4,3,2,1,0:T(2,128)(2,1)S(1)}, bf16[2,2,220,2,220]{4,3,2,1,0:T(2,128)(2,1)S(1)}, bf16[2,456,220]{2,1,0:T(8,128)(2,1)S(1)}, f32[256,16]{1,0:T(8,128)S(1)}, f32[1,896]{1,0:T(1,128)S(1)}) custom-call(s32[8]{0:T(128)} %refs_0_.1, f32[8,220]{1,0:T(8,128)} %refs_1_.1, bf16[1,8,220,2,220]{4,3,2,1,0:T(2,128)(2,1)} %bitcast.47, ...), custom_call_target="tpu_custom_call" | custom-call | tf_op jit(solution)/shard_map/fetch/pallas_call | solution.py:336
  2.0 2.3 %encode.4 = (bf16[2,224,896]{2,1,0:T(8,128)(2,1)S(1)}, bf16[112,896]{1,0:T(8,128)(2,1)S(1)}, bf16[112,896]{1,0:T(8,128)(2,1)S(1)}, bf16[1,2,220,2,220]{4,3,2,1,0...) custom-call(f32[256,16]{1,0:T(8,128)S(1)} %get-tuple-element.55.refs_0_, bf16[1,2,2,220,220]{4,3,2,1,0:T(8,128)(2,1)S(1)} %bitcast.39, ...), custom_call_target="tpu_custom_call" | custom-call | flops 1022208000 | bytes 6000000 | tf_op jit(solution)/shard_map/encode/pallas_call | solution.py:369
  4.3 3.1 %collective-permute-start = (bf16[112,896]{1,0:T(8,128)(2,1)S(1)}, bf16[112,896]{1,0:T(8,128)(2,1)S(1)}, u32[]{:S(2)}, u32[]{:S(2)}) collective-permute-start(bf16[112,896]{1,0:T(8,128)(2,1)S(1)} %get-tuple-element.83.refs_0_), channel_id=1, source_target_pairs={{0,4},{4,0},{8,12},{12,8},{1,5},{5,1},{9,13},{13,9},{2,6},{6,2},{1... | collective-permute-start | bytes 602120 | tf_op jit(solution)/shard_map/ppermute | solution.py:250
  7.6 2.3 %encode.5 = (bf16[2,224,896]{2,1,0:T(8,128)(2,1)S(1)}, bf16[112,896]{1,0:T(8,128)(2,1)S(1)}, bf16[112,896]{1,0:T(8,128)(2,1)S(1)}, bf16[1,2,220,2,220]{4,3,2,1,0...) custom-call(f32[256,16]{1,0:T(8,128)S(1)} %get-tuple-element.55.refs_0_, bf16[1,2,2,220,220]{4,3,2,1,0:T(8,128)(2,1)S(1)} %bitcast.40, ...), custom_call_target="tpu_custom_call" | custom-call | flops 1022208000 | bytes 6000000 | tf_op jit(solution)/shard_map/encode/pallas_call | solution.py:369
  9.9 0.4 collective-permute-start.3
  10.5 2.3 %encode.6 = (bf16[2,224,896]{2,1,0:T(8,128)(2,1)S(1)}, bf16[112,896]{1,0:T(8,128)(2,1)S(1)}, bf16[112,896]{1,0:T(8,128)(2,1)S(1)}, bf16[1,2,220,2,220]{4,3,2,1,0...) custom-call(f32[256,16]{1,0:T(8,128)S(1)} %get-tuple-element.55.refs_0_, bf16[1,2,2,220,220]{4,3,2,1,0:T(8,128)(2,1)S(1)} %bitcast.41, ...), custom_call_target="tpu_custom_call" | custom-call | flops 1022208000 | bytes 6000000 | tf_op jit(solution)/shard_map/encode/pallas_call | solution.py:369
  13.2 3.6 %collective-permute-start.1 = (bf16[112,896]{1,0:T(8,128)(2,1)S(1)}, bf16[112,896]{1,0:T(8,128)(2,1)S(1)}, u32[]{:S(2)}, u32[]{:S(2)}) collective-permute-start(bf16[112,896]{1,0:T(8,128)(2,1)S(1)} %get-tuple-element.91.refs_0_), channel_id=1, source_target_pairs={{0,4},{4,0},{8,12},{12,8},{1,5},{5,1},{9,13},{13,9},{2,6},{6,2},{1... | collective-permute-start | bytes 602120 | tf_op jit(solution)/shard_map/ppermute | solution.py:250
  16.9 2.8 %encode.7 = (bf16[2,224,896]{2,1,0:T(8,128)(2,1)S(1)}, bf16[112,896]{1,0:T(8,128)(2,1)S(1)}, bf16[112,896]{1,0:T(8,128)(2,1)S(1)}) custom-call(f32[256,16]{1,0:T(8,128)S(1)} %get-tuple-element.55.refs_0_, bf16[1,2,2,220,220]{4,3,2,1,0:T(8,128)(2,1)S(1)} %bitcast.38, bf16[2,2,2,220,220]{4,3,2,1,0:T(8,128)(2,1)S(1)} %bitcast.34, ...), custom_call_target="tpu_custom_call" | custom-call | flops 1022208000 | bytes 6000000 | tf_op jit(solution)/shard_map/encode/pallas_call | solution.py:369
  19.9 1.8 %collective-permute-start.5 = (bf16[112,896]{1,0:T(8,128)(2,1)S(1)}, bf16[112,896]{1,0:T(8,128)(2,1)S(1)}, u32[]{:S(2)}, u32[]{:S(2)}) collective-permute-start(bf16[112,896]{1,0:T(8,128)(2,1)S(1)} %add_select_fusion.4), channel_id=1, source_target_pairs={{0,4},{4,0},{8,12},{12,8},{1,5},{5,1},{9,13},{13,9},{2,6},{6,2},{1... | collective-permute-start | bytes 602120 | tf_op jit(solution)/shard_map/ppermute | solution.py:250
  21.9 5.9 %collective-permute-start.8 = (bf16[112,896]{1,0:T(8,128)(2,1)S(1)}, bf16[112,896]{1,0:T(8,128)(2,1)S(1)}, u32[]{:S(2)}, u32[]{:S(2)}) collective-permute-start(bf16[112,896]{1,0:T(8,128)(2,1)S(1)} %add_select_fusion.3), channel_id=1, source_target_pairs={{0,4},{4,0},{8,12},{12,8},{1,5},{5,1},{9,13},{13,9},{2,6},{6,2},{1... | collective-permute-start | bytes 602120 | tf_op jit(solution)/shard_map/ppermute | solution.py:250
  28.0 4.1 %collective-permute-start.10 = (bf16[112,896]{1,0:T(8,128)(2,1)S(1)}, bf16[112,896]{1,0:T(8,128)(2,1)S(1)}, u32[]{:S(2)}, u32[]{:S(2)}) collective-permute-start(bf16[112,896]{1,0:T(8,128)(2,1)S(1)} %add_select_fusion.2), channel_id=1, source_target_pairs={{0,4},{4,0},{8,12},{12,8},{1,5},{5,1},{9,13},{13,9},{2,6},{6,2},{1... | collective-permute-start | bytes 602120 | tf_op jit(solution)/shard_map/ppermute | solution.py:250
  32.3 4.4 %collective-permute-start.12 = (bf16[112,896]{1,0:T(8,128)(2,1)S(1)}, bf16[112,896]{1,0:T(8,128)(2,1)S(1)}, u32[]{:S(2)}, u32[]{:S(2)}) collective-permute-start(bf16[112,896]{1,0:T(8,128)(2,1)S(1)} %add_select_fusion.1), channel_id=1, source_target_pairs={{0,4},{4,0},{8,12},{12,8},{1,5},{5,1},{9,13},{13,9},{2,6},{6,2},{1... | collective-permute-start | bytes 602120 | tf_op jit(solution)/shard_map/ppermute | solution.py:250
  36.9 4.4 %collective-permute-start.14 = (bf16[112,896]{1,0:T(8,128)(2,1)S(1)}, bf16[112,896]{1,0:T(8,128)(2,1)S(1)}, u32[]{:S(2)}, u32[]{:S(2)}) collective-permute-start(bf16[112,896]{1,0:T(8,128)(2,1)S(1)} %add_select_fusion), channel_id=1, source_target_pairs={{0,4},{4,0},{8,12},{12,8},{1,5},{5,1},{9,13},{13,9},{2,6},{6,2},{1... | collective-permute-start | bytes 602120 | tf_op jit(solution)/shard_map/ppermute | solution.py:250
  41.7 3.4 %collective-permute-done.14.refs_3_.refs_1_ = bf16[112,896]{1,0:T(8,128)(2,1)S(1)} collective-permute-done((bf16[112,896]{1,0:T(8,128)(2,1)S(1)}, bf16[112,896]{1,0:T(8,128)(2,1)S(1)}, u32[]{:S(2)}, u32[]{:S(2)}) %collective-permute-start.14) | collective-permute-done | bytes 200736 | tf_op jit(solution)/shard_map/ppermute | solution.py:250
  45.2 3.8 %collective-permute-start.16 = (bf16[112,896]{1,0:T(8,128)(2,1)S(1)}, bf16[112,896]{1,0:T(8,128)(2,1)S(1)}, u32[]{:S(2)}, u32[]{:S(2)}) collective-permute-start(bf16[112,896]{1,0:T(8,128)(2,1)S(1)} %add.69), channel_id=1, source_target_pairs={{0,4},{4,0},{8,12},{12,8},{1,5},{5,1},{9,13},{13,9},{2,6},{6,2},{1... | collective-permute-start | bytes 602120 | tf_op jit(solution)/shard_map/ppermute | solution.py:250
  50.2 1.7 %collective-permute-start.17 = (bf16[112,896]{1,0:T(8,128)(2,1)S(1)}, bf16[112,896]{1,0:T(8,128)(2,1)S(1)}, u32[]{:S(2)}, u32[]{:S(2)}) collective-permute-start(bf16[112,896]{1,0:T(8,128)(2,1)S(1)} %add.71), channel_id=1, source_target_pairs={{0,4},{4,0},{8,12},{12,8},{1,5},{5,1},{9,13},{13,9},{2,6},{6,2},{1... | collective-permute-start | bytes 602120 | tf_op jit(solution)/shard_map/ppermute | solution.py:250
  51.8 3.0 %collective-permute-done.16.refs_3_ = bf16[112,896]{1,0:T(8,128)(2,1)S(1)} collective-permute-done((bf16[112,896]{1,0:T(8,128)(2,1)S(1)}, bf16[112,896]{1,0:T(8,128)(2,1)S(1)}, u32[]{:S(2)}, u32[]{:S(2)}) %collective-permute-start.16) | collective-permute-done | bytes 200736 | tf_op jit(solution)/shard_map/ppermute | solution.py:250
  54.9 2.0 %collective-permute-start.18 = (bf16[112,896]{1,0:T(8,128)(2,1)S(1)}, bf16[112,896]{1,0:T(8,128)(2,1)S(1)}, u32[]{:S(2)}, u32[]{:S(2)}) collective-permute-start(bf16[112,896]{1,0:T(8,128)(2,1)S(1)} %add.72), channel_id=1, source_target_pairs={{0,4},{4,0},{8,12},{12,8},{1,5},{5,1},{9,13},{13,9},{2,6},{6,2},{1... | collective-permute-start | bytes 602120 | tf_op jit(solution)/shard_map/ppermute | solution.py:250
  57.6 1.4 %collective-permute-done.17.refs_3_ = bf16[112,896]{1,0:T(8,128)(2,1)S(1)} collective-permute-done((bf16[112,896]{1,0:T(8,128)(2,1)S(1)}, bf16[112,896]{1,0:T(8,128)(2,1)S(1)}, u32[]{:S(2)}, u32[]{:S(2)}) %collective-permute-start.17) | collective-permute-done | bytes 200736 | tf_op jit(solution)/shard_map/ppermute | solution.py:250
  59.3 1.9 %collective-permute-done.18.refs_3_ = bf16[112,896]{1,0:T(8,128)(2,1)S(1)} collective-permute-done((bf16[112,896]{1,0:T(8,128)(2,1)S(1)}, bf16[112,896]{1,0:T(8,128)(2,1)S(1)}, u32[]{:S(2)}, u32[]{:S(2)}) %collective-permute-start.18) | collective-permute-done | bytes 200736 | tf_op jit(solution)/shard_map/ppermute | solution.py:250
  61.7 1.5 %collective-permute-start.20 = (f32[8,220]{1,0:T(8,128)S(1)}, f32[8,220]{1,0:T(8,128)S(1)}, u32[]{:S(2)}, u32[]{:S(2)}) collective-permute-start(f32[8,220]{1,0:T(8,128)S(1)} %reshape.3), channel_id=1, source_target_pairs={{0,2},{1,3},{2,0},{3,1},{4,6},{5,7},{6,4},{7,5},{8,10},{9,11},{10,... | collective-permute-start | bytes 21128 | tf_op jit(solution)/shard_map/ppermute | solution.py:233
  63.5 1.9 %collective-permute-done.20 = f32[8,220]{1,0:T(8,128)S(1)} collective-permute-done((f32[8,220]{1,0:T(8,128)S(1)}, f32[8,220]{1,0:T(8,128)S(1)}, u32[]{:S(2)}, u32[]{:S(2)}) %collective-permute-start.20) | collective-permute-done | bytes 7072 | tf_op jit(solution)/shard_map/ppermute | solution.py:233
  65.4 0.9 %collective-permute-done.21 = f32[8,220]{1,0:T(8,128)S(1)} collective-permute-done((f32[8,220]{1,0:T(8,128)S(1)}, f32[8,220]{1,0:T(8,128)S(1)}, u32[]{:S(2)}, u32[]{:S(2)}) %collective-permute-start.21) | collective-permute-done | bytes 7072 | tf_op jit(solution)/shard_map/ppermute | solution.py:233
  66.3 0.6 add_add_fusion
  (69 shorter events, 5.2 us)
Async XLA Ops:
  0.0 1.9 %copy-start = (bf16[1,1,2,2,220,220]{5,3,4,2,1,0:T(2,128)(2,1)S(1)}, bf16[1,1,2,2,220,220]{5,3,4,2,1,0:T(2,128)(2,1)}, u32[]{:S(2)}) copy-start(bf16[1,1,2,2,220,220]{5,3,4,2,1,0:T(2,128)(2,1)} %param.11) | copy-start | bytes 1161604
  4.3 8.8 %collective-permute-start = (bf16[112,896]{1,0:T(8,128)(2,1)S(1)}, bf16[112,896]{1,0:T(8,128)(2,1)S(1)}, u32[]{:S(2)}, u32[]{:S(2)}) collective-permute-start(bf16[112,896]{1,0:T(8,128)(2,1)S(1)} %get-tuple-element.83.refs_0_), channel_id=1, source_target_pairs={{0,4},{4,0},{8,12},{12,8},{1,5},{5,1},{9,13},{13,9},{2,6},{6,2},{1... | collective-permute-start | bytes 602120 | tf_op jit(solution)/shard_map/ppermute | solution.py:250
  9.9 9.8 %collective-permute-start.3 = (bf16[112,896]{1,0:T(8,128)(2,1)S(1)}, bf16[112,896]{1,0:T(8,128)(2,1)S(1)}, u32[]{:S(2)}, u32[]{:S(2)}) collective-permute-start(bf16[112,896]{1,0:T(8,128)(2,1)S(1)} %get-tuple-element.88.refs_0_), channel_id=1, source_target_pairs={{0,4},{4,0},{8,12},{12,8},{1,5},{5,1},{9,13},{13,9},{2,6},{6,2},{1... | collective-permute-start | bytes 602120 | tf_op jit(solution)/shard_map/ppermute | solution.py:250
  13.1 6.7 %collective-permute-start.2 = (bf16[112,896]{1,0:T(8,128)(2,1)S(1)}, bf16[112,896]{1,0:T(8,128)(2,1)S(1)}, u32[]{:S(2)}, u32[]{:S(2)}) collective-permute-start(bf16[112,896]{1,0:T(8,128)(2,1)S(1)} %add.57), channel_id=1, source_target_pairs={{0,1},{1,0},{4,8},{5,9},{8,4},{9,5},{12,13},{13,12},{2,3},{3,2},{6... | collective-permute-start | bytes 602120 | tf_op jit(solution)/shard_map/ppermute | solution.py:253
  13.2 8.5 %collective-permute-start.1 = (bf16[112,896]{1,0:T(8,128)(2,1)S(1)}, bf16[112,896]{1,0:T(8,128)(2,1)S(1)}, u32[]{:S(2)}, u32[]{:S(2)}) collective-permute-start(bf16[112,896]{1,0:T(8,128)(2,1)S(1)} %get-tuple-element.91.refs_0_), channel_id=1, source_target_pairs={{0,4},{4,0},{8,12},{12,8},{1,5},{5,1},{9,13},{13,9},{2,6},{6,2},{1... | collective-permute-start | bytes 602120 | tf_op jit(solution)/shard_map/ppermute | solution.py:250
  19.8 2.1 %collective-permute-start.6 = (bf16[112,896]{1,0:T(8,128)(2,1)S(1)}, bf16[112,896]{1,0:T(8,128)(2,1)S(1)}, u32[]{:S(2)}, u32[]{:S(2)}) collective-permute-start(bf16[112,896]{1,0:T(8,128)(2,1)S(1)} %add.58), channel_id=1, source_target_pairs={{0,1},{1,0},{4,8},{5,9},{8,4},{9,5},{12,13},{13,12},{2,3},{3,2},{6... | collective-permute-start | bytes 602120 | tf_op jit(solution)/shard_map/ppermute | solution.py:253
  19.9 7.9 %collective-permute-start.5 = (bf16[112,896]{1,0:T(8,128)(2,1)S(1)}, bf16[112,896]{1,0:T(8,128)(2,1)S(1)}, u32[]{:S(2)}, u32[]{:S(2)}) collective-permute-start(bf16[112,896]{1,0:T(8,128)(2,1)S(1)} %add_select_fusion.4), channel_id=1, source_target_pairs={{0,4},{4,0},{8,12},{12,8},{1,5},{5,1},{9,13},{13,9},{2,6},{6,2},{1... | collective-permute-start | bytes 602120 | tf_op jit(solution)/shard_map/ppermute | solution.py:250
  21.8 6.2 %collective-permute-start.4 = (bf16[112,896]{1,0:T(8,128)(2,1)S(1)}, bf16[112,896]{1,0:T(8,128)(2,1)S(1)}, u32[]{:S(2)}, u32[]{:S(2)}) collective-permute-start(bf16[112,896]{1,0:T(8,128)(2,1)S(1)} %add.60), channel_id=1, source_target_pairs={{0,1},{1,0},{4,8},{5,9},{8,4},{9,5},{12,13},{13,12},{2,3},{3,2},{6... | collective-permute-start | bytes 602120 | tf_op jit(solution)/shard_map/ppermute | solution.py:253
  21.9 10.2 %collective-permute-start.8 = (bf16[112,896]{1,0:T(8,128)(2,1)S(1)}, bf16[112,896]{1,0:T(8,128)(2,1)S(1)}, u32[]{:S(2)}, u32[]{:S(2)}) collective-permute-start(bf16[112,896]{1,0:T(8,128)(2,1)S(1)} %add_select_fusion.3), channel_id=1, source_target_pairs={{0,4},{4,0},{8,12},{12,8},{1,5},{5,1},{9,13},{13,9},{2,6},{6,2},{1... | collective-permute-start | bytes 602120 | tf_op jit(solution)/shard_map/ppermute | solution.py:250
  27.9 4.4 %collective-permute-start.7 = (bf16[112,896]{1,0:T(8,128)(2,1)S(1)}, bf16[112,896]{1,0:T(8,128)(2,1)S(1)}, u32[]{:S(2)}, u32[]{:S(2)}) collective-permute-start(bf16[112,896]{1,0:T(8,128)(2,1)S(1)} %add.62), channel_id=1, source_target_pairs={{0,1},{1,0},{4,8},{5,9},{8,4},{9,5},{12,13},{13,12},{2,3},{3,2},{6... | collective-permute-start | bytes 602120 | tf_op jit(solution)/shard_map/ppermute | solution.py:253
  28.0 8.7 %collective-permute-start.10 = (bf16[112,896]{1,0:T(8,128)(2,1)S(1)}, bf16[112,896]{1,0:T(8,128)(2,1)S(1)}, u32[]{:S(2)}, u32[]{:S(2)}) collective-permute-start(bf16[112,896]{1,0:T(8,128)(2,1)S(1)} %add_select_fusion.2), channel_id=1, source_target_pairs={{0,4},{4,0},{8,12},{12,8},{1,5},{5,1},{9,13},{13,9},{2,6},{6,2},{1... | collective-permute-start | bytes 602120 | tf_op jit(solution)/shard_map/ppermute | solution.py:250
  32.2 4.7 %collective-permute-start.9 = (bf16[112,896]{1,0:T(8,128)(2,1)S(1)}, bf16[112,896]{1,0:T(8,128)(2,1)S(1)}, u32[]{:S(2)}, u32[]{:S(2)}) collective-permute-start(bf16[112,896]{1,0:T(8,128)(2,1)S(1)} %add.64), channel_id=1, source_target_pairs={{0,1},{1,0},{4,8},{5,9},{8,4},{9,5},{12,13},{13,12},{2,3},{3,2},{6... | collective-permute-start | bytes 602120 | tf_op jit(solution)/shard_map/ppermute | solution.py:253
  32.3 9.2 %collective-permute-start.12 = (bf16[112,896]{1,0:T(8,128)(2,1)S(1)}, bf16[112,896]{1,0:T(8,128)(2,1)S(1)}, u32[]{:S(2)}, u32[]{:S(2)}) collective-permute-start(bf16[112,896]{1,0:T(8,128)(2,1)S(1)} %add_select_fusion.1), channel_id=1, source_target_pairs={{0,4},{4,0},{8,12},{12,8},{1,5},{5,1},{9,13},{13,9},{2,6},{6,2},{1... | collective-permute-start | bytes 602120 | tf_op jit(solution)/shard_map/ppermute | solution.py:250
  36.8 4.8 %collective-permute-start.11 = (bf16[112,896]{1,0:T(8,128)(2,1)S(1)}, bf16[112,896]{1,0:T(8,128)(2,1)S(1)}, u32[]{:S(2)}, u32[]{:S(2)}) collective-permute-start(bf16[112,896]{1,0:T(8,128)(2,1)S(1)} %add.66), channel_id=1, source_target_pairs={{0,1},{1,0},{4,8},{5,9},{8,4},{9,5},{12,13},{13,12},{2,3},{3,2},{6... | collective-permute-start | bytes 602120 | tf_op jit(solution)/shard_map/ppermute | solution.py:253
  36.9 8.1 %collective-permute-start.14 = (bf16[112,896]{1,0:T(8,128)(2,1)S(1)}, bf16[112,896]{1,0:T(8,128)(2,1)S(1)}, u32[]{:S(2)}, u32[]{:S(2)}) collective-permute-start(bf16[112,896]{1,0:T(8,128)(2,1)S(1)} %add_select_fusion), channel_id=1, source_target_pairs={{0,4},{4,0},{8,12},{12,8},{1,5},{5,1},{9,13},{13,9},{2,6},{6,2},{1... | collective-permute-start | bytes 602120 | tf_op jit(solution)/shard_map/ppermute | solution.py:250
  41.5 8.6 %collective-permute-start.13 = (bf16[112,896]{1,0:T(8,128)(2,1)S(1)}, bf16[112,896]{1,0:T(8,128)(2,1)S(1)}, u32[]{:S(2)}, u32[]{:S(2)}) collective-permute-start(bf16[112,896]{1,0:T(8,128)(2,1)S(1)} %add.68), channel_id=1, source_target_pairs={{0,1},{1,0},{4,8},{5,9},{8,4},{9,5},{12,13},{13,12},{2,3},{3,2},{6... | collective-permute-start | bytes 602120 | tf_op jit(solution)/shard_map/ppermute | solution.py:253
  45.1 6.7 %collective-permute-start.15 = (bf16[112,896]{1,0:T(8,128)(2,1)S(1)}, bf16[112,896]{1,0:T(8,128)(2,1)S(1)}, u32[]{:S(2)}, u32[]{:S(2)}) collective-permute-start(bf16[112,896]{1,0:T(8,128)(2,1)S(1)} %add.70), channel_id=1, source_target_pairs={{0,1},{1,0},{4,8},{5,9},{8,4},{9,5},{12,13},{13,12},{2,3},{3,2},{6... | collective-permute-start | bytes 602120 | tf_op jit(solution)/shard_map/ppermute | solution.py:253
  45.2 9.7 %collective-permute-start.16 = (bf16[112,896]{1,0:T(8,128)(2,1)S(1)}, bf16[112,896]{1,0:T(8,128)(2,1)S(1)}, u32[]{:S(2)}, u32[]{:S(2)}) collective-permute-start(bf16[112,896]{1,0:T(8,128)(2,1)S(1)} %add.69), channel_id=1, source_target_pairs={{0,4},{4,0},{8,12},{12,8},{1,5},{5,1},{9,13},{13,9},{2,6},{6,2},{1... | collective-permute-start | bytes 602120 | tf_op jit(solution)/shard_map/ppermute | solution.py:250
  50.2 8.9 %collective-permute-start.17 = (bf16[112,896]{1,0:T(8,128)(2,1)S(1)}, bf16[112,896]{1,0:T(8,128)(2,1)S(1)}, u32[]{:S(2)}, u32[]{:S(2)}) collective-permute-start(bf16[112,896]{1,0:T(8,128)(2,1)S(1)} %add.71), channel_id=1, source_target_pairs={{0,4},{4,0},{8,12},{12,8},{1,5},{5,1},{9,13},{13,9},{2,6},{6,2},{1... | collective-permute-start | bytes 602120 | tf_op jit(solution)/shard_map/ppermute | solution.py:250
  54.9 6.3 %collective-permute-start.18 = (bf16[112,896]{1,0:T(8,128)(2,1)S(1)}, bf16[112,896]{1,0:T(8,128)(2,1)S(1)}, u32[]{:S(2)}, u32[]{:S(2)}) collective-permute-start(bf16[112,896]{1,0:T(8,128)(2,1)S(1)} %add.72), channel_id=1, source_target_pairs={{0,4},{4,0},{8,12},{12,8},{1,5},{5,1},{9,13},{13,9},{2,6},{6,2},{1... | collective-permute-start | bytes 602120 | tf_op jit(solution)/shard_map/ppermute | solution.py:250
  61.6 1.9 %collective-permute-start.19 = (f32[8,220]{1,0:T(8,128)S(1)}, f32[8,220]{1,0:T(8,128)S(1)}, u32[]{:S(2)}, u32[]{:S(2)}) collective-permute-start(f32[8,220]{1,0:T(8,128)S(1)} %reshape.3), channel_id=1, source_target_pairs={{0,1},{1,0},{2,3},{3,2},{4,5},{5,4},{6,7},{7,6},{8,9},{9,8},{10,11... | collective-permute-start | bytes 21128 | tf_op jit(solution)/shard_map/ppermute | solution.py:233
  61.7 3.7 %collective-permute-start.20 = (f32[8,220]{1,0:T(8,128)S(1)}, f32[8,220]{1,0:T(8,128)S(1)}, u32[]{:S(2)}, u32[]{:S(2)}) collective-permute-start(f32[8,220]{1,0:T(8,128)S(1)} %reshape.3), channel_id=1, source_target_pairs={{0,2},{1,3},{2,0},{3,1},{4,6},{5,7},{6,4},{7,5},{8,10},{9,11},{10,... | collective-permute-start | bytes 21128 | tf_op jit(solution)/shard_map/ppermute | solution.py:233
  63.2 3.1 %collective-permute-start.21 = (f32[8,220]{1,0:T(8,128)S(1)}, f32[8,220]{1,0:T(8,128)S(1)}, u32[]{:S(2)}, u32[]{:S(2)}) collective-permute-start(f32[8,220]{1,0:T(8,128)S(1)} %reshape.3), channel_id=1, source_target_pairs={{0,3},{1,2},{2,1},{3,0},{4,7},{5,6},{6,5},{7,4},{8,11},{9,10},{10,... | collective-permute-start | bytes 21128 | tf_op jit(solution)/shard_map/ppermute | solution.py:233
